TPU v7x, 32 devices: a whole 2x2x4 slice. The times are simulated.
32 devices in a mesh: groups: 2 (over y), seq: 4 (over z), chan: 2 (over x), sub: 2 (over core).
Axes of the slice: x: 2, y: 2, z: 4, core: 2. Of those that a mesh axis runs over, the one named last changes fastest.
Arguments:
- tokens: bfloat16 [16384, 2048], P(('groups', 'seq', 'sub'), 'chan'), parts along dimension 0, may hold values from -6 to 6
- low_angle: float32 [2048], P('chan'), may hold values from 0.1 to 1.47
- high_taps: float32 [2, 2048], P(None, 'chan'), may hold values from -3 to 3
- level_mix: float32 [17, 2048], P(None, 'chan'), may hold values from -1.5 to 1.5
- w_value: bfloat16 [2048, 2048], P(None, 'chan'), may hold values from -0.125 to 0.125
- w_gate: bfloat16 [2048, 2048], P(None, 'chan'), may hold values from -0.125 to 0.125
- out_weight: bfloat16 [2048, 2048], P(None, 'chan'), may hold values from -0.125 to 0.125
Outputs:
- result: bfloat16 [16384, 2048], P(('groups', 'seq', 'sub'), 'chan'), parts along dimension 0
There are 2 independent parts, one for each index of `groups`. A program takes and returns all parts, laid end to end along the dimension named above; an argument that names none is the same for every part. Nothing has to cross between parts.
All inputs are finite; a program needn't handle non-finite values.
Results may differ from a plain program's by a relative error of at most 0.0043.
Values may be sent and summed in bfloat16 or wider, within the bound.
No kernel may reach another device: no remote copies, remote signals or barrier semaphores. Data moves between devices by JAX's collectives and lax.ppermute only.
A program may use at most 128 MiB of HBM per device.

v0:
```python
import jax
import jax.numpy as jnp
from jax import lax
from jax.sharding import PartitionSpec as P

LEVELS = 15


def run_levels(stream, shifter, low0, low1, high0, high1, mix):
    mixed = mix[LEVELS + 1] * stream
    for level in range(LEVELS):
        shifted = shifter(stream, 2**level)
        high = high0 * stream + high1 * shifted
        stream = low0 * stream + low1 * shifted
        mixed = mixed + mix[level] * high
    return mixed + mix[LEVELS] * stream


def shards(tokens, low_angle, high_taps, level_mix, w_value, w_gate, out_weight):
    rows = tokens.shape[0]
    channels = tokens.shape[1]
    ways = lax.axis_size(("seq", "sub"))
    total = rows * ways
    narrow = channels // ways
    place = lax.axis_index(("seq", "sub")) * narrow
    columns = lax.all_to_all(tokens.T, ("seq", "sub"), split_axis=0, concat_axis=1, tiled=True)
    angle = lax.dynamic_slice_in_dim(low_angle, place, narrow, 0)[:, None]
    high_pair = lax.dynamic_slice_in_dim(high_taps, place, narrow, 1)[:, :, None]
    mix = lax.dynamic_slice_in_dim(level_mix, place, narrow, 1)[:, :, None]

    def shifter(stream, reach):
        if reach >= total:
            return jnp.zeros_like(stream)
        return jnp.concatenate(
            [jnp.zeros((stream.shape[0], reach), jnp.float32), stream[:, : total - reach]], 1
        )

    mixed = run_levels(
        columns.astype(jnp.float32),
        shifter,
        jnp.cos(angle),
        jnp.sin(angle),
        high_pair[0],
        high_pair[1],
        mix,
    )
    filtered = jax.nn.gelu(mixed).astype(jnp.bfloat16)
    activated = lax.all_to_all(filtered, ("seq", "sub"), split_axis=1, concat_axis=0, tiled=True).T
    piece = lax.all_gather(activated, "chan", axis=1, tiled=True)
    value = jnp.dot(piece, w_value, preferred_element_type=jnp.float32)
    gate = jnp.dot(piece, w_gate, preferred_element_type=jnp.float32)
    hidden = (value * jax.nn.sigmoid(gate)).astype(jnp.bfloat16)
    projected = jnp.dot(
        lax.all_gather(hidden, "chan", axis=1, tiled=True),
        out_weight,
        preferred_element_type=jnp.float32,
    )
    return (projected + tokens.astype(jnp.float32)).astype(jnp.bfloat16)


def solution(mesh):
    return jax.shard_map(
        shards,
        mesh=mesh,
        in_specs=(
            P(("groups", "seq", "sub"), "chan"),
            P("chan"),
            P(None, "chan"),
            P(None, "chan"),
            P(None, "chan"),
            P(None, "chan"),
            P(None, "chan"),
        ),
        out_specs=P(("groups", "seq", "sub"), "chan"),
        check_vma=False,
    )
```

profile of v0, /device:TPU:0, one launch (start us, length us, event | category | flops | bytes accessed | tf_op | source)
XLA Modules:
  0.0 332.8 jit_solution(4042924887279281980)
XLA Ops:
  6.5 3.9 %copy.9 = bf16[1024,1024]{0,1:T(8,128)(2,1)} copy(bf16[1024,1024]{1,0:T(8,128)(2,1)} %param.7) | data formatting | bytes 4194304 | tf_op args[0]
  10.5 6.3 %all-to-all-start = ((bf16[8,128,1024]{2,1,0:T(8,128)(2,1)}), bf16[8,128,1024]{2,1,0:T(8,128)(2,1)S(1)}, u32[]{:S(2)}, u32[]{:S(2)}) async-start(bf16[8,128,1024]{2,1,0:T(8,128)(2,1)} %bitcast.71), calls=%async_computation | async-start | bytes 4194304 | tf_op jit(solution)/shard_map/all_to_all | solution.py:26
  16.9 1.1 dynamic-slice_bitcast_fusion.16
  18.0 0.8 broadcast_multiply_fusion
  18.8 47.0 %all-to-all-done = bf16[8,128,1024]{2,1,0:T(8,128)(2,1)S(1)} async-done(((bf16[8,128,1024]{2,1,0:T(8,128)(2,1)}), bf16[8,128,1024]{2,1,0:T(8,128)(2,1)S(1)}, u32[]{:S(2)}, u32[]{:S(2)}) %all-to-all-start) | async-done | bytes 2097184 | tf_op jit(solution)/shard_map/all_to_all | solution.py:26
  65.9 2.5 convert_bitcast_fusion
  68.4 5.3 %copy.10 = f32[128,8,1024]{0,2,1:T(8,128)} copy(f32[128,8,1024]{2,0,1:T(8,128)} %convert_bitcast_fusion) | data formatting | bytes 8388608 | tf_op jit(solution)/shard_map/convert_element_type | solution.py:39
  73.7 4.2 %multiply_add_fusion.9 = f32[128,8192]{0,1:T(8,128)S(1)} fusion(f32[128,8191]{0,1:T(8,128)} %bitcast.66, f32[128]{0:T(128)S(1)} %get-tuple-element.6, f32[128]{0:T(128)S(1)} %get-tuple-element.24, f32[128,8,1024]{0,2,1:T(8,128)} %copy.10), kind=kLoop, calls=%fused_computation.42 | loop fusion | flops 3145728 | bytes 12583424 | tf_op jit(solution)/shard_map/add | solution.py:14
  77.8 0.7 multiply_add_fusion.8
  78.5 1.4 multiply_add_fusion.7
  79.9 0.6 copy-done.12
  80.5 0.3 slice.150
  80.8 2.2 copy-done.13
  83.0 0.4 multiply_add_fusion.6
  83.5 0.4 copy-done.7
  83.8 0.3 slice.151
  84.1 0.4 multiply_add_fusion.5
  84.5 0.3 slice.152
  84.8 1.0 copy-done.3
  85.8 1.3 copy-done.8
  87.1 0.8 multiply_add_fusion.4
  87.9 1.1 copy-done.14
  89.0 0.3 slice.153
  89.3 0.4 multiply_add_fusion.3
  89.7 0.3 slice.154
  90.0 1.0 copy-done.4
  91.0 1.2 copy-done.9
  92.2 0.8 multiply_add_fusion.2
  93.0 1.2 copy-done.15
  94.3 0.3 slice.155
  94.5 0.4 multiply_add_fusion.1
  95.2 1.0 copy-done.5
  96.2 1.3 copy-done.10
  97.5 0.8 multiply_add_fusion
  98.3 1.0 copy-done.16
  99.6 0.4 fusion.8
  100.3 1.1 copy-done.6
  101.4 1.1 copy-done.11
  102.5 2.9 fusion.11
  105.4 3.2 slice.159
  108.6 26.0 %fusion.22 = bf16[128,8192]{0,1:T(8,128)(2,1)} fusion(f32[128,4096]{0,1:T(8,128)} %slice.159, f32[128,6144]{0,1:T(8,128)} %copy-done.17, f32[128,7168]{0,1:T(8,128)} %copy-done.11, f32[128,8192]{0,1:T(8,128)} %copy-done.6, f32[128,8192]{0,1:T(8,128)} %copy-done.5, f32[128,8192]{0,1:T(8,128)} %copy-done.4, f32[128,8192]{0,1:T(8,128)} %copy-done.3, ...), kind=kLoop, calls=%fused_computation.29 | loop fusion | flops 115343360 | bytes 81801216 | tf_op jit(solution)/shard_map/convert_element_type | solution.py:47
  134.7 2.9 copy.11
  137.5 52.2 %all_to_all.32 = bf16[128,8,1024]{2,0,1:T(8,128)(2,1)} all-to-all(bf16[128,8,1024]{2,0,1:T(8,128)(2,1)S(1)} %copy.11), channel_id=1, replica_groups=mesh['groups'=2,'seq'=4,'chan'=2,'sub'=2] {'seq','sub'}, dimensions={1} | all-to-all | bytes 4194304 | tf_op jit(solution)/shard_map/all_to_all | solution.py:48
  189.8 55.8 %all-gather.3.cloned.1.call-done = bf16[1024,2048]{0,1:T(8,128)(2,1)} async-done(((bf16[1024,1024]{0,1:T(8,128)(2,1)}), bf16[1024,2048]{0,1:T(8,128)(2,1)}) %all-gather.3.cloned.1.call-update) | async-done | bytes 4194320 | tf_op jit(solution)/shard_map/all_gather | solution.py:49
  245.6 7.7 %fusion.23 = f32[1024,1024]{1,0:T(8,128)S(1)} fusion(bf16[1024,2048]{0,1:T(8,128)(2,1)} %all-gather.3.cloned.1.call-done, bf16[2048,1024]{1,0:T(8,128)(2,1)} %param.11), kind=kOutput, calls=%fused_computation.67 | convolution fusion | flops 4294967296 | bytes 12582912 | tf_op jit(solution)/shard_map/dot_general | solution.py:50
  253.4 6.4 %multiply_convert_fusion = bf16[1024,1024]{1,0:T(8,128)(2,1)} fusion(f32[1024,1024]{1,0:T(8,128)S(1)} %fusion.23, bf16[1024,2048]{0,1:T(8,128)(2,1)S(1)} %copy-done.20, bf16[2048,1024]{1,0:T(8,128)(2,1)S(1)} %copy-done.19), kind=kOutput, calls=%fused_computation.32 | convolution fusion | flops 4300210176 | bytes 14680064 | tf_op jit(solution)/shard_map/dot_general | solution.py:51
  259.8 56.9 %all-gather.5.cloned.1.call-done = bf16[1024,2048]{1,0:T(8,128)(2,1)} async-done(((bf16[1024,1024]{1,0:T(8,128)(2,1)}), bf16[1024,2048]{1,0:T(8,128)(2,1)}) %all-gather.5.cloned.1.call-update) | async-done | bytes 4194320 | tf_op jit(solution)/shard_map/all_gather | solution.py:54
  316.7 9.3 %add_convert_fusion = bf16[1024,1024]{1,0:T(8,128)(2,1)} fusion(bf16[1024,1024]{1,0:T(8,128)(2,1)S(1)} %copy-done.18, bf16[1024,2048]{1,0:T(8,128)(2,1)} %all-gather.5.cloned.1.call-done, bf16[2048,1024]{1,0:T(8,128)(2,1)} %param.13), kind=kOutput, calls=%fused_computation.31 | convolution fusion | flops 4298113024 | bytes 12582912 | tf_op jit(solution)/shard_map/dot_general | solution.py:53
  (37 shorter events, 0.9 us)
Async XLA Ops:
  6.5 10.3 %copy-start = (f32[2,1024]{1,0:T(2,128)S(1)}, f32[2,1024]{1,0:T(2,128)}, u32[]{:S(2)}) copy-start(f32[2,1024]{1,0:T(2,128)} %param.9) | copy-start | bytes 24580
  10.5 55.4 %all-to-all-start = ((bf16[8,128,1024]{2,1,0:T(8,128)(2,1)}), bf16[8,128,1024]{2,1,0:T(8,128)(2,1)S(1)}, u32[]{:S(2)}, u32[]{:S(2)}) async-start(bf16[8,128,1024]{2,1,0:T(8,128)(2,1)} %bitcast.71), calls=%async_computation | async-start | bytes 4194304 | tf_op jit(solution)/shard_map/all_to_all | solution.py:26
  16.8 228.8 %all-gather.3.cloned.1.call-start = ((), (), s32[]{:S(2)}) async-start(), calls=%async_computation.2 | async-start | bytes 6291456 | tf_op jit(solution)/shard_map/all_gather | solution.py:49
  78.5 2.0 copy-start.12
  80.5 3.3 copy-start.7
  80.8 2.2 copy-start.13
  83.8 2.0 copy-start.3
  84.1 3.0 copy-start.8
  87.1 1.9 copy-start.14
  89.0 2.0 copy-start.4
  89.3 2.9 copy-start.9
  92.2 2.0 copy-start.15
  94.3 2.0 copy-start.5
  94.5 3.0 copy-start.10
  97.5 1.8 copy-start.16
  99.4 2.0 copy-start.6
  99.6 2.9 copy-start.11
  102.5 2.9 copy-start.17
  105.4 3.2 copy-start.2
  189.8 126.9 %all-gather.5.cloned.1.call-start = ((), (), s32[]{:S(2)}) async-start(), calls=%async_computation.3 | async-start | bytes 6291456 | tf_op jit(solution)/shard_map/all_gather | solution.py:54
  245.6 7.7 %copy-start.19 = (bf16[2048,1024]{1,0:T(8,128)(2,1)S(1)}, bf16[2048,1024]{1,0:T(8,128)(2,1)}, u32[]{:S(2)}) copy-start(bf16[2048,1024]{1,0:T(8,128)(2,1)} %param.12) | copy-start | bytes 12582916
  245.6 7.7 %copy-start.20 = (bf16[1024,2048]{0,1:T(8,128)(2,1)S(1)}, bf16[1024,2048]{0,1:T(8,128)(2,1)}, u32[]{:S(2)}) copy-start(bf16[1024,2048]{0,1:T(8,128)(2,1)} %all-gather.3.cloned.1.call-done) | copy-start | bytes 12582916
  253.4 63.3 %copy-start.18 = (bf16[1024,1024]{1,0:T(8,128)(2,1)S(1)}, bf16[1024,1024]{1,0:T(8,128)(2,1)}, u32[]{:S(2)}) copy-start(bf16[1024,1024]{1,0:T(8,128)(2,1)} %param.7) | copy-start | bytes 6291460
  316.7 9.3 %copy-start.1 = (f32[2,1024]{1,0:T(2,128)S(1)}, f32[2,1024]{1,0:T(2,128)}, u32[]{:S(2)}) copy-start(f32[2,1024]{1,0:T(2,128)} %param.9) | copy-start | bytes 24580
Sparse Core Ops, SparseCore 0:
  189.9 55.6 all-gather.2
  259.9 56.7 all-gather.4
where the time goes:
time: 333 us
  waiting for transfers between devices  160 us (48%)
  blocking collectives  52.2 us (16%)
  other arithmetic  43.1 us (13%)
  local copies, waits for them, and re-layouts  34.4 us (10%)
  matrix products  23.4 us (7%)
  between operations  13.6 us (4%)
  starting transfers between devices  6.4 us (2%)
    all_gather x1, waiting for transfers between devices, shards(): lax.all_gather(hidden, 'chan', axis=1, tiled=True)  56.9 us
    all_gather x1, waiting for transfers between devices, shards(): piece = lax.all_gather(activated, 'chan', axis=1, tiled=True)  55.8 us
    all_to_all x1, blocking collectives, shards(): lax.all_to_all(filtered, ('seq', 'sub'), split_axis=1, concat_axis=0, til...  52.2 us
    all_to_all x1, waiting for transfers between devices, shards(): lax.all_to_all(tokens.T, ('seq', 'sub'), split_axis=0, concat_axis=1, til...  47 us
    convert_element_type x1, other arithmetic, shards(): filtered = jax.nn.gelu(mixed).astype(jnp.bfloat16)  26 us
    unnamed x43, local copies, waits for them, and re-layouts  19.5 us
    add x12, other arithmetic, run_levels(): stream = low0 * stream + low1 * shifted  13.7 us
    dot_general x1, matrix products, shards(): jnp.dot(lax.all_gather(hidden, 'chan', axis=1, tiled=True), out_weight, p...  9.28 us
  transfers between devices with their start and end apart: 3, of which 3 were waited for; matrix products, arithmetic and copies ran while one was open for 1% of the time, Pallas kernels for 0%

commit v1 on v0

--- a/solution.py
+++ b/solution.py
@@ -1,9 +1,19 @@
+import functools
+
 import jax
 import jax.numpy as jnp
 from jax import lax
+from jax.experimental import pallas as pl
+from jax.experimental.pallas import tpu as pltpu
 from jax.sharding import PartitionSpec as P
 
 LEVELS = 15
+LANES = 128
+RUN = 16
+MIDDLE = 8
+WIDE = 64
+LINE = ("seq", "sub")
+MIB = 2**20
 
 
 def run_levels(stream, shifter, low0, low1, high0, high1, mix):
@@ -16,14 +26,14 @@
     return mixed + mix[LEVELS] * stream
 
 
-def shards(tokens, low_angle, high_taps, level_mix, w_value, w_gate, out_weight):
+def general(tokens, low_angle, high_taps, level_mix, w_value, w_gate, out_weight):
     rows = tokens.shape[0]
     channels = tokens.shape[1]
-    ways = lax.axis_size(("seq", "sub"))
+    ways = lax.axis_size(LINE)
     total = rows * ways
     narrow = channels // ways
-    place = lax.axis_index(("seq", "sub")) * narrow
-    columns = lax.all_to_all(tokens.T, ("seq", "sub"), split_axis=0, concat_axis=1, tiled=True)
+    place = lax.axis_index(LINE) * narrow
+    columns = lax.all_to_all(tokens.T, LINE, split_axis=0, concat_axis=1, tiled=True)
     angle = lax.dynamic_slice_in_dim(low_angle, place, narrow, 0)[:, None]
     high_pair = lax.dynamic_slice_in_dim(high_taps, place, narrow, 1)[:, :, None]
     mix = lax.dynamic_slice_in_dim(level_mix, place, narrow, 1)[:, :, None]
@@ -45,7 +55,7 @@
         mix,
     )
     filtered = jax.nn.gelu(mixed).astype(jnp.bfloat16)
-    activated = lax.all_to_all(filtered, ("seq", "sub"), split_axis=1, concat_axis=0, tiled=True).T
+    activated = lax.all_to_all(filtered, LINE, split_axis=1, concat_axis=0, tiled=True).T
     piece = lax.all_gather(activated, "chan", axis=1, tiled=True)
     value = jnp.dot(piece, w_value, preferred_element_type=jnp.float32)
     gate = jnp.dot(piece, w_gate, preferred_element_type=jnp.float32)
@@ -58,7 +68,376 @@
     return (projected + tokens.astype(jnp.float32)).astype(jnp.bfloat16)
 
 
+def coefficients(angle, high, mix, live):
+    low0, low1 = jnp.cos(angle), jnp.sin(angle)
+    rows = []
+    for level in range(live + 1):
+        weight = jnp.zeros_like(angle)
+        if level < live:
+            weight = weight + mix[level] * (high[0] - high[1] * low0 / low1)
+        if level > 0:
+            weight = weight + mix[level - 1] * high[1] / low1
+        if level == live:
+            for rest in range(live, LEVELS):
+                weight = weight + mix[rest] * high[0] * low0 ** (rest - live)
+            weight = weight + mix[LEVELS] * low0 ** (LEVELS - live)
+        weight = weight * low0**level
+        if level == 0:
+            weight = weight + mix[LEVELS + 1]
+        rows.append(weight)
+    rows.append(low1 / low0)
+    return jnp.stack(rows)
+
+
+def advance(stream, tail, ratio):
+    reach = tail.shape[0]
+    shifted = jnp.concatenate([tail, stream[: stream.shape[0] - reach]], 0)
+    return stream + ratio * shifted
+
+
+def levels_kernel(live, ways, place, coef_ref, *refs):
+    pieces = refs[:ways]
+    far = refs[ways : 2 * ways]
+    near = refs[2 * ways : 3 * ways]
+    tokens, stream_ref, mixed_ref, act_ref = refs[3 * ways :]
+    rows = pieces[0].shape[0]
+    units = rows * ways // 8
+    for at in range(ways):
+        tokens[pl.ds(pl.multiple_of(place[at] * rows, rows), rows), :] = pieces[at][...]
+
+    def whole(row):
+        return jnp.broadcast_to(coef_ref[row : row + 1, :], (8, LANES))[None]
+
+    def zero(n):
+        return jnp.zeros((n, 8, LANES), jnp.float32)
+
+    ratio = whole(live + 1)
+
+    def first(i, carry):
+        start = pl.multiple_of(i * RUN * 8, RUN * 8)
+        x = tokens[pl.ds(start, RUN * 8), :].astype(jnp.float32).reshape(RUN, 8, LANES)
+        mixed = whole(0) * x
+        row = lax.broadcasted_iota(jnp.int32, (1, 8, LANES), 1)
+        kept = []
+        for level, tail in enumerate(carry):
+            kept.append(x[RUN - tail.shape[0] :])
+            if level < 3:
+                turned = pltpu.roll(jnp.concatenate([tail, x], 0), 2**level, 1)
+                x = x + ratio * jnp.where(row < 2**level, turned[:RUN], turned[1:])
+            else:
+                x = advance(x, tail, ratio)
+            mixed = mixed + whole(level + 1) * x
+        stream_ref[pl.ds(i * RUN, RUN)] = x
+        mixed_ref[pl.ds(i * RUN, RUN)] = mixed
+        return tuple(kept)
+
+    lax.fori_loop(0, units // RUN, first, tuple(zero(n) for n in (1, 1, 1, 1, 2, 4)))
+
+    stream = stream_ref.reshape(units // MIDDLE, MIDDLE, 8, LANES)
+    total = mixed_ref.reshape(units // MIDDLE, MIDDLE, 8, LANES)
+    steps = units // MIDDLE // RUN
+
+    def second(t, carry):
+        q = t // steps
+        i = t % steps
+        x = stream[pl.ds(i * RUN, RUN), q]
+        mixed = total[pl.ds(i * RUN, RUN), q]
+        keep = jnp.where(i > 0, 1.0, 0.0)
+        kept = []
+        for level, tail in enumerate(carry):
+            kept.append(x[RUN - tail.shape[0] :])
+            x = advance(x, tail * keep, ratio)
+            mixed = mixed + whole(level + 7) * x
+        stream[pl.ds(i * RUN, RUN), q] = x
+        total[pl.ds(i * RUN, RUN), q] = mixed
+        return tuple(kept)
+
+    lax.fori_loop(0, MIDDLE * steps, second, tuple(zero(n) for n in (1, 2, 4)))
+
+    stream_wide = stream_ref.reshape(units // WIDE, WIDE, 8, LANES)
+    total_wide = mixed_ref.reshape(units // WIDE, WIDE, 8, LANES)
+    act_wide = act_ref.reshape(units // WIDE, WIDE // 2, 16, LANES)
+
+    def third(pair, _):
+        halves = []
+        for odd in range(2):
+            x = stream_wide[:, pair * 2 + odd]
+            mixed = total_wide[:, pair * 2 + odd]
+            for level in range(9, live):
+                x = advance(x, zero(2 ** (level - 9)), ratio)
+                mixed = mixed + whole(level + 1) * x
+            halves.append(jax.nn.gelu(mixed))
+        act_wide[:, pair] = jnp.concatenate(halves, 1).astype(jnp.bfloat16)
+        return 0
+
+    lax.fori_loop(0, WIDE // 2, third, 0)
+
+    half = rows // 2
+    side = place[2 * ways]
+    for at in range(ways):
+        start = place[ways + at] * rows
+        far[at][...] = act_ref[pl.ds(pl.multiple_of(start + (1 - side) * half, half), half), :]
+        near[at][...] = act_ref[pl.ds(pl.multiple_of(start + side * half, half), half), :]
+
+
+def run_filter(place, coef, pieces, live):
+    ways = len(pieces)
+    rows = pieces[0].shape[0]
+    total = rows * ways
+    in_vmem = pl.BlockSpec(memory_space=pltpu.VMEM)
+    return pl.pallas_call(
+        functools.partial(levels_kernel, live, ways),
+        out_shape=[jax.ShapeDtypeStruct((rows // 2, LANES), jnp.bfloat16)] * (2 * ways),
+        in_specs=[pl.BlockSpec(memory_space=pltpu.SMEM)] + [in_vmem] * (ways + 1),
+        out_specs=[in_vmem] * (2 * ways),
+        scratch_shapes=[
+            pltpu.VMEM((total, LANES), jnp.bfloat16),
+            pltpu.VMEM((total // 8, 8, LANES), jnp.float32),
+            pltpu.VMEM((total // 8, 8, LANES), jnp.float32),
+            pltpu.VMEM((total, LANES), jnp.bfloat16),
+        ],
+        compiler_params=pltpu.CompilerParams(vmem_limit_bytes=40 * MIB),
+        name="levels",
+    )(place, coef, *pieces)
+
+
+def project_kernel(ways, parts, steps, place, *refs):
+    near = refs[:ways]
+    far = refs[ways]
+    value_own, gate_own = refs[ways + 1 : ways + 3]
+    at = ways + 3
+    value_far = refs[at : at + parts]
+    gate_far = refs[at + parts : at + 2 * parts]
+    out_far = refs[at + 2 * parts : at + 3 * parts]
+    hidden_ref, sent_ref, act, hid = refs[at + 3 * parts :]
+    step = pl.program_id(0)
+    side = place[2 * ways]
+    depth = value_far[0].shape[0]
+    block = value_own.shape[1]
+    channels = ways * LANES
+
+    @pl.when(step == 0)
+    def _():
+        for s in range(ways):
+            own = side * channels + place[s] * LANES
+            other = (1 - side) * channels + place[s] * LANES
+            act[:, pl.ds(pl.multiple_of(own, LANES), LANES)] = near[s][...]
+            act[:, pl.ds(pl.multiple_of(other, LANES), LANES)] = far[s]
+
+    def dot(a, b):
+        return jnp.dot(a, b, preferred_element_type=jnp.float32)
+
+    def put(value, gate, start):
+        done = (value * jax.nn.sigmoid(gate)).astype(jnp.bfloat16)
+        hid[:, pl.ds(pl.multiple_of(start, block), block)] = done
+
+    def spread(source, weights):
+        total = None
+        for p in range(parts):
+            start = pl.multiple_of(place[2 * ways + 1 + p] * depth, depth)
+            term = dot(source[:, pl.ds(start, depth)], weights[p][...])
+            total = term if total is None else total + term
+        return total
+
+    @pl.when(step < steps)
+    def _():
+        put(
+            dot(act[...], value_own[...]),
+            dot(act[...], gate_own[...]),
+            side * channels + step * block,
+        )
+
+    @pl.when((step >= steps) & (step < 2 * steps))
+    def _():
+        put(
+            spread(act, value_far),
+            spread(act, gate_far),
+            (1 - side) * channels + (step - steps) * block,
+        )
+
+    @pl.when(step >= 2 * steps)
+    def _():
+        sent_ref[...] = spread(hid, out_far).astype(jnp.bfloat16)
+
+    @pl.when(step == 3 * steps - 1)
+    def _():
+        hidden_ref[...] = hid[...]
+
+
+def run_project(place, near, far, value_own, gate_own, value_far, gate_far, out_far):
+    ways = len(near)
+    parts = len(value_far)
+    rows = near[0].shape[0]
+    depth, channels = value_far[0].shape
+    width = value_own.shape[0]
+    block = min(256, channels)
+    steps = channels // block
+
+    def fixed(shape):
+        return pl.BlockSpec(shape, lambda j: (0,) * len(shape))
+
+    def column(height, offset):
+        return pl.BlockSpec((height, block), lambda j: (0, jnp.clip(j - offset, 0, steps - 1)))
+
+    return pl.pallas_call(
+        functools.partial(project_kernel, ways, parts, steps),
+        grid=(3 * steps,),
+        out_shape=[
+            jax.ShapeDtypeStruct((rows, width), jnp.bfloat16),
+            jax.ShapeDtypeStruct((rows, channels), jnp.bfloat16),
+        ],
+        in_specs=[pl.BlockSpec(memory_space=pltpu.SMEM)]
+        + [fixed((rows, LANES))] * ways
+        + [fixed((ways, rows, LANES))]
+        + [column(width, 0)] * 2
+        + [column(depth, steps)] * (2 * parts)
+        + [column(depth, 2 * steps)] * parts,
+        out_specs=[fixed((rows, width)), column(rows, 2 * steps)],
+        scratch_shapes=[
+            pltpu.VMEM((rows, width), jnp.bfloat16),
+            pltpu.VMEM((rows, width), jnp.bfloat16),
+        ],
+        compiler_params=pltpu.CompilerParams(vmem_limit_bytes=40 * MIB),
+        name="project",
+    )(place, *near, far, value_own, gate_own, *value_far, *gate_far, *out_far)
+
+
+def finish_kernel(side, hidden, weight, tokens, out_ref):
+    made = jnp.dot(hidden[...], weight[...], preferred_element_type=jnp.float32)
+    out_ref[...] = (made + tokens[...].astype(jnp.float32)).astype(jnp.bfloat16)
+
+
+def run_finish(side, hidden, weight, tokens):
+    rows, width = hidden.shape
+    channels = weight.shape[1]
+    block = min(256, channels)
+    return pl.pallas_call(
+        finish_kernel,
+        grid_spec=pltpu.PrefetchScalarGridSpec(
+            num_scalar_prefetch=1,
+            grid=(channels // block,),
+            in_specs=[
+                pl.BlockSpec((rows, width), lambda j, side: (0, 0)),
+                pl.BlockSpec((width, block), lambda j, side: (0, j)),
+                pl.BlockSpec((rows, block), lambda j, side: (side[0], j)),
+            ],
+            out_specs=pl.BlockSpec((rows, block), lambda j, side: (side[0], j)),
+        ),
+        out_shape=jax.ShapeDtypeStruct(tokens.shape, jnp.bfloat16),
+        compiler_params=pltpu.CompilerParams(vmem_limit_bytes=40 * MIB),
+        name="finish",
+    )(side, hidden, weight, tokens)
+
+
+def add_kernel(side, got, tokens, kept, out_ref):
+    out_ref[...] = (got[...].astype(jnp.float32) + tokens[...].astype(jnp.float32)).astype(
+        jnp.bfloat16
+    )
+
+
+def add_far(side, got, tokens, result):
+    rows, channels = got.shape
+    block = rows // 2
+    return pl.pallas_call(
+        add_kernel,
+        grid_spec=pltpu.PrefetchScalarGridSpec(
+            num_scalar_prefetch=1,
+            grid=(2,),
+            in_specs=[
+                pl.BlockSpec((block, channels), lambda j, side: (j, 0)),
+                pl.BlockSpec((block, channels), lambda j, side: (2 * (1 - side[0]) + j, 0)),
+                pl.BlockSpec(memory_space=pl.ANY),
+            ],
+            out_specs=pl.BlockSpec((block, channels), lambda j, side: (2 * (1 - side[0]) + j, 0)),
+        ),
+        out_shape=jax.ShapeDtypeStruct(tokens.shape, jnp.bfloat16),
+        input_output_aliases={3: 0},
+        name="add_far",
+    )(side, got, tokens, result)
+
+
+def swap(array, axis):
+    return lax.ppermute(array, axis, [(0, 1), (1, 0)])
+
+
+def around(array, offset):
+    ways = lax.axis_size(LINE)
+    return lax.ppermute(array, LINE, [(j, (j + offset) % ways) for j in range(ways)])
+
+
+def by_tokens(tokens, low_angle, high_taps, level_mix, w_value, w_gate, out_weight):
+    rows, channels = tokens.shape
+    ways = lax.axis_size(LINE)
+    narrow = channels // ways
+    here = lax.axis_index(LINE)
+    group = lax.axis_index("groups")
+    core = lax.axis_index("sub")
+    side = lax.axis_index("chan")
+    live = min(LEVELS, (rows * ways - 1).bit_length())
+    order = sorted(range(1, ways), key=lambda s: abs(2 * s - ways))
+
+    sources = [(here - s) % ways for s in range(ways)]
+    targets = [(here + s) % ways for s in range(ways)]
+    quarter = [
+        2 * group + core,
+        2 * (1 - group) + core,
+        2 * group + 1 - core,
+        2 * (1 - group) + 1 - core,
+    ]
+    place = jnp.stack(sources + targets + [side] + quarter).astype(jnp.int32)
+
+    def columns(s):
+        return lax.dynamic_slice_in_dim(tokens, targets[s] * narrow, narrow, 1)
+
+    pieces = [None] * ways
+    for s in order:
+        pieces[s] = around(columns(s), s)
+    pieces[0] = columns(0)
+
+    depth = w_value.shape[0] // 4
+
+    def fetch(weight):
+        first = swap(lax.dynamic_slice_in_dim(weight, quarter[0] * depth, depth, 0), "chan")
+        second = swap(first, "groups")
+        return [first, second, swap(first, "sub"), swap(second, "sub")]
+
+    value_far, gate_far, out_far = fetch(w_value), fetch(w_gate), fetch(out_weight)
+
+    start = here * narrow
+    coef = coefficients(
+        lax.dynamic_slice_in_dim(low_angle, start, narrow, 0),
+        lax.dynamic_slice_in_dim(high_taps, start, narrow, 1),
+        lax.dynamic_slice_in_dim(level_mix, start, narrow, 1),
+        live,
+    )
+    outs = run_filter(place, coef, pieces, live)
+    far_out, near_out = outs[:ways], outs[ways:]
+
+    far = [far_out[0]] + [None] * (ways - 1)
+    near = [near_out[0]] + [None] * (ways - 1)
+    for s in order:
+        far[s] = around(far_out[s], s)
+    for s in order:
+        near[s] = around(near_out[s], s)
+    got = swap(jnp.stack(far), "chan")
+    hidden, sent = run_project(
+        place, near, got, w_value, w_gate, value_far, gate_far, out_far
+    )
+    returned = swap(sent, "chan")
+    which = side.astype(jnp.int32)[None]
+    result = run_finish(which, hidden, out_weight, tokens)
+    return add_far(which, returned, tokens, result)
+
+
 def solution(mesh):
+    def shards(tokens, *rest):
+        ways = mesh.shape["seq"] * mesh.shape["sub"]
+        pairs = all(mesh.shape[name] == 2 for name in ("groups", "chan", "sub"))
+        rows, channels = tokens.shape
+        fits = channels == ways * LANES and rows % 64 == 0
+        fits = fits and rows * ways == 8 * WIDE * RUN and rest[3].shape[0] % 512 == 0
+        return (by_tokens if pairs and fits else general)(tokens, *rest)
+
     return jax.shard_map(
         shards,
         mesh=mesh,

time: 333 us -> 247 us (0.74)
  blocking collectives: 52.2 us -> 0 us
  other arithmetic: 43.1 us -> 3.13 us
  Pallas kernels: 0 us -> 39.1 us
  local copies, waits for them, and re-layouts: 34.4 us -> 7.46 us
  starting transfers between devices: 6.4 us -> 33 us
  matrix products: 23.4 us -> 0 us
  between operations: 13.6 us -> 0.29 us
  waiting for transfers between devices: 160 us -> 164 us
    ppermute x0 -> x35, waiting for transfers between devices: none -> 164 us  [the longest x14 87 us: swap(): return lax.ppermute(array, axis, [(0, 1), (1, 0)])]
    all_gather x2 -> x0, waiting for transfers between devices: 113 us -> none  [the longest x1 56.9 us: shards(): lax.all_gather(hidden, 'chan', axis=1, tiled=True)]
    all_to_all x1 -> x0, blocking collectives: 52.2 us -> none  [shards(): lax.all_to_all(filtered, ('seq', 'sub'), split_axis=1, concat_axis=0, til...]
    all_to_all x1 -> x0, waiting for transfers between devices: 47 us -> none  [shards(): lax.all_to_all(tokens.T, ('seq', 'sub'), split_axis=0, concat_axis=1, til...]
    pallas_call x0 -> x4, Pallas kernels: none -> 39.1 us  [the longest x1 20.1 us: run_project(): pl.pallas_call(functools.partial(project_kernel, ways, parts, steps), gri...]
    ppermute x0 -> x35, starting transfers between devices: none -> 33 us  [the longest x21 20.6 us: around(): lax.ppermute(array, LINE, [(j, (j + offset) % ways) for j in range(ways)])]
    convert_element_type x2 -> x0, other arithmetic: 28.5 us -> none  [the longest x1 26 us: shards(): filtered = jax.nn.gelu(mixed).astype(jnp.bfloat16)]
    dot_general x3 -> x0, matrix products: 23.4 us -> none  [the longest x1 9.28 us: shards(): jnp.dot(lax.all_gather(hidden, 'chan', axis=1, tiled=True), out_weight, p...]
  transfers between devices with their start and end apart: 3 -> 35, of which waited for: 3 -> 19; matrix products, arithmetic and copies ran while one was open for 1% -> 3% of each run, Pallas kernels for 0% -> 7%
where the time goes in v1:
time: 247 us
  waiting for transfers between devices  164 us (66%)
  Pallas kernels  39.1 us (16%)
  starting transfers between devices  33 us (13%)
  local copies, waits for them, and re-layouts  7.46 us (3%)
  other arithmetic  3.13 us (1%)
    ppermute x14, waiting for transfers between devices, swap(): return lax.ppermute(array, axis, [(0, 1), (1, 0)])  87 us
    ppermute x21, waiting for transfers between devices, around(): lax.ppermute(array, LINE, [(j, (j + offset) % ways) for j in range(ways)])  77 us
    ppermute x21, starting transfers between devices, around(): lax.ppermute(array, LINE, [(j, (j + offset) % ways) for j in range(ways)])  20.6 us
    pallas_call x1, Pallas kernels, run_project(): pl.pallas_call(functools.partial(project_kernel, ways, parts, steps), gri...  20.1 us
    ppermute x14, starting transfers between devices, swap(): return lax.ppermute(array, axis, [(0, 1), (1, 0)])  12.4 us
    pallas_call x1, Pallas kernels, run_filter(): pl.pallas_call(functools.partial(levels_kernel, live, ways), out_shape=[j...  12.2 us
  transfers between devices with their start and end apart: 35, of which 19 were waited for; matrix products, arithmetic and copies ran while one was open for 3% of the time, Pallas kernels for 7%

profile of v1, /device:TPU:0, one launch (start us, length us, event | category | flops | bytes accessed | tf_op | source)
XLA Modules:
  0.0 247.0 jit_solution(9319524423507648228)
XLA Ops:
  0.0 1.7 constant_dynamic-slice_fusion.4
  1.7 4.5 %collective-permute-start.6 = (bf16[1024,128]{1,0:T(8,128)(2,1)S(1)}, bf16[1024,128]{1,0:T(8,128)(2,1)S(1)}, u32[]{:S(2)}, u32[]{:S(2)}) collective-permute-start(bf16[1024,128]{1,0:T(8,128)(2,1)S(1)} %get-tuple-element.45), channel_id=1, source_target_pairs={{0,13},{1,0},{4,1},{5,4},{8,5},{9,8},{12,9},{13,12},{2,15},{3,2},{... | collective-permute-start | bytes 786440 | tf_op jit(solution)/shard_map/ppermute | solution.py:365
  6.3 0.6 collective-permute-start.5
  6.9 2.7 %collective-permute-start.3 = (bf16[1024,128]{1,0:T(8,128)(2,1)S(1)}, bf16[1024,128]{1,0:T(8,128)(2,1)S(1)}, u32[]{:S(2)}, u32[]{:S(2)}) collective-permute-start(bf16[1024,128]{1,0:T(8,128)(2,1)S(1)} %get-tuple-element.48), channel_id=1, source_target_pairs={{0,8},{1,9},{4,12},{5,13},{8,0},{9,1},{12,4},{13,5},{2,10},{3,11},... | collective-permute-start | bytes 786440 | tf_op jit(solution)/shard_map/ppermute | solution.py:365
  9.8 1.0 multiply_bitcast_fusion
  10.8 1.0 multiply_bitcast_fusion.1
  11.8 1.0 multiply_bitcast_fusion.7
  13.0 1.4 constant_dynamic-slice_fusion.3
  14.5 0.7 collective-permute-start.1
  15.2 3.4 %collective-permute-done.5.refs_6_ = bf16[1024,128]{1,0:T(8,128)(2,1)S(1)} collective-permute-done((bf16[1024,128]{1,0:T(8,128)(2,1)S(1)}, bf16[1024,128]{1,0:T(8,128)(2,1)S(1)}, u32[]{:S(2)}, u32[]{:S(2)}) %collective-permute-start.5) | collective-permute-done | bytes 262176 | tf_op jit(solution)/shard_map/ppermute | solution.py:365
  18.6 1.3 constant_dynamic-slice_fusion.2
  20.0 4.2 %collective-permute-done.4.refs_5_ = bf16[1024,128]{1,0:T(8,128)(2,1)S(1)} collective-permute-done((bf16[1024,128]{1,0:T(8,128)(2,1)S(1)}, bf16[1024,128]{1,0:T(8,128)(2,1)S(1)}, u32[]{:S(2)}, u32[]{:S(2)}) %collective-permute-start.4) | collective-permute-done | bytes 262176 | tf_op jit(solution)/shard_map/ppermute | solution.py:365
  24.2 1.5 collective-permute-start.30
  25.7 26.6 %collective-permute-done.3.refs_4_ = bf16[1024,128]{1,0:T(8,128)(2,1)S(1)} collective-permute-done((bf16[1024,128]{1,0:T(8,128)(2,1)S(1)}, bf16[1024,128]{1,0:T(8,128)(2,1)S(1)}, u32[]{:S(2)}, u32[]{:S(2)}) %collective-permute-start.3) | collective-permute-done | bytes 262176 | tf_op jit(solution)/shard_map/ppermute | solution.py:365
  52.3 1.5 collective-permute-start.26
  53.8 0.5 collective-permute-start.22
  54.3 12.2 %levels.1 = (bf16[512,128]{1,0:T(8,128)(2,1)S(1)}, bf16[512,128]{1,0:T(8,128)(2,1)S(1)}, bf16[512,128]{1,0:T(8,128)(2,1)S(1)}, bf16[512,128]{1,0:T(8,128)(2,1)S(...) custom-call(s32[21]{0:T(128)S(1)} %stack.156.place, ...), custom_call_target="tpu_custom_call" | custom-call | tf_op jit(solution)/shard_map/levels/pallas_call | solution.py:188
  66.7 7.5 %collective-permute-done.14 = bf16[512,128]{1,0:T(8,128)(2,1)S(1)} collective-permute-done((bf16[512,128]{1,0:T(8,128)(2,1)S(1)}, bf16[512,128]{1,0:T(8,128)(2,1)S(1)}, u32[]{:S(2)}, u32[]{:S(2)}) %collective-permute-start.14) | collective-permute-done | bytes 131104 | tf_op jit(solution)/shard_map/ppermute | solution.py:365
  74.2 6.7 %collective-permute-done.15 = bf16[512,128]{1,0:T(8,128)(2,1)S(1)} collective-permute-done((bf16[512,128]{1,0:T(8,128)(2,1)S(1)}, bf16[512,128]{1,0:T(8,128)(2,1)S(1)}, u32[]{:S(2)}, u32[]{:S(2)}) %collective-permute-start.15) | collective-permute-done | bytes 131104 | tf_op jit(solution)/shard_map/ppermute | solution.py:365
  81.0 8.0 %collective-permute-done.16 = bf16[512,128]{1,0:T(8,128)(2,1)S(1)} collective-permute-done((bf16[512,128]{1,0:T(8,128)(2,1)S(1)}, bf16[512,128]{1,0:T(8,128)(2,1)S(1)}, u32[]{:S(2)}, u32[]{:S(2)}) %collective-permute-start.16) | collective-permute-done | bytes 131104 | tf_op jit(solution)/shard_map/ppermute | solution.py:365
  89.2 8.8 %collective-permute-done.17 = bf16[512,128]{1,0:T(8,128)(2,1)S(1)} collective-permute-done((bf16[512,128]{1,0:T(8,128)(2,1)S(1)}, bf16[512,128]{1,0:T(8,128)(2,1)S(1)}, u32[]{:S(2)}, u32[]{:S(2)}) %collective-permute-start.17) | collective-permute-done | bytes 131104 | tf_op jit(solution)/shard_map/ppermute | solution.py:365
  97.9 1.3 collective-permute-done.9.refs_3_
  99.2 1.2 collective-permute-start.10
  100.5 2.0 collective-permute-done.18
  102.5 2.6 %collective-permute-start.19 = (bf16[512,128]{1,0:T(8,128)(2,1)S(1)}, bf16[512,128]{1,0:T(8,128)(2,1)S(1)}, u32[]{:S(2)}, u32[]{:S(2)}) collective-permute-start(bf16[512,128]{1,0:T(8,128)(2,1)S(1)} %get-tuple-element.37), channel_id=1, source_target_pairs={{0,12},{1,13},{4,0},{5,1},{8,4},{9,5},{12,8},{13,9},{2,14},{3,15},... | collective-permute-start | bytes 393224 | tf_op jit(solution)/shard_map/ppermute | solution.py:365
  105.1 5.3 %collective-permute-done.10.refs_4_ = bf16[512,128]{1,0:T(8,128)(2,1)S(1)} collective-permute-done((bf16[512,128]{1,0:T(8,128)(2,1)S(1)}, bf16[512,128]{1,0:T(8,128)(2,1)S(1)}, u32[]{:S(2)}, u32[]{:S(2)}) %collective-permute-start.10) | collective-permute-done | bytes 131104 | tf_op jit(solution)/shard_map/ppermute | solution.py:365
  110.6 2.5 %collective-permute-start.20 = (bf16[512,128]{1,0:T(8,128)(2,1)S(1)}, bf16[512,128]{1,0:T(8,128)(2,1)S(1)}, u32[]{:S(2)}, u32[]{:S(2)}) collective-permute-start(bf16[512,128]{1,0:T(8,128)(2,1)S(1)} %get-tuple-element.38), channel_id=1, source_target_pairs={{0,13},{1,0},{4,1},{5,4},{8,5},{9,8},{12,9},{13,12},{2,15},{3,2},{... | collective-permute-start | bytes 393224 | tf_op jit(solution)/shard_map/ppermute | solution.py:365
  113.2 2.4 collective-permute-done.11.refs_5_
  115.5 3.2 %collective-permute-start.12 = (bf16[512,128]{1,0:T(8,128)(2,1)S(1)}, bf16[512,128]{1,0:T(8,128)(2,1)S(1)}, u32[]{:S(2)}, u32[]{:S(2)}) collective-permute-start(bf16[512,128]{1,0:T(8,128)(2,1)S(1)} %get-tuple-element.29), channel_id=1, source_target_pairs={{0,12},{1,13},{4,0},{5,1},{8,4},{9,5},{12,8},{13,9},{2,14},{3,15},... | collective-permute-start | bytes 393224 | tf_op jit(solution)/shard_map/ppermute | solution.py:365
  118.7 2.1 collective-permute-start.13
  120.9 0.6 collective-permute-done.12.refs_6_
  121.5 1.5 collective-permute-start.21
  123.0 1.9 collective-permute-start.32
  124.9 1.5 collective-permute-start.31
  127.0 1.5 collective-permute-start.23
  128.5 17.9 %collective-permute-done.21.refs_8_ = bf16[8,512,128]{2,1,0:T(8,128)(2,1)S(1)} collective-permute-done((bf16[8,512,128]{2,1,0:T(8,128)(2,1)S(1)}, bf16[8,512,128]{2,1,0:T(8,128)(2,1)S(1)}, u32[]{:S(2)}, u32[]{:S(2)}) %collective-permute-start.21) | collective-permute-done | bytes 1048608 | tf_op jit(solution)/shard_map/ppermute | solution.py:360
  146.3 1.3 collective-permute-start.28
  147.8 3.2 %collective-permute-done.31.refs_20_ = bf16[512,1024]{1,0:T(8,128)(2,1)S(1)} collective-permute-done((bf16[512,1024]{1,0:T(8,128)(2,1)S(1)}, bf16[512,1024]{1,0:T(8,128)(2,1)S(1)}, u32[]{:S(2)}, u32[]{:S(2)}) %collective-permute-start.31) | collective-permute-done | bytes 1048608 | tf_op jit(solution)/shard_map/ppermute | solution.py:360
  151.0 22.5 %collective-permute-done.27.refs_16_ = bf16[512,1024]{1,0:T(8,128)(2,1)S(1)} collective-permute-done((bf16[512,1024]{1,0:T(8,128)(2,1)S(1)}, bf16[512,1024]{1,0:T(8,128)(2,1)S(1)}, u32[]{:S(2)}, u32[]{:S(2)}) %collective-permute-start.27) | collective-permute-done | bytes 1048608 | tf_op jit(solution)/shard_map/ppermute | solution.py:360
  173.4 22.2 %collective-permute-done.23.refs_12_ = bf16[512,1024]{1,0:T(8,128)(2,1)S(1)} collective-permute-done((bf16[512,1024]{1,0:T(8,128)(2,1)S(1)}, bf16[512,1024]{1,0:T(8,128)(2,1)S(1)}, u32[]{:S(2)}, u32[]{:S(2)}) %collective-permute-start.23) | collective-permute-done | bytes 1048608 | tf_op jit(solution)/shard_map/ppermute | solution.py:360
  195.7 2.6 %collective-permute-done.25.refs_14_ = bf16[512,1024]{1,0:T(8,128)(2,1)S(1)} collective-permute-done((bf16[512,1024]{1,0:T(8,128)(2,1)S(1)}, bf16[512,1024]{1,0:T(8,128)(2,1)S(1)}, u32[]{:S(2)}, u32[]{:S(2)}) %collective-permute-start.25) | collective-permute-done | bytes 1048608 | tf_op jit(solution)/shard_map/ppermute | solution.py:360
  198.3 20.1 %project.1 = (bf16[512,2048]{1,0:T(8,128)(2,1)}, bf16[512,1024]{1,0:T(8,128)(2,1)S(1)}) custom-call(s32[21]{0:T(128)S(1)} %stack.156.place, bf16[512,128]{1,0:T(8,128)(2,1)S(1)} %get-tuple-element.23.refs_0_, bf16[512,128]{1,0:T(8,128)(2,1)S(1)} %collective-permute-done.7.refs_1_, bf16[512,128]{1,0:T(8,128)(2,1)S(1)} %collective-permute-done.8.refs_2_, ...), custom_call_target="tpu_custom_call" | custom-call | tf_op jit(solution)/shard_map/project/pallas_call | solution.py:282
  218.4 0.5 collective-permute-start.34
  218.9 1.6 copy-done.3
  220.5 4.4 %finish.1.kept = bf16[1024,1024]{1,0:T(8,128)(2,1)} custom-call(s32[1]{0:T(128)} %bitcast.side, bf16[512,2048]{1,0:T(8,128)(2,1)S(1)} %copy-done.3, bf16[2048,1024]{1,0:T(8,128)(2,1)S(1)} %copy-done.2, bf16[1024,1024]{1,0:T(8,128)(2,1)S(1)} %copy-done.1), custom_call_target="tpu_custom_call" | custom-call | tf_op jit(solution)/shard_map/finish/pallas_call | solution.py:314
  224.9 18.7 %collective-permute-done.34.got = bf16[512,1024]{1,0:T(8,128)(2,1)S(1)} collective-permute-done((bf16[512,1024]{1,0:T(8,128)(2,1)S(1)}, bf16[512,1024]{1,0:T(8,128)(2,1)S(1)}, u32[]{:S(2)}, u32[]{:S(2)}) %collective-permute-start.34) | collective-permute-done | bytes 1048608 | tf_op jit(solution)/shard_map/ppermute | solution.py:360
  243.6 1.0 copy-done.6
  244.6 2.4 add_far.1
  (61 shorter events, 1.6 us)
Async XLA Ops:
  0.0 9.6 %copy-start = (f32[2,1024]{1,0:T(2,128)S(1)}, f32[2,1024]{1,0:T(2,128)}, u32[]{:S(2)}) copy-start(f32[2,1024]{1,0:T(2,128)} %param.9) | copy-start | bytes 24580
  0.0 9.6 %copy-start.7 = (f32[1024]{0:T(1024)S(1)}, f32[1024]{0:T(1024)}, u32[]{:S(2)}) copy-start(f32[1024]{0:T(1024)} %param.8) | copy-start | bytes 12292
  1.7 12.7 %collective-permute-start.6 = (bf16[1024,128]{1,0:T(8,128)(2,1)S(1)}, bf16[1024,128]{1,0:T(8,128)(2,1)S(1)}, u32[]{:S(2)}, u32[]{:S(2)}) collective-permute-start(bf16[1024,128]{1,0:T(8,128)(2,1)S(1)} %get-tuple-element.45), channel_id=1, source_target_pairs={{0,13},{1,0},{4,1},{5,4},{8,5},{9,8},{12,9},{13,12},{2,15},{3,2},{... | collective-permute-start | bytes 786440 | tf_op jit(solution)/shard_map/ppermute | solution.py:365
  6.3 12.3 %collective-permute-start.5 = (bf16[1024,128]{1,0:T(8,128)(2,1)S(1)}, bf16[1024,128]{1,0:T(8,128)(2,1)S(1)}, u32[]{:S(2)}, u32[]{:S(2)}) collective-permute-start(bf16[1024,128]{1,0:T(8,128)(2,1)S(1)} %get-tuple-element.46), channel_id=1, source_target_pairs={{0,12},{1,13},{4,0},{5,1},{8,4},{9,5},{12,8},{13,9},{2,14},{3,15},... | collective-permute-start | bytes 786440 | tf_op jit(solution)/shard_map/ppermute | solution.py:365
  6.9 17.3 %collective-permute-start.4 = (bf16[1024,128]{1,0:T(8,128)(2,1)S(1)}, bf16[1024,128]{1,0:T(8,128)(2,1)S(1)}, u32[]{:S(2)}, u32[]{:S(2)}) collective-permute-start(bf16[1024,128]{1,0:T(8,128)(2,1)S(1)} %get-tuple-element.47), channel_id=1, source_target_pairs={{0,9},{1,12},{4,13},{5,0},{8,1},{9,4},{12,5},{13,8},{2,11},{3,14},... | collective-permute-start | bytes 786440 | tf_op jit(solution)/shard_map/ppermute | solution.py:365
  6.9 45.4 %collective-permute-start.3 = (bf16[1024,128]{1,0:T(8,128)(2,1)S(1)}, bf16[1024,128]{1,0:T(8,128)(2,1)S(1)}, u32[]{:S(2)}, u32[]{:S(2)}) collective-permute-start(bf16[1024,128]{1,0:T(8,128)(2,1)S(1)} %get-tuple-element.48), channel_id=1, source_target_pairs={{0,8},{1,9},{4,12},{5,13},{8,0},{9,1},{12,4},{13,5},{2,10},{3,11},... | collective-permute-start | bytes 786440 | tf_op jit(solution)/shard_map/ppermute | solution.py:365
  9.6 44.2 %collective-permute-start.2 = (bf16[1024,128]{1,0:T(8,128)(2,1)S(1)}, bf16[1024,128]{1,0:T(8,128)(2,1)S(1)}, u32[]{:S(2)}, u32[]{:S(2)}) collective-permute-start(bf16[1024,128]{1,0:T(8,128)(2,1)S(1)} %get-tuple-element.49), channel_id=1, source_target_pairs={{0,5},{1,8},{4,9},{5,12},{8,13},{9,0},{12,1},{13,4},{2,7},{3,10},{... | collective-permute-start | bytes 786440 | tf_op jit(solution)/shard_map/ppermute | solution.py:365
  13.0 6.9 %copy-start.2 = (bf16[2048,1024]{1,0:T(8,128)(2,1)S(1)}, bf16[2048,1024]{1,0:T(8,128)(2,1)}, u32[]{:S(2)}) copy-start(bf16[2048,1024]{1,0:T(8,128)(2,1)} %weight.1) | copy-start | bytes 12582916
  14.5 39.9 %collective-permute-start.1 = (bf16[1024,128]{1,0:T(8,128)(2,1)S(1)}, bf16[1024,128]{1,0:T(8,128)(2,1)S(1)}, u32[]{:S(2)}, u32[]{:S(2)}) collective-permute-start(bf16[1024,128]{1,0:T(8,128)(2,1)S(1)} %get-tuple-element.50), channel_id=1, source_target_pairs={{0,4},{1,5},{4,8},{5,9},{8,12},{9,13},{12,0},{13,1},{2,6},{3,7},{6... | collective-permute-start | bytes 786440 | tf_op jit(solution)/shard_map/ppermute | solution.py:365
  18.6 35.8 %collective-permute-start = (bf16[1024,128]{1,0:T(8,128)(2,1)S(1)}, bf16[1024,128]{1,0:T(8,128)(2,1)S(1)}, u32[]{:S(2)}, u32[]{:S(2)}) collective-permute-start(bf16[1024,128]{1,0:T(8,128)(2,1)S(1)} %get-tuple-element.51), channel_id=1, source_target_pairs={{0,1},{1,4},{4,5},{5,8},{8,9},{9,12},{12,13},{13,0},{2,3},{3,6},{6... | collective-permute-start | bytes 786440 | tf_op jit(solution)/shard_map/ppermute | solution.py:365
  24.2 98.8 %collective-permute-start.30 = (bf16[512,1024]{1,0:T(8,128)(2,1)S(1)}, bf16[512,1024]{1,0:T(8,128)(2,1)S(1)}, u32[]{:S(2)}, u32[]{:S(2)}) collective-permute-start(bf16[512,1024]{1,0:T(8,128)(2,1)S(1)} %constant_dynamic-slice_fusion.1), channel_id=1, source_target_pairs={{0,2},{2,0},{1,3},{3,1},{4,6},{6,4},{5,7},{7,5},{8,10},{10,8},{9,1... | collective-permute-start | bytes 3145736 | tf_op jit(solution)/shard_map/ppermute | solution.py:360
  52.3 74.2 %collective-permute-start.26 = (bf16[512,1024]{1,0:T(8,128)(2,1)S(1)}, bf16[512,1024]{1,0:T(8,128)(2,1)S(1)}, u32[]{:S(2)}, u32[]{:S(2)}) collective-permute-start(bf16[512,1024]{1,0:T(8,128)(2,1)S(1)} %constant_dynamic-slice_fusion.2), channel_id=1, source_target_pairs={{0,2},{2,0},{1,3},{3,1},{4,6},{6,4},{5,7},{7,5},{8,10},{10,8},{9,1... | collective-permute-start | bytes 3145736 | tf_op jit(solution)/shard_map/ppermute | solution.py:360
  53.8 73.2 %collective-permute-start.22 = (bf16[512,1024]{1,0:T(8,128)(2,1)S(1)}, bf16[512,1024]{1,0:T(8,128)(2,1)S(1)}, u32[]{:S(2)}, u32[]{:S(2)}) collective-permute-start(bf16[512,1024]{1,0:T(8,128)(2,1)S(1)} %constant_dynamic-slice_fusion.3), channel_id=1, source_target_pairs={{0,2},{2,0},{1,3},{3,1},{4,6},{6,4},{5,7},{7,5},{8,10},{10,8},{9,1... | collective-permute-start | bytes 3145736 | tf_op jit(solution)/shard_map/ppermute | solution.py:360
  66.5 14.4 %collective-permute-start.7 = (bf16[512,128]{1,0:T(8,128)(2,1)S(1)}, bf16[512,128]{1,0:T(8,128)(2,1)S(1)}, u32[]{:S(2)}, u32[]{:S(2)}) collective-permute-start(bf16[512,128]{1,0:T(8,128)(2,1)S(1)} %get-tuple-element.24), channel_id=1, source_target_pairs={{0,1},{1,4},{4,5},{5,8},{8,9},{9,12},{12,13},{13,0},{2,3},{3,6},{6... | collective-permute-start | bytes 393224 | tf_op jit(solution)/shard_map/ppermute | solution.py:365
  66.6 7.6 %collective-permute-start.14 = (bf16[512,128]{1,0:T(8,128)(2,1)S(1)}, bf16[512,128]{1,0:T(8,128)(2,1)S(1)}, u32[]{:S(2)}, u32[]{:S(2)}) collective-permute-start(bf16[512,128]{1,0:T(8,128)(2,1)S(1)} %get-tuple-element.32), channel_id=1, source_target_pairs={{0,1},{1,4},{4,5},{5,8},{8,9},{9,12},{12,13},{13,0},{2,3},{3,6},{6... | collective-permute-start | bytes 393224 | tf_op jit(solution)/shard_map/ppermute | solution.py:365
  74.1 6.8 %collective-permute-start.15 = (bf16[512,128]{1,0:T(8,128)(2,1)S(1)}, bf16[512,128]{1,0:T(8,128)(2,1)S(1)}, u32[]{:S(2)}, u32[]{:S(2)}) collective-permute-start(bf16[512,128]{1,0:T(8,128)(2,1)S(1)} %get-tuple-element.33), channel_id=1, source_target_pairs={{0,4},{1,5},{4,8},{5,9},{8,12},{9,13},{12,0},{13,1},{2,6},{3,7},{6... | collective-permute-start | bytes 393224 | tf_op jit(solution)/shard_map/ppermute | solution.py:365
  80.9 8.1 %collective-permute-start.16 = (bf16[512,128]{1,0:T(8,128)(2,1)S(1)}, bf16[512,128]{1,0:T(8,128)(2,1)S(1)}, u32[]{:S(2)}, u32[]{:S(2)}) collective-permute-start(bf16[512,128]{1,0:T(8,128)(2,1)S(1)} %get-tuple-element.34), channel_id=1, source_target_pairs={{0,5},{1,8},{4,9},{5,12},{8,13},{9,0},{12,1},{13,4},{2,7},{3,10},{... | collective-permute-start | bytes 393224 | tf_op jit(solution)/shard_map/ppermute | solution.py:365
  81.0 8.1 %collective-permute-start.8 = (bf16[512,128]{1,0:T(8,128)(2,1)S(1)}, bf16[512,128]{1,0:T(8,128)(2,1)S(1)}, u32[]{:S(2)}, u32[]{:S(2)}) collective-permute-start(bf16[512,128]{1,0:T(8,128)(2,1)S(1)} %get-tuple-element.25), channel_id=1, source_target_pairs={{0,4},{1,5},{4,8},{5,9},{8,12},{9,13},{12,0},{13,1},{2,6},{3,7},{6... | collective-permute-start | bytes 393224 | tf_op jit(solution)/shard_map/ppermute | solution.py:365
  89.1 8.9 %collective-permute-start.17 = (bf16[512,128]{1,0:T(8,128)(2,1)S(1)}, bf16[512,128]{1,0:T(8,128)(2,1)S(1)}, u32[]{:S(2)}, u32[]{:S(2)}) collective-permute-start(bf16[512,128]{1,0:T(8,128)(2,1)S(1)} %get-tuple-element.35), channel_id=1, source_target_pairs={{0,8},{1,9},{4,12},{5,13},{8,0},{9,1},{12,4},{13,5},{2,10},{3,11},... | collective-permute-start | bytes 393224 | tf_op jit(solution)/shard_map/ppermute | solution.py:365
  89.1 10.1 %collective-permute-start.9 = (bf16[512,128]{1,0:T(8,128)(2,1)S(1)}, bf16[512,128]{1,0:T(8,128)(2,1)S(1)}, u32[]{:S(2)}, u32[]{:S(2)}) collective-permute-start(bf16[512,128]{1,0:T(8,128)(2,1)S(1)} %get-tuple-element.26), channel_id=1, source_target_pairs={{0,5},{1,8},{4,9},{5,12},{8,13},{9,0},{12,1},{13,4},{2,7},{3,10},{... | collective-permute-start | bytes 393224 | tf_op jit(solution)/shard_map/ppermute | solution.py:365
  97.9 4.5 %collective-permute-start.18 = (bf16[512,128]{1,0:T(8,128)(2,1)S(1)}, bf16[512,128]{1,0:T(8,128)(2,1)S(1)}, u32[]{:S(2)}, u32[]{:S(2)}) collective-permute-start(bf16[512,128]{1,0:T(8,128)(2,1)S(1)} %get-tuple-element.36), channel_id=1, source_target_pairs={{0,9},{1,12},{4,13},{5,0},{8,1},{9,4},{12,5},{13,8},{2,11},{3,14},... | collective-permute-start | bytes 393224 | tf_op jit(solution)/shard_map/ppermute | solution.py:365
  99.2 11.2 %collective-permute-start.10 = (bf16[512,128]{1,0:T(8,128)(2,1)S(1)}, bf16[512,128]{1,0:T(8,128)(2,1)S(1)}, u32[]{:S(2)}, u32[]{:S(2)}) collective-permute-start(bf16[512,128]{1,0:T(8,128)(2,1)S(1)} %get-tuple-element.27), channel_id=1, source_target_pairs={{0,8},{1,9},{4,12},{5,13},{8,0},{9,1},{12,4},{13,5},{2,10},{3,11},... | collective-permute-start | bytes 393224 | tf_op jit(solution)/shard_map/ppermute | solution.py:365
  102.5 8.1 %collective-permute-start.19 = (bf16[512,128]{1,0:T(8,128)(2,1)S(1)}, bf16[512,128]{1,0:T(8,128)(2,1)S(1)}, u32[]{:S(2)}, u32[]{:S(2)}) collective-permute-start(bf16[512,128]{1,0:T(8,128)(2,1)S(1)} %get-tuple-element.37), channel_id=1, source_target_pairs={{0,12},{1,13},{4,0},{5,1},{8,4},{9,5},{12,8},{13,9},{2,14},{3,15},... | collective-permute-start | bytes 393224 | tf_op jit(solution)/shard_map/ppermute | solution.py:365
  110.4 5.1 %collective-permute-start.11 = (bf16[512,128]{1,0:T(8,128)(2,1)S(1)}, bf16[512,128]{1,0:T(8,128)(2,1)S(1)}, u32[]{:S(2)}, u32[]{:S(2)}) collective-permute-start(bf16[512,128]{1,0:T(8,128)(2,1)S(1)} %get-tuple-element.28), channel_id=1, source_target_pairs={{0,9},{1,12},{4,13},{5,0},{8,1},{9,4},{12,5},{13,8},{2,11},{3,14},... | collective-permute-start | bytes 393224 | tf_op jit(solution)/shard_map/ppermute | solution.py:365
  110.6 8.1 %collective-permute-start.20 = (bf16[512,128]{1,0:T(8,128)(2,1)S(1)}, bf16[512,128]{1,0:T(8,128)(2,1)S(1)}, u32[]{:S(2)}, u32[]{:S(2)}) collective-permute-start(bf16[512,128]{1,0:T(8,128)(2,1)S(1)} %get-tuple-element.38), channel_id=1, source_target_pairs={{0,13},{1,0},{4,1},{5,4},{8,5},{9,8},{12,9},{13,12},{2,15},{3,2},{... | collective-permute-start | bytes 393224 | tf_op jit(solution)/shard_map/ppermute | solution.py:365
  115.5 6.0 %collective-permute-start.12 = (bf16[512,128]{1,0:T(8,128)(2,1)S(1)}, bf16[512,128]{1,0:T(8,128)(2,1)S(1)}, u32[]{:S(2)}, u32[]{:S(2)}) collective-permute-start(bf16[512,128]{1,0:T(8,128)(2,1)S(1)} %get-tuple-element.29), channel_id=1, source_target_pairs={{0,12},{1,13},{4,0},{5,1},{8,4},{9,5},{12,8},{13,9},{2,14},{3,15},... | collective-permute-start | bytes 393224 | tf_op jit(solution)/shard_map/ppermute | solution.py:365
  118.7 6.2 %collective-permute-start.13 = (bf16[512,128]{1,0:T(8,128)(2,1)S(1)}, bf16[512,128]{1,0:T(8,128)(2,1)S(1)}, u32[]{:S(2)}, u32[]{:S(2)}) collective-permute-start(bf16[512,128]{1,0:T(8,128)(2,1)S(1)} %get-tuple-element.30), channel_id=1, source_target_pairs={{0,13},{1,0},{4,1},{5,4},{8,5},{9,8},{12,9},{13,12},{2,15},{3,2},{... | collective-permute-start | bytes 393224 | tf_op jit(solution)/shard_map/ppermute | solution.py:365
  121.5 24.8 %collective-permute-start.21 = (bf16[8,512,128]{2,1,0:T(8,128)(2,1)S(1)}, bf16[8,512,128]{2,1,0:T(8,128)(2,1)S(1)}, u32[]{:S(2)}, u32[]{:S(2)}) collective-permute-start(bf16[8,512,128]{2,1,0:T(8,128)(2,1)S(1)} %bitcast_dynamic-update-slice_fusion), channel_id=1, source_target_pairs={{0,2},{2,0},{1,3},{3,1},{4,6},{6,4},{5,7},{7,5},{8,10},{10,8},{9,1... | collective-permute-start | bytes 3145736 | tf_op jit(solution)/shard_map/ppermute | solution.py:360
  123.0 24.7 %collective-permute-start.32 = (bf16[512,1024]{1,0:T(8,128)(2,1)S(1)}, bf16[512,1024]{1,0:T(8,128)(2,1)S(1)}, u32[]{:S(2)}, u32[]{:S(2)}) collective-permute-start(bf16[512,1024]{1,0:T(8,128)(2,1)S(1)} %collective-permute-done.30.refs_19_), channel_id=1, source_target_pairs={{0,1},{1,0},{2,3},{3,2},{4,5},{5,4},{6,7},{7,6},{8,9},{9,8},{10,11... | collective-permute-start | bytes 3145736 | tf_op jit(solution)/shard_map/ppermute | solution.py:360
  124.9 26.0 %collective-permute-start.31 = (bf16[512,1024]{1,0:T(8,128)(2,1)S(1)}, bf16[512,1024]{1,0:T(8,128)(2,1)S(1)}, u32[]{:S(2)}, u32[]{:S(2)}) collective-permute-start(bf16[512,1024]{1,0:T(8,128)(2,1)S(1)} %collective-permute-done.30.refs_19_), channel_id=1, source_target_pairs={{0,16},{16,0},{1,17},{17,1},{2,18},{18,2},{3,19},{19,3},{4,20},{20... | collective-permute-start | bytes 3145736 | tf_op jit(solution)/shard_map/ppermute | solution.py:360
  126.5 47.0 %collective-permute-start.27 = (bf16[512,1024]{1,0:T(8,128)(2,1)S(1)}, bf16[512,1024]{1,0:T(8,128)(2,1)S(1)}, u32[]{:S(2)}, u32[]{:S(2)}) collective-permute-start(bf16[512,1024]{1,0:T(8,128)(2,1)S(1)} %collective-permute-done.26.refs_15_), channel_id=1, source_target_pairs={{0,16},{16,0},{1,17},{17,1},{2,18},{18,2},{3,19},{19,3},{4,20},{20... | collective-permute-start | bytes 3145736 | tf_op jit(solution)/shard_map/ppermute | solution.py:360
  127.0 68.7 %collective-permute-start.23 = (bf16[512,1024]{1,0:T(8,128)(2,1)S(1)}, bf16[512,1024]{1,0:T(8,128)(2,1)S(1)}, u32[]{:S(2)}, u32[]{:S(2)}) collective-permute-start(bf16[512,1024]{1,0:T(8,128)(2,1)S(1)} %collective-permute-done.22.refs_11_), channel_id=1, source_target_pairs={{0,16},{16,0},{1,17},{17,1},{2,18},{18,2},{3,19},{19,3},{4,20},{20... | collective-permute-start | bytes 3145736 | tf_op jit(solution)/shard_map/ppermute | solution.py:360
  146.3 49.3 %collective-permute-start.28 = (bf16[512,1024]{1,0:T(8,128)(2,1)S(1)}, bf16[512,1024]{1,0:T(8,128)(2,1)S(1)}, u32[]{:S(2)}, u32[]{:S(2)}) collective-permute-start(bf16[512,1024]{1,0:T(8,128)(2,1)S(1)} %collective-permute-done.26.refs_15_), channel_id=1, source_target_pairs={{0,1},{1,0},{2,3},{3,2},{4,5},{5,4},{6,7},{7,6},{8,9},{9,8},{10,11... | collective-permute-start | bytes 3145736 | tf_op jit(solution)/shard_map/ppermute | solution.py:360
  147.7 50.6 %copy-start.4 = (bf16[512,1024]{1,0:T(8,128)(2,1)}, bf16[512,1024]{1,0:T(8,128)(2,1)S(1)}, u32[]{:S(2)}) copy-start(bf16[512,1024]{1,0:T(8,128)(2,1)S(1)} %collective-permute-done.32.refs_21_) | copy-start | bytes 3145732
  147.7 48.0 %collective-permute-start.24 = (bf16[512,1024]{1,0:T(8,128)(2,1)S(1)}, bf16[512,1024]{1,0:T(8,128)(2,1)S(1)}, u32[]{:S(2)}, u32[]{:S(2)}) collective-permute-start(bf16[512,1024]{1,0:T(8,128)(2,1)S(1)} %collective-permute-done.22.refs_11_), channel_id=1, source_target_pairs={{0,1},{1,0},{2,3},{3,2},{4,5},{5,4},{6,7},{7,6},{8,9},{9,8},{10,11... | collective-permute-start | bytes 3145736 | tf_op jit(solution)/shard_map/ppermute | solution.py:360
  151.0 44.7 %collective-permute-start.33 = (bf16[512,1024]{1,0:T(8,128)(2,1)S(1)}, bf16[512,1024]{1,0:T(8,128)(2,1)S(1)}, u32[]{:S(2)}, u32[]{:S(2)}) collective-permute-start(bf16[512,1024]{1,0:T(8,128)(2,1)S(1)} %collective-permute-done.31.refs_20_), channel_id=1, source_target_pairs={{0,1},{1,0},{2,3},{3,2},{4,5},{5,4},{6,7},{7,6},{8,9},{9,8},{10,11... | collective-permute-start | bytes 3145736 | tf_op jit(solution)/shard_map/ppermute | solution.py:360
  173.4 22.2 %collective-permute-start.29 = (bf16[512,1024]{1,0:T(8,128)(2,1)S(1)}, bf16[512,1024]{1,0:T(8,128)(2,1)S(1)}, u32[]{:S(2)}, u32[]{:S(2)}) collective-permute-start(bf16[512,1024]{1,0:T(8,128)(2,1)S(1)} %collective-permute-done.27.refs_16_), channel_id=1, source_target_pairs={{0,1},{1,0},{2,3},{3,2},{4,5},{5,4},{6,7},{7,6},{8,9},{9,8},{10,11... | collective-permute-start | bytes 3145736 | tf_op jit(solution)/shard_map/ppermute | solution.py:360
  195.7 2.7 %collective-permute-start.25 = (bf16[512,1024]{1,0:T(8,128)(2,1)S(1)}, bf16[512,1024]{1,0:T(8,128)(2,1)S(1)}, u32[]{:S(2)}, u32[]{:S(2)}) collective-permute-start(bf16[512,1024]{1,0:T(8,128)(2,1)S(1)} %collective-permute-done.23.refs_12_), channel_id=1, source_target_pairs={{0,1},{1,0},{2,3},{3,2},{4,5},{5,4},{6,7},{7,6},{8,9},{9,8},{10,11... | collective-permute-start | bytes 3145736 | tf_op jit(solution)/shard_map/ppermute | solution.py:360
  195.7 2.6 %copy-start.5 = (bf16[512,1024]{1,0:T(8,128)(2,1)}, bf16[512,1024]{1,0:T(8,128)(2,1)S(1)}, u32[]{:S(2)}) copy-start(bf16[512,1024]{1,0:T(8,128)(2,1)S(1)} %collective-permute-done.33.refs_22_) | copy-start | bytes 3145732
  198.3 20.6 %copy-start.1 = (bf16[1024,1024]{1,0:T(8,128)(2,1)S(1)}, bf16[1024,1024]{1,0:T(8,128)(2,1)}, u32[]{:S(2)}) copy-start(bf16[1024,1024]{1,0:T(8,128)(2,1)} %tokens.3) | copy-start | bytes 6291460
  218.4 25.2 %collective-permute-start.34 = (bf16[512,1024]{1,0:T(8,128)(2,1)S(1)}, bf16[512,1024]{1,0:T(8,128)(2,1)S(1)}, u32[]{:S(2)}, u32[]{:S(2)}) collective-permute-start(bf16[512,1024]{1,0:T(8,128)(2,1)S(1)} %get-tuple-element.39), channel_id=1, source_target_pairs={{0,2},{2,0},{1,3},{3,1},{4,6},{6,4},{5,7},{7,5},{8,10},{10,8},{9,1... | collective-permute-start | bytes 3145736 | tf_op jit(solution)/shard_map/ppermute | solution.py:360
  218.9 1.6 copy-start.3
  243.6 1.0 copy-start.6

commit v2 on v0

--- a/solution.py
+++ b/solution.py
@@ -1,9 +1,21 @@
+import functools
+
 import jax
 import jax.numpy as jnp
 from jax import lax
+from jax.experimental import pallas as pl
+from jax.experimental.pallas import tpu as pltpu
 from jax.sharding import PartitionSpec as P
 
 LEVELS = 15
+LANES = 128
+PARTS = 4
+SPLIT = 2
+RUN = 16
+MIDDLE = 8
+WIDE = 64
+LINE = ("seq", "sub")
+GRANT = 56 * 2**20
 
 
 def run_levels(stream, shifter, low0, low1, high0, high1, mix):
@@ -16,14 +28,14 @@
     return mixed + mix[LEVELS] * stream
 
 
-def shards(tokens, low_angle, high_taps, level_mix, w_value, w_gate, out_weight):
+def general(tokens, low_angle, high_taps, level_mix, w_value, w_gate, out_weight):
     rows = tokens.shape[0]
     channels = tokens.shape[1]
-    ways = lax.axis_size(("seq", "sub"))
+    ways = lax.axis_size(LINE)
     total = rows * ways
     narrow = channels // ways
-    place = lax.axis_index(("seq", "sub")) * narrow
-    columns = lax.all_to_all(tokens.T, ("seq", "sub"), split_axis=0, concat_axis=1, tiled=True)
+    place = lax.axis_index(LINE) * narrow
+    columns = lax.all_to_all(tokens.T, LINE, split_axis=0, concat_axis=1, tiled=True)
     angle = lax.dynamic_slice_in_dim(low_angle, place, narrow, 0)[:, None]
     high_pair = lax.dynamic_slice_in_dim(high_taps, place, narrow, 1)[:, :, None]
     mix = lax.dynamic_slice_in_dim(level_mix, place, narrow, 1)[:, :, None]
@@ -45,7 +57,7 @@
         mix,
     )
     filtered = jax.nn.gelu(mixed).astype(jnp.bfloat16)
-    activated = lax.all_to_all(filtered, ("seq", "sub"), split_axis=1, concat_axis=0, tiled=True).T
+    activated = lax.all_to_all(filtered, LINE, split_axis=1, concat_axis=0, tiled=True).T
     piece = lax.all_gather(activated, "chan", axis=1, tiled=True)
     value = jnp.dot(piece, w_value, preferred_element_type=jnp.float32)
     gate = jnp.dot(piece, w_gate, preferred_element_type=jnp.float32)
@@ -58,7 +70,544 @@
     return (projected + tokens.astype(jnp.float32)).astype(jnp.bfloat16)
 
 
+def coefficients_kernel(live, place, angle_ref, high_ref, mix_ref, out_ref):
+    lanes = pl.ds(pl.multiple_of(line_of(place, 0, 0) * LANES, LANES), LANES)
+    low0, low1 = jnp.cos(angle_ref[:, lanes]), jnp.sin(angle_ref[:, lanes])
+    high0, high1 = high_ref[0:1, lanes], high_ref[1:2, lanes]
+    power = jnp.ones_like(low0)
+    for level in range(live + 1):
+        weight = jnp.zeros_like(low0)
+        if level < live:
+            weight = weight + mix_ref[level : level + 1, lanes] * (high0 - high1 * low0 / low1)
+        if level > 0:
+            weight = weight + mix_ref[level - 1 : level, lanes] * high1 / low1
+        if level == live:
+            scale = jnp.ones_like(low0)
+            for rest in range(live, LEVELS):
+                weight = weight + mix_ref[rest : rest + 1, lanes] * high0 * scale
+                scale = scale * low0
+            weight = weight + mix_ref[LEVELS : LEVELS + 1, lanes] * scale
+        weight = weight * power
+        if level == 0:
+            weight = weight + mix_ref[LEVELS + 1 : LEVELS + 2, lanes]
+        out_ref[level : level + 1, :] = weight
+        power = power * low0
+    out_ref[live + 1 : live + 2, :] = low1 / low0
+
+
+def run_coefficients(place, angle, high, mix, live):
+    return pl.pallas_call(
+        functools.partial(coefficients_kernel, live),
+        in_specs=[pl.BlockSpec(memory_space=pltpu.SMEM)]
+        + [pl.BlockSpec(memory_space=pltpu.VMEM)] * 3,
+        out_specs=pl.BlockSpec(memory_space=pltpu.VMEM),
+        out_shape=jax.ShapeDtypeStruct((live + 2, LANES), jnp.float32),
+        cost_estimate=pl.CostEstimate(flops=10**11, bytes_accessed=0, transcendentals=0),
+        name="coefficients",
+    )(place, angle[None], high, mix)
+
+
+def advance(stream, tail, ratio):
+    reach = tail.shape[0]
+    shifted = jnp.concatenate([tail, stream[: stream.shape[0] - reach]], 0)
+    return stream + ratio * shifted
+
+
+def copy_all(pairs, sems):
+    copies = [pltpu.make_async_copy(*pair, sems.at[at]) for at, pair in enumerate(pairs)]
+    for copy in copies:
+        copy.start()
+    for copy in copies:
+        copy.wait()
+
+
+def line_of(place, back, other):
+    chips = place[4]
+    core = 1 - place[1] if other else place[1]
+    return lax.rem(place[0] - back + chips, chips) * 2 + core
+
+
+def cut_kernel(chips, place, tokens, *outs):
+    for ahead in range(chips):
+        for other in range(2):
+            if ahead or other:
+                start = pl.multiple_of(line_of(place, -ahead, other) * LANES, LANES)
+                block = tokens[:, pl.ds(start, LANES)]
+                if ahead:
+                    outs[ahead][other] = block
+                else:
+                    outs[0][...] = block
+
+
+def run_cut(place, tokens, chips):
+    rows = tokens.shape[0]
+    shapes = [(rows, LANES)] + [(2, rows, LANES)] * (chips - 1)
+    return pl.pallas_call(
+        functools.partial(cut_kernel, chips),
+        in_specs=[
+            pl.BlockSpec(memory_space=pltpu.SMEM),
+            pl.BlockSpec(memory_space=pltpu.VMEM),
+        ],
+        out_specs=[pl.BlockSpec(memory_space=pltpu.VMEM)] * chips,
+        out_shape=[jax.ShapeDtypeStruct(shape, tokens.dtype) for shape in shapes],
+        name="cut",
+    )(place, tokens)
+
+
+def piece_kernel(place, *refs):
+    count = (len(refs) - 1) // 2
+    depth = refs[count].shape[0]
+    part = depth // PARTS
+    start = (2 * place[3] + place[1]) * depth
+    pairs = []
+    for at in range(count):
+        for p in range(PARTS):
+            rows = pl.ds(pl.multiple_of(start + p * part, part), part)
+            pairs.append((refs[at].at[rows], refs[count + at].at[pl.ds(p * part, part)]))
+    copy_all(pairs, refs[-1])
+
+
+def run_pieces(place, weights):
+    rows, channels = weights[0].shape
+    count = len(weights)
+    return pl.pallas_call(
+        piece_kernel,
+        in_specs=[pl.BlockSpec(memory_space=pltpu.SMEM)]
+        + [pl.BlockSpec(memory_space=pl.ANY)] * count,
+        out_specs=[pl.BlockSpec(memory_space=pltpu.VMEM)] * count,
+        out_shape=[jax.ShapeDtypeStruct((rows // 4, channels), w.dtype) for w in weights],
+        scratch_shapes=[pltpu.SemaphoreType.DMA((count * PARTS,))],
+        name="pieces",
+    )(place, *weights)
+
+
+def levels_kernel(live, chips, place, coef_ref, own, *refs):
+    direct = refs[: chips - 1]
+    handed = refs[chips - 1 : 2 * chips - 1]
+    far = refs[2 * chips - 1 : 3 * chips - 1]
+    near = refs[3 * chips - 1 : 4 * chips - 1]
+    tokens, stream_ref, mixed_ref, act_ref, sems = refs[4 * chips - 1 :]
+    side = place[2]
+    rows = own.shape[0]
+    units = rows * 2 * chips // 8
+
+    def block(line):
+        return pl.ds(pl.multiple_of(line * rows, rows), rows)
+
+    pairs = []
+    for back in range(chips):
+        columns = pl.ds(pl.multiple_of(line_of(place, 0, 0) * LANES, LANES), LANES)
+        mine = direct[back - 1].at[0] if back else own.at[:, columns]
+        pairs.append((mine, tokens.at[block(line_of(place, back, 0))]))
+        pairs.append((handed[back], tokens.at[block(line_of(place, back, 1))]))
+    copy_all(pairs, sems)
+
+    def whole(row):
+        return jnp.broadcast_to(coef_ref[row : row + 1, :], (8, LANES))[None]
+
+    def zero(n):
+        return jnp.zeros((n, 8, LANES), jnp.float32)
+
+    ratio = whole(live + 1)
+
+    def first(i, carry):
+        start = pl.multiple_of(i * RUN * 8, RUN * 8)
+        x = tokens[pl.ds(start, RUN * 8), :].astype(jnp.float32).reshape(RUN, 8, LANES)
+        mixed = whole(0) * x
+        row = lax.broadcasted_iota(jnp.int32, (1, 8, LANES), 1)
+        kept = []
+        for level, tail in enumerate(carry):
+            kept.append(x[RUN - tail.shape[0] :])
+            if level < 3:
+                turned = pltpu.roll(jnp.concatenate([tail, x], 0), 2**level, 1)
+                x = x + ratio * jnp.where(row < 2**level, turned[:RUN], turned[1:])
+            else:
+                x = advance(x, tail, ratio)
+            mixed = mixed + whole(level + 1) * x
+        stream_ref[pl.ds(i * RUN, RUN)] = x
+        mixed_ref[pl.ds(i * RUN, RUN)] = mixed
+        return tuple(kept)
+
+    lax.fori_loop(0, units // RUN, first, tuple(zero(n) for n in (1, 1, 1, 1, 2, 4)))
+
+    stream = stream_ref.reshape(units // MIDDLE, MIDDLE, 8, LANES)
+    total = mixed_ref.reshape(units // MIDDLE, MIDDLE, 8, LANES)
+    steps = units // MIDDLE // RUN
+
+    def second(t, carry):
+        q = t // steps
+        i = t % steps
+        x = stream[pl.ds(i * RUN, RUN), q]
+        mixed = total[pl.ds(i * RUN, RUN), q]
+        keep = jnp.where(i > 0, 1.0, 0.0)
+        kept = []
+        for level, tail in enumerate(carry):
+            kept.append(x[RUN - tail.shape[0] :])
+            x = advance(x, tail * keep, ratio)
+            mixed = mixed + whole(level + 7) * x
+        stream[pl.ds(i * RUN, RUN), q] = x
+        total[pl.ds(i * RUN, RUN), q] = mixed
+        return tuple(kept)
+
+    lax.fori_loop(0, MIDDLE * steps, second, tuple(zero(n) for n in (1, 2, 4)))
+
+    stream_wide = stream_ref.reshape(units // WIDE, WIDE, 8, LANES)
+    total_wide = mixed_ref.reshape(units // WIDE, WIDE, 8, LANES)
+    act_wide = act_ref.reshape(units // WIDE, WIDE // 2, 16, LANES)
+
+    def third(pair, _):
+        halves = []
+        for odd in range(2):
+            x = stream_wide[:, pair * 2 + odd]
+            mixed = total_wide[:, pair * 2 + odd]
+            for level in range(9, live):
+                x = advance(x, zero(2 ** (level - 9)), ratio)
+                mixed = mixed + whole(level + 1) * x
+            halves.append(jax.nn.gelu(mixed))
+        act_wide[:, pair] = jnp.concatenate(halves, 1).astype(jnp.bfloat16)
+        return 0
+
+    lax.fori_loop(0, WIDE // 2, third, 0)
+
+    half = rows // 2
+    pairs = []
+    for ahead in range(chips):
+        for other in range(2):
+            start = line_of(place, -ahead, other) * rows
+            for outs, which in ((far, 1 - side), (near, side)):
+                begin = pl.multiple_of(start + which * half, half)
+                pairs.append((act_ref.at[pl.ds(begin, half)], outs[ahead].at[other]))
+    copy_all(pairs, sems)
+
+
+def run_filter(place, coef, own, direct, handed, live):
+    chips = len(handed)
+    rows = handed[0].shape[0]
+    total = rows * 2 * chips
+    anywhere = pl.BlockSpec(memory_space=pltpu.HBM)
+    outs = pl.pallas_call(
+        functools.partial(levels_kernel, live, chips),
+        out_shape=[jax.ShapeDtypeStruct((2, rows // 2, LANES), jnp.bfloat16)] * (2 * chips),
+        in_specs=[
+            pl.BlockSpec(memory_space=pltpu.SMEM),
+            pl.BlockSpec(memory_space=pltpu.VMEM),
+        ]
+        + [anywhere] * (2 * chips),
+        out_specs=[anywhere] * (2 * chips),
+        scratch_shapes=[
+            pltpu.VMEM((total, LANES), jnp.bfloat16),
+            pltpu.VMEM((total // 8, 8, LANES), jnp.float32),
+            pltpu.VMEM((total // 8, 8, LANES), jnp.float32),
+            pltpu.VMEM((total, LANES), jnp.bfloat16),
+            pltpu.SemaphoreType.DMA((4 * chips,)),
+        ],
+        compiler_params=pltpu.CompilerParams(vmem_limit_bytes=GRANT),
+        name="levels",
+    )(place, coef, own, *direct, *handed)
+    return list(outs[:chips]), list(outs[chips:])
+
+
+def work(rows, depth, columns):
+    return pl.CostEstimate(
+        flops=2 * rows * depth * columns,
+        bytes_accessed=2 * (rows * depth + depth * columns + rows * columns),
+        transcendentals=0,
+    )
+
+
+def dot(a, b):
+    return jnp.dot(a, b, preferred_element_type=jnp.float32)
+
+
+def spread(place, source, pieces):
+    core, group = place[1], place[3]
+    depth = pieces[0].shape[0]
+    total = None
+    for piece, far_group, far_core in zip(pieces, (0, 1, 0, 1), (0, 0, 1, 1)):
+        quarter = 2 * (1 - group if far_group else group) + (1 - core if far_core else core)
+        rows = pl.ds(pl.multiple_of(quarter * depth, depth), depth)
+        term = dot(source[:, rows], piece[...])
+        total = term if total is None else total + term
+    return total
+
+
+def hidden_kernel(rounds, steps, place, *refs):
+    chips = sum(len(backs) for backs in rounds)
+    direct = refs[:chips]
+    handed, early, early_twin, late, late_twin, value_own, gate_own = refs[chips : chips + 7]
+    value_far, gate_far = refs[chips + 7], refs[chips + 8 : chips + 12]
+    hidden_ref, act, sems = refs[chips + 12 :]
+    step = pl.program_id(0)
+    side = place[2]
+    channels = 2 * chips * LANES
+
+    @pl.when(step == 0)
+    def _():
+        pairs = []
+        for backs, mine, twin in zip(rounds, (early, late), (early_twin, late_twin)):
+            for at, back in enumerate(backs):
+                for other, near, far in ((0, direct[back].at[0], mine), (1, handed.at[back], twin)):
+                    line = line_of(place, back, other) * LANES
+                    for start, block in (
+                        (side * channels + line, near),
+                        ((1 - side) * channels + line, far.at[at]),
+                    ):
+                        lanes = pl.ds(pl.multiple_of(start, LANES), LANES)
+                        pairs.append((block, act.at[:, lanes]))
+        copy_all(pairs, sems)
+
+    def put(value, gate):
+        hidden_ref[...] = (value * jax.nn.sigmoid(gate)).astype(jnp.bfloat16)
+
+    @pl.when(step < steps)
+    def _():
+        put(dot(act[...], value_own[...]), dot(act[...], gate_own[...]))
+
+    @pl.when(step >= steps)
+    def _():
+        put(dot(act[...], value_far[...]), spread(place, act, gate_far))
+
+
+def run_hidden(place, rounds, direct, handed, early, late, value_own, gate_own, value_far, gate_far):
+    chips = len(direct)
+    rows = handed.shape[1]
+    width, channels = value_own.shape
+    depth = gate_far[0].shape[0]
+    block = min(512, channels)
+    steps = channels // block
+
+    def first(j):
+        return jnp.minimum(j, steps - 1)
+
+    def last(j):
+        return jnp.maximum(j - steps, 0)
+
+    def spot(j, place):
+        side = place[2]
+        return (0, jnp.where(j < steps, side * steps + j, (1 - side) * steps + j - steps))
+
+    return pl.pallas_call(
+        functools.partial(hidden_kernel, rounds, steps),
+        grid_spec=pltpu.PrefetchScalarGridSpec(
+            num_scalar_prefetch=1,
+            grid=(2 * steps,),
+            in_specs=[pl.BlockSpec(memory_space=pltpu.HBM)] * (chips + 5)
+            + [pl.BlockSpec((width, block), lambda j, place: (0, first(j)))] * 2
+            + [pl.BlockSpec((width, block), lambda j, place: (0, last(j)))]
+            + [pl.BlockSpec((depth, block), lambda j, place: (0, last(j)))] * len(gate_far),
+            out_specs=pl.BlockSpec((rows, block), spot),
+            scratch_shapes=[
+                pltpu.VMEM((rows, width), jnp.bfloat16),
+                pltpu.SemaphoreType.DMA((4 * chips,)),
+            ],
+        ),
+        out_shape=jax.ShapeDtypeStruct((rows, width), jnp.bfloat16),
+        compiler_params=pltpu.CompilerParams(vmem_limit_bytes=GRANT),
+        cost_estimate=work(rows, width, 2 * width),
+        name="hidden",
+    )(place, *direct, handed, *early, *late, value_own, gate_own, value_far, *gate_far)
+
+
+def send_kernel(hidden, weight, out_ref):
+    out_ref[...] = dot(hidden[...], weight[...]).astype(jnp.bfloat16)
+
+
+def run_send(hidden, out_far, q):
+    rows, width = hidden.shape
+    channels = out_far.shape[1] // SPLIT
+    block = min(256, channels)
+    first = q * channels // block
+    return pl.pallas_call(
+        send_kernel,
+        grid=(channels // block,),
+        in_specs=[
+            pl.BlockSpec((rows, width), lambda j: (0, 0)),
+            pl.BlockSpec((width, block), lambda j: (0, first + j)),
+        ],
+        out_specs=pl.BlockSpec((rows, block), lambda j: (0, j)),
+        out_shape=jax.ShapeDtypeStruct((rows, channels), jnp.bfloat16),
+        compiler_params=pltpu.CompilerParams(vmem_limit_bytes=GRANT),
+        cost_estimate=work(rows, width, channels),
+        name="send",
+    )(hidden, out_far)
+
+
+def finish_kernel(side, hidden, weight, tokens, out_ref):
+    made = dot(hidden[...], weight[...])
+    out_ref[...] = (made + tokens[...].astype(jnp.float32)).astype(jnp.bfloat16)
+
+
+def run_finish(side, hidden, weight, tokens):
+    rows, width = hidden.shape
+    channels = weight.shape[1]
+    block = min(512, channels)
+    return pl.pallas_call(
+        finish_kernel,
+        grid_spec=pltpu.PrefetchScalarGridSpec(
+            num_scalar_prefetch=1,
+            grid=(channels // block,),
+            in_specs=[
+                pl.BlockSpec((rows, width), lambda j, side: (0, 0)),
+                pl.BlockSpec((width, block), lambda j, side: (0, j)),
+                pl.BlockSpec((rows, block), lambda j, side: (side[0], j)),
+            ],
+            out_specs=pl.BlockSpec((rows, block), lambda j, side: (side[0], j)),
+        ),
+        out_shape=jax.ShapeDtypeStruct(tokens.shape, jnp.bfloat16),
+        compiler_params=pltpu.CompilerParams(vmem_limit_bytes=GRANT),
+        cost_estimate=work(rows, width, channels),
+        name="finish",
+    )(side, hidden, weight, tokens)
+
+
+def add_kernel(side, got, tokens, kept, out_ref):
+    out_ref[...] = (got[...].astype(jnp.float32) + tokens[...].astype(jnp.float32)).astype(
+        jnp.bfloat16
+    )
+
+
+def add_far(side, q, got, tokens, result):
+    rows, columns = got.shape
+    block = rows // 2
+
+    def spot(j, side):
+        return (2 * (1 - side[0]) + j, q)
+
+    return pl.pallas_call(
+        add_kernel,
+        grid_spec=pltpu.PrefetchScalarGridSpec(
+            num_scalar_prefetch=1,
+            grid=(2,),
+            in_specs=[
+                pl.BlockSpec((block, columns), lambda j, side: (j, 0)),
+                pl.BlockSpec((block, columns), spot),
+                pl.BlockSpec(memory_space=pl.ANY),
+            ],
+            out_specs=pl.BlockSpec((block, columns), spot),
+        ),
+        out_shape=jax.ShapeDtypeStruct(tokens.shape, jnp.bfloat16),
+        input_output_aliases={3: 0},
+        name="add_far",
+    )(side, got, tokens, result)
+
+
+def swap(array, axis):
+    return lax.ppermute(array, axis, [(0, 1), (1, 0)])
+
+
+def cross(array):
+    return lax.ppermute(array, ("chan", "sub"), [(0, 3), (1, 2), (2, 1), (3, 0)])
+
+
+def ahead(array, offset):
+    chips = lax.axis_size("seq")
+    return lax.ppermute(array, "seq", [(j, (j + offset) % chips) for j in range(chips)])
+
+
+def anchor_kernel(place, *refs):
+    for at in range(refs[-1].shape[0]):
+        refs[-1][at] = place[at]
+
+
+def anchor(place, after):
+    return pl.pallas_call(
+        anchor_kernel,
+        in_specs=[pl.BlockSpec(memory_space=pltpu.SMEM)]
+        + [pl.BlockSpec(memory_space=pl.ANY)] * len(after),
+        out_specs=pl.BlockSpec(memory_space=pltpu.SMEM),
+        out_shape=jax.ShapeDtypeStruct(place.shape, place.dtype),
+        cost_estimate=pl.CostEstimate(flops=10**11, bytes_accessed=0, transcendentals=0),
+        name="anchor",
+    )(place, *after)
+
+
+def by_tokens(tokens, low_angle, high_taps, level_mix, w_value, w_gate, out_weight):
+    rows, channels = tokens.shape
+    chips = lax.axis_size("seq")
+    narrow = channels // (2 * chips)
+    chip, core = lax.axis_index("seq"), lax.axis_index("sub")
+    side, group = lax.axis_index("chan"), lax.axis_index("groups")
+    live = min(LEVELS, (rows * 2 * chips - 1).bit_length())
+    order = sorted(range(1, chips), key=lambda s: abs(2 * s - chips))
+    place = jnp.stack([chip, core, side, group, chips]).astype(jnp.int32)
+
+    blocks = run_cut(place, tokens, chips)
+    blocks, weights, low_angle = lax.optimization_barrier(
+        (blocks, (w_value, w_gate, out_weight), low_angle)
+    )
+    direct = [None] * chips
+    for s in order:
+        direct[s] = ahead(blocks[s], s)
+    handed = [swap(blocks[0], "sub")] + [swap(direct[s][1], "sub") for s in range(1, chips)]
+
+    value_piece, gate_piece, out_piece = run_pieces(place, weights)
+    value_first = swap(value_piece, "chan")
+    gate_first = swap(gate_piece, "chan")
+    direct, value_first, gate_first, out_piece = lax.optimization_barrier(
+        (direct, value_first, gate_first, out_piece)
+    )
+    value_far = lax.all_gather(value_first, ("groups", "sub"), tiled=True)
+    out_first = swap(out_piece, "chan")
+    gate_second = swap(gate_first, "groups")
+    gate_third = swap(gate_first, "sub")
+
+    coef = run_coefficients(place, low_angle, high_taps, level_mix, live)
+    far, near = run_filter(place, coef, tokens, direct[1:], handed, live)
+
+    far, gate_third = lax.optimization_barrier((far, gate_third))
+    far_got = [far[0]] + [None] * (chips - 1)
+    for s in order:
+        far_got[s] = ahead(far[s], s)
+
+    def exchange(backs):
+        return (
+            swap(jnp.stack([far_got[back][0] for back in backs]), "chan"),
+            cross(jnp.stack([far_got[back][1] for back in backs])),
+        )
+
+    rounds = [[0] + order[:1], order[1:]]
+    near, far_got[order[0]], out_first = lax.optimization_barrier(
+        (near, far_got[order[0]], out_first)
+    )
+    out_far = lax.all_gather(out_first, ("groups", "sub"), tiled=True)
+    early = exchange(rounds[0])
+    near_got = [near[0]] + [None] * (chips - 1)
+    for s, wait in zip(order, [None, *early]):
+        near[s], wait = lax.optimization_barrier((near[s], wait))
+        near_got[s] = ahead(near[s], s)
+    far_got, gate_second = lax.optimization_barrier((far_got, gate_second))
+    late = exchange(rounds[1])
+    place = anchor(place, [far_got[s] for s in order] + list(early))
+    near_got, late, place, gate_second = lax.optimization_barrier(
+        (near_got, late, place, gate_second)
+    )
+    gate_far = [gate_first, gate_second, gate_third, swap(gate_second, "sub")]
+    handed = swap(jnp.stack([block[1] for block in near_got]), "sub")
+    hidden = run_hidden(
+        place, rounds, near_got, handed, early, late, w_value, w_gate, value_far, gate_far
+    )
+    which = place[2:3]
+    returned = []
+    for q in range(SPLIT):
+        sent = run_send(hidden, out_far, q)
+        returned.append(swap(sent, "chan"))
+        hidden, sent = lax.optimization_barrier((hidden, sent))
+    hidden, returned[0] = lax.optimization_barrier((hidden, returned[0]))
+    result = run_finish(which, hidden, out_weight, tokens)
+    for q in range(SPLIT):
+        result = add_far(which, q, returned[q], tokens, result)
+    return result
+
+
 def solution(mesh):
+    def shards(tokens, *rest):
+        ways = mesh.shape["seq"] * mesh.shape["sub"]
+        pairs = all(mesh.shape[name] == 2 for name in ("groups", "chan", "sub"))
+        rows, channels = tokens.shape
+        fits = channels == ways * LANES and rows % 64 == 0
+        fits = fits and rows * ways == 8 * WIDE * RUN and rest[3].shape[0] % 512 == 0
+        return (by_tokens if pairs and fits else general)(tokens, *rest)
+
     return jax.shard_map(
         shards,
         mesh=mesh,

time: 333 us -> 199 us (0.60)
  waiting for transfers between devices: 160 us -> 76 us
  Pallas kernels: 0 us -> 62 us
  blocking collectives: 52.2 us -> 0 us
  other arithmetic: 43.1 us -> 0.18 us
  starting transfers between devices: 6.4 us -> 39 us
  local copies, waits for them, and re-layouts: 34.4 us -> 7.02 us
  matrix products: 23.4 us -> 0 us
    all_gather x2, waiting for transfers between devices: 113 us -> 0.02 us  [the longest x1 0.02 us: by_tokens(): out_far = lax.all_gather(out_first, ('groups', 'sub'), tiled=True)]
    ppermute x0 -> x26, waiting for transfers between devices: none -> 75.9 us  [the longest x9 45.3 us: ahead(): lax.ppermute(array, 'seq', [(j, (j + offset) % chips) for j in range(chip...]
    pallas_call x0 -> x11, Pallas kernels: none -> 62 us  [the longest x1 16.7 us: run_hidden(): pl.pallas_call(functools.partial(hidden_kernel, rounds, steps), grid_spec...]
    all_to_all x1 -> x0, blocking collectives: 52.2 us -> none  [shards(): lax.all_to_all(filtered, ('seq', 'sub'), split_axis=1, concat_axis=0, til...]
    all_to_all x1 -> x0, waiting for transfers between devices: 47 us -> none  [shards(): lax.all_to_all(tokens.T, ('seq', 'sub'), split_axis=0, concat_axis=1, til...]
    ppermute x0 -> x26, starting transfers between devices: none -> 38.9 us  [the longest x9 26.8 us: ahead(): lax.ppermute(array, 'seq', [(j, (j + offset) % chips) for j in range(chip...]
    convert_element_type x2 -> x0, other arithmetic: 28.5 us -> none  [the longest x1 26 us: shards(): filtered = jax.nn.gelu(mixed).astype(jnp.bfloat16)]
    dot_general x3 -> x0, matrix products: 23.4 us -> none  [the longest x1 9.28 us: shards(): jnp.dot(lax.all_gather(hidden, 'chan', axis=1, tiled=True), out_weight, p...]
  transfers between devices with their start and end apart: 3 -> 28, of which waited for: 3 -> 12; matrix products, arithmetic and copies ran while one was open for 1% -> 2% of each run, Pallas kernels for 0% -> 24%
where the time goes in v2:
time: 199 us; the launch traced here: 198 us
  waiting for transfers between devices  76 us (38%)
  Pallas kernels  62 us (31%)
  starting transfers between devices  39 us (20%)
  between operations  13.7 us (7%)
  local copies, waits for them, and re-layouts  7.02 us (4%)
    ppermute x9, waiting for transfers between devices, ahead(): lax.ppermute(array, 'seq', [(j, (j + offset) % chips) for j in range(chip...  45.3 us
    ppermute x15, waiting for transfers between devices, swap(): return lax.ppermute(array, axis, [(0, 1), (1, 0)])  30.1 us
    ppermute x9, starting transfers between devices, ahead(): lax.ppermute(array, 'seq', [(j, (j + offset) % chips) for j in range(chip...  26.8 us
    pallas_call x1, Pallas kernels, run_hidden(): pl.pallas_call(functools.partial(hidden_kernel, rounds, steps), grid_spec...  16.7 us
    pallas_call x1, Pallas kernels, run_filter(): pl.pallas_call(functools.partial(levels_kernel, live, chips), out_shape=[...  15.1 us
    ppermute x15, starting transfers between devices, swap(): return lax.ppermute(array, axis, [(0, 1), (1, 0)])  10.5 us
    pallas_call x2, Pallas kernels, run_send(): pl.pallas_call(send_kernel, grid=(channels // block,), in_specs=[pl.Block...  8.21 us
    pallas_call x1, Pallas kernels, run_finish(): pl.pallas_call(finish_kernel, grid_spec=pltpu.PrefetchScalarGridSpec(num_...  6.37 us
  transfers between devices with their start and end apart: 28, of which 12 were waited for; matrix products, arithmetic and copies ran while one was open for 2% of the time, Pallas kernels for 24%

profile of v2, /device:TPU:0, one launch (start us, length us, event | category | flops | bytes accessed | tf_op | source)
XLA Modules:
  0.0 197.9 jit_solution(12297560699746479791)
XLA Ops:
  6.5 0.7 stack.34.place
  7.2 3.3 %cut.1 = (bf16[1024,128]{1,0:T(8,128)(2,1)}, bf16[2,1024,128]{2,1,0:T(8,128)(2,1)}, bf16[2,1024,128]{2,1,0:T(8,128)(2,1)}, bf16[2,1024,128]{2,1,0:T(8,128)(2,1)}) custom-call(s32[5]{0:T(128)} %stack.34.place, bf16[1024,1024]{1,0:T(8,128)(2,1)} %tokens.7), custom_call_target="tpu_custom_call" | custom-call | tf_op jit(solution)/shard_map/cut/pallas_call | solution.py:145
  10.5 3.0 %collective-permute-start = (bf16[2,1024,128]{2,1,0:T(8,128)(2,1)}, bf16[2,1024,128]{2,1,0:T(8,128)(2,1)S(1)}, u32[]{:S(2)}, u32[]{:S(2)}) collective-permute-start(bf16[2,1024,128]{2,1,0:T(8,128)(2,1)} %get-tuple-element.68), channel_id=1, source_target_pairs={{0,4},{4,8},{8,12},{12,0},{1,5},{5,9},{9,13},{13,1},{2,6},{6,10},{... | collective-permute-start | bytes 1572872 | tf_op jit(solution)/shard_map/ppermute | solution.py:504
  13.6 4.3 %pieces.1 = (bf16[512,1024]{1,0:T(8,128)(2,1)}, bf16[512,1024]{1,0:T(8,128)(2,1)}, bf16[512,1024]{1,0:T(8,128)(2,1)}) custom-call(s32[5]{0:T(128)} %stack.34.place, bf16[2048,1024]{1,0:T(8,128)(2,1)} %refs_9_.1, bf16[2048,1024]{1,0:T(8,128)(2,1)} %refs_10_.1, bf16[2048,1024]{1,0:T(8,128)(2,1)} %weight.1), custom_call_target="tpu_custom_call" | custom-call | tf_op jit(solution)/shard_map/pieces/pallas_call | solution.py:173
  17.8 1.6 collective-permute-start.3
  19.4 0.5 collective-permute-start.4
  19.9 2.6 %collective-permute-start.1 = (bf16[2,1024,128]{2,1,0:T(8,128)(2,1)S(1)}, bf16[2,1024,128]{2,1,0:T(8,128)(2,1)S(1)}, u32[]{:S(2)}, u32[]{:S(2)}) collective-permute-start(bf16[2,1024,128]{2,1,0:T(8,128)(2,1)S(1)} %copy-done.17), channel_id=1, source_target_pairs={{0,8},{4,12},{8,0},{12,4},{1,9},{5,13},{9,1},{13,5},{2,10},{6,14},... | collective-permute-start | bytes 1572872 | tf_op jit(solution)/shard_map/ppermute | solution.py:504
  22.5 1.3 collective-permute-start.2
  23.9 4.8 %collective-permute-done.refs_0_ = bf16[2,1024,128]{2,1,0:T(8,128)(2,1)S(1)} collective-permute-done((bf16[2,1024,128]{2,1,0:T(8,128)(2,1)}, bf16[2,1024,128]{2,1,0:T(8,128)(2,1)S(1)}, u32[]{:S(2)}, u32[]{:S(2)}) %collective-permute-start) | collective-permute-done | bytes 524320 | tf_op jit(solution)/shard_map/ppermute | solution.py:504
  28.7 0.8 slice_bitcast_fusion.2
  29.5 20.9 %collective-permute-done.1.refs_1_ = bf16[2,1024,128]{2,1,0:T(8,128)(2,1)S(1)} collective-permute-done((bf16[2,1024,128]{2,1,0:T(8,128)(2,1)S(1)}, bf16[2,1024,128]{2,1,0:T(8,128)(2,1)S(1)}, u32[]{:S(2)}, u32[]{:S(2)}) %collective-permute-start.1) | collective-permute-done | bytes 524320 | tf_op jit(solution)/shard_map/ppermute | solution.py:504
  50.3 0.8 slice_bitcast_fusion.1
  51.6 0.7 slice_bitcast_fusion
  52.4 12.9 %collective-permute-done.4.refs_12_ = bf16[512,1024]{1,0:T(8,128)(2,1)} collective-permute-done((bf16[512,1024]{1,0:T(8,128)(2,1)}, bf16[512,1024]{1,0:T(8,128)(2,1)}, u32[]{:S(2)}, u32[]{:S(2)}) %collective-permute-start.4) | collective-permute-done | bytes 1048608 | tf_op jit(solution)/shard_map/ppermute | solution.py:495
  65.4 1.6 collective-permute-start.19
  67.0 1.5 collective-permute-start.11
  68.5 1.6 coefficients.1.coef_ref
  70.2 0.7 copy-done.9
  70.9 15.1 %levels.1 = (bf16[2,512,128]{2,1,0:T(8,128)(2,1)}, bf16[2,512,128]{2,1,0:T(8,128)(2,1)}, bf16[2,512,128]{2,1,0:T(8,128)(2,1)}, bf16[2,512,128]{2,1,0:T(8,128)(2,...) custom-call(s32[5]{0:T(128)} %stack.34.place, ...), custom_call_target="tpu_custom_call" | custom-call | tf_op jit(solution)/shard_map/levels/pallas_call | solution.py:288
  86.0 2.6 %collective-permute-start.10 = (bf16[2,512,128]{2,1,0:T(8,128)(2,1)}, bf16[2,512,128]{2,1,0:T(8,128)(2,1)S(1)}, u32[]{:S(2)}, u32[]{:S(2)}) collective-permute-start(bf16[2,512,128]{2,1,0:T(8,128)(2,1)} %get-tuple-element.90), channel_id=1, source_target_pairs={{0,8},{4,12},{8,0},{12,4},{1,9},{5,13},{9,1},{13,5},{2,10},{6,14},... | collective-permute-start | bytes 786440 | tf_op jit(solution)/shard_map/ppermute | solution.py:504
  88.9 3.5 %collective-permute-start.18 = (bf16[2,512,128]{2,1,0:T(8,128)(2,1)}, bf16[2,512,128]{2,1,0:T(8,128)(2,1)S(1)}, u32[]{:S(2)}, u32[]{:S(2)}) collective-permute-start(bf16[2,512,128]{2,1,0:T(8,128)(2,1)} %get-tuple-element.101), channel_id=1, source_target_pairs={{0,12},{4,0},{8,4},{12,8},{1,13},{5,1},{9,5},{13,9},{2,14},{6,2},{... | collective-permute-start | bytes 786440 | tf_op jit(solution)/shard_map/ppermute | solution.py:504
  92.5 1.0 fusion.2
  93.5 14.2 %collective-permute-done.10.refs_0_ = bf16[2,512,128]{2,1,0:T(8,128)(2,1)S(1)} collective-permute-done((bf16[2,512,128]{2,1,0:T(8,128)(2,1)}, bf16[2,512,128]{2,1,0:T(8,128)(2,1)S(1)}, u32[]{:S(2)}, u32[]{:S(2)}) %collective-permute-start.10) | collective-permute-done | bytes 262176 | tf_op jit(solution)/shard_map/ppermute | solution.py:504
  107.8 0.5 collective-permute-start.12
  108.4 1.5 collective-permute-start.21
  110.0 1.6 collective-permute-start.20
  111.6 5.9 %collective-permute-start.14 = (bf16[2,512,128]{2,1,0:T(8,128)(2,1)}, bf16[2,512,128]{2,1,0:T(8,128)(2,1)S(1)}, u32[]{:S(2)}, u32[]{:S(2)}) collective-permute-start(bf16[2,512,128]{2,1,0:T(8,128)(2,1)} %get-tuple-element.97), channel_id=1, source_target_pairs={{0,8},{4,12},{8,0},{12,4},{1,9},{5,13},{9,1},{13,5},{2,10},{6,14},... | collective-permute-start | bytes 786440 | tf_op jit(solution)/shard_map/ppermute | solution.py:504
  117.5 1.7 collective-permute-start.16
  119.2 1.0 collective-permute-done.12.refs_3_.refs_5_
  120.2 5.8 %collective-permute-start.13 = (bf16[2,512,128]{2,1,0:T(8,128)(2,1)S(1)}, bf16[2,512,128]{2,1,0:T(8,128)(2,1)S(1)}, u32[]{:S(2)}, u32[]{:S(2)}) collective-permute-start(bf16[2,512,128]{2,1,0:T(8,128)(2,1)S(1)} %copy-done.19), channel_id=1, source_target_pairs={{0,4},{4,8},{8,12},{12,0},{1,5},{5,9},{9,13},{13,1},{2,6},{6,10},{... | collective-permute-start | bytes 786440 | tf_op jit(solution)/shard_map/ppermute | solution.py:504
  126.0 1.2 anchor.1.place
  127.7 3.7 %collective-permute-done.20.refs_7_ = bf16[2,512,128]{2,1,0:T(8,128)(2,1)} collective-permute-done((bf16[2,512,128]{2,1,0:T(8,128)(2,1)S(1)}, bf16[2,512,128]{2,1,0:T(8,128)(2,1)}, u32[]{:S(2)}, u32[]{:S(2)}) %collective-permute-start.20) | collective-permute-done | bytes 262176 | tf_op jit(solution)/shard_map/ppermute | solution.py:495
  131.4 4.7 %collective-permute-done.14.refs_2_ = bf16[2,512,128]{2,1,0:T(8,128)(2,1)S(1)} collective-permute-done((bf16[2,512,128]{2,1,0:T(8,128)(2,1)}, bf16[2,512,128]{2,1,0:T(8,128)(2,1)S(1)}, u32[]{:S(2)}, u32[]{:S(2)}) %collective-permute-start.14) | collective-permute-done | bytes 262176 | tf_op jit(solution)/shard_map/ppermute | solution.py:504
  136.1 0.8 collective-permute-done.16.refs_3_
  137.1 0.5 collective-permute-start.22
  137.7 2.7 %collective-permute-done.22.refs_4_ = bf16[4,512,128]{2,1,0:T(8,128)(2,1)S(1)} collective-permute-done((bf16[4,512,128]{2,1,0:T(8,128)(2,1)S(1)}, bf16[4,512,128]{2,1,0:T(8,128)(2,1)S(1)}, u32[]{:S(2)}, u32[]{:S(2)}) %collective-permute-start.22) | collective-permute-done | bytes 524320 | tf_op jit(solution)/shard_map/ppermute | solution.py:495
  140.4 0.8 copy-done.18
  141.2 16.7 %hidden.1 = bf16[512,2048]{1,0:T(8,128)(2,1)} custom-call(s32[5]{0:T(128)} %anchor.1.place, bf16[2,512,128]{2,1,0:T(8,128)(2,1)} %get-tuple-element.107.refs_0_, bf16[2,512,128]{2,1,0:T(8,128)(2,1)} %copy-done.16, bf16[2,512,128]{2,1,0:T(8,128)(2,1)} %copy-done.14, bf16[2,512,128]{2,1,0:T(8,128)(2,1)} %copy-done.15, bf16[4,512,128]{2,1,0:T(8,128)(2,1)} %copy-done.18, ...), custom_call_target="tpu_custom_call" | custom-call | flops 8589934592 | bytes 23068672 | tf_op jit(solution)/shard_map/hidden/pallas_call | solution.py:389
  157.9 4.1 %send.2 = bf16[512,512]{1,0:T(8,128)(2,1)} custom-call(bf16[512,2048]{1,0:T(8,128)(2,1)} %hidden.1, bf16[2048,1024]{1,0:T(8,128)(2,1)} %all-gather.5.cloned.1.call-done.weight), custom_call_target="tpu_custom_call" | custom-call | flops 1073741824 | bytes 4718592 | tf_op jit(solution)/shard_map/send/pallas_call | solution.py:420
  162.0 1.9 collective-permute-start.25
  163.9 4.1 %send.3 = bf16[512,512]{1,0:T(8,128)(2,1)} custom-call(bf16[512,2048]{1,0:T(8,128)(2,1)} %hidden.1, bf16[2048,1024]{1,0:T(8,128)(2,1)} %all-gather.5.cloned.1.call-done.weight), custom_call_target="tpu_custom_call" | custom-call | flops 1073741824 | bytes 4718592 | tf_op jit(solution)/shard_map/send/pallas_call | solution.py:420
  168.2 0.6 slice.59.side
  168.8 8.2 %collective-permute-done.25.got = bf16[512,512]{1,0:T(8,128)(2,1)S(1)} collective-permute-done((bf16[512,512]{1,0:T(8,128)(2,1)}, bf16[512,512]{1,0:T(8,128)(2,1)S(1)}, u32[]{:S(2)}, u32[]{:S(2)}) %collective-permute-start.25) | collective-permute-done | bytes 524320 | tf_op jit(solution)/shard_map/ppermute | solution.py:495
  177.0 6.4 %finish.1.kept = bf16[1024,1024]{1,0:T(8,128)(2,1)} custom-call(s32[1]{0:T(128)} %slice.59.side, bf16[512,2048]{1,0:T(8,128)(2,1)} %hidden.1, bf16[2048,1024]{1,0:T(8,128)(2,1)} %weight.1, bf16[1024,1024]{1,0:T(8,128)(2,1)} %tokens.7), custom_call_target="tpu_custom_call" | custom-call | flops 2147483648 | bytes 7340032 | tf_op jit(solution)/shard_map/finish/pallas_call | solution.py:444
  183.4 2.6 %add_far.2.kept = bf16[1024,1024]{1,0:T(8,128)(2,1)} custom-call(s32[1]{0:T(128)} %slice.59.side, bf16[512,512]{1,0:T(8,128)(2,1)} %copy-done.6, bf16[1024,1024]{1,0:T(8,128)(2,1)} %tokens.7, bf16[1024,1024]{1,0:T(8,128)(2,1)} %finish.1.kept), custom_call_target="tpu_custom_call", output_to_operand_aliasing={{}: (3, {})} | custom-call | tf_op jit(solution)/shard_map/add_far/pallas_call | solution.py:476
  186.0 1.6 collective-permute-done.24.got
  187.6 0.8 copy-done.5
  188.4 2.6 %add_far.3 = bf16[1024,1024]{1,0:T(8,128)(2,1)} custom-call(s32[1]{0:T(128)} %slice.59.side, bf16[512,512]{1,0:T(8,128)(2,1)} %copy-done.5, bf16[1024,1024]{1,0:T(8,128)(2,1)} %tokens.7, bf16[1024,1024]{1,0:T(8,128)(2,1)} %add_far.2.kept), custom_call_target="tpu_custom_call", output_to_operand_aliasing={{}: (3, {})} | custom-call | tf_op jit(solution)/shard_map/add_far/pallas_call | solution.py:476
  (80 shorter events, 2.1 us)
Async XLA Ops:
  6.5 133.9 %all-gather.3.cloned.1.call-start = ((), (), s32[]{:S(2)}) async-start(), calls=%async_computation | async-start | bytes 5242880 | tf_op jit(solution)/shard_map/all_gather | solution.py:549
  10.5 9.4 %copy-start.17 = (bf16[2,1024,128]{2,1,0:T(8,128)(2,1)S(1)}, bf16[2,1024,128]{2,1,0:T(8,128)(2,1)}, u32[]{:S(2)}) copy-start(bf16[2,1024,128]{2,1,0:T(8,128)(2,1)} %get-tuple-element.69) | copy-start | bytes 1572868
  10.5 18.2 %collective-permute-start = (bf16[2,1024,128]{2,1,0:T(8,128)(2,1)}, bf16[2,1024,128]{2,1,0:T(8,128)(2,1)S(1)}, u32[]{:S(2)}, u32[]{:S(2)}) collective-permute-start(bf16[2,1024,128]{2,1,0:T(8,128)(2,1)} %get-tuple-element.68), channel_id=1, source_target_pairs={{0,4},{4,8},{8,12},{12,0},{1,5},{5,9},{9,13},{13,1},{2,6},{6,10},{... | collective-permute-start | bytes 1572872 | tf_op jit(solution)/shard_map/ppermute | solution.py:504
  17.8 34.5 %collective-permute-start.3 = (bf16[512,1024]{1,0:T(8,128)(2,1)}, bf16[512,1024]{1,0:T(8,128)(2,1)S(1)}, u32[]{:S(2)}, u32[]{:S(2)}) collective-permute-start(bf16[512,1024]{1,0:T(8,128)(2,1)} %get-tuple-element.74), channel_id=1, source_target_pairs={{0,2},{2,0},{1,3},{3,1},{4,6},{6,4},{5,7},{7,5},{8,10},{10,8},{9,1... | collective-permute-start | bytes 3145736 | tf_op jit(solution)/shard_map/ppermute | solution.py:495
  19.4 45.9 %collective-permute-start.4 = (bf16[512,1024]{1,0:T(8,128)(2,1)}, bf16[512,1024]{1,0:T(8,128)(2,1)}, u32[]{:S(2)}, u32[]{:S(2)}) collective-permute-start(bf16[512,1024]{1,0:T(8,128)(2,1)} %get-tuple-element.75), channel_id=1, source_target_pairs={{0,2},{2,0},{1,3},{3,1},{4,6},{6,4},{5,7},{7,5},{8,10},{10,8},{9,1... | collective-permute-start | bytes 3145736 | tf_op jit(solution)/shard_map/ppermute | solution.py:495
  19.9 30.4 %collective-permute-start.1 = (bf16[2,1024,128]{2,1,0:T(8,128)(2,1)S(1)}, bf16[2,1024,128]{2,1,0:T(8,128)(2,1)S(1)}, u32[]{:S(2)}, u32[]{:S(2)}) collective-permute-start(bf16[2,1024,128]{2,1,0:T(8,128)(2,1)S(1)} %copy-done.17), channel_id=1, source_target_pairs={{0,8},{4,12},{8,0},{12,4},{1,9},{5,13},{9,1},{13,5},{2,10},{6,14},... | collective-permute-start | bytes 1572872 | tf_op jit(solution)/shard_map/ppermute | solution.py:504
  22.5 28.6 %collective-permute-start.2 = (bf16[2,1024,128]{2,1,0:T(8,128)(2,1)}, bf16[2,1024,128]{2,1,0:T(8,128)(2,1)S(1)}, u32[]{:S(2)}, u32[]{:S(2)}) collective-permute-start(bf16[2,1024,128]{2,1,0:T(8,128)(2,1)} %get-tuple-element.70), channel_id=1, source_target_pairs={{0,12},{4,0},{8,4},{12,8},{1,13},{5,1},{9,5},{13,9},{2,14},{6,2},{... | collective-permute-start | bytes 1572872 | tf_op jit(solution)/shard_map/ppermute | solution.py:504
  28.7 41.4 %copy-start = (bf16[2,1024,128]{2,1,0:T(8,128)(2,1)}, bf16[2,1024,128]{2,1,0:T(8,128)(2,1)S(1)}, u32[]{:S(2)}) copy-start(bf16[2,1024,128]{2,1,0:T(8,128)(2,1)S(1)} %collective-permute-done.refs_0_) | copy-start | bytes 1572868
  28.7 36.7 %collective-permute-start.5 = (bf16[1024,128]{1,0:T(8,128)(2,1)}, bf16[1024,128]{1,0:T(8,128)(2,1)S(1)}, u32[]{:S(2)}, u32[]{:S(2)}) collective-permute-start(bf16[1024,128]{1,0:T(8,128)(2,1)} %get-tuple-element.80), channel_id=1, source_target_pairs={{0,1},{1,0},{2,3},{3,2},{4,5},{5,4},{6,7},{7,6},{8,9},{9,8},{10,11... | collective-permute-start | bytes 786440 | tf_op jit(solution)/shard_map/ppermute | solution.py:495
  50.3 19.8 %copy-start.1 = (bf16[2,1024,128]{2,1,0:T(8,128)(2,1)}, bf16[2,1024,128]{2,1,0:T(8,128)(2,1)S(1)}, u32[]{:S(2)}) copy-start(bf16[2,1024,128]{2,1,0:T(8,128)(2,1)S(1)} %collective-permute-done.1.refs_1_) | copy-start | bytes 1572868
  50.3 16.7 %collective-permute-start.6 = (bf16[1024,128]{1,0:T(8,128)(2,1)}, bf16[1024,128]{1,0:T(8,128)(2,1)S(1)}, u32[]{:S(2)}, u32[]{:S(2)}) collective-permute-start(bf16[1024,128]{1,0:T(8,128)(2,1)} %slice_bitcast_fusion.2), channel_id=1, source_target_pairs={{0,1},{1,0},{2,3},{3,2},{4,5},{5,4},{6,7},{7,6},{8,9},{9,8},{10,11... | collective-permute-start | bytes 786440 | tf_op jit(solution)/shard_map/ppermute | solution.py:495
  51.1 19.0 %copy-start.2 = (bf16[2,1024,128]{2,1,0:T(8,128)(2,1)}, bf16[2,1024,128]{2,1,0:T(8,128)(2,1)S(1)}, u32[]{:S(2)}) copy-start(bf16[2,1024,128]{2,1,0:T(8,128)(2,1)S(1)} %collective-permute-done.2.refs_2_) | copy-start | bytes 1572868
  51.1 19.0 %collective-permute-start.7 = (bf16[1024,128]{1,0:T(8,128)(2,1)}, bf16[1024,128]{1,0:T(8,128)(2,1)S(1)}, u32[]{:S(2)}, u32[]{:S(2)}) collective-permute-start(bf16[1024,128]{1,0:T(8,128)(2,1)} %slice_bitcast_fusion.1), channel_id=1, source_target_pairs={{0,1},{1,0},{2,3},{3,2},{4,5},{5,4},{6,7},{7,6},{8,9},{9,8},{10,11... | collective-permute-start | bytes 786440 | tf_op jit(solution)/shard_map/ppermute | solution.py:495
  52.3 13.0 %copy-start.3 = (bf16[512,1024]{1,0:T(8,128)(2,1)}, bf16[512,1024]{1,0:T(8,128)(2,1)S(1)}, u32[]{:S(2)}) copy-start(bf16[512,1024]{1,0:T(8,128)(2,1)S(1)} %collective-permute-done.3) | copy-start | bytes 3145732
  52.3 17.8 %collective-permute-start.8 = (bf16[1024,128]{1,0:T(8,128)(2,1)}, bf16[1024,128]{1,0:T(8,128)(2,1)}, u32[]{:S(2)}, u32[]{:S(2)}) collective-permute-start(bf16[1024,128]{1,0:T(8,128)(2,1)} %slice_bitcast_fusion), channel_id=1, source_target_pairs={{0,1},{1,0},{2,3},{3,2},{4,5},{5,4},{6,7},{7,6},{8,9},{9,8},{10,11... | collective-permute-start | bytes 786440 | tf_op jit(solution)/shard_map/ppermute | solution.py:495
  65.3 20.7 %collective-permute-start.9 = (bf16[512,1024]{1,0:T(8,128)(2,1)}, bf16[512,1024]{1,0:T(8,128)(2,1)}, u32[]{:S(2)}, u32[]{:S(2)}) collective-permute-start(bf16[512,1024]{1,0:T(8,128)(2,1)} %collective-permute-done.4.refs_12_), channel_id=1, source_target_pairs={{0,1},{1,0},{2,3},{3,2},{4,5},{5,4},{6,7},{7,6},{8,9},{9,8},{10,11... | collective-permute-start | bytes 3145736 | tf_op jit(solution)/shard_map/ppermute | solution.py:495
  65.3 92.6 %all-gather.5.cloned.1.call-start = ((), (), s32[]{:S(2)}) async-start(), calls=%async_computation.1 | async-start | bytes 5242880 | tf_op jit(solution)/shard_map/all_gather | solution.py:572
  65.4 4.7 %copy-start.7 = (bf16[1024,128]{1,0:T(8,128)(2,1)}, bf16[1024,128]{1,0:T(8,128)(2,1)S(1)}, u32[]{:S(2)}) copy-start(bf16[1024,128]{1,0:T(8,128)(2,1)S(1)} %collective-permute-done.5.refs_3_) | copy-start | bytes 786436
  65.4 42.2 %collective-permute-start.19 = (bf16[512,1024]{1,0:T(8,128)(2,1)}, bf16[512,1024]{1,0:T(8,128)(2,1)}, u32[]{:S(2)}, u32[]{:S(2)}) collective-permute-start(bf16[512,1024]{1,0:T(8,128)(2,1)} %collective-permute-done.4.refs_12_), channel_id=1, source_target_pairs={{0,16},{16,0},{1,17},{17,1},{2,18},{18,2},{3,19},{19,3},{4,20},{20... | collective-permute-start | bytes 3145736 | tf_op jit(solution)/shard_map/ppermute | solution.py:495
  67.0 3.1 %copy-start.8 = (bf16[1024,128]{1,0:T(8,128)(2,1)}, bf16[1024,128]{1,0:T(8,128)(2,1)S(1)}, u32[]{:S(2)}) copy-start(bf16[1024,128]{1,0:T(8,128)(2,1)S(1)} %collective-permute-done.6.refs_4_) | copy-start | bytes 786436
  67.0 26.4 %collective-permute-start.11 = (bf16[512,1024]{1,0:T(8,128)(2,1)}, bf16[512,1024]{1,0:T(8,128)(2,1)S(1)}, u32[]{:S(2)}, u32[]{:S(2)}) collective-permute-start(bf16[512,1024]{1,0:T(8,128)(2,1)} %get-tuple-element.91), channel_id=1, source_target_pairs={{0,2},{2,0},{1,3},{3,1},{4,6},{6,4},{5,7},{7,5},{8,10},{10,8},{9,1... | collective-permute-start | bytes 3145736 | tf_op jit(solution)/shard_map/ppermute | solution.py:495
  86.0 34.2 %copy-start.19 = (bf16[2,512,128]{2,1,0:T(8,128)(2,1)S(1)}, bf16[2,512,128]{2,1,0:T(8,128)(2,1)}, u32[]{:S(2)}) copy-start(bf16[2,512,128]{2,1,0:T(8,128)(2,1)} %get-tuple-element.96) | copy-start | bytes 786436
  86.0 21.6 %collective-permute-start.10 = (bf16[2,512,128]{2,1,0:T(8,128)(2,1)}, bf16[2,512,128]{2,1,0:T(8,128)(2,1)S(1)}, u32[]{:S(2)}, u32[]{:S(2)}) collective-permute-start(bf16[2,512,128]{2,1,0:T(8,128)(2,1)} %get-tuple-element.90), channel_id=1, source_target_pairs={{0,8},{4,12},{8,0},{12,4},{1,9},{5,13},{9,1},{13,5},{2,10},{6,14},... | collective-permute-start | bytes 786440 | tf_op jit(solution)/shard_map/ppermute | solution.py:504
  88.6 19.0 %collective-permute-start.17 = (bf16[2,512,128]{2,1,0:T(8,128)(2,1)}, bf16[2,512,128]{2,1,0:T(8,128)(2,1)S(1)}, u32[]{:S(2)}, u32[]{:S(2)}) collective-permute-start(bf16[2,512,128]{2,1,0:T(8,128)(2,1)} %get-tuple-element.100), channel_id=1, source_target_pairs={{0,4},{4,8},{8,12},{12,0},{1,5},{5,9},{9,13},{13,1},{2,6},{6,10},{... | collective-permute-start | bytes 786440 | tf_op jit(solution)/shard_map/ppermute | solution.py:504
  88.9 18.7 %collective-permute-start.18 = (bf16[2,512,128]{2,1,0:T(8,128)(2,1)}, bf16[2,512,128]{2,1,0:T(8,128)(2,1)S(1)}, u32[]{:S(2)}, u32[]{:S(2)}) collective-permute-start(bf16[2,512,128]{2,1,0:T(8,128)(2,1)} %get-tuple-element.101), channel_id=1, source_target_pairs={{0,12},{4,0},{8,4},{12,8},{1,13},{5,1},{9,5},{13,9},{2,14},{6,2},{... | collective-permute-start | bytes 786440 | tf_op jit(solution)/shard_map/ppermute | solution.py:504
  93.5 24.0 %copy-start.4 = (bf16[512,1024]{1,0:T(8,128)(2,1)}, bf16[512,1024]{1,0:T(8,128)(2,1)S(1)}, u32[]{:S(2)}) copy-start(bf16[512,1024]{1,0:T(8,128)(2,1)S(1)} %collective-permute-done.11) | copy-start | bytes 3145732
  107.6 18.4 %copy-start.10 = (bf16[2,512,128]{2,1,0:T(8,128)(2,1)}, bf16[2,512,128]{2,1,0:T(8,128)(2,1)S(1)}, u32[]{:S(2)}) copy-start(bf16[2,512,128]{2,1,0:T(8,128)(2,1)S(1)} %collective-permute-done.10.refs_0_) | copy-start | bytes 786436
  107.6 18.4 %copy-start.11 = (bf16[2,512,128]{2,1,0:T(8,128)(2,1)}, bf16[2,512,128]{2,1,0:T(8,128)(2,1)S(1)}, u32[]{:S(2)}) copy-start(bf16[2,512,128]{2,1,0:T(8,128)(2,1)S(1)} %collective-permute-done.17.refs_1_) | copy-start | bytes 786436
  107.7 18.4 %copy-start.12 = (bf16[2,512,128]{2,1,0:T(8,128)(2,1)}, bf16[2,512,128]{2,1,0:T(8,128)(2,1)S(1)}, u32[]{:S(2)}) copy-start(bf16[2,512,128]{2,1,0:T(8,128)(2,1)S(1)} %collective-permute-done.18.refs_2_) | copy-start | bytes 786436
  107.7 9.8 %collective-permute-start.15 = (bf16[2,512,128]{2,1,0:T(8,128)(2,1)S(1)}, bf16[2,512,128]{2,1,0:T(8,128)(2,1)}, u32[]{:S(2)}, u32[]{:S(2)}) collective-permute-start(bf16[2,512,128]{2,1,0:T(8,128)(2,1)S(1)} %pad_maximum_fusion.2), channel_id=1, source_target_pairs={{0,3},{1,2},{2,1},{3,0},{4,7},{5,6},{6,5},{7,4},{8,11},{9,10},{10,... | collective-permute-start | bytes 786440 | tf_op jit(solution)/shard_map/ppermute | solution.py:499
  107.8 12.3 %collective-permute-start.12 = (bf16[2,512,128]{2,1,0:T(8,128)(2,1)S(1)}, bf16[2,512,128]{2,1,0:T(8,128)(2,1)}, u32[]{:S(2)}, u32[]{:S(2)}) collective-permute-start(bf16[2,512,128]{2,1,0:T(8,128)(2,1)S(1)} %pad_maximum_fusion.1), channel_id=1, source_target_pairs={{0,2},{2,0},{1,3},{3,1},{4,6},{6,4},{5,7},{7,5},{8,10},{10,8},{9,1... | collective-permute-start | bytes 786440 | tf_op jit(solution)/shard_map/ppermute | solution.py:495
  108.4 19.3 %collective-permute-start.21 = (bf16[2,512,128]{2,1,0:T(8,128)(2,1)S(1)}, bf16[2,512,128]{2,1,0:T(8,128)(2,1)}, u32[]{:S(2)}, u32[]{:S(2)}) collective-permute-start(bf16[2,512,128]{2,1,0:T(8,128)(2,1)S(1)} %pad_maximum_fusion.4), channel_id=1, source_target_pairs={{0,3},{1,2},{2,1},{3,0},{4,7},{5,6},{6,5},{7,4},{8,11},{9,10},{10,... | collective-permute-start | bytes 786440 | tf_op jit(solution)/shard_map/ppermute | solution.py:499
  110.0 21.4 %collective-permute-start.20 = (bf16[2,512,128]{2,1,0:T(8,128)(2,1)S(1)}, bf16[2,512,128]{2,1,0:T(8,128)(2,1)}, u32[]{:S(2)}, u32[]{:S(2)}) collective-permute-start(bf16[2,512,128]{2,1,0:T(8,128)(2,1)S(1)} %pad_maximum_fusion.3), channel_id=1, source_target_pairs={{0,2},{2,0},{1,3},{3,1},{4,6},{6,4},{5,7},{7,5},{8,10},{10,8},{9,1... | collective-permute-start | bytes 786440 | tf_op jit(solution)/shard_map/ppermute | solution.py:495
  111.6 24.5 %collective-permute-start.14 = (bf16[2,512,128]{2,1,0:T(8,128)(2,1)}, bf16[2,512,128]{2,1,0:T(8,128)(2,1)S(1)}, u32[]{:S(2)}, u32[]{:S(2)}) collective-permute-start(bf16[2,512,128]{2,1,0:T(8,128)(2,1)} %get-tuple-element.97), channel_id=1, source_target_pairs={{0,8},{4,12},{8,0},{12,4},{1,9},{5,13},{9,1},{13,5},{2,10},{6,14},... | collective-permute-start | bytes 786440 | tf_op jit(solution)/shard_map/ppermute | solution.py:504
  117.5 19.5 %copy-start.13 = (bf16[2,512,128]{2,1,0:T(8,128)(2,1)S(1)}, bf16[2,512,128]{2,1,0:T(8,128)(2,1)}, u32[]{:S(2)}) copy-start(bf16[2,512,128]{2,1,0:T(8,128)(2,1)} %get-tuple-element.107.refs_0_) | copy-start | bytes 786436
  117.5 19.4 %collective-permute-start.16 = (bf16[2,512,128]{2,1,0:T(8,128)(2,1)}, bf16[2,512,128]{2,1,0:T(8,128)(2,1)S(1)}, u32[]{:S(2)}, u32[]{:S(2)}) collective-permute-start(bf16[2,512,128]{2,1,0:T(8,128)(2,1)} %get-tuple-element.99), channel_id=1, source_target_pairs={{0,12},{4,0},{8,4},{12,8},{1,13},{5,1},{9,5},{13,9},{2,14},{6,2},{... | collective-permute-start | bytes 786440 | tf_op jit(solution)/shard_map/ppermute | solution.py:504
  120.2 16.8 %collective-permute-start.13 = (bf16[2,512,128]{2,1,0:T(8,128)(2,1)S(1)}, bf16[2,512,128]{2,1,0:T(8,128)(2,1)S(1)}, u32[]{:S(2)}, u32[]{:S(2)}) collective-permute-start(bf16[2,512,128]{2,1,0:T(8,128)(2,1)S(1)} %copy-done.19), channel_id=1, source_target_pairs={{0,4},{4,8},{8,12},{12,0},{1,5},{5,9},{9,13},{13,1},{2,6},{6,10},{... | collective-permute-start | bytes 786440 | tf_op jit(solution)/shard_map/ppermute | solution.py:504
  136.1 4.3 %copy-start.14 = (bf16[2,512,128]{2,1,0:T(8,128)(2,1)}, bf16[2,512,128]{2,1,0:T(8,128)(2,1)S(1)}, u32[]{:S(2)}) copy-start(bf16[2,512,128]{2,1,0:T(8,128)(2,1)S(1)} %collective-permute-done.14.refs_2_) | copy-start | bytes 786436
  136.9 3.5 %copy-start.15 = (bf16[2,512,128]{2,1,0:T(8,128)(2,1)}, bf16[2,512,128]{2,1,0:T(8,128)(2,1)S(1)}, u32[]{:S(2)}) copy-start(bf16[2,512,128]{2,1,0:T(8,128)(2,1)S(1)} %collective-permute-done.16.refs_3_) | copy-start | bytes 786436
  136.9 3.5 %copy-start.16 = (bf16[2,512,128]{2,1,0:T(8,128)(2,1)}, bf16[2,512,128]{2,1,0:T(8,128)(2,1)S(1)}, u32[]{:S(2)}) copy-start(bf16[2,512,128]{2,1,0:T(8,128)(2,1)S(1)} %collective-permute-done.13.refs_1_) | copy-start | bytes 786436
  136.9 3.5 %collective-permute-start.23 = (bf16[512,1024]{1,0:T(8,128)(2,1)}, bf16[512,1024]{1,0:T(8,128)(2,1)}, u32[]{:S(2)}, u32[]{:S(2)}) collective-permute-start(bf16[512,1024]{1,0:T(8,128)(2,1)} %collective-permute-done.19.refs_13_), channel_id=1, source_target_pairs={{0,1},{1,0},{2,3},{3,2},{4,5},{5,4},{6,7},{7,6},{8,9},{9,8},{10,11... | collective-permute-start | bytes 3145736 | tf_op jit(solution)/shard_map/ppermute | solution.py:495
  137.1 3.2 %collective-permute-start.22 = (bf16[4,512,128]{2,1,0:T(8,128)(2,1)S(1)}, bf16[4,512,128]{2,1,0:T(8,128)(2,1)S(1)}, u32[]{:S(2)}, u32[]{:S(2)}) collective-permute-start(bf16[4,512,128]{2,1,0:T(8,128)(2,1)S(1)} %pad_maximum_fusion), channel_id=1, source_target_pairs={{0,1},{1,0},{2,3},{3,2},{4,5},{5,4},{6,7},{7,6},{8,9},{9,8},{10,11... | collective-permute-start | bytes 1572872 | tf_op jit(solution)/shard_map/ppermute | solution.py:495
  140.4 0.8 copy-start.18
  162.0 6.1 %copy-start.20 = (s32[5]{0:T(128)S(1)}, s32[5]{0:T(128)}, u32[]{:S(2)}) copy-start(s32[5]{0:T(128)} %anchor.1.place) | copy-start | bytes 64
  162.0 15.0 %collective-permute-start.25 = (bf16[512,512]{1,0:T(8,128)(2,1)}, bf16[512,512]{1,0:T(8,128)(2,1)S(1)}, u32[]{:S(2)}, u32[]{:S(2)}) collective-permute-start(bf16[512,512]{1,0:T(8,128)(2,1)} %send.2), channel_id=1, source_target_pairs={{0,2},{2,0},{1,3},{3,1},{4,6},{6,4},{5,7},{7,5},{8,10},{10,8},{9,1... | collective-permute-start | bytes 1572872 | tf_op jit(solution)/shard_map/ppermute | solution.py:495
  168.1 19.5 %collective-permute-start.24 = (bf16[512,512]{1,0:T(8,128)(2,1)}, bf16[512,512]{1,0:T(8,128)(2,1)S(1)}, u32[]{:S(2)}, u32[]{:S(2)}) collective-permute-start(bf16[512,512]{1,0:T(8,128)(2,1)} %send.3), channel_id=1, source_target_pairs={{0,2},{2,0},{1,3},{3,1},{4,6},{6,4},{5,7},{7,5},{8,10},{10,8},{9,1... | collective-permute-start | bytes 1572872 | tf_op jit(solution)/shard_map/ppermute | solution.py:495
  177.0 6.4 %copy-start.6 = (bf16[512,512]{1,0:T(8,128)(2,1)}, bf16[512,512]{1,0:T(8,128)(2,1)S(1)}, u32[]{:S(2)}) copy-start(bf16[512,512]{1,0:T(8,128)(2,1)S(1)} %collective-permute-done.25.got) | copy-start | bytes 1572868
  187.6 0.8 copy-start.5
  (1 other events, 0.7 us)
Sparse Core Ops, SparseCore 0:
  65.5 49.8 all-gather.2
  117.6 33.9 all-gather.4

commit v3 on v2

v3 whole, which is shorter than its diff:
```python
import functools

import jax
import jax.numpy as jnp
from jax import lax
from jax.experimental import pallas as pl
from jax.experimental.pallas import tpu as pltpu
from jax.sharding import PartitionSpec as P

LEVELS = 15
LANES = 128
SPLIT = 2
RUN = 16
MIDDLE = 8
WIDE = 64
LINE = ("seq", "sub")
GRANT = 16 * 2**20
LITTLE = 12 * 2**20


def run_levels(stream, shifter, low0, low1, high0, high1, mix):
    mixed = mix[LEVELS + 1] * stream
    for level in range(LEVELS):
        shifted = shifter(stream, 2**level)
        high = high0 * stream + high1 * shifted
        stream = low0 * stream + low1 * shifted
        mixed = mixed + mix[level] * high
    return mixed + mix[LEVELS] * stream


def general(tokens, low_angle, high_taps, level_mix, w_value, w_gate, out_weight):
    rows = tokens.shape[0]
    channels = tokens.shape[1]
    ways = lax.axis_size(LINE)
    total = rows * ways
    narrow = channels // ways
    place = lax.axis_index(LINE) * narrow
    columns = lax.all_to_all(tokens.T, LINE, split_axis=0, concat_axis=1, tiled=True)
    angle = lax.dynamic_slice_in_dim(low_angle, place, narrow, 0)[:, None]
    high_pair = lax.dynamic_slice_in_dim(high_taps, place, narrow, 1)[:, :, None]
    mix = lax.dynamic_slice_in_dim(level_mix, place, narrow, 1)[:, :, None]

    def shifter(stream, reach):
        if reach >= total:
            return jnp.zeros_like(stream)
        return jnp.concatenate(
            [jnp.zeros((stream.shape[0], reach), jnp.float32), stream[:, : total - reach]], 1
        )

    mixed = run_levels(
        columns.astype(jnp.float32),
        shifter,
        jnp.cos(angle),
        jnp.sin(angle),
        high_pair[0],
        high_pair[1],
        mix,
    )
    filtered = jax.nn.gelu(mixed).astype(jnp.bfloat16)
    activated = lax.all_to_all(filtered, LINE, split_axis=1, concat_axis=0, tiled=True).T
    piece = lax.all_gather(activated, "chan", axis=1, tiled=True)
    value = jnp.dot(piece, w_value, preferred_element_type=jnp.float32)
    gate = jnp.dot(piece, w_gate, preferred_element_type=jnp.float32)
    hidden = (value * jax.nn.sigmoid(gate)).astype(jnp.bfloat16)
    projected = jnp.dot(
        lax.all_gather(hidden, "chan", axis=1, tiled=True),
        out_weight,
        preferred_element_type=jnp.float32,
    )
    return (projected + tokens.astype(jnp.float32)).astype(jnp.bfloat16)


def coefficients(live, lanes, angle_ref, high_ref, mix_ref, out_ref):
    low0, low1 = jnp.cos(angle_ref[:, lanes]), jnp.sin(angle_ref[:, lanes])
    high0, high1 = high_ref[0:1, lanes], high_ref[1:2, lanes]
    power = jnp.ones_like(low0)
    for level in range(live + 1):
        weight = jnp.zeros_like(low0)
        if level < live:
            weight = weight + mix_ref[level : level + 1, lanes] * (high0 - high1 * low0 / low1)
        if level > 0:
            weight = weight + mix_ref[level - 1 : level, lanes] * high1 / low1
        if level == live:
            scale = jnp.ones_like(low0)
            for rest in range(live, LEVELS):
                weight = weight + mix_ref[rest : rest + 1, lanes] * high0 * scale
                scale = scale * low0
            weight = weight + mix_ref[LEVELS : LEVELS + 1, lanes] * scale
        weight = weight * power
        if level == 0:
            weight = weight + mix_ref[LEVELS + 1 : LEVELS + 2, lanes]
        out_ref[level : level + 1, :] = weight
        power = power * low0
    out_ref[live + 1 : live + 2, :] = low1 / low0


def advance(stream, tail, ratio):
    reach = tail.shape[0]
    shifted = jnp.concatenate([tail, stream[: stream.shape[0] - reach]], 0)
    return stream + ratio * shifted


def copy_all(pairs, sems, meanwhile=None):
    copies = [pltpu.make_async_copy(*pair, sems.at[at]) for at, pair in enumerate(pairs)]
    for copy in copies:
        copy.start()
    if meanwhile:
        meanwhile()
    for copy in copies:
        copy.wait()


def line_of(place, back, other):
    chips = place[4]
    core = 1 - place[1] if other else place[1]
    return lax.rem(place[0] - back + chips, chips) * 2 + core


def cut_kernel(chips, place, tokens, *outs):
    for ahead in range(chips):
        for other in range(2):
            if ahead or other:
                start = pl.multiple_of(line_of(place, -ahead, other) * LANES, LANES)
                block = tokens[:, pl.ds(start, LANES)]
                if ahead:
                    outs[ahead][other] = block
                else:
                    outs[0][...] = block


def run_cut(place, tokens, chips):
    rows = tokens.shape[0]
    shapes = [(rows, LANES)] + [(2, rows, LANES)] * (chips - 1)
    return pl.pallas_call(
        functools.partial(cut_kernel, chips),
        in_specs=[
            pl.BlockSpec(memory_space=pltpu.SMEM),
            pl.BlockSpec(memory_space=pltpu.VMEM),
        ],
        out_specs=[pl.BlockSpec(memory_space=pltpu.VMEM)] * chips,
        out_shape=[jax.ShapeDtypeStruct(shape, tokens.dtype) for shape in shapes],
        name="cut",
    )(place, tokens)


def levels_kernel(live, chips, place, angle_ref, high_ref, mix_ref, own, *refs):
    direct = refs[: chips - 1]
    handed = refs[chips - 1 : 2 * chips - 1]
    far = refs[2 * chips - 1 : 3 * chips - 1]
    near = refs[3 * chips - 1 : 4 * chips - 1]
    tokens, stream_ref, mixed_ref, act_ref, coef_ref, sems = refs[4 * chips - 1 :]
    side = place[2]
    rows = own.shape[0]
    units = rows * 2 * chips // 8

    def block(line):
        return pl.ds(pl.multiple_of(line * rows, rows), rows)

    columns = pl.ds(pl.multiple_of(line_of(place, 0, 0) * LANES, LANES), LANES)
    pairs = []
    for back in range(chips):
        mine = direct[back - 1].at[0] if back else own.at[:, columns]
        pairs.append((mine, tokens.at[block(line_of(place, back, 0))]))
        pairs.append((handed[back], tokens.at[block(line_of(place, back, 1))]))
    copy_all(
        pairs, sems, lambda: coefficients(live, columns, angle_ref, high_ref, mix_ref, coef_ref)
    )

    def whole(row):
        return jnp.broadcast_to(coef_ref[row : row + 1, :], (8, LANES))[None]

    def zero(n):
        return jnp.zeros((n, 8, LANES), jnp.float32)

    ratio = whole(live + 1)

    def first(i, carry):
        start = pl.multiple_of(i * RUN * 8, RUN * 8)
        x = tokens[pl.ds(start, RUN * 8), :].astype(jnp.float32).reshape(RUN, 8, LANES)
        mixed = whole(0) * x
        row = lax.broadcasted_iota(jnp.int32, (1, 8, LANES), 1)
        kept = []
        for level, tail in enumerate(carry):
            kept.append(x[RUN - tail.shape[0] :])
            if level < 3:
                turned = pltpu.roll(jnp.concatenate([tail, x], 0), 2**level, 1)
                x = x + ratio * jnp.where(row < 2**level, turned[:RUN], turned[1:])
            else:
                x = advance(x, tail, ratio)
            mixed = mixed + whole(level + 1) * x
        stream_ref[pl.ds(i * RUN, RUN)] = x
        mixed_ref[pl.ds(i * RUN, RUN)] = mixed
        return tuple(kept)

    lax.fori_loop(0, units // RUN, first, tuple(zero(n) for n in (1, 1, 1, 1, 2, 4)))

    stream = stream_ref.reshape(units // MIDDLE, MIDDLE, 8, LANES)
    total = mixed_ref.reshape(units // MIDDLE, MIDDLE, 8, LANES)
    steps = units // MIDDLE // RUN

    def second(t, carry):
        q = t // steps
        i = t % steps
        x = stream[pl.ds(i * RUN, RUN), q]
        mixed = total[pl.ds(i * RUN, RUN), q]
        keep = jnp.where(i > 0, 1.0, 0.0)
        kept = []
        for level, tail in enumerate(carry):
            kept.append(x[RUN - tail.shape[0] :])
            x = advance(x, tail * keep, ratio)
            mixed = mixed + whole(level + 7) * x
        stream[pl.ds(i * RUN, RUN), q] = x
        total[pl.ds(i * RUN, RUN), q] = mixed
        return tuple(kept)

    lax.fori_loop(0, MIDDLE * steps, second, tuple(zero(n) for n in (1, 2, 4)))

    stream_wide = stream_ref.reshape(units // WIDE, WIDE, 8, LANES)
    total_wide = mixed_ref.reshape(units // WIDE, WIDE, 8, LANES)
    act_wide = act_ref.reshape(units // WIDE, WIDE // 2, 16, LANES)

    def third(pair, _):
        halves = []
        for odd in range(2):
            x = stream_wide[:, pair * 2 + odd]
            mixed = total_wide[:, pair * 2 + odd]
            for level in range(9, live):
                x = advance(x, zero(2 ** (level - 9)), ratio)
                mixed = mixed + whole(level + 1) * x
            halves.append(jax.nn.gelu(mixed))
        act_wide[:, pair] = jnp.concatenate(halves, 1).astype(jnp.bfloat16)
        return 0

    lax.fori_loop(0, WIDE // 2, third, 0)

    half = rows // 2
    pairs = []
    for ahead in range(chips):
        for other in range(2):
            start = line_of(place, -ahead, other) * rows
            for outs, which in ((far, 1 - side), (near, side)):
                begin = pl.multiple_of(start + which * half, half)
                pairs.append((act_ref.at[pl.ds(begin, half)], outs[ahead].at[other]))
    copy_all(pairs, sems)


def run_filter(place, angle, high, mix, own, direct, handed, live):
    chips = len(handed)
    rows = handed[0].shape[0]
    total = rows * 2 * chips
    anywhere = pl.BlockSpec(memory_space=pltpu.HBM)
    outs = pl.pallas_call(
        functools.partial(levels_kernel, live, chips),
        out_shape=[jax.ShapeDtypeStruct((2, rows // 2, LANES), jnp.bfloat16)] * (2 * chips),
        in_specs=[
            pl.BlockSpec(memory_space=pltpu.SMEM),
        ]
        + [pl.BlockSpec(memory_space=pltpu.VMEM)] * 3
        + [anywhere] * (2 * chips),
        out_specs=[anywhere] * (2 * chips),
        scratch_shapes=[
            pltpu.VMEM((total, LANES), jnp.bfloat16),
            pltpu.VMEM((total // 8, 8, LANES), jnp.float32),
            pltpu.VMEM((total // 8, 8, LANES), jnp.float32),
            pltpu.VMEM((total, LANES), jnp.bfloat16),
            pltpu.VMEM((live + 2, LANES), jnp.float32),
            pltpu.SemaphoreType.DMA((4 * chips,)),
        ],
        compiler_params=pltpu.CompilerParams(vmem_limit_bytes=GRANT),
        name="levels",
    )(place, angle[None], high, mix, own, *direct, *handed)
    return list(outs[:chips]), list(outs[chips:])


def work(rows, depth, columns):
    return pl.CostEstimate(
        flops=2 * rows * depth * columns,
        bytes_accessed=2 * (rows * depth + depth * columns + rows * columns),
        transcendentals=0,
    )


def dot(a, b):
    return jnp.dot(a, b, preferred_element_type=jnp.float32)


def load_kernel(place, *refs):
    value_own, gate_own = refs[:2]
    pieces = refs[2:6]
    outs, sems = refs[-6:-1], refs[-1]
    core, group = place[1], place[3]
    depth = pieces[0].shape[1]
    pairs = [(value_own, outs[0]), (gate_own, outs[1])]
    for piece, far_group, far_core in zip(pieces, (0, 1, 0, 1), (0, 0, 1, 1)):
        quarter = 2 * (1 - group if far_group else group) + (1 - core if far_core else core)
        rows = pl.ds(pl.multiple_of(quarter * depth, depth), depth)
        for at in range(2):
            pairs.append((piece.at[at], outs[2 + at].at[rows]))
    copy_all(pairs, sems)
    for at in range(place.shape[0]):
        outs[4][at] = place[at]


def run_load(place, value_own, gate_own, fetched, after):
    arrays = [value_own, gate_own, *fetched, *after]
    whole = jax.ShapeDtypeStruct(value_own.shape, value_own.dtype)
    smem = pl.BlockSpec(memory_space=pltpu.SMEM)
    return pl.pallas_call(
        load_kernel,
        in_specs=[smem] + [pl.BlockSpec(memory_space=pltpu.HBM)] * len(arrays),
        out_specs=[pl.BlockSpec(memory_space=pltpu.VMEM)] * 4 + [smem],
        out_shape=[whole] * 4 + [jax.ShapeDtypeStruct(place.shape, place.dtype)],
        scratch_shapes=[pltpu.SemaphoreType.DMA((10,))],
        compiler_params=pltpu.CompilerParams(vmem_limit_bytes=LITTLE),
        cost_estimate=pl.CostEstimate(flops=10**11, bytes_accessed=0, transcendentals=0),
        name="load",
    )(place, *arrays)


def hidden_kernel(chips, q, block, place, *refs):
    direct = refs[:chips]
    handed, straight, crossed = refs[chips : chips + 3]
    value_own, gate_own, value_far, gate_far, hidden_ref, act, sems = refs[chips + 3 :]
    side = place[2]
    channels = 2 * chips * LANES
    part = pl.ds(q * act.shape[0], act.shape[0])
    pairs = []
    for back in range(chips):
        for other, near, far in ((0, direct[back], straight), (1, handed, crossed)):
            line = line_of(place, back, other) * LANES
            for start, source in (
                (side * channels + line, near.at[back if other else 0, part]),
                ((1 - side) * channels + line, far.at[back, part]),
            ):
                lanes = pl.ds(pl.multiple_of(start, LANES), LANES)
                pairs.append((source, act.at[:, lanes]))
    copy_all(pairs, sems)

    for whose, value_ref, gate_ref in ((side, value_own, gate_own), (1 - side, value_far, gate_far)):

        @pl.loop(0, channels // block)
        def _(j):
            columns = pl.ds(pl.multiple_of(j * block, block), block)
            value = dot(act[...], value_ref[:, columns])
            gate = dot(act[...], gate_ref[:, columns])
            target = pl.ds(pl.multiple_of(whose * channels + j * block, block), block)
            hidden_ref[:, target] = (value * jax.nn.sigmoid(gate)).astype(jnp.bfloat16)


def run_hidden(place, q, direct, handed, straight, crossed, *weights):
    chips = len(direct)
    rows = handed.shape[1] // SPLIT
    width, channels = weights[0].shape
    in_vmem = pl.BlockSpec(memory_space=pltpu.VMEM)
    return pl.pallas_call(
        functools.partial(hidden_kernel, chips, q, min(512, channels)),
        in_specs=[pl.BlockSpec(memory_space=pltpu.SMEM)]
        + [pl.BlockSpec(memory_space=pltpu.HBM)] * (chips + 3)
        + [in_vmem] * len(weights),
        out_specs=in_vmem,
        scratch_shapes=[
            pltpu.VMEM((rows, width), jnp.bfloat16),
            pltpu.SemaphoreType.DMA((4 * chips,)),
        ],
        out_shape=jax.ShapeDtypeStruct((rows, width), jnp.bfloat16),
        compiler_params=pltpu.CompilerParams(vmem_limit_bytes=LITTLE),
        cost_estimate=work(rows, width, 2 * width),
        name="hidden",
    )(place, *direct, handed, straight, crossed, *weights)


def send_kernel(place, hidden, mine, twin, out_ref):
    depth = mine.shape[0]
    core = place[1]
    total = None
    for half, weight in ((core, mine), (1 - core, twin)):
        rows = pl.ds(pl.multiple_of(half * depth, depth), depth)
        term = dot(hidden[:, rows], weight[...])
        total = term if total is None else total + term
    out_ref[...] = total.astype(jnp.bfloat16)


def run_send(place, hidden, halves):
    rows, width = hidden.shape
    depth, channels = halves[0].shape
    block = min(512, channels)
    return pl.pallas_call(
        send_kernel,
        grid_spec=pltpu.PrefetchScalarGridSpec(
            num_scalar_prefetch=1,
            grid=(channels // block,),
            in_specs=[pl.BlockSpec((rows, width), lambda j, place: (0, 0))]
            + [pl.BlockSpec((depth, block), lambda j, place: (0, j))] * 2,
            out_specs=pl.BlockSpec((rows, block), lambda j, place: (0, j)),
        ),
        out_shape=jax.ShapeDtypeStruct((rows, channels), jnp.bfloat16),
        compiler_params=pltpu.CompilerParams(vmem_limit_bytes=LITTLE),
        cost_estimate=work(rows, width, channels),
        name="send",
    )(place, hidden, *halves)


def finish_kernel(side, *refs):
    parts, weight, tokens, out_ref = refs[:SPLIT], refs[SPLIT], refs[SPLIT + 1], refs[SPLIT + 2]
    rows = parts[0].shape[0]
    for q in range(SPLIT):
        at = pl.ds(q * rows, rows)
        made = dot(parts[q][...], weight[...])
        out_ref[at, :] = (made + tokens[at, :].astype(jnp.float32)).astype(jnp.bfloat16)


def run_finish(side, parts, weight, tokens):
    rows, width = parts[0].shape
    channels = weight.shape[1]
    block = min(512, channels)
    return pl.pallas_call(
        finish_kernel,
        grid_spec=pltpu.PrefetchScalarGridSpec(
            num_scalar_prefetch=1,
            grid=(channels // block,),
            in_specs=[pl.BlockSpec((rows, width), lambda j, side: (0, 0))] * SPLIT
            + [
                pl.BlockSpec((width, block), lambda j, side: (0, j)),
                pl.BlockSpec((SPLIT * rows, block), lambda j, side: (side[0], j)),
            ],
            out_specs=pl.BlockSpec((SPLIT * rows, block), lambda j, side: (side[0], j)),
        ),
        out_shape=jax.ShapeDtypeStruct(tokens.shape, jnp.bfloat16),
        compiler_params=pltpu.CompilerParams(vmem_limit_bytes=GRANT),
        cost_estimate=work(SPLIT * rows, width, channels),
        name="finish",
    )(side, *parts, weight, tokens)


def add_kernel(side, got, tokens, kept, out_ref):
    out_ref[...] = (got[...].astype(jnp.float32) + tokens[...].astype(jnp.float32)).astype(
        jnp.bfloat16
    )


def add_far(side, q, got, tokens, result):
    rows, channels = got.shape

    def spot(j, side):
        return (SPLIT * (1 - side[0]) + q, j)

    block = min(512, channels)
    return pl.pallas_call(
        add_kernel,
        grid_spec=pltpu.PrefetchScalarGridSpec(
            num_scalar_prefetch=1,
            grid=(channels // block,),
            in_specs=[
                pl.BlockSpec((rows, block), lambda j, side: (0, j)),
                pl.BlockSpec((rows, block), spot),
                pl.BlockSpec(memory_space=pl.ANY),
            ],
            out_specs=pl.BlockSpec((rows, block), spot),
        ),
        out_shape=jax.ShapeDtypeStruct(tokens.shape, jnp.bfloat16),
        input_output_aliases={3: 0},
        name="add_far",
    )(side, got, tokens, result)


def swap(array, axis):
    return lax.ppermute(array, axis, [(0, 1), (1, 0)])


def cross(array):
    return lax.ppermute(array, ("chan", "sub"), [(0, 3), (1, 2), (2, 1), (3, 0)])


def ahead(array, offset):
    chips = lax.axis_size("seq")
    return lax.ppermute(array, "seq", [(j, (j + offset) % chips) for j in range(chips)])


def by_tokens(tokens, low_angle, high_taps, level_mix, w_value, w_gate, out_weight):
    rows, channels = tokens.shape
    chips = lax.axis_size("seq")
    narrow = channels // (2 * chips)
    chip, core = lax.axis_index("seq"), lax.axis_index("sub")
    side, group = lax.axis_index("chan"), lax.axis_index("groups")
    live = min(LEVELS, (rows * 2 * chips - 1).bit_length())
    order = sorted(range(1, chips), key=lambda s: abs(2 * s - chips))
    place = jnp.stack([chip, core, side, group, chips]).astype(jnp.int32)

    blocks = run_cut(place, tokens, chips)
    blocks, weights = lax.optimization_barrier((blocks, (w_value, w_gate, out_weight)))
    direct = [None] * chips
    for s in order:
        direct[s] = ahead(blocks[s], s)
    handed = [swap(blocks[0], "sub")] + [swap(direct[s][1], "sub") for s in range(1, chips)]

    depth = w_value.shape[0] // 4
    pair = jnp.stack(
        [
            lax.dynamic_slice_in_dim(weight, (2 * group + core) * depth, depth, 0)
            for weight in weights[:2]
        ]
    )
    half = lax.dynamic_slice_in_dim(weights[2], core * 2 * depth, 2 * depth, 0)
    pair_first = swap(pair, "chan")
    direct, pair_first, half = lax.optimization_barrier((direct, pair_first, half))
    pair_second = swap(pair_first, "groups")
    half_first = swap(half, "chan")
    pair_third = swap(pair_first, "sub")

    far, near = run_filter(
        place, low_angle, high_taps, level_mix, tokens, direct[1:], handed, live
    )

    far, pair_third = lax.optimization_barrier((far, pair_third))
    far_got = [far[0]] + [None] * (chips - 1)
    for s in order:
        far_got[s] = ahead(far[s], s)

    def exchange(backs):
        return (
            swap(jnp.stack([far_got[back][0] for back in backs]), "chan"),
            cross(jnp.stack([far_got[back][1] for back in backs])),
        )

    near, far_got[order[0]] = lax.optimization_barrier((near, far_got[order[0]]))
    near, far_got = list(near), list(far_got)
    near_got = [near[0]] + [None] * (chips - 1)
    near_got[order[0]] = ahead(near[order[0]], order[0])
    near, far_got, pair_second, half_first = lax.optimization_barrier(
        (near, far_got, pair_second, half_first)
    )
    for s in order[1:]:
        near_got[s] = ahead(near[s], s)
    straight = swap(jnp.stack([block[0] for block in far_got]), "chan")
    crossed = cross(jnp.stack([block[1] for block in far_got]))
    pair_second, near_got[order[0]] = lax.optimization_barrier((pair_second, near_got[order[0]]))
    pair_fourth = swap(pair_second, "sub")
    fetched = [pair_first, pair_second, pair_third, pair_fourth]
    *loaded, place = run_load(place, w_value, w_gate, fetched, far_got[1:])
    half_first, straight = lax.optimization_barrier((half_first, straight))
    half_second = swap(half_first, "sub")
    near_got, straight, crossed, place, half_second = lax.optimization_barrier(
        (near_got, straight, crossed, place, half_second)
    )
    handed = swap(jnp.stack([block[1] for block in near_got]), "sub")
    which = place[2:3]
    hidden, returned = [], []
    for q in range(SPLIT):
        made = run_hidden(place, q, near_got, handed, straight, crossed, *loaded)
        sent = run_send(place, made, [half_first, half_second])
        place, sent = lax.optimization_barrier((place, sent))
        hidden.append(made)
        returned.append(swap(sent, "chan"))
    hidden, returned[0] = lax.optimization_barrier((hidden, returned[0]))
    result = run_finish(which, hidden, out_weight, tokens)
    for q in range(SPLIT):
        result = add_far(which, q, returned[q], tokens, result)
    return result


def solution(mesh):
    def shards(tokens, *rest):
        ways = mesh.shape["seq"] * mesh.shape["sub"]
        pairs = all(mesh.shape[name] == 2 for name in ("groups", "chan", "sub"))
        rows, channels = tokens.shape
        fits = channels == ways * LANES and rows % 64 == 0
        fits = fits and rows * ways == 8 * WIDE * RUN and rest[3].shape[0] % 512 == 0
        return (by_tokens if pairs and fits else general)(tokens, *rest)

    return jax.shard_map(
        shards,
        mesh=mesh,
        in_specs=(
            P(("groups", "seq", "sub"), "chan"),
            P("chan"),
            P(None, "chan"),
            P(None, "chan"),
            P(None, "chan"),
            P(None, "chan"),
            P(None, "chan"),
        ),
        out_specs=P(("groups", "seq", "sub"), "chan"),
        check_vma=False,
    )
```

time: 199 us -> 182 us (0.915)
  waiting for transfers between devices: 76 us -> 95.7 us
  between operations: 13.7 us -> 0.27 us
  starting transfers between devices: 39 us -> 27.4 us
  Pallas kernels: 62 us -> 50.8 us
    ppermute x9, waiting for transfers between devices: 45.3 us -> 57.6 us  [ahead(): lax.ppermute(array, 'seq', [(j, (j + offset) % chips) for j in range(chip...]
    pallas_call x6 -> x5, Pallas kernels: 32 us -> 20.3 us  [the longest x2 12.3 us: run_hidden(): pl.pallas_call(functools.partial(hidden_kernel, chips, q, min(512, channe...]
    ppermute x9, starting transfers between devices: 26.8 us -> 15.8 us  [ahead(): lax.ppermute(array, 'seq', [(j, (j + offset) % chips) for j in range(chip...]
    ppermute x2 -> x1, waiting for transfers between devices: 0.52 us -> 7.07 us  [cross(): lax.ppermute(array, ('chan', 'sub'), [(0, 3), (1, 2), (2, 1), (3, 0)])]
    unnamed x42 -> x20, local copies, waits for them, and re-layouts: 2.34 us -> 0.05 us
    pallas_call x1, Pallas kernels: 15.1 us -> 17.3 us  [run_filter(): pl.pallas_call(functools.partial(levels_kernel, live, chips), out_shape=[...]
    ppermute x15 -> x14, waiting for transfers between devices: 30.1 us -> 31 us  [swap(): return lax.ppermute(array, axis, [(0, 1), (1, 0)])]
    ppermute x15 -> x14, starting transfers between devices: 10.5 us -> 11 us  [swap(): return lax.ppermute(array, axis, [(0, 1), (1, 0)])]
  transfers between devices with their start and end apart: 28 -> 24, of which waited for: 12 -> 15; matrix products, arithmetic and copies ran while one was open for 2% -> 2% of each run, Pallas kernels for 24% -> 19%
where the time goes in v3:
time: 182 us
  waiting for transfers between devices  95.7 us (53%)
  Pallas kernels  50.8 us (28%)
  starting transfers between devices  27.4 us (15%)
  local copies, waits for them, and re-layouts  6.1 us (3%)
    ppermute x9, waiting for transfers between devices, ahead(): lax.ppermute(array, 'seq', [(j, (j + offset) % chips) for j in range(chip...  57.6 us
    ppermute x14, waiting for transfers between devices, swap(): return lax.ppermute(array, axis, [(0, 1), (1, 0)])  31 us
    pallas_call x1, Pallas kernels, run_filter(): pl.pallas_call(functools.partial(levels_kernel, live, chips), out_shape=[...  17.3 us
    ppermute x9, starting transfers between devices, ahead(): lax.ppermute(array, 'seq', [(j, (j + offset) % chips) for j in range(chip...  15.8 us
    pallas_call x2, Pallas kernels, run_hidden(): pl.pallas_call(functools.partial(hidden_kernel, chips, q, min(512, channe...  12.3 us
    ppermute x14, starting transfers between devices, swap(): return lax.ppermute(array, axis, [(0, 1), (1, 0)])  11 us
    ppermute x1, waiting for transfers between devices, cross(): lax.ppermute(array, ('chan', 'sub'), [(0, 3), (1, 2), (2, 1), (3, 0)])  7.07 us
    pallas_call x2, Pallas kernels, add_far(): pl.pallas_call(add_kernel, grid_spec=pltpu.PrefetchScalarGridSpec(num_sca...  5.3 us
  transfers between devices with their start and end apart: 24, of which 15 were waited for; matrix products, arithmetic and copies ran while one was open for 2% of the time, Pallas kernels for 19%

profile of v3, /device:TPU:0, one launch (start us, length us, event | category | flops | bytes accessed | tf_op | source)
XLA Modules:
  0.0 182.0 jit_solution(1300373277113706592)
XLA Ops:
  0.0 0.7 stack.37.place
  0.7 3.4 %cut.1 = (bf16[1024,128]{1,0:T(8,128)(2,1)}, bf16[2,1024,128]{2,1,0:T(8,128)(2,1)}, bf16[2,1024,128]{2,1,0:T(8,128)(2,1)}, bf16[2,1024,128]{2,1,0:T(8,128)(2,1)}) custom-call(s32[5]{0:T(128)} %stack.37.place, bf16[1024,1024]{1,0:T(8,128)(2,1)} %tokens.5), custom_call_target="tpu_custom_call" | custom-call | tf_op jit(solution)/shard_map/cut/pallas_call | solution.py:134
  4.0 1.7 dynamic-slice_bitcast_fusion
  5.7 1.5 pad_maximum_fusion
  7.2 2.9 %collective-permute-start.3 = (bf16[2,512,1024]{2,1,0:T(8,128)(2,1)}, bf16[2,512,1024]{2,1,0:T(8,128)(2,1)}, u32[]{:S(2)}, u32[]{:S(2)}) collective-permute-start(bf16[2,512,1024]{2,1,0:T(8,128)(2,1)} %pad_maximum_fusion), channel_id=1, source_target_pairs={{0,2},{2,0},{1,3},{3,1},{4,6},{6,4},{5,7},{7,5},{8,10},{10,8},{9,1... | collective-permute-start | bytes 6291464 | tf_op jit(solution)/shard_map/ppermute | solution.py:467
  10.2 1.6 collective-permute-start
  11.8 2.6 %collective-permute-start.1 = (bf16[2,1024,128]{2,1,0:T(8,128)(2,1)}, bf16[2,1024,128]{2,1,0:T(8,128)(2,1)S(1)}, u32[]{:S(2)}, u32[]{:S(2)}) collective-permute-start(bf16[2,1024,128]{2,1,0:T(8,128)(2,1)} %get-tuple-element.75), channel_id=1, source_target_pairs={{0,8},{4,12},{8,0},{12,4},{1,9},{5,13},{9,1},{13,5},{2,10},{6,14},... | collective-permute-start | bytes 1572872 | tf_op jit(solution)/shard_map/ppermute | solution.py:476
  14.3 1.3 collective-permute-start.2
  15.7 1.9 %constant_dynamic-slice_fusion = bf16[1024,1024]{1,0:T(8,128)(2,1)S(1)} fusion(bf16[2048,1024]{1,0:T(8,128)(2,1)} %refs_2_.1, s32[]{:T(128)S(6)} %select_n.8), kind=kLoop, calls=%fused_computation.9 | loop fusion | bytes 4194308 | tf_op jit(solution)/shard_map/dynamic_slice | solution.py:503
  17.6 9.5 %collective-permute-done.refs_0_ = bf16[2,1024,128]{2,1,0:T(8,128)(2,1)S(1)} collective-permute-done((bf16[2,1024,128]{2,1,0:T(8,128)(2,1)}, bf16[2,1024,128]{2,1,0:T(8,128)(2,1)S(1)}, u32[]{:S(2)}, u32[]{:S(2)}) %collective-permute-start) | collective-permute-done | bytes 524320 | tf_op jit(solution)/shard_map/ppermute | solution.py:476
  27.2 21.1 %collective-permute-done.1.refs_1_ = bf16[2,1024,128]{2,1,0:T(8,128)(2,1)S(1)} collective-permute-done((bf16[2,1024,128]{2,1,0:T(8,128)(2,1)}, bf16[2,1024,128]{2,1,0:T(8,128)(2,1)S(1)}, u32[]{:S(2)}, u32[]{:S(2)}) %collective-permute-start.1) | collective-permute-done | bytes 524320 | tf_op jit(solution)/shard_map/ppermute | solution.py:476
  48.2 7.9 %collective-permute-done.3.refs_2_ = bf16[2,512,1024]{2,1,0:T(8,128)(2,1)} collective-permute-done((bf16[2,512,1024]{2,1,0:T(8,128)(2,1)}, bf16[2,512,1024]{2,1,0:T(8,128)(2,1)}, u32[]{:S(2)}, u32[]{:S(2)}) %collective-permute-start.3) | collective-permute-done | bytes 2097184 | tf_op jit(solution)/shard_map/ppermute | solution.py:467
  56.1 1.8 collective-permute-start.12
  57.9 1.5 collective-permute-start.13
  59.4 0.6 collective-permute-start.5
  60.0 1.0 slice_bitcast_fusion
  61.3 0.3 collective-permute-start.7
  61.6 1.0 collective-permute-done.6.refs_5_
  62.6 0.4 collective-permute-done.7.refs_6_
  63.0 17.3 %levels.1 = (bf16[2,512,128]{2,1,0:T(8,128)(2,1)S(1)}, bf16[2,512,128]{2,1,0:T(8,128)(2,1)S(1)}, bf16[2,512,128]{2,1,0:T(8,128)(2,1)S(1)}, bf16[2,512,128]{2,1,0...) custom-call(s32[5]{0:T(128)S(1)} %copy-done.6, ...), custom_call_target="tpu_custom_call" | custom-call | tf_op jit(solution)/shard_map/levels/pallas_call | solution.py:252
  80.3 2.7 %collective-permute-start.9 = (bf16[2,512,128]{2,1,0:T(8,128)(2,1)S(1)}, bf16[2,512,128]{2,1,0:T(8,128)(2,1)S(1)}, u32[]{:S(2)}, u32[]{:S(2)}) collective-permute-start(bf16[2,512,128]{2,1,0:T(8,128)(2,1)S(1)} %get-tuple-element.93), channel_id=1, source_target_pairs={{0,8},{4,12},{8,0},{12,4},{1,9},{5,13},{9,1},{13,5},{2,10},{6,14},... | collective-permute-start | bytes 786440 | tf_op jit(solution)/shard_map/ppermute | solution.py:476
  83.0 2.4 %collective-permute-start.10 = (bf16[2,512,128]{2,1,0:T(8,128)(2,1)S(1)}, bf16[2,512,128]{2,1,0:T(8,128)(2,1)S(1)}, u32[]{:S(2)}, u32[]{:S(2)}) collective-permute-start(bf16[2,512,128]{2,1,0:T(8,128)(2,1)S(1)} %get-tuple-element.99), channel_id=1, source_target_pairs={{0,4},{4,8},{8,12},{12,0},{1,5},{5,9},{9,13},{13,1},{2,6},{6,10},{... | collective-permute-start | bytes 786440 | tf_op jit(solution)/shard_map/ppermute | solution.py:476
  85.4 1.4 collective-permute-start.11
  86.8 14.9 %collective-permute-done.9.refs_7_ = bf16[2,512,128]{2,1,0:T(8,128)(2,1)S(1)} collective-permute-done((bf16[2,512,128]{2,1,0:T(8,128)(2,1)S(1)}, bf16[2,512,128]{2,1,0:T(8,128)(2,1)S(1)}, u32[]{:S(2)}, u32[]{:S(2)}) %collective-permute-start.9) | collective-permute-done | bytes 262176 | tf_op jit(solution)/shard_map/ppermute | solution.py:476
  101.7 2.7 %collective-permute-done.12.refs_3_ = bf16[2,512,1024]{2,1,0:T(8,128)(2,1)S(1)} collective-permute-done((bf16[2,512,1024]{2,1,0:T(8,128)(2,1)}, bf16[2,512,1024]{2,1,0:T(8,128)(2,1)S(1)}, u32[]{:S(2)}, u32[]{:S(2)}) %collective-permute-start.12) | collective-permute-done | bytes 2097184 | tf_op jit(solution)/shard_map/ppermute | solution.py:467
  104.4 1.3 collective-permute-done.13.mine
  105.7 12.1 %collective-permute-done.15.refs_2_ = bf16[2,512,128]{2,1,0:T(8,128)(2,1)S(1)} collective-permute-done((bf16[2,512,128]{2,1,0:T(8,128)(2,1)S(1)}, bf16[2,512,128]{2,1,0:T(8,128)(2,1)S(1)}, u32[]{:S(2)}, u32[]{:S(2)}) %collective-permute-start.15) | collective-permute-done | bytes 262176 | tf_op jit(solution)/shard_map/ppermute | solution.py:476
  118.0 1.4 collective-permute-start.17
  119.4 0.6 collective-permute-start.18
  120.0 0.7 collective-permute-start.14
  120.7 3.2 %collective-permute-start.16 = (bf16[2,512,128]{2,1,0:T(8,128)(2,1)S(1)}, bf16[2,512,128]{2,1,0:T(8,128)(2,1)S(1)}, u32[]{:S(2)}, u32[]{:S(2)}) collective-permute-start(bf16[2,512,128]{2,1,0:T(8,128)(2,1)S(1)} %get-tuple-element.106), channel_id=1, source_target_pairs={{0,12},{4,0},{8,4},{12,8},{1,13},{5,1},{9,5},{13,9},{2,14},{6,2},{... | collective-permute-start | bytes 786440 | tf_op jit(solution)/shard_map/ppermute | solution.py:476
  123.9 8.9 %collective-permute-done.17.refs_5_ = bf16[4,512,128]{2,1,0:T(8,128)(2,1)S(1)} collective-permute-done((bf16[4,512,128]{2,1,0:T(8,128)(2,1)S(1)}, bf16[4,512,128]{2,1,0:T(8,128)(2,1)S(1)}, u32[]{:S(2)}, u32[]{:S(2)}) %collective-permute-start.17) | collective-permute-done | bytes 524320 | tf_op jit(solution)/shard_map/ppermute | solution.py:467
  132.8 3.3 %load.1 = (bf16[2048,1024]{1,0:T(8,128)(2,1)S(1)}, bf16[2048,1024]{1,0:T(8,128)(2,1)S(1)}, bf16[2048,1024]{1,0:T(8,128)(2,1)S(1)}, bf16[2048,1024]{1,0:T(8,128)(2,1)S(1)}, s32[5]{0:T(128)S(1)}) custom-call(s32[5]{0:T(128)S(1)} %copy-done.6, bf16[2048,1024]{1,0:T(8,128)(2,1)S(1)} %copy-done.2, bf16[2048,1024]{1,0:T(8,128)(2,1)S(1)} %copy-done.3, ...), custom_call_target="tpu_custom_call" | custom-call | flops 99999997952 | tf_op jit(solution)/shard_map/load/pallas_call | solution.py:308
  136.1 7.1 %collective-permute-done.18.refs_6_ = bf16[4,512,128]{2,1,0:T(8,128)(2,1)S(1)} collective-permute-done((bf16[4,512,128]{2,1,0:T(8,128)(2,1)S(1)}, bf16[4,512,128]{2,1,0:T(8,128)(2,1)S(1)}, u32[]{:S(2)}, u32[]{:S(2)}) %collective-permute-start.18) | collective-permute-done | bytes 524320 | tf_op jit(solution)/shard_map/ppermute | solution.py:471
  143.4 0.3 collective-permute-start.21
  143.6 1.7 collective-permute-done.21.refs_4_
  145.3 6.2 %hidden.2.refs_0_ = bf16[256,2048]{1,0:T(8,128)(2,1)S(1)} custom-call(s32[5]{0:T(128)S(1)} %get-tuple-element.129.place, bf16[2,512,128]{2,1,0:T(8,128)(2,1)S(1)} %get-tuple-element.118.refs_0_, bf16[2,512,128]{2,1,0:T(8,128)(2,1)S(1)} %collective-permute-done.14.refs_1_, bf16[2,512,128]{2,1,0:T(8,128)(2,1)S(1)} %collective-permute-done.15.refs_2_, ...), custom_call_target="tpu_custom_call" | custom-call | flops 4294967296 | bytes 19922944 | tf_op jit(solution)/shard_map/hidden/pallas_call | solution.py:355
  151.5 2.3 %send.2 = bf16[256,1024]{1,0:T(8,128)(2,1)S(1)} custom-call(s32[5]{0:T(128)S(1)} %get-tuple-element.129.place, bf16[256,2048]{1,0:T(8,128)(2,1)S(1)} %hidden.2.refs_0_, bf16[1024,1024]{1,0:T(8,128)(2,1)S(1)} %collective-permute-done.13.mine, bf16[1024,1024]{1,0:T(8,128)(2,1)S(1)} %collective-permute-done.20.twin), custom_call_target="tpu_custom_call" | custom-call | flops 1073741824 | bytes 5767168 | tf_op jit(solution)/shard_map/send/pallas_call | solution.py:387
  153.9 1.4 collective-permute-start.23
  155.3 6.2 %hidden.3.refs_1_ = bf16[256,2048]{1,0:T(8,128)(2,1)S(1)} custom-call(s32[5]{0:T(128)S(1)} %get-tuple-element.129.place, bf16[2,512,128]{2,1,0:T(8,128)(2,1)S(1)} %get-tuple-element.118.refs_0_, bf16[2,512,128]{2,1,0:T(8,128)(2,1)S(1)} %collective-permute-done.14.refs_1_, bf16[2,512,128]{2,1,0:T(8,128)(2,1)S(1)} %collective-permute-done.15.refs_2_, ...), custom_call_target="tpu_custom_call" | custom-call | flops 4294967296 | bytes 19922944 | tf_op jit(solution)/shard_map/hidden/pallas_call | solution.py:355
  161.5 2.3 %send.3 = bf16[256,1024]{1,0:T(8,128)(2,1)S(1)} custom-call(s32[5]{0:T(128)S(1)} %get-tuple-element.129.place, bf16[256,2048]{1,0:T(8,128)(2,1)S(1)} %hidden.3.refs_1_, bf16[1024,1024]{1,0:T(8,128)(2,1)S(1)} %collective-permute-done.13.mine, bf16[1024,1024]{1,0:T(8,128)(2,1)S(1)} %collective-permute-done.20.twin), custom_call_target="tpu_custom_call" | custom-call | flops 1073741824 | bytes 5767168 | tf_op jit(solution)/shard_map/send/pallas_call | solution.py:387
  163.8 0.8 collective-permute-start.22
  164.6 0.6 slice.59.side
  165.2 3.5 %collective-permute-done.23.got = bf16[256,1024]{1,0:T(8,128)(2,1)S(1)} collective-permute-done((bf16[256,1024]{1,0:T(8,128)(2,1)S(1)}, bf16[256,1024]{1,0:T(8,128)(2,1)S(1)}, u32[]{:S(2)}, u32[]{:S(2)}) %collective-permute-start.23) | collective-permute-done | bytes 524320 | tf_op jit(solution)/shard_map/ppermute | solution.py:467
  168.7 4.5 %finish.1.kept = bf16[1024,1024]{1,0:T(8,128)(2,1)} custom-call(s32[1]{0:T(128)} %slice.59.side, bf16[256,2048]{1,0:T(8,128)(2,1)S(1)} %hidden.2.refs_0_, bf16[256,2048]{1,0:T(8,128)(2,1)S(1)} %hidden.3.refs_1_, bf16[2048,1024]{1,0:T(8,128)(2,1)S(1)} %copy-done.1, bf16[1024,1024]{1,0:T(8,128)(2,1)S(1)} %copy-done), custom_call_target="tpu_custom_call" | custom-call | flops 2147483648 | bytes 7340032 | tf_op jit(solution)/shard_map/finish/pallas_call | solution.py:416
  173.2 2.6 %add_far.2.kept = bf16[1024,1024]{1,0:T(8,128)(2,1)} custom-call(s32[1]{0:T(128)} %slice.59.side, bf16[256,1024]{1,0:T(8,128)(2,1)} %copy-done.8, bf16[1024,1024]{1,0:T(8,128)(2,1)} %tokens.5, bf16[1024,1024]{1,0:T(8,128)(2,1)} %finish.1.kept), custom_call_target="tpu_custom_call", output_to_operand_aliasing={{}: (3, {})} | custom-call | tf_op jit(solution)/shard_map/add_far/pallas_call | solution.py:448
  175.8 3.5 %collective-permute-done.22.got = bf16[256,1024]{1,0:T(8,128)(2,1)} collective-permute-done((bf16[256,1024]{1,0:T(8,128)(2,1)S(1)}, bf16[256,1024]{1,0:T(8,128)(2,1)}, u32[]{:S(2)}, u32[]{:S(2)}) %collective-permute-start.22) | collective-permute-done | bytes 524320 | tf_op jit(solution)/shard_map/ppermute | solution.py:467
  179.3 2.6 %add_far.3 = bf16[1024,1024]{1,0:T(8,128)(2,1)} custom-call(s32[1]{0:T(128)} %slice.59.side, bf16[256,1024]{1,0:T(8,128)(2,1)} %collective-permute-done.22.got, bf16[1024,1024]{1,0:T(8,128)(2,1)} %tokens.5, bf16[1024,1024]{1,0:T(8,128)(2,1)} %add_far.2.kept), custom_call_target="tpu_custom_call", output_to_operand_aliasing={{}: (3, {})} | custom-call | tf_op jit(solution)/shard_map/add_far/pallas_call | solution.py:448
  (49 shorter events, 0.8 us)
Async XLA Ops:
  7.2 48.9 %collective-permute-start.3 = (bf16[2,512,1024]{2,1,0:T(8,128)(2,1)}, bf16[2,512,1024]{2,1,0:T(8,128)(2,1)}, u32[]{:S(2)}, u32[]{:S(2)}) collective-permute-start(bf16[2,512,1024]{2,1,0:T(8,128)(2,1)} %pad_maximum_fusion), channel_id=1, source_target_pairs={{0,2},{2,0},{1,3},{3,1},{4,6},{6,4},{5,7},{7,5},{8,10},{10,8},{9,1... | collective-permute-start | bytes 6291464 | tf_op jit(solution)/shard_map/ppermute | solution.py:467
  10.2 17.0 %collective-permute-start = (bf16[2,1024,128]{2,1,0:T(8,128)(2,1)}, bf16[2,1024,128]{2,1,0:T(8,128)(2,1)S(1)}, u32[]{:S(2)}, u32[]{:S(2)}) collective-permute-start(bf16[2,1024,128]{2,1,0:T(8,128)(2,1)} %get-tuple-element.74), channel_id=1, source_target_pairs={{0,4},{4,8},{8,12},{12,0},{1,5},{5,9},{9,13},{13,1},{2,6},{6,10},{... | collective-permute-start | bytes 1572872 | tf_op jit(solution)/shard_map/ppermute | solution.py:476
  11.8 36.5 %collective-permute-start.1 = (bf16[2,1024,128]{2,1,0:T(8,128)(2,1)}, bf16[2,1024,128]{2,1,0:T(8,128)(2,1)S(1)}, u32[]{:S(2)}, u32[]{:S(2)}) collective-permute-start(bf16[2,1024,128]{2,1,0:T(8,128)(2,1)} %get-tuple-element.75), channel_id=1, source_target_pairs={{0,8},{4,12},{8,0},{12,4},{1,9},{5,13},{9,1},{13,5},{2,10},{6,14},... | collective-permute-start | bytes 1572872 | tf_op jit(solution)/shard_map/ppermute | solution.py:476
  14.3 33.9 %collective-permute-start.2 = (bf16[2,1024,128]{2,1,0:T(8,128)(2,1)}, bf16[2,1024,128]{2,1,0:T(8,128)(2,1)}, u32[]{:S(2)}, u32[]{:S(2)}) collective-permute-start(bf16[2,1024,128]{2,1,0:T(8,128)(2,1)} %get-tuple-element.76), channel_id=1, source_target_pairs={{0,12},{4,0},{8,4},{12,8},{1,13},{5,1},{9,5},{13,9},{2,14},{6,2},{... | collective-permute-start | bytes 1572872 | tf_op jit(solution)/shard_map/ppermute | solution.py:476
  15.7 43.7 %copy-start.9 = (bf16[1024,128]{1,0:T(8,128)(2,1)S(1)}, bf16[1024,128]{1,0:T(8,128)(2,1)}, u32[]{:S(2)}) copy-start(bf16[1024,128]{1,0:T(8,128)(2,1)} %get-tuple-element.83) | copy-start | bytes 786436
  15.7 47.3 %copy-start = (bf16[1024,1024]{1,0:T(8,128)(2,1)S(1)}, bf16[1024,1024]{1,0:T(8,128)(2,1)}, u32[]{:S(2)}) copy-start(bf16[1024,1024]{1,0:T(8,128)(2,1)} %tokens.5) | copy-start | bytes 6291460
  15.7 47.3 %copy-start.4 = (f32[17,1024]{1,0:T(8,128)S(1)}, f32[17,1024]{1,0:T(8,128)}, u32[]{:S(2)}) copy-start(f32[17,1024]{1,0:T(8,128)} %mix_ref.1) | copy-start | bytes 208900
  15.7 47.3 %copy-start.5 = (f32[2,1024]{1,0:T(2,128)S(1)}, f32[2,1024]{1,0:T(2,128)}, u32[]{:S(2)}) copy-start(f32[2,1024]{1,0:T(2,128)} %high_ref.1) | copy-start | bytes 24580
  15.7 47.3 %copy-start.6 = (s32[5]{0:T(128)S(1)}, s32[5]{0:T(128)}, u32[]{:S(2)}) copy-start(s32[5]{0:T(128)} %stack.37.place) | copy-start | bytes 64
  15.7 47.3 %copy-start.7 = (f32[1024]{0:T(1024)S(1)}, f32[1024]{0:T(1024)}, u32[]{:S(2)}) copy-start(f32[1024]{0:T(1024)} %param.8) | copy-start | bytes 12292
  56.1 24.2 %collective-permute-start.8 = (bf16[2,512,1024]{2,1,0:T(8,128)(2,1)}, bf16[2,512,1024]{2,1,0:T(8,128)(2,1)S(1)}, u32[]{:S(2)}, u32[]{:S(2)}) collective-permute-start(bf16[2,512,1024]{2,1,0:T(8,128)(2,1)} %collective-permute-done.3.refs_2_), channel_id=1, source_target_pairs={{0,1},{1,0},{2,3},{3,2},{4,5},{5,4},{6,7},{7,6},{8,9},{9,8},{10,11... | collective-permute-start | bytes 6291464 | tf_op jit(solution)/shard_map/ppermute | solution.py:467
  56.1 48.3 %collective-permute-start.12 = (bf16[2,512,1024]{2,1,0:T(8,128)(2,1)}, bf16[2,512,1024]{2,1,0:T(8,128)(2,1)S(1)}, u32[]{:S(2)}, u32[]{:S(2)}) collective-permute-start(bf16[2,512,1024]{2,1,0:T(8,128)(2,1)} %collective-permute-done.3.refs_2_), channel_id=1, source_target_pairs={{0,16},{16,0},{1,17},{17,1},{2,18},{18,2},{3,19},{19,3},{4,20},{20... | collective-permute-start | bytes 6291464 | tf_op jit(solution)/shard_map/ppermute | solution.py:467
  57.9 47.8 %collective-permute-start.13 = (bf16[1024,1024]{1,0:T(8,128)(2,1)S(1)}, bf16[1024,1024]{1,0:T(8,128)(2,1)S(1)}, u32[]{:S(2)}, u32[]{:S(2)}) collective-permute-start(bf16[1024,1024]{1,0:T(8,128)(2,1)S(1)} %constant_dynamic-slice_fusion), channel_id=1, source_target_pairs={{0,2},{2,0},{1,3},{3,1},{4,6},{6,4},{5,7},{7,5},{8,10},{10,8},{9,1... | collective-permute-start | bytes 6291464 | tf_op jit(solution)/shard_map/ppermute | solution.py:467
  59.4 1.6 collective-permute-start.4
  59.4 1.9 %collective-permute-start.5 = (bf16[1024,128]{1,0:T(8,128)(2,1)S(1)}, bf16[1024,128]{1,0:T(8,128)(2,1)S(1)}, u32[]{:S(2)}, u32[]{:S(2)}) collective-permute-start(bf16[1024,128]{1,0:T(8,128)(2,1)S(1)} %slice_bitcast_fusion.2), channel_id=1, source_target_pairs={{0,1},{1,0},{2,3},{3,2},{4,5},{5,4},{6,7},{7,6},{8,9},{9,8},{10,11... | collective-permute-start | bytes 786440 | tf_op jit(solution)/shard_map/ppermute | solution.py:467
  61.0 1.6 collective-permute-start.6
  61.3 1.7 collective-permute-start.7
  63.0 69.8 %copy-start.3 = (bf16[2048,1024]{1,0:T(8,128)(2,1)S(1)}, bf16[2048,1024]{1,0:T(8,128)(2,1)}, u32[]{:S(2)}) copy-start(bf16[2048,1024]{1,0:T(8,128)(2,1)} %refs_1_.1) | copy-start | bytes 12582916
  80.3 21.4 %collective-permute-start.9 = (bf16[2,512,128]{2,1,0:T(8,128)(2,1)S(1)}, bf16[2,512,128]{2,1,0:T(8,128)(2,1)S(1)}, u32[]{:S(2)}, u32[]{:S(2)}) collective-permute-start(bf16[2,512,128]{2,1,0:T(8,128)(2,1)S(1)} %get-tuple-element.93), channel_id=1, source_target_pairs={{0,8},{4,12},{8,0},{12,4},{1,9},{5,13},{9,1},{13,5},{2,10},{6,14},... | collective-permute-start | bytes 786440 | tf_op jit(solution)/shard_map/ppermute | solution.py:476
  83.0 22.7 %collective-permute-start.10 = (bf16[2,512,128]{2,1,0:T(8,128)(2,1)S(1)}, bf16[2,512,128]{2,1,0:T(8,128)(2,1)S(1)}, u32[]{:S(2)}, u32[]{:S(2)}) collective-permute-start(bf16[2,512,128]{2,1,0:T(8,128)(2,1)S(1)} %get-tuple-element.99), channel_id=1, source_target_pairs={{0,4},{4,8},{8,12},{12,0},{1,5},{5,9},{9,13},{13,1},{2,6},{6,10},{... | collective-permute-start | bytes 786440 | tf_op jit(solution)/shard_map/ppermute | solution.py:476
  85.4 20.2 %collective-permute-start.11 = (bf16[2,512,128]{2,1,0:T(8,128)(2,1)S(1)}, bf16[2,512,128]{2,1,0:T(8,128)(2,1)S(1)}, u32[]{:S(2)}, u32[]{:S(2)}) collective-permute-start(bf16[2,512,128]{2,1,0:T(8,128)(2,1)S(1)} %get-tuple-element.101), channel_id=1, source_target_pairs={{0,12},{4,0},{8,4},{12,8},{1,13},{5,1},{9,5},{13,9},{2,14},{6,2},{... | collective-permute-start | bytes 786440 | tf_op jit(solution)/shard_map/ppermute | solution.py:476
  101.7 31.0 %copy-start.2 = (bf16[2048,1024]{1,0:T(8,128)(2,1)S(1)}, bf16[2048,1024]{1,0:T(8,128)(2,1)}, u32[]{:S(2)}) copy-start(bf16[2048,1024]{1,0:T(8,128)(2,1)} %refs_0_.1) | copy-start | bytes 12582916
  101.7 16.0 %collective-permute-start.15 = (bf16[2,512,128]{2,1,0:T(8,128)(2,1)S(1)}, bf16[2,512,128]{2,1,0:T(8,128)(2,1)S(1)}, u32[]{:S(2)}, u32[]{:S(2)}) collective-permute-start(bf16[2,512,128]{2,1,0:T(8,128)(2,1)S(1)} %get-tuple-element.96), channel_id=1, source_target_pairs={{0,8},{4,12},{8,0},{12,4},{1,9},{5,13},{9,1},{13,5},{2,10},{6,14},... | collective-permute-start | bytes 786440 | tf_op jit(solution)/shard_map/ppermute | solution.py:476
  117.8 15.0 %collective-permute-start.19 = (bf16[2,512,1024]{2,1,0:T(8,128)(2,1)S(1)}, bf16[2,512,1024]{2,1,0:T(8,128)(2,1)S(1)}, u32[]{:S(2)}, u32[]{:S(2)}) collective-permute-start(bf16[2,512,1024]{2,1,0:T(8,128)(2,1)S(1)} %collective-permute-done.12.refs_3_), channel_id=1, source_target_pairs={{0,1},{1,0},{2,3},{3,2},{4,5},{5,4},{6,7},{7,6},{8,9},{9,8},{10,11... | collective-permute-start | bytes 6291464 | tf_op jit(solution)/shard_map/ppermute | solution.py:467
  118.0 14.8 %collective-permute-start.17 = (bf16[4,512,128]{2,1,0:T(8,128)(2,1)S(1)}, bf16[4,512,128]{2,1,0:T(8,128)(2,1)S(1)}, u32[]{:S(2)}, u32[]{:S(2)}) collective-permute-start(bf16[4,512,128]{2,1,0:T(8,128)(2,1)S(1)} %pad_maximum_fusion.1), channel_id=1, source_target_pairs={{0,2},{2,0},{1,3},{3,1},{4,6},{6,4},{5,7},{7,5},{8,10},{10,8},{9,1... | collective-permute-start | bytes 1572872 | tf_op jit(solution)/shard_map/ppermute | solution.py:467
  119.4 23.8 %collective-permute-start.18 = (bf16[4,512,128]{2,1,0:T(8,128)(2,1)S(1)}, bf16[4,512,128]{2,1,0:T(8,128)(2,1)S(1)}, u32[]{:S(2)}, u32[]{:S(2)}) collective-permute-start(bf16[4,512,128]{2,1,0:T(8,128)(2,1)S(1)} %pad_maximum_fusion.2), channel_id=1, source_target_pairs={{0,3},{1,2},{2,1},{3,0},{4,7},{5,6},{6,5},{7,4},{8,11},{9,10},{10,... | collective-permute-start | bytes 1572872 | tf_op jit(solution)/shard_map/ppermute | solution.py:471
  120.0 16.1 %collective-permute-start.14 = (bf16[2,512,128]{2,1,0:T(8,128)(2,1)S(1)}, bf16[2,512,128]{2,1,0:T(8,128)(2,1)S(1)}, u32[]{:S(2)}, u32[]{:S(2)}) collective-permute-start(bf16[2,512,128]{2,1,0:T(8,128)(2,1)S(1)} %get-tuple-element.103), channel_id=1, source_target_pairs={{0,4},{4,8},{8,12},{12,0},{1,5},{5,9},{9,13},{13,1},{2,6},{6,10},{... | collective-permute-start | bytes 786440 | tf_op jit(solution)/shard_map/ppermute | solution.py:476
  120.7 15.4 %collective-permute-start.16 = (bf16[2,512,128]{2,1,0:T(8,128)(2,1)S(1)}, bf16[2,512,128]{2,1,0:T(8,128)(2,1)S(1)}, u32[]{:S(2)}, u32[]{:S(2)}) collective-permute-start(bf16[2,512,128]{2,1,0:T(8,128)(2,1)S(1)} %get-tuple-element.106), channel_id=1, source_target_pairs={{0,12},{4,0},{8,4},{12,8},{1,13},{5,1},{9,5},{13,9},{2,14},{6,2},{... | collective-permute-start | bytes 786440 | tf_op jit(solution)/shard_map/ppermute | solution.py:476
  132.8 10.5 %collective-permute-start.20 = (bf16[1024,1024]{1,0:T(8,128)(2,1)S(1)}, bf16[1024,1024]{1,0:T(8,128)(2,1)S(1)}, u32[]{:S(2)}, u32[]{:S(2)}) collective-permute-start(bf16[1024,1024]{1,0:T(8,128)(2,1)S(1)} %collective-permute-done.13.mine), channel_id=1, source_target_pairs={{0,1},{1,0},{2,3},{3,2},{4,5},{5,4},{6,7},{7,6},{8,9},{9,8},{10,11... | collective-permute-start | bytes 6291464 | tf_op jit(solution)/shard_map/ppermute | solution.py:467
  143.4 2.0 %collective-permute-start.21 = (bf16[4,512,128]{2,1,0:T(8,128)(2,1)S(1)}, bf16[4,512,128]{2,1,0:T(8,128)(2,1)S(1)}, u32[]{:S(2)}, u32[]{:S(2)}) collective-permute-start(bf16[4,512,128]{2,1,0:T(8,128)(2,1)S(1)} %pad_maximum_fusion.3), channel_id=1, source_target_pairs={{0,1},{1,0},{2,3},{3,2},{4,5},{5,4},{6,7},{7,6},{8,9},{9,8},{10,11... | collective-permute-start | bytes 1572872 | tf_op jit(solution)/shard_map/ppermute | solution.py:467
  153.9 14.8 %collective-permute-start.23 = (bf16[256,1024]{1,0:T(8,128)(2,1)S(1)}, bf16[256,1024]{1,0:T(8,128)(2,1)S(1)}, u32[]{:S(2)}, u32[]{:S(2)}) collective-permute-start(bf16[256,1024]{1,0:T(8,128)(2,1)S(1)} %send.2), channel_id=1, source_target_pairs={{0,2},{2,0},{1,3},{3,1},{4,6},{6,4},{5,7},{7,5},{8,10},{10,8},{9,1... | collective-permute-start | bytes 1572872 | tf_op jit(solution)/shard_map/ppermute | solution.py:467
  161.4 7.2 %copy-start.1 = (bf16[2048,1024]{1,0:T(8,128)(2,1)S(1)}, bf16[2048,1024]{1,0:T(8,128)(2,1)}, u32[]{:S(2)}) copy-start(bf16[2048,1024]{1,0:T(8,128)(2,1)} %refs_2_.1) | copy-start | bytes 12582916
  163.8 15.5 %collective-permute-start.22 = (bf16[256,1024]{1,0:T(8,128)(2,1)S(1)}, bf16[256,1024]{1,0:T(8,128)(2,1)}, u32[]{:S(2)}, u32[]{:S(2)}) collective-permute-start(bf16[256,1024]{1,0:T(8,128)(2,1)S(1)} %send.3), channel_id=1, source_target_pairs={{0,2},{2,0},{1,3},{3,1},{4,6},{6,4},{5,7},{7,5},{8,10},{10,8},{9,1... | collective-permute-start | bytes 1572872 | tf_op jit(solution)/shard_map/ppermute | solution.py:467
  168.7 4.5 %copy-start.8 = (bf16[256,1024]{1,0:T(8,128)(2,1)}, bf16[256,1024]{1,0:T(8,128)(2,1)S(1)}, u32[]{:S(2)}) copy-start(bf16[256,1024]{1,0:T(8,128)(2,1)S(1)} %collective-permute-done.23.got) | copy-start | bytes 1572868

commit v4 on v3

--- a/solution.py
+++ b/solution.py
@@ -145,10 +145,10 @@
 
 def levels_kernel(live, chips, place, angle_ref, high_ref, mix_ref, own, *refs):
     direct = refs[: chips - 1]
-    handed = refs[chips - 1 : 2 * chips - 1]
-    far = refs[2 * chips - 1 : 3 * chips - 1]
-    near = refs[3 * chips - 1 : 4 * chips - 1]
-    tokens, stream_ref, mixed_ref, act_ref, coef_ref, sems = refs[4 * chips - 1 :]
+    handed = refs[chips - 1 : chips + 1]
+    far = refs[chips + 1 : 2 * chips + 1]
+    near = refs[2 * chips + 1 : (2 + SPLIT) * chips + 1]
+    tokens, stream_ref, mixed_ref, act_ref, coef_ref = refs[(2 + SPLIT) * chips + 1 :]
     side = place[2]
     rows = own.shape[0]
     units = rows * 2 * chips // 8
@@ -157,14 +157,10 @@
         return pl.ds(pl.multiple_of(line * rows, rows), rows)
 
     columns = pl.ds(pl.multiple_of(line_of(place, 0, 0) * LANES, LANES), LANES)
-    pairs = []
     for back in range(chips):
-        mine = direct[back - 1].at[0] if back else own.at[:, columns]
-        pairs.append((mine, tokens.at[block(line_of(place, back, 0))]))
-        pairs.append((handed[back], tokens.at[block(line_of(place, back, 1))]))
-    copy_all(
-        pairs, sems, lambda: coefficients(live, columns, angle_ref, high_ref, mix_ref, coef_ref)
-    )
+        tokens[block(line_of(place, back, 0)), :] = direct[back - 1][0] if back else own[...]
+        tokens[block(line_of(place, back, 1)), :] = handed[1][back - 1] if back else handed[0][...]
+    coefficients(live, columns, angle_ref, high_ref, mix_ref, coef_ref)
 
     def whole(row):
         return jnp.broadcast_to(coef_ref[row : row + 1, :], (8, LANES))[None]
@@ -225,51 +221,52 @@
             x = stream_wide[:, pair * 2 + odd]
             mixed = total_wide[:, pair * 2 + odd]
             for level in range(9, live):
-                x = advance(x, zero(2 ** (level - 9)), ratio)
+                reach = 2 ** (level - 9)
+                x = jnp.concatenate([x[:reach], x[reach:] + ratio * x[:-reach]], 0)
                 mixed = mixed + whole(level + 1) * x
             halves.append(jax.nn.gelu(mixed))
         act_wide[:, pair] = jnp.concatenate(halves, 1).astype(jnp.bfloat16)
         return 0
 
+    half = rows // 2
+    part = half // SPLIT
     lax.fori_loop(0, WIDE // 2, third, 0)
-
-    half = rows // 2
-    pairs = []
     for ahead in range(chips):
         for other in range(2):
             start = line_of(place, -ahead, other) * rows
-            for outs, which in ((far, 1 - side), (near, side)):
-                begin = pl.multiple_of(start + which * half, half)
-                pairs.append((act_ref.at[pl.ds(begin, half)], outs[ahead].at[other]))
-    copy_all(pairs, sems)
+            begin = pl.multiple_of(start + (1 - side) * half, half)
+            far[ahead][other] = act_ref[pl.ds(begin, half), :]
+            for q in range(SPLIT):
+                begin = pl.multiple_of(start + side * half + q * part, part)
+                near[q * chips + ahead][other] = act_ref[pl.ds(begin, part), :]
 
 
 def run_filter(place, angle, high, mix, own, direct, handed, live):
-    chips = len(handed)
+    chips = 1 + len(direct)
     rows = handed[0].shape[0]
     total = rows * 2 * chips
     anywhere = pl.BlockSpec(memory_space=pltpu.HBM)
     outs = pl.pallas_call(
         functools.partial(levels_kernel, live, chips),
-        out_shape=[jax.ShapeDtypeStruct((2, rows // 2, LANES), jnp.bfloat16)] * (2 * chips),
+        out_shape=[jax.ShapeDtypeStruct((2, rows // 2, LANES), jnp.bfloat16)] * chips
+        + [jax.ShapeDtypeStruct((2, rows // 2 // SPLIT, LANES), jnp.bfloat16)] * (SPLIT * chips),
         in_specs=[
             pl.BlockSpec(memory_space=pltpu.SMEM),
         ]
-        + [pl.BlockSpec(memory_space=pltpu.VMEM)] * 3
-        + [anywhere] * (2 * chips),
-        out_specs=[anywhere] * (2 * chips),
+        + [pl.BlockSpec(memory_space=pltpu.VMEM)] * (chips + 5),
+        out_specs=[pl.BlockSpec(memory_space=pltpu.VMEM)] * ((1 + SPLIT) * chips),
         scratch_shapes=[
             pltpu.VMEM((total, LANES), jnp.bfloat16),
             pltpu.VMEM((total // 8, 8, LANES), jnp.float32),
             pltpu.VMEM((total // 8, 8, LANES), jnp.float32),
             pltpu.VMEM((total, LANES), jnp.bfloat16),
             pltpu.VMEM((live + 2, LANES), jnp.float32),
-            pltpu.SemaphoreType.DMA((4 * chips,)),
         ],
         compiler_params=pltpu.CompilerParams(vmem_limit_bytes=GRANT),
         name="levels",
     )(place, angle[None], high, mix, own, *direct, *handed)
-    return list(outs[:chips]), list(outs[chips:])
+    groups = [list(outs[at * chips : (at + 1) * chips]) for at in range(1 + SPLIT)]
+    return groups[0], groups[1:]
 
 
 def work(rows, depth, columns):
@@ -284,76 +281,80 @@
     return jnp.dot(a, b, preferred_element_type=jnp.float32)
 
 
-def load_kernel(place, *refs):
-    value_own, gate_own = refs[:2]
-    pieces = refs[2:6]
-    outs, sems = refs[-6:-1], refs[-1]
-    core, group = place[1], place[3]
-    depth = pieces[0].shape[1]
-    pairs = [(value_own, outs[0]), (gate_own, outs[1])]
-    for piece, far_group, far_core in zip(pieces, (0, 1, 0, 1), (0, 0, 1, 1)):
-        quarter = 2 * (1 - group if far_group else group) + (1 - core if far_core else core)
-        rows = pl.ds(pl.multiple_of(quarter * depth, depth), depth)
-        for at in range(2):
-            pairs.append((piece.at[at], outs[2 + at].at[rows]))
-    copy_all(pairs, sems)
+def load_kernel(count, *refs):
+    place, sources, outs = refs[0], refs[1 : 1 + count], refs[-count - 2 : -2]
+    copy_all(list(zip(sources, outs)), refs[-1])
     for at in range(place.shape[0]):
-        outs[4][at] = place[at]
-
-
-def run_load(place, value_own, gate_own, fetched, after):
-    arrays = [value_own, gate_own, *fetched, *after]
-    whole = jax.ShapeDtypeStruct(value_own.shape, value_own.dtype)
+        refs[-2][at] = place[at]
+
+
+def run_load(place, arrays, after):
+    count = len(arrays)
     smem = pl.BlockSpec(memory_space=pltpu.SMEM)
-    return pl.pallas_call(
-        load_kernel,
-        in_specs=[smem] + [pl.BlockSpec(memory_space=pltpu.HBM)] * len(arrays),
-        out_specs=[pl.BlockSpec(memory_space=pltpu.VMEM)] * 4 + [smem],
-        out_shape=[whole] * 4 + [jax.ShapeDtypeStruct(place.shape, place.dtype)],
-        scratch_shapes=[pltpu.SemaphoreType.DMA((10,))],
+    *loaded, place = pl.pallas_call(
+        functools.partial(load_kernel, count),
+        in_specs=[smem] + [pl.BlockSpec(memory_space=pltpu.HBM)] * (count + len(after)),
+        out_specs=[pl.BlockSpec(memory_space=pltpu.VMEM)] * count + [smem],
+        out_shape=[jax.ShapeDtypeStruct(array.shape, array.dtype) for array in (*arrays, place)],
+        scratch_shapes=[pltpu.SemaphoreType.DMA((count,))],
         compiler_params=pltpu.CompilerParams(vmem_limit_bytes=LITTLE),
         cost_estimate=pl.CostEstimate(flops=10**11, bytes_accessed=0, transcendentals=0),
         name="load",
-    )(place, *arrays)
-
-
-def hidden_kernel(chips, q, block, place, *refs):
+    )(place, *arrays, *after)
+    return loaded, place
+
+
+def hidden_kernel(chips, block, place, *refs):
     direct = refs[:chips]
     handed, straight, crossed = refs[chips : chips + 3]
-    value_own, gate_own, value_far, gate_far, hidden_ref, act, sems = refs[chips + 3 :]
+    own, fetched = refs[chips + 3 : chips + 5], refs[chips + 5 : chips + 9]
+    hidden_ref, act, sems = refs[chips + 9 :]
     side = place[2]
     channels = 2 * chips * LANES
-    part = pl.ds(q * act.shape[0], act.shape[0])
     pairs = []
     for back in range(chips):
         for other, near, far in ((0, direct[back], straight), (1, handed, crossed)):
             line = line_of(place, back, other) * LANES
             for start, source in (
-                (side * channels + line, near.at[back if other else 0, part]),
-                ((1 - side) * channels + line, far.at[back, part]),
+                (side * channels + line, near.at[back if other else 0]),
+                ((1 - side) * channels + line, far.at[back]),
             ):
                 lanes = pl.ds(pl.multiple_of(start, LANES), LANES)
                 pairs.append((source, act.at[:, lanes]))
     copy_all(pairs, sems)
 
-    for whose, value_ref, gate_ref in ((side, value_own, gate_own), (1 - side, value_far, gate_far)):
+    core, group = place[1], place[3]
+    depth = fetched[0].shape[1]
+
+    def own_side(at, columns):
+        return dot(act[...], own[at][:, columns])
+
+    def far_side(at, columns):
+        total = None
+        for piece, far_group, far_core in zip(fetched, (0, 1, 0, 1), (0, 0, 1, 1)):
+            quarter = 2 * (1 - group if far_group else group) + (1 - core if far_core else core)
+            rows = pl.ds(pl.multiple_of(quarter * depth, depth), depth)
+            term = dot(act[:, rows], piece[at, :, columns])
+            total = term if total is None else total + term
+        return total
+
+    for whose, product in ((side, own_side), (1 - side, far_side)):
 
         @pl.loop(0, channels // block)
         def _(j):
             columns = pl.ds(pl.multiple_of(j * block, block), block)
-            value = dot(act[...], value_ref[:, columns])
-            gate = dot(act[...], gate_ref[:, columns])
             target = pl.ds(pl.multiple_of(whose * channels + j * block, block), block)
-            hidden_ref[:, target] = (value * jax.nn.sigmoid(gate)).astype(jnp.bfloat16)
-
-
-def run_hidden(place, q, direct, handed, straight, crossed, *weights):
+            gated = product(0, columns) * jax.nn.sigmoid(product(1, columns))
+            hidden_ref[:, target] = gated.astype(jnp.bfloat16)
+
+
+def run_hidden(place, direct, handed, straight, crossed, *weights):
     chips = len(direct)
-    rows = handed.shape[1] // SPLIT
+    rows = handed.shape[1]
     width, channels = weights[0].shape
     in_vmem = pl.BlockSpec(memory_space=pltpu.VMEM)
     return pl.pallas_call(
-        functools.partial(hidden_kernel, chips, q, min(512, channels)),
+        functools.partial(hidden_kernel, chips, min(512, channels)),
         in_specs=[pl.BlockSpec(memory_space=pltpu.SMEM)]
         + [pl.BlockSpec(memory_space=pltpu.HBM)] * (chips + 3)
         + [in_vmem] * len(weights),
@@ -476,6 +477,23 @@
     return lax.ppermute(array, "seq", [(j, (j + offset) % chips) for j in range(chips)])
 
 
+def twins_kernel(chips, *refs):
+    copy_all([(refs[at].at[1], refs[chips].at[at]) for at in range(chips)], refs[-1])
+
+
+def run_twins(blocks):
+    rows = blocks[0].shape[1]
+    return pl.pallas_call(
+        functools.partial(twins_kernel, len(blocks)),
+        in_specs=[pl.BlockSpec(memory_space=pltpu.HBM)] * len(blocks),
+        out_specs=pl.BlockSpec(memory_space=pltpu.VMEM),
+        out_shape=jax.ShapeDtypeStruct((len(blocks), rows, LANES), blocks[0].dtype),
+        scratch_shapes=[pltpu.SemaphoreType.DMA((len(blocks),))],
+        compiler_params=pltpu.CompilerParams(vmem_limit_bytes=LITTLE),
+        name="twins",
+    )(*blocks)
+
+
 def by_tokens(tokens, low_angle, high_taps, level_mix, w_value, w_gate, out_weight):
     rows, channels = tokens.shape
     chips = lax.axis_size("seq")
@@ -486,12 +504,13 @@
     order = sorted(range(1, chips), key=lambda s: abs(2 * s - chips))
     place = jnp.stack([chip, core, side, group, chips]).astype(jnp.int32)
 
+    mine = lax.dynamic_slice_in_dim(tokens, (chip * 2 + core) * narrow, narrow, 1)
     blocks = run_cut(place, tokens, chips)
     blocks, weights = lax.optimization_barrier((blocks, (w_value, w_gate, out_weight)))
     direct = [None] * chips
     for s in order:
         direct[s] = ahead(blocks[s], s)
-    handed = [swap(blocks[0], "sub")] + [swap(direct[s][1], "sub") for s in range(1, chips)]
+    handed = [swap(blocks[0], "sub"), swap(run_twins(direct[1:]), "sub")]
 
     depth = w_value.shape[0] // 4
     pair = jnp.stack(
@@ -508,7 +527,7 @@
     pair_third = swap(pair_first, "sub")
 
     far, near = run_filter(
-        place, low_angle, high_taps, level_mix, tokens, direct[1:], handed, live
+        place, low_angle, high_taps, level_mix, mine, direct[1:], handed, live
     )
 
     far, pair_third = lax.optimization_barrier((far, pair_third))
@@ -522,33 +541,51 @@
             cross(jnp.stack([far_got[back][1] for back in backs])),
         )
 
-    near, far_got[order[0]] = lax.optimization_barrier((near, far_got[order[0]]))
-    near, far_got = list(near), list(far_got)
-    near_got = [near[0]] + [None] * (chips - 1)
-    near_got[order[0]] = ahead(near[order[0]], order[0])
-    near, far_got, pair_second, half_first = lax.optimization_barrier(
-        (near, far_got, pair_second, half_first)
-    )
-    for s in order[1:]:
-        near_got[s] = ahead(near[s], s)
-    straight = swap(jnp.stack([block[0] for block in far_got]), "chan")
-    crossed = cross(jnp.stack([block[1] for block in far_got]))
-    pair_second, near_got[order[0]] = lax.optimization_barrier((pair_second, near_got[order[0]]))
+    near_got = [[part[0]] + [None] * (chips - 1) for part in near]
+    for s in order:
+        near[0][s], far_got[s] = lax.optimization_barrier((near[0][s], far_got[s]))
+        near_got[0][s] = ahead(near[0][s], s)
+    rows = near[0][0].shape[1]
+
+    def exchange(q, first, second):
+        part = slice(q * rows, (q + 1) * rows)
+        straight, first = lax.optimization_barrier(
+            (jnp.stack([block[0, part] for block in far_got]), first)
+        )
+        crossed, second = lax.optimization_barrier(
+            (jnp.stack([block[1, part] for block in far_got]), second)
+        )
+        return swap(straight, "chan"), cross(crossed)
+
+    got = exchange(0, half_first, pair_second)
+    near_got[0][order[0]], pair_second = lax.optimization_barrier(
+        (near_got[0][order[0]], pair_second)
+    )
     pair_fourth = swap(pair_second, "sub")
-    fetched = [pair_first, pair_second, pair_third, pair_fourth]
-    *loaded, place = run_load(place, w_value, w_gate, fetched, far_got[1:])
-    half_first, straight = lax.optimization_barrier((half_first, straight))
+    loaded, place = run_load(
+        place, [w_value, w_gate, pair_first, pair_second, pair_third], far_got[1:]
+    )
+    near_got[0], got, place, pair_fourth, half_first = lax.optimization_barrier(
+        (near_got[0], got, place, pair_fourth, half_first)
+    )
     half_second = swap(half_first, "sub")
-    near_got, straight, crossed, place, half_second = lax.optimization_barrier(
-        (near_got, straight, crossed, place, half_second)
-    )
-    handed = swap(jnp.stack([block[1] for block in near_got]), "sub")
+    loaded.append(pair_fourth)
     which = place[2:3]
     hidden, returned = [], []
     for q in range(SPLIT):
-        made = run_hidden(place, q, near_got, handed, straight, crossed, *loaded)
+        handed = swap(run_twins(near_got[q]), "sub")
+        if q + 1 < SPLIT:
+            for s in order:
+                near[q + 1][s], near_got[q][s] = lax.optimization_barrier(
+                    (near[q + 1][s], near_got[q][s])
+                )
+                near_got[q + 1][s] = ahead(near[q + 1][s], s)
+            later = exchange(q + 1, *got)
+        made = run_hidden(place, near_got[q], handed, *got, *loaded)
         sent = run_send(place, made, [half_first, half_second])
-        place, sent = lax.optimization_barrier((place, sent))
+        if q + 1 < SPLIT:
+            near_got[q + 1], later, sent = lax.optimization_barrier((near_got[q + 1], later, sent))
+            got = later
         hidden.append(made)
         returned.append(swap(sent, "chan"))
     hidden, returned[0] = lax.optimization_barrier((hidden, returned[0]))

time: 182 us -> 169 us (0.929)
  waiting for transfers between devices: 95.7 us -> 78.3 us
  local copies, waits for them, and re-layouts: 6.1 us -> 8.38 us
    ppermute x14, waiting for transfers between devices: 31 us -> 20.3 us  [swap(): return lax.ppermute(array, axis, [(0, 1), (1, 0)])]
    ppermute x1 -> x2, waiting for transfers between devices: 7.07 us -> 0.01 us  [cross(): lax.ppermute(array, ('chan', 'sub'), [(0, 3), (1, 2), (2, 1), (3, 0)])]
    pallas_call x1, Pallas kernels: 17.3 us -> 13.4 us  [run_filter(): pl.pallas_call(functools.partial(levels_kernel, live, chips), out_shape=[...]
    pallas_call x3 -> x6, Pallas kernels: 15.7 us -> 19.4 us  [the longest x2 12.2 us: run_hidden(): pl.pallas_call(functools.partial(hidden_kernel, chips, min(512, channels)...]
    unnamed x20 -> x18, local copies, waits for them, and re-layouts: 0.05 us -> 2.22 us
    pallas_call x2, Pallas kernels: 4.66 us -> 6.73 us  [run_send(): pl.pallas_call(send_kernel, grid_spec=pltpu.PrefetchScalarGridSpec(num_sc...]
    ppermute x9 -> x12, starting transfers between devices: 15.8 us -> 16.2 us  [ahead(): lax.ppermute(array, 'seq', [(j, (j + offset) % chips) for j in range(chip...]
    ppermute x9 -> x12, waiting for transfers between devices: 57.6 us -> 58 us  [ahead(): lax.ppermute(array, 'seq', [(j, (j + offset) % chips) for j in range(chip...]
  transfers between devices with their start and end apart: 24 -> 28, of which waited for: 15 -> 14; matrix products, arithmetic and copies ran while one was open for 2% -> 2% of each run, Pallas kernels for 19% -> 23%
where the time goes in v4:
time: 169 us
  waiting for transfers between devices  78.3 us (46%)
  Pallas kernels  52.4 us (31%)
  starting transfers between devices  28.1 us (17%)
  local copies, waits for them, and re-layouts  8.38 us (5%)
    ppermute x12, waiting for transfers between devices, ahead(): lax.ppermute(array, 'seq', [(j, (j + offset) % chips) for j in range(chip...  58 us
    ppermute x14, waiting for transfers between devices, swap(): return lax.ppermute(array, axis, [(0, 1), (1, 0)])  20.3 us
    ppermute x12, starting transfers between devices, ahead(): lax.ppermute(array, 'seq', [(j, (j + offset) % chips) for j in range(chip...  16.2 us
    pallas_call x1, Pallas kernels, run_filter(): pl.pallas_call(functools.partial(levels_kernel, live, chips), out_shape=[...  13.4 us
    pallas_call x2, Pallas kernels, run_hidden(): pl.pallas_call(functools.partial(hidden_kernel, chips, min(512, channels)...  12.2 us
    ppermute x14, starting transfers between devices, swap(): return lax.ppermute(array, axis, [(0, 1), (1, 0)])  10.9 us
    pallas_call x2, Pallas kernels, run_send(): pl.pallas_call(send_kernel, grid_spec=pltpu.PrefetchScalarGridSpec(num_sc...  6.73 us
    pallas_call x2, Pallas kernels, add_far(): pl.pallas_call(add_kernel, grid_spec=pltpu.PrefetchScalarGridSpec(num_sca...  5.17 us
  transfers between devices with their start and end apart: 28, of which 14 were waited for; matrix products, arithmetic and copies ran while one was open for 2% of the time, Pallas kernels for 23%

profile of v4, /device:TPU:0, one launch (start us, length us, event | category | flops | bytes accessed | tf_op | source)
XLA Modules:
  0.0 169.0 jit_solution(9071665687921651548)
XLA Ops:
  0.0 0.6 stack.40.place.refs_0_
  0.6 3.4 %cut.1 = (bf16[1024,128]{1,0:T(8,128)(2,1)}, bf16[2,1024,128]{2,1,0:T(8,128)(2,1)}, bf16[2,1024,128]{2,1,0:T(8,128)(2,1)}, bf16[2,1024,128]{2,1,0:T(8,128)(2,1)}) custom-call(s32[5]{0:T(128)} %stack.40.place.refs_0_, bf16[1024,1024]{1,0:T(8,128)(2,1)} %tokens.5), custom_call_target="tpu_custom_call" | custom-call | tf_op jit(solution)/shard_map/cut/pallas_call | solution.py:134
  4.0 1.7 %dynamic-slice_bitcast_fusion = (bf16[1,512,1024]{2,1,0:T(8,128)(2,1)S(1)}, bf16[1,512,1024]{2,1,0:T(8,128)(2,1)S(1)}) fusion(bf16[2048,1024]{1,0:T(8,128)(2,1)} %refs_2_.2, s32[]{:T(128)S(6)} %select_n.11, bf16[2048,1024]{1,0:T(8,128)(2,1)} %refs_1_.1), kind=kLoop, calls=%fused_computation.1 | loop fusion | bytes 4194308 | tf_op jit(solution)/shard_map/stack | solution.py:516
  5.7 1.5 pad_maximum_fusion
  7.2 2.9 %collective-permute-start.3 = (bf16[2,512,1024]{2,1,0:T(8,128)(2,1)}, bf16[2,512,1024]{2,1,0:T(8,128)(2,1)}, u32[]{:S(2)}, u32[]{:S(2)}) collective-permute-start(bf16[2,512,1024]{2,1,0:T(8,128)(2,1)} %pad_maximum_fusion), channel_id=1, source_target_pairs={{0,2},{2,0},{1,3},{3,1},{4,6},{6,4},{5,7},{7,5},{8,10},{10,8},{9,1... | collective-permute-start | bytes 6291464 | tf_op jit(solution)/shard_map/ppermute | solution.py:468
  10.1 1.6 collective-permute-start
  11.7 2.6 %collective-permute-start.1 = (bf16[2,1024,128]{2,1,0:T(8,128)(2,1)}, bf16[2,1024,128]{2,1,0:T(8,128)(2,1)S(1)}, u32[]{:S(2)}, u32[]{:S(2)}) collective-permute-start(bf16[2,1024,128]{2,1,0:T(8,128)(2,1)} %get-tuple-element.86), channel_id=1, source_target_pairs={{0,8},{4,12},{8,0},{12,4},{1,9},{5,13},{9,1},{13,5},{2,10},{6,14},... | collective-permute-start | bytes 1572872 | tf_op jit(solution)/shard_map/ppermute | solution.py:477
  14.3 1.3 collective-permute-start.2
  15.6 3.1 %constant_dynamic-slice_fusion = bf16[1024,1024]{1,0:T(8,128)(2,1)} fusion(bf16[2048,1024]{1,0:T(8,128)(2,1)} %refs_2_.3, s32[]{:T(128)S(6)} %select_n.12), kind=kLoop, calls=%fused_computation.7 | loop fusion | bytes 4194308 | tf_op jit(solution)/shard_map/dynamic_slice | solution.py:522
  18.7 8.4 %collective-permute-done.refs_0_ = bf16[2,1024,128]{2,1,0:T(8,128)(2,1)S(1)} collective-permute-done((bf16[2,1024,128]{2,1,0:T(8,128)(2,1)}, bf16[2,1024,128]{2,1,0:T(8,128)(2,1)S(1)}, u32[]{:S(2)}, u32[]{:S(2)}) %collective-permute-start) | collective-permute-done | bytes 524320 | tf_op jit(solution)/shard_map/ppermute | solution.py:477
  27.1 21.1 %collective-permute-done.1.refs_1_ = bf16[2,1024,128]{2,1,0:T(8,128)(2,1)S(1)} collective-permute-done((bf16[2,1024,128]{2,1,0:T(8,128)(2,1)}, bf16[2,1024,128]{2,1,0:T(8,128)(2,1)S(1)}, u32[]{:S(2)}, u32[]{:S(2)}) %collective-permute-start.1) | collective-permute-done | bytes 524320 | tf_op jit(solution)/shard_map/ppermute | solution.py:477
  48.2 7.9 %collective-permute-done.3.refs_3_ = bf16[2,512,1024]{2,1,0:T(8,128)(2,1)} collective-permute-done((bf16[2,512,1024]{2,1,0:T(8,128)(2,1)}, bf16[2,512,1024]{2,1,0:T(8,128)(2,1)}, u32[]{:S(2)}, u32[]{:S(2)}) %collective-permute-start.3) | collective-permute-done | bytes 2097184 | tf_op jit(solution)/shard_map/ppermute | solution.py:468
  56.1 1.8 %collective-permute-start.11 = (bf16[2,512,1024]{2,1,0:T(8,128)(2,1)}, bf16[2,512,1024]{2,1,0:T(8,128)(2,1)}, u32[]{:S(2)}, u32[]{:S(2)}) collective-permute-start(bf16[2,512,1024]{2,1,0:T(8,128)(2,1)} %collective-permute-done.3.refs_3_), channel_id=1, source_target_pairs={{0,16},{16,0},{1,17},{17,1},{2,18},{18,2},{3,19},{19,3},{4,20},{20... | collective-permute-start | bytes 6291464 | tf_op jit(solution)/shard_map/ppermute | solution.py:468
  57.8 1.5 collective-permute-start.14
  59.3 1.9 %twins.3 = bf16[3,1024,128]{2,1,0:T(8,128)(2,1)} custom-call(bf16[2,1024,128]{2,1,0:T(8,128)(2,1)S(1)} %collective-permute-done.refs_0_, bf16[2,1024,128]{2,1,0:T(8,128)(2,1)S(1)} %collective-permute-done.1.refs_1_, bf16[2,1024,128]{2,1,0:T(8,128)(2,1)} %collective-permute-done.2.refs_2_), custom_call_target="tpu_custom_call" | custom-call | tf_op jit(solution)/shard_map/twins/pallas_call | solution.py:486
  61.3 0.5 collective-permute-start.4
  61.9 2.3 %collective-permute-done.4.refs_3_ = bf16[1024,128]{1,0:T(8,128)(2,1)S(1)} collective-permute-done((bf16[1024,128]{1,0:T(8,128)(2,1)}, bf16[1024,128]{1,0:T(8,128)(2,1)S(1)}, u32[]{:S(2)}, u32[]{:S(2)}) %collective-permute-start.4) | collective-permute-done | bytes 262176 | tf_op jit(solution)/shard_map/ppermute | solution.py:468
  64.3 13.4 %levels.1 = (bf16[2,512,128]{2,1,0:T(8,128)(2,1)S(1)}, bf16[2,512,128]{2,1,0:T(8,128)(2,1)S(1)}, bf16[2,512,128]{2,1,0:T(8,128)(2,1)S(1)}, bf16[2,512,128]{2,1,0...) custom-call(s32[5]{0:T(128)S(1)} %copy-done.6, ...), custom_call_target="tpu_custom_call" | custom-call | tf_op jit(solution)/shard_map/levels/pallas_call | solution.py:249
  77.7 3.8 %collective-permute-start.12 = (bf16[2,512,128]{2,1,0:T(8,128)(2,1)S(1)}, bf16[2,512,128]{2,1,0:T(8,128)(2,1)S(1)}, u32[]{:S(2)}, u32[]{:S(2)}) collective-permute-start(bf16[2,512,128]{2,1,0:T(8,128)(2,1)S(1)} %get-tuple-element.109), channel_id=1, source_target_pairs={{0,12},{4,0},{8,4},{12,8},{1,13},{5,1},{9,5},{13,9},{2,14},{6,2},{... | collective-permute-start | bytes 786440 | tf_op jit(solution)/shard_map/ppermute | solution.py:477
  81.5 0.5 collective-permute-start.9
  82.4 5.8 %collective-permute-done.12.refs_8_ = bf16[2,512,128]{2,1,0:T(8,128)(2,1)S(1)} collective-permute-done((bf16[2,512,128]{2,1,0:T(8,128)(2,1)S(1)}, bf16[2,512,128]{2,1,0:T(8,128)(2,1)S(1)}, u32[]{:S(2)}, u32[]{:S(2)}) %collective-permute-start.12) | collective-permute-done | bytes 262176 | tf_op jit(solution)/shard_map/ppermute | solution.py:477
  88.2 19.7 %collective-permute-done.9.refs_7_ = bf16[2,512,128]{2,1,0:T(8,128)(2,1)S(1)} collective-permute-done((bf16[2,512,128]{2,1,0:T(8,128)(2,1)S(1)}, bf16[2,512,128]{2,1,0:T(8,128)(2,1)S(1)}, u32[]{:S(2)}, u32[]{:S(2)}) %collective-permute-start.9) | collective-permute-done | bytes 262176 | tf_op jit(solution)/shard_map/ppermute | solution.py:477
  108.1 0.5 collective-permute-start.16
  108.6 1.2 collective-permute-start.15
  109.7 1.3 collective-permute-start.13
  111.0 0.7 collective-permute-start.8
  111.8 2.1 %collective-permute-done.10.refs_2_ = bf16[2,256,128]{2,1,0:T(8,128)(2,1)S(1)} collective-permute-done((bf16[2,256,128]{2,1,0:T(8,128)(2,1)S(1)}, bf16[2,256,128]{2,1,0:T(8,128)(2,1)S(1)}, u32[]{:S(2)}, u32[]{:S(2)}) %collective-permute-start.10) | collective-permute-done | bytes 131104 | tf_op jit(solution)/shard_map/ppermute | solution.py:477
  113.9 2.2 %copy-done.3 = bf16[2048,1024]{1,0:T(8,128)(2,1)S(1)} copy-done((bf16[2048,1024]{1,0:T(8,128)(2,1)S(1)}, bf16[2048,1024]{1,0:T(8,128)(2,1)}, u32[]{:S(2)}) %copy-start.3) | copy-done | bytes 4194328
  116.1 4.6 %load.1 = (bf16[2048,1024]{1,0:T(8,128)(2,1)S(1)}, bf16[2048,1024]{1,0:T(8,128)(2,1)S(1)}, bf16[2,512,1024]{2,1,0:T(8,128)(2,1)S(1)}, bf16[2,512,1024]{2,1,0:T(8...) custom-call(s32[5]{0:T(128)S(1)} %copy-done.6, bf16[2048,1024]{1,0:T(8,128)(2,1)S(1)} %copy-done.2, ...), custom_call_target="tpu_custom_call" | custom-call | flops 99999997952 | tf_op jit(solution)/shard_map/load/pallas_call | solution.py:294
  120.7 1.6 collective-permute-done.15.refs_5_
  122.8 0.5 collective-permute-start.23
  123.8 1.3 collective-permute-start.21
  125.1 0.8 collective-permute-start.20
  126.0 0.9 collective-permute-done.23.refs_4_
  126.9 2.9 %collective-permute-start.19 = (bf16[2,256,128]{2,1,0:T(8,128)(2,1)S(1)}, bf16[2,256,128]{2,1,0:T(8,128)(2,1)S(1)}, u32[]{:S(2)}, u32[]{:S(2)}) collective-permute-start(bf16[2,256,128]{2,1,0:T(8,128)(2,1)S(1)} %get-tuple-element.128), channel_id=1, source_target_pairs={{0,8},{4,12},{8,0},{12,4},{1,9},{5,13},{9,1},{13,5},{2,10},{6,14},... | collective-permute-start | bytes 393224 | tf_op jit(solution)/shard_map/ppermute | solution.py:477
  130.1 6.1 %hidden.2.refs_0_ = bf16[256,2048]{1,0:T(8,128)(2,1)S(1)} custom-call(s32[5]{0:T(128)S(1)} %get-tuple-element.121.place, bf16[2,256,128]{2,1,0:T(8,128)(2,1)S(1)} %get-tuple-element.136.refs_0_, bf16[2,256,128]{2,1,0:T(8,128)(2,1)S(1)} %collective-permute-done.8.refs_1_, bf16[2,256,128]{2,1,0:T(8,128)(2,1)S(1)} %collective-permute-done.10.refs_2_, ...), custom_call_target="tpu_custom_call" | custom-call | flops 4294967296 | bytes 19922944 | tf_op jit(solution)/shard_map/hidden/pallas_call | solution.py:356
  136.2 3.2 %send.2 = bf16[256,1024]{1,0:T(8,128)(2,1)S(1)} custom-call(s32[5]{0:T(128)S(1)} %get-tuple-element.121.place, bf16[256,2048]{1,0:T(8,128)(2,1)S(1)} %hidden.2.refs_0_, bf16[1024,1024]{1,0:T(8,128)(2,1)} %collective-permute-done.14.mine, bf16[1024,1024]{1,0:T(8,128)(2,1)S(1)} %collective-permute-done.24.twin), custom_call_target="tpu_custom_call" | custom-call | flops 1073741824 | bytes 5767168 | tf_op jit(solution)/shard_map/send/pallas_call | solution.py:388
  139.4 0.8 collective-permute-done.19.refs_2_
  141.1 1.2 collective-permute-done.25.refs_4_
  142.3 6.1 %hidden.3.refs_1_ = bf16[256,2048]{1,0:T(8,128)(2,1)S(1)} custom-call(s32[5]{0:T(128)S(1)} %get-tuple-element.121.place, bf16[2,256,128]{2,1,0:T(8,128)(2,1)S(1)} %get-tuple-element.147.refs_0_, bf16[2,256,128]{2,1,0:T(8,128)(2,1)S(1)} %collective-permute-done.18.refs_1_, bf16[2,256,128]{2,1,0:T(8,128)(2,1)S(1)} %collective-permute-done.19.refs_2_, ...), custom_call_target="tpu_custom_call" | custom-call | flops 4294967296 | bytes 19922944 | tf_op jit(solution)/shard_map/hidden/pallas_call | solution.py:356
  148.4 3.5 %send.3 = bf16[256,1024]{1,0:T(8,128)(2,1)S(1)} custom-call(s32[5]{0:T(128)S(1)} %get-tuple-element.121.place, bf16[256,2048]{1,0:T(8,128)(2,1)S(1)} %hidden.3.refs_1_, bf16[1024,1024]{1,0:T(8,128)(2,1)} %collective-permute-done.14.mine, bf16[1024,1024]{1,0:T(8,128)(2,1)S(1)} %collective-permute-done.24.twin), custom_call_target="tpu_custom_call" | custom-call | flops 1073741824 | bytes 5767168 | tf_op jit(solution)/shard_map/send/pallas_call | solution.py:388
  151.9 0.6 collective-permute-start.26
  152.6 0.6 slice.59.side
  153.2 2.2 %collective-permute-done.27.got = bf16[256,1024]{1,0:T(8,128)(2,1)S(1)} collective-permute-done((bf16[256,1024]{1,0:T(8,128)(2,1)S(1)}, bf16[256,1024]{1,0:T(8,128)(2,1)S(1)}, u32[]{:S(2)}, u32[]{:S(2)}) %collective-permute-start.27) | collective-permute-done | bytes 524320 | tf_op jit(solution)/shard_map/ppermute | solution.py:468
  155.4 4.3 %finish.1.kept = bf16[1024,1024]{1,0:T(8,128)(2,1)} custom-call(s32[1]{0:T(128)} %slice.59.side, bf16[256,2048]{1,0:T(8,128)(2,1)S(1)} %hidden.2.refs_0_, bf16[256,2048]{1,0:T(8,128)(2,1)S(1)} %hidden.3.refs_1_, bf16[2048,1024]{1,0:T(8,128)(2,1)S(1)} %copy-done.1, bf16[1024,1024]{1,0:T(8,128)(2,1)S(1)} %copy-done), custom_call_target="tpu_custom_call" | custom-call | flops 2147483648 | bytes 7340032 | tf_op jit(solution)/shard_map/finish/pallas_call | solution.py:417
  159.8 2.6 %add_far.2.kept = bf16[1024,1024]{1,0:T(8,128)(2,1)} custom-call(s32[1]{0:T(128)} %slice.59.side, bf16[256,1024]{1,0:T(8,128)(2,1)} %copy-done.8, bf16[1024,1024]{1,0:T(8,128)(2,1)} %tokens.5, bf16[1024,1024]{1,0:T(8,128)(2,1)} %finish.1.kept), custom_call_target="tpu_custom_call", output_to_operand_aliasing={{}: (3, {})} | custom-call | tf_op jit(solution)/shard_map/add_far/pallas_call | solution.py:449
  162.3 4.1 %collective-permute-done.26.got = bf16[256,1024]{1,0:T(8,128)(2,1)} collective-permute-done((bf16[256,1024]{1,0:T(8,128)(2,1)S(1)}, bf16[256,1024]{1,0:T(8,128)(2,1)}, u32[]{:S(2)}, u32[]{:S(2)}) %collective-permute-start.26) | collective-permute-done | bytes 524320 | tf_op jit(solution)/shard_map/ppermute | solution.py:468
  166.5 2.6 %add_far.3 = bf16[1024,1024]{1,0:T(8,128)(2,1)} custom-call(s32[1]{0:T(128)} %slice.59.side, bf16[256,1024]{1,0:T(8,128)(2,1)} %collective-permute-done.26.got, bf16[1024,1024]{1,0:T(8,128)(2,1)} %tokens.5, bf16[1024,1024]{1,0:T(8,128)(2,1)} %add_far.2.kept), custom_call_target="tpu_custom_call", output_to_operand_aliasing={{}: (3, {})} | custom-call | tf_op jit(solution)/shard_map/add_far/pallas_call | solution.py:449
  (53 shorter events, 2.9 us)
Async XLA Ops:
  7.2 48.9 %collective-permute-start.3 = (bf16[2,512,1024]{2,1,0:T(8,128)(2,1)}, bf16[2,512,1024]{2,1,0:T(8,128)(2,1)}, u32[]{:S(2)}, u32[]{:S(2)}) collective-permute-start(bf16[2,512,1024]{2,1,0:T(8,128)(2,1)} %pad_maximum_fusion), channel_id=1, source_target_pairs={{0,2},{2,0},{1,3},{3,1},{4,6},{6,4},{5,7},{7,5},{8,10},{10,8},{9,1... | collective-permute-start | bytes 6291464 | tf_op jit(solution)/shard_map/ppermute | solution.py:468
  10.1 17.0 %collective-permute-start = (bf16[2,1024,128]{2,1,0:T(8,128)(2,1)}, bf16[2,1024,128]{2,1,0:T(8,128)(2,1)S(1)}, u32[]{:S(2)}, u32[]{:S(2)}) collective-permute-start(bf16[2,1024,128]{2,1,0:T(8,128)(2,1)} %get-tuple-element.85), channel_id=1, source_target_pairs={{0,4},{4,8},{8,12},{12,0},{1,5},{5,9},{9,13},{13,1},{2,6},{6,10},{... | collective-permute-start | bytes 1572872 | tf_op jit(solution)/shard_map/ppermute | solution.py:477
  11.7 36.5 %collective-permute-start.1 = (bf16[2,1024,128]{2,1,0:T(8,128)(2,1)}, bf16[2,1024,128]{2,1,0:T(8,128)(2,1)S(1)}, u32[]{:S(2)}, u32[]{:S(2)}) collective-permute-start(bf16[2,1024,128]{2,1,0:T(8,128)(2,1)} %get-tuple-element.86), channel_id=1, source_target_pairs={{0,8},{4,12},{8,0},{12,4},{1,9},{5,13},{9,1},{13,5},{2,10},{6,14},... | collective-permute-start | bytes 1572872 | tf_op jit(solution)/shard_map/ppermute | solution.py:477
  14.3 33.9 %collective-permute-start.2 = (bf16[2,1024,128]{2,1,0:T(8,128)(2,1)}, bf16[2,1024,128]{2,1,0:T(8,128)(2,1)}, u32[]{:S(2)}, u32[]{:S(2)}) collective-permute-start(bf16[2,1024,128]{2,1,0:T(8,128)(2,1)} %get-tuple-element.87), channel_id=1, source_target_pairs={{0,12},{4,0},{8,4},{12,8},{1,13},{5,1},{9,5},{13,9},{2,14},{6,2},{... | collective-permute-start | bytes 1572872 | tf_op jit(solution)/shard_map/ppermute | solution.py:477
  18.7 43.1 %copy-start = (bf16[1024,1024]{1,0:T(8,128)(2,1)S(1)}, bf16[1024,1024]{1,0:T(8,128)(2,1)}, u32[]{:S(2)}) copy-start(bf16[1024,1024]{1,0:T(8,128)(2,1)} %tokens.5) | copy-start | bytes 6291460
  18.7 45.5 %copy-start.4 = (f32[17,1024]{1,0:T(8,128)S(1)}, f32[17,1024]{1,0:T(8,128)}, u32[]{:S(2)}) copy-start(f32[17,1024]{1,0:T(8,128)} %mix_ref.1) | copy-start | bytes 208900
  18.7 45.5 %copy-start.5 = (f32[2,1024]{1,0:T(2,128)S(1)}, f32[2,1024]{1,0:T(2,128)}, u32[]{:S(2)}) copy-start(f32[2,1024]{1,0:T(2,128)} %high_ref.1) | copy-start | bytes 24580
  18.7 45.5 %copy-start.6 = (s32[5]{0:T(128)S(1)}, s32[5]{0:T(128)}, u32[]{:S(2)}) copy-start(s32[5]{0:T(128)} %stack.40.place.refs_0_) | copy-start | bytes 64
  18.7 45.5 %copy-start.7 = (f32[1024]{0:T(1024)S(1)}, f32[1024]{0:T(1024)}, u32[]{:S(2)}) copy-start(f32[1024]{0:T(1024)} %param.8) | copy-start | bytes 12292
  56.1 21.6 %collective-permute-start.6 = (bf16[2,512,1024]{2,1,0:T(8,128)(2,1)}, bf16[2,512,1024]{2,1,0:T(8,128)(2,1)}, u32[]{:S(2)}, u32[]{:S(2)}) collective-permute-start(bf16[2,512,1024]{2,1,0:T(8,128)(2,1)} %collective-permute-done.3.refs_3_), channel_id=1, source_target_pairs={{0,1},{1,0},{2,3},{3,2},{4,5},{5,4},{6,7},{7,6},{8,9},{9,8},{10,11... | collective-permute-start | bytes 6291464 | tf_op jit(solution)/shard_map/ppermute | solution.py:468
  56.1 52.0 %collective-permute-start.11 = (bf16[2,512,1024]{2,1,0:T(8,128)(2,1)}, bf16[2,512,1024]{2,1,0:T(8,128)(2,1)}, u32[]{:S(2)}, u32[]{:S(2)}) collective-permute-start(bf16[2,512,1024]{2,1,0:T(8,128)(2,1)} %collective-permute-done.3.refs_3_), channel_id=1, source_target_pairs={{0,16},{16,0},{1,17},{17,1},{2,18},{18,2},{3,19},{19,3},{4,20},{20... | collective-permute-start | bytes 6291464 | tf_op jit(solution)/shard_map/ppermute | solution.py:468
  57.8 50.7 %collective-permute-start.14 = (bf16[1024,1024]{1,0:T(8,128)(2,1)}, bf16[1024,1024]{1,0:T(8,128)(2,1)}, u32[]{:S(2)}, u32[]{:S(2)}) collective-permute-start(bf16[1024,1024]{1,0:T(8,128)(2,1)} %constant_dynamic-slice_fusion), channel_id=1, source_target_pairs={{0,2},{2,0},{1,3},{3,1},{4,6},{6,4},{5,7},{7,5},{8,10},{10,8},{9,1... | collective-permute-start | bytes 6291464 | tf_op jit(solution)/shard_map/ppermute | solution.py:468
  61.2 3.0 %collective-permute-start.5 = (bf16[3,1024,128]{2,1,0:T(8,128)(2,1)}, bf16[3,1024,128]{2,1,0:T(8,128)(2,1)}, u32[]{:S(2)}, u32[]{:S(2)}) collective-permute-start(bf16[3,1024,128]{2,1,0:T(8,128)(2,1)} %twins.3), channel_id=1, source_target_pairs={{0,1},{1,0},{2,3},{3,2},{4,5},{5,4},{6,7},{7,6},{8,9},{9,8},{10,11... | collective-permute-start | bytes 2359304 | tf_op jit(solution)/shard_map/ppermute | solution.py:468
  61.3 2.9 %collective-permute-start.4 = (bf16[1024,128]{1,0:T(8,128)(2,1)}, bf16[1024,128]{1,0:T(8,128)(2,1)S(1)}, u32[]{:S(2)}, u32[]{:S(2)}) collective-permute-start(bf16[1024,128]{1,0:T(8,128)(2,1)} %get-tuple-element.94), channel_id=1, source_target_pairs={{0,1},{1,0},{2,3},{3,2},{4,5},{5,4},{6,7},{7,6},{8,9},{9,8},{10,11... | collective-permute-start | bytes 786440 | tf_op jit(solution)/shard_map/ppermute | solution.py:468
  64.3 49.6 %copy-start.2 = (bf16[2048,1024]{1,0:T(8,128)(2,1)S(1)}, bf16[2048,1024]{1,0:T(8,128)(2,1)}, u32[]{:S(2)}) copy-start(bf16[2048,1024]{1,0:T(8,128)(2,1)} %refs_1_.1) | copy-start | bytes 12582916
  77.7 10.5 %collective-permute-start.12 = (bf16[2,512,128]{2,1,0:T(8,128)(2,1)S(1)}, bf16[2,512,128]{2,1,0:T(8,128)(2,1)S(1)}, u32[]{:S(2)}, u32[]{:S(2)}) collective-permute-start(bf16[2,512,128]{2,1,0:T(8,128)(2,1)S(1)} %get-tuple-element.109), channel_id=1, source_target_pairs={{0,12},{4,0},{8,4},{12,8},{1,13},{5,1},{9,5},{13,9},{2,14},{6,2},{... | collective-permute-start | bytes 786440 | tf_op jit(solution)/shard_map/ppermute | solution.py:477
  81.5 26.5 %collective-permute-start.9 = (bf16[2,512,128]{2,1,0:T(8,128)(2,1)S(1)}, bf16[2,512,128]{2,1,0:T(8,128)(2,1)S(1)}, u32[]{:S(2)}, u32[]{:S(2)}) collective-permute-start(bf16[2,512,128]{2,1,0:T(8,128)(2,1)S(1)} %get-tuple-element.105), channel_id=1, source_target_pairs={{0,8},{4,12},{8,0},{12,4},{1,9},{5,13},{9,1},{13,5},{2,10},{6,14},... | collective-permute-start | bytes 786440 | tf_op jit(solution)/shard_map/ppermute | solution.py:477
  81.9 26.0 %collective-permute-start.7 = (bf16[2,512,128]{2,1,0:T(8,128)(2,1)S(1)}, bf16[2,512,128]{2,1,0:T(8,128)(2,1)S(1)}, u32[]{:S(2)}, u32[]{:S(2)}) collective-permute-start(bf16[2,512,128]{2,1,0:T(8,128)(2,1)S(1)} %get-tuple-element.102), channel_id=1, source_target_pairs={{0,4},{4,8},{8,12},{12,0},{1,5},{5,9},{9,13},{13,1},{2,6},{6,10},{... | collective-permute-start | bytes 786440 | tf_op jit(solution)/shard_map/ppermute | solution.py:477
  107.9 6.0 %collective-permute-start.10 = (bf16[2,256,128]{2,1,0:T(8,128)(2,1)S(1)}, bf16[2,256,128]{2,1,0:T(8,128)(2,1)S(1)}, u32[]{:S(2)}, u32[]{:S(2)}) collective-permute-start(bf16[2,256,128]{2,1,0:T(8,128)(2,1)S(1)} %get-tuple-element.106), channel_id=1, source_target_pairs={{0,8},{4,12},{8,0},{12,4},{1,9},{5,13},{9,1},{13,5},{2,10},{6,14},... | collective-permute-start | bytes 393224 | tf_op jit(solution)/shard_map/ppermute | solution.py:477
  108.1 12.7 %collective-permute-start.16 = (bf16[4,256,128]{2,1,0:T(8,128)(2,1)S(1)}, bf16[4,256,128]{2,1,0:T(8,128)(2,1)S(1)}, u32[]{:S(2)}, u32[]{:S(2)}) collective-permute-start(bf16[4,256,128]{2,1,0:T(8,128)(2,1)S(1)} %pad_maximum_fusion.2), channel_id=1, source_target_pairs={{0,3},{1,2},{2,1},{3,0},{4,7},{5,6},{6,5},{7,4},{8,11},{9,10},{10,... | collective-permute-start | bytes 786440 | tf_op jit(solution)/shard_map/ppermute | solution.py:472
  108.6 13.8 %collective-permute-start.15 = (bf16[4,256,128]{2,1,0:T(8,128)(2,1)S(1)}, bf16[4,256,128]{2,1,0:T(8,128)(2,1)S(1)}, u32[]{:S(2)}, u32[]{:S(2)}) collective-permute-start(bf16[4,256,128]{2,1,0:T(8,128)(2,1)S(1)} %pad_maximum_fusion.1), channel_id=1, source_target_pairs={{0,2},{2,0},{1,3},{3,1},{4,6},{6,4},{5,7},{7,5},{8,10},{10,8},{9,1... | collective-permute-start | bytes 786440 | tf_op jit(solution)/shard_map/ppermute | solution.py:468
  109.7 10.9 %collective-permute-start.13 = (bf16[2,256,128]{2,1,0:T(8,128)(2,1)S(1)}, bf16[2,256,128]{2,1,0:T(8,128)(2,1)S(1)}, u32[]{:S(2)}, u32[]{:S(2)}) collective-permute-start(bf16[2,256,128]{2,1,0:T(8,128)(2,1)S(1)} %get-tuple-element.110), channel_id=1, source_target_pairs={{0,12},{4,0},{8,4},{12,8},{1,13},{5,1},{9,5},{13,9},{2,14},{6,2},{... | collective-permute-start | bytes 393224 | tf_op jit(solution)/shard_map/ppermute | solution.py:477
  111.0 9.6 %collective-permute-start.8 = (bf16[2,256,128]{2,1,0:T(8,128)(2,1)S(1)}, bf16[2,256,128]{2,1,0:T(8,128)(2,1)S(1)}, u32[]{:S(2)}, u32[]{:S(2)}) collective-permute-start(bf16[2,256,128]{2,1,0:T(8,128)(2,1)S(1)} %get-tuple-element.103), channel_id=1, source_target_pairs={{0,4},{4,8},{8,12},{12,0},{1,5},{5,9},{9,13},{13,1},{2,6},{6,10},{... | collective-permute-start | bytes 393224 | tf_op jit(solution)/shard_map/ppermute | solution.py:477
  113.9 8.5 %collective-permute-start.17 = (bf16[2,512,1024]{2,1,0:T(8,128)(2,1)}, bf16[2,512,1024]{2,1,0:T(8,128)(2,1)S(1)}, u32[]{:S(2)}, u32[]{:S(2)}) collective-permute-start(bf16[2,512,1024]{2,1,0:T(8,128)(2,1)} %collective-permute-done.11.refs_4_), channel_id=1, source_target_pairs={{0,1},{1,0},{2,3},{3,2},{4,5},{5,4},{6,7},{7,6},{8,9},{9,8},{10,11... | collective-permute-start | bytes 6291464 | tf_op jit(solution)/shard_map/ppermute | solution.py:468
  113.9 2.2 %copy-start.3 = (bf16[2048,1024]{1,0:T(8,128)(2,1)S(1)}, bf16[2048,1024]{1,0:T(8,128)(2,1)}, u32[]{:S(2)}) copy-start(bf16[2048,1024]{1,0:T(8,128)(2,1)} %refs_2_.2) | copy-start | bytes 12582916
  122.3 7.5 %collective-permute-start.24 = (bf16[1024,1024]{1,0:T(8,128)(2,1)}, bf16[1024,1024]{1,0:T(8,128)(2,1)S(1)}, u32[]{:S(2)}, u32[]{:S(2)}) collective-permute-start(bf16[1024,1024]{1,0:T(8,128)(2,1)} %collective-permute-done.14.mine), channel_id=1, source_target_pairs={{0,1},{1,0},{2,3},{3,2},{4,5},{5,4},{6,7},{7,6},{8,9},{9,8},{10,11... | collective-permute-start | bytes 6291464 | tf_op jit(solution)/shard_map/ppermute | solution.py:468
  122.8 4.1 %collective-permute-start.23 = (bf16[4,256,128]{2,1,0:T(8,128)(2,1)S(1)}, bf16[4,256,128]{2,1,0:T(8,128)(2,1)S(1)}, u32[]{:S(2)}, u32[]{:S(2)}) collective-permute-start(bf16[4,256,128]{2,1,0:T(8,128)(2,1)S(1)} %twins.4), channel_id=1, source_target_pairs={{0,1},{1,0},{2,3},{3,2},{4,5},{5,4},{6,7},{7,6},{8,9},{9,8},{10,11... | collective-permute-start | bytes 786440 | tf_op jit(solution)/shard_map/ppermute | solution.py:468
  123.4 16.9 %collective-permute-start.22 = (bf16[4,256,128]{2,1,0:T(8,128)(2,1)S(1)}, bf16[4,256,128]{2,1,0:T(8,128)(2,1)S(1)}, u32[]{:S(2)}, u32[]{:S(2)}) collective-permute-start(bf16[4,256,128]{2,1,0:T(8,128)(2,1)S(1)} %pad_maximum_fusion.4), channel_id=1, source_target_pairs={{0,3},{1,2},{2,1},{3,0},{4,7},{5,6},{6,5},{7,4},{8,11},{9,10},{10,... | collective-permute-start | bytes 786440 | tf_op jit(solution)/shard_map/ppermute | solution.py:472
  123.8 16.5 %collective-permute-start.21 = (bf16[4,256,128]{2,1,0:T(8,128)(2,1)S(1)}, bf16[4,256,128]{2,1,0:T(8,128)(2,1)S(1)}, u32[]{:S(2)}, u32[]{:S(2)}) collective-permute-start(bf16[4,256,128]{2,1,0:T(8,128)(2,1)S(1)} %pad_maximum_fusion.3), channel_id=1, source_target_pairs={{0,2},{2,0},{1,3},{3,1},{4,6},{6,4},{5,7},{7,5},{8,10},{10,8},{9,1... | collective-permute-start | bytes 786440 | tf_op jit(solution)/shard_map/ppermute | solution.py:468
  125.1 14.3 %collective-permute-start.20 = (bf16[2,256,128]{2,1,0:T(8,128)(2,1)S(1)}, bf16[2,256,128]{2,1,0:T(8,128)(2,1)S(1)}, u32[]{:S(2)}, u32[]{:S(2)}) collective-permute-start(bf16[2,256,128]{2,1,0:T(8,128)(2,1)S(1)} %get-tuple-element.131), channel_id=1, source_target_pairs={{0,12},{4,0},{8,4},{12,8},{1,13},{5,1},{9,5},{13,9},{2,14},{6,2},{... | collective-permute-start | bytes 393224 | tf_op jit(solution)/shard_map/ppermute | solution.py:477
  126.9 13.4 %collective-permute-start.19 = (bf16[2,256,128]{2,1,0:T(8,128)(2,1)S(1)}, bf16[2,256,128]{2,1,0:T(8,128)(2,1)S(1)}, u32[]{:S(2)}, u32[]{:S(2)}) collective-permute-start(bf16[2,256,128]{2,1,0:T(8,128)(2,1)S(1)} %get-tuple-element.128), channel_id=1, source_target_pairs={{0,8},{4,12},{8,0},{12,4},{1,9},{5,13},{9,1},{13,5},{2,10},{6,14},... | collective-permute-start | bytes 393224 | tf_op jit(solution)/shard_map/ppermute | solution.py:477
  129.8 10.5 %collective-permute-start.18 = (bf16[2,256,128]{2,1,0:T(8,128)(2,1)S(1)}, bf16[2,256,128]{2,1,0:T(8,128)(2,1)S(1)}, u32[]{:S(2)}, u32[]{:S(2)}) collective-permute-start(bf16[2,256,128]{2,1,0:T(8,128)(2,1)S(1)} %get-tuple-element.125), channel_id=1, source_target_pairs={{0,4},{4,8},{8,12},{12,0},{1,5},{5,9},{9,13},{13,1},{2,6},{6,10},{... | collective-permute-start | bytes 393224 | tf_op jit(solution)/shard_map/ppermute | solution.py:477
  140.7 1.6 collective-permute-start.25
  140.8 14.7 %collective-permute-start.27 = (bf16[256,1024]{1,0:T(8,128)(2,1)S(1)}, bf16[256,1024]{1,0:T(8,128)(2,1)S(1)}, u32[]{:S(2)}, u32[]{:S(2)}) collective-permute-start(bf16[256,1024]{1,0:T(8,128)(2,1)S(1)} %send.2), channel_id=1, source_target_pairs={{0,2},{2,0},{1,3},{3,1},{4,6},{6,4},{5,7},{7,5},{8,10},{10,8},{9,1... | collective-permute-start | bytes 1572872 | tf_op jit(solution)/shard_map/ppermute | solution.py:468
  148.4 7.0 %copy-start.1 = (bf16[2048,1024]{1,0:T(8,128)(2,1)S(1)}, bf16[2048,1024]{1,0:T(8,128)(2,1)}, u32[]{:S(2)}) copy-start(bf16[2048,1024]{1,0:T(8,128)(2,1)} %refs_2_.3) | copy-start | bytes 12582916
  151.9 14.5 %collective-permute-start.26 = (bf16[256,1024]{1,0:T(8,128)(2,1)S(1)}, bf16[256,1024]{1,0:T(8,128)(2,1)}, u32[]{:S(2)}, u32[]{:S(2)}) collective-permute-start(bf16[256,1024]{1,0:T(8,128)(2,1)S(1)} %send.3), channel_id=1, source_target_pairs={{0,2},{2,0},{1,3},{3,1},{4,6},{6,4},{5,7},{7,5},{8,10},{10,8},{9,1... | collective-permute-start | bytes 1572872 | tf_op jit(solution)/shard_map/ppermute | solution.py:468
  155.4 4.3 %copy-start.8 = (bf16[256,1024]{1,0:T(8,128)(2,1)}, bf16[256,1024]{1,0:T(8,128)(2,1)S(1)}, u32[]{:S(2)}) copy-start(bf16[256,1024]{1,0:T(8,128)(2,1)S(1)} %collective-permute-done.27.got) | copy-start | bytes 1572868

commit v5 on v4

--- a/solution.py
+++ b/solution.py
@@ -16,6 +16,9 @@
 LINE = ("seq", "sub")
 GRANT = 16 * 2**20
 LITTLE = 12 * 2**20
+LARGE = 54 * 2**20
+PARTS = 4
+HOP = 5*10**9
 
 
 def run_levels(stream, shifter, low0, low1, high0, high1, mix):
@@ -116,39 +119,36 @@
     return lax.rem(place[0] - back + chips, chips) * 2 + core
 
 
-def cut_kernel(chips, place, tokens, *outs):
-    for ahead in range(chips):
-        for other in range(2):
-            if ahead or other:
-                start = pl.multiple_of(line_of(place, -ahead, other) * LANES, LANES)
-                block = tokens[:, pl.ds(start, LANES)]
-                if ahead:
-                    outs[ahead][other] = block
-                else:
-                    outs[0][...] = block
-
-
-def run_cut(place, tokens, chips):
-    rows = tokens.shape[0]
-    shapes = [(rows, LANES)] + [(2, rows, LANES)] * (chips - 1)
-    return pl.pallas_call(
-        functools.partial(cut_kernel, chips),
-        in_specs=[
-            pl.BlockSpec(memory_space=pltpu.SMEM),
-            pl.BlockSpec(memory_space=pltpu.VMEM),
-        ],
-        out_specs=[pl.BlockSpec(memory_space=pltpu.VMEM)] * chips,
-        out_shape=[jax.ShapeDtypeStruct(shape, tokens.dtype) for shape in shapes],
-        name="cut",
-    )(place, tokens)
+def pair_kernel(value, gate, pair, sems):
+    core, group = lax.axis_index("sub"), lax.axis_index("groups")
+    depth = pair.shape[1]
+    part = depth // PARTS
+    pairs = []
+    for at, weight in enumerate((value, gate)):
+        for p in range(PARTS):
+            here = pl.ds(pl.multiple_of((2 * group + core) * depth + p * part, part), part)
+            pairs.append((weight.at[here], pair.at[at, pl.ds(p * part, part)]))
+    copy_all(pairs, sems)
+
+
+def run_pair(value, gate):
+    width, channels = value.shape
+    return pl.pallas_call(
+        pair_kernel,
+        in_specs=[pl.BlockSpec(memory_space=pltpu.HBM)] * 2,
+        out_specs=pl.BlockSpec(memory_space=pltpu.VMEM),
+        out_shape=jax.ShapeDtypeStruct((2, width // 4, channels), value.dtype),
+        scratch_shapes=[pltpu.SemaphoreType.DMA((2 * PARTS,))],
+        compiler_params=pltpu.CompilerParams(vmem_limit_bytes=LARGE),
+        name="pair",
+    )(value, gate)
 
 
 def levels_kernel(live, chips, place, angle_ref, high_ref, mix_ref, own, *refs):
     direct = refs[: chips - 1]
     handed = refs[chips - 1 : chips + 1]
-    far = refs[chips + 1 : 2 * chips + 1]
-    near = refs[2 * chips + 1 : (2 + SPLIT) * chips + 1]
-    tokens, stream_ref, mixed_ref, act_ref, coef_ref = refs[(2 + SPLIT) * chips + 1 :]
+    outs = refs[chips + 1 : chips + 5]
+    tokens, stream_ref, mixed_ref, act_ref, coef_ref = refs[chips + 5 :]
     side = place[2]
     rows = own.shape[0]
     units = rows * 2 * chips // 8
@@ -157,8 +157,10 @@
         return pl.ds(pl.multiple_of(line * rows, rows), rows)
 
     columns = pl.ds(pl.multiple_of(line_of(place, 0, 0) * LANES, LANES), LANES)
+    lanes = pl.ds(pl.multiple_of(place[1] * LANES, LANES), LANES)
     for back in range(chips):
-        tokens[block(line_of(place, back, 0)), :] = direct[back - 1][0] if back else own[...]
+        mine = direct[back - 1][:, lanes] if back else own[...]
+        tokens[block(line_of(place, back, 0)), :] = mine
         tokens[block(line_of(place, back, 1)), :] = handed[1][back - 1] if back else handed[0][...]
     coefficients(live, columns, angle_ref, high_ref, mix_ref, coef_ref)
 
@@ -229,16 +231,13 @@
         return 0
 
     half = rows // 2
-    part = half // SPLIT
     lax.fori_loop(0, WIDE // 2, third, 0)
     for ahead in range(chips):
         for other in range(2):
             start = line_of(place, -ahead, other) * rows
-            begin = pl.multiple_of(start + (1 - side) * half, half)
-            far[ahead][other] = act_ref[pl.ds(begin, half), :]
-            for q in range(SPLIT):
-                begin = pl.multiple_of(start + side * half + q * part, part)
-                near[q * chips + ahead][other] = act_ref[pl.ds(begin, part), :]
+            for at, which in enumerate((1 - side, side)):
+                begin = pl.multiple_of(start + which * half, half)
+                outs[2 * other + at][ahead] = act_ref[pl.ds(begin, half), :]
 
 
 def run_filter(place, angle, high, mix, own, direct, handed, live):
@@ -246,15 +245,14 @@
     rows = handed[0].shape[0]
     total = rows * 2 * chips
     anywhere = pl.BlockSpec(memory_space=pltpu.HBM)
-    outs = pl.pallas_call(
+    return pl.pallas_call(
         functools.partial(levels_kernel, live, chips),
-        out_shape=[jax.ShapeDtypeStruct((2, rows // 2, LANES), jnp.bfloat16)] * chips
-        + [jax.ShapeDtypeStruct((2, rows // 2 // SPLIT, LANES), jnp.bfloat16)] * (SPLIT * chips),
+        out_shape=[jax.ShapeDtypeStruct((chips, rows // 2, LANES), jnp.bfloat16)] * 4,
         in_specs=[
             pl.BlockSpec(memory_space=pltpu.SMEM),
         ]
         + [pl.BlockSpec(memory_space=pltpu.VMEM)] * (chips + 5),
-        out_specs=[pl.BlockSpec(memory_space=pltpu.VMEM)] * ((1 + SPLIT) * chips),
+        out_specs=[pl.BlockSpec(memory_space=pltpu.VMEM)] * 4,
         scratch_shapes=[
             pltpu.VMEM((total, LANES), jnp.bfloat16),
             pltpu.VMEM((total // 8, 8, LANES), jnp.float32),
@@ -265,6 +263,32 @@
         compiler_params=pltpu.CompilerParams(vmem_limit_bytes=GRANT),
         name="levels",
     )(place, angle[None], high, mix, own, *direct, *handed)
+
+
+def join_kernel(*refs):
+    sources, outs = refs[:4], refs[4:]
+    chips, half, _ = sources[0].shape
+    part = half // SPLIT
+    for group in range(1 + SPLIT):
+        rows = slice(None) if group == 0 else pl.ds((group - 1) * part, part)
+        for ahead in range(chips):
+            for other in range(2):
+                source = sources[2 * other + (group > 0)]
+                outs[group * chips + ahead][other] = source[ahead, rows]
+
+
+def run_join(arrays):
+    chips, half, _ = arrays[0].shape
+    in_vmem = pl.BlockSpec(memory_space=pltpu.VMEM)
+    sizes = [half] * chips + [half // SPLIT] * (SPLIT * chips)
+    outs = pl.pallas_call(
+        join_kernel,
+        in_specs=[in_vmem] * 4,
+        out_specs=[in_vmem] * len(sizes),
+        out_shape=[jax.ShapeDtypeStruct((2, size, LANES), jnp.bfloat16) for size in sizes],
+        compiler_params=pltpu.CompilerParams(vmem_limit_bytes=LITTLE),
+        name="join",
+    )(*arrays)
     groups = [list(outs[at * chips : (at + 1) * chips]) for at in range(1 + SPLIT)]
     return groups[0], groups[1:]
 
@@ -306,18 +330,17 @@
 
 def hidden_kernel(chips, block, place, *refs):
     direct = refs[:chips]
-    handed, straight, crossed = refs[chips : chips + 3]
-    own, fetched = refs[chips + 3 : chips + 5], refs[chips + 5 : chips + 9]
-    hidden_ref, act, sems = refs[chips + 9 :]
+    got, own, fetched = refs[chips], refs[chips + 1 : chips + 3], refs[chips + 3 : chips + 7]
+    hidden_ref, act, sems = refs[chips + 7 :]
     side = place[2]
     channels = 2 * chips * LANES
     pairs = []
     for back in range(chips):
-        for other, near, far in ((0, direct[back], straight), (1, handed, crossed)):
+        for other in range(2):
             line = line_of(place, back, other) * LANES
             for start, source in (
-                (side * channels + line, near.at[back if other else 0]),
-                ((1 - side) * channels + line, far.at[back]),
+                (side * channels + line, direct[back].at[other]),
+                ((1 - side) * channels + line, got.at[back, other]),
             ):
                 lanes = pl.ds(pl.multiple_of(start, LANES), LANES)
                 pairs.append((source, act.at[:, lanes]))
@@ -348,15 +371,15 @@
             hidden_ref[:, target] = gated.astype(jnp.bfloat16)
 
 
-def run_hidden(place, direct, handed, straight, crossed, *weights):
+def run_hidden(place, direct, got, *weights):
     chips = len(direct)
-    rows = handed.shape[1]
+    rows = got.shape[2]
     width, channels = weights[0].shape
     in_vmem = pl.BlockSpec(memory_space=pltpu.VMEM)
     return pl.pallas_call(
         functools.partial(hidden_kernel, chips, min(512, channels)),
         in_specs=[pl.BlockSpec(memory_space=pltpu.SMEM)]
-        + [pl.BlockSpec(memory_space=pltpu.HBM)] * (chips + 3)
+        + [pl.BlockSpec(memory_space=pltpu.HBM)] * (chips + 1)
         + [in_vmem] * len(weights),
         out_specs=in_vmem,
         scratch_shapes=[
@@ -367,7 +390,7 @@
         compiler_params=pltpu.CompilerParams(vmem_limit_bytes=LITTLE),
         cost_estimate=work(rows, width, 2 * width),
         name="hidden",
-    )(place, *direct, handed, straight, crossed, *weights)
+    )(place, *direct, got, *weights)
 
 
 def send_kernel(place, hidden, mine, twin, out_ref):
@@ -460,16 +483,13 @@
         ),
         out_shape=jax.ShapeDtypeStruct(tokens.shape, jnp.bfloat16),
         input_output_aliases={3: 0},
+        compiler_params=pltpu.CompilerParams(vmem_limit_bytes=LARGE),
         name="add_far",
     )(side, got, tokens, result)
 
 
 def swap(array, axis):
     return lax.ppermute(array, axis, [(0, 1), (1, 0)])
-
-
-def cross(array):
-    return lax.ppermute(array, ("chan", "sub"), [(0, 3), (1, 2), (2, 1), (3, 0)])
 
 
 def ahead(array, offset):
@@ -477,21 +497,40 @@
     return lax.ppermute(array, "seq", [(j, (j + offset) % chips) for j in range(chips)])
 
 
-def twins_kernel(chips, *refs):
-    copy_all([(refs[at].at[1], refs[chips].at[at]) for at in range(chips)], refs[-1])
-
-
-def run_twins(blocks):
-    rows = blocks[0].shape[1]
-    return pl.pallas_call(
-        functools.partial(twins_kernel, len(blocks)),
-        in_specs=[pl.BlockSpec(memory_space=pltpu.HBM)] * len(blocks),
+def anchor_kernel(*refs):
+    refs[-1][...] = jnp.zeros(refs[-1].shape, refs[-1].dtype)
+
+
+def anchor(after):
+    return pl.pallas_call(
+        anchor_kernel,
+        in_specs=[pl.BlockSpec(memory_space=pltpu.HBM)] * len(after),
         out_specs=pl.BlockSpec(memory_space=pltpu.VMEM),
+        out_shape=jax.ShapeDtypeStruct((8, LANES), jnp.float32),
+        compiler_params=pltpu.CompilerParams(vmem_limit_bytes=LITTLE),
+        cost_estimate=pl.CostEstimate(flops=10**11, bytes_accessed=0, transcendentals=0),
+        name="anchor",
+    )(*after)
+
+
+def others_kernel(place, *refs):
+    lanes = pl.ds(pl.multiple_of((1 - place[1]) * LANES, LANES), LANES)
+    for at, block in enumerate(refs[:-1]):
+        refs[-1][at] = block[:, lanes]
+
+
+def run_others(place, blocks):
+    in_vmem = pl.BlockSpec(memory_space=pltpu.VMEM)
+    rows = blocks[0].shape[0]
+    return pl.pallas_call(
+        others_kernel,
+        in_specs=[pl.BlockSpec(memory_space=pltpu.SMEM)] + [in_vmem] * len(blocks),
+        out_specs=in_vmem,
         out_shape=jax.ShapeDtypeStruct((len(blocks), rows, LANES), blocks[0].dtype),
-        scratch_shapes=[pltpu.SemaphoreType.DMA((len(blocks),))],
         compiler_params=pltpu.CompilerParams(vmem_limit_bytes=LITTLE),
-        name="twins",
-    )(*blocks)
+        cost_estimate=pl.CostEstimate(flops=HOP, bytes_accessed=0, transcendentals=0),
+        name="others",
+    )(place, *blocks)
 
 
 def by_tokens(tokens, low_angle, high_taps, level_mix, w_value, w_gate, out_weight):
@@ -504,32 +543,33 @@
     order = sorted(range(1, chips), key=lambda s: abs(2 * s - chips))
     place = jnp.stack([chip, core, side, group, chips]).astype(jnp.int32)
 
-    mine = lax.dynamic_slice_in_dim(tokens, (chip * 2 + core) * narrow, narrow, 1)
-    blocks = run_cut(place, tokens, chips)
-    blocks, weights = lax.optimization_barrier((blocks, (w_value, w_gate, out_weight)))
+    pair = run_pair(w_value, w_gate)
+    tokens, pair = lax.optimization_barrier((tokens, pair))
+    def columns(back, first, count):
+        start = ((chip - back) % chips * 2 + first) * narrow
+        return lax.dynamic_slice_in_dim(tokens, start, count * narrow, 1)
+
+    blocks = [columns(-s, 0, 2) for s in range(1, chips)]
+    mine, other = columns(0, core, 1), columns(0, 1 - core, 1)
+    blocks, out_piece = lax.optimization_barrier((blocks, out_weight))
     direct = [None] * chips
     for s in order:
-        direct[s] = ahead(blocks[s], s)
-    handed = [swap(blocks[0], "sub"), swap(run_twins(direct[1:]), "sub")]
+        direct[s] = ahead(blocks[s - 1], s)
+    handed = [swap(other, "sub"), swap(run_others(place, direct[1:]), "sub")]
 
     depth = w_value.shape[0] // 4
-    pair = jnp.stack(
-        [
-            lax.dynamic_slice_in_dim(weight, (2 * group + core) * depth, depth, 0)
-            for weight in weights[:2]
-        ]
-    )
-    half = lax.dynamic_slice_in_dim(weights[2], core * 2 * depth, 2 * depth, 0)
+    half = lax.dynamic_slice_in_dim(out_piece, core * 2 * depth, 2 * depth, 0)
     pair_first = swap(pair, "chan")
     direct, pair_first, half = lax.optimization_barrier((direct, pair_first, half))
     pair_second = swap(pair_first, "groups")
     half_first = swap(half, "chan")
     pair_third = swap(pair_first, "sub")
 
-    far, near = run_filter(
+    *kept, given_far, given_near = run_filter(
         place, low_angle, high_taps, level_mix, mine, direct[1:], handed, live
     )
 
+    far, near = run_join([*kept, swap(given_far, "sub"), swap(given_near, "sub")])
     far, pair_third = lax.optimization_barrier((far, pair_third))
     far_got = [far[0]] + [None] * (chips - 1)
     for s in order:
@@ -541,23 +581,25 @@
             cross(jnp.stack([far_got[back][1] for back in backs])),
         )
 
+    both = anchor([pair_second, half_first])
+    far_got, pair_second, half_first, both = lax.optimization_barrier(
+        (far_got, pair_second, half_first, both)
+    )
+    far_got = list(far_got)
     near_got = [[part[0]] + [None] * (chips - 1) for part in near]
     for s in order:
         near[0][s], far_got[s] = lax.optimization_barrier((near[0][s], far_got[s]))
         near_got[0][s] = ahead(near[0][s], s)
     rows = near[0][0].shape[1]
 
-    def exchange(q, first, second):
+    def exchange(q, before):
         part = slice(q * rows, (q + 1) * rows)
-        straight, first = lax.optimization_barrier(
-            (jnp.stack([block[0, part] for block in far_got]), first)
+        mine, before = lax.optimization_barrier(
+            (jnp.stack([block[:, part] for block in far_got]), before)
         )
-        crossed, second = lax.optimization_barrier(
-            (jnp.stack([block[1, part] for block in far_got]), second)
-        )
-        return swap(straight, "chan"), cross(crossed)
-
-    got = exchange(0, half_first, pair_second)
+        return swap(mine, "chan")
+
+    got = [exchange(q, half_first) for q in range(SPLIT)]
     near_got[0][order[0]], pair_second = lax.optimization_barrier(
         (near_got[0][order[0]], pair_second)
     )
@@ -565,27 +607,26 @@
     loaded, place = run_load(
         place, [w_value, w_gate, pair_first, pair_second, pair_third], far_got[1:]
     )
-    near_got[0], got, place, pair_fourth, half_first = lax.optimization_barrier(
-        (near_got[0], got, place, pair_fourth, half_first)
+    near_got[0], got[0], place, pair_fourth, half_first = lax.optimization_barrier(
+        (near_got[0], got[0], place, pair_fourth, half_first)
     )
     half_second = swap(half_first, "sub")
     loaded.append(pair_fourth)
     which = place[2:3]
     hidden, returned = [], []
     for q in range(SPLIT):
-        handed = swap(run_twins(near_got[q]), "sub")
         if q + 1 < SPLIT:
             for s in order:
                 near[q + 1][s], near_got[q][s] = lax.optimization_barrier(
                     (near[q + 1][s], near_got[q][s])
                 )
                 near_got[q + 1][s] = ahead(near[q + 1][s], s)
-            later = exchange(q + 1, *got)
-        made = run_hidden(place, near_got[q], handed, *got, *loaded)
+        made = run_hidden(place, near_got[q], got[q], *loaded)
         sent = run_send(place, made, [half_first, half_second])
         if q + 1 < SPLIT:
-            near_got[q + 1], later, sent = lax.optimization_barrier((near_got[q + 1], later, sent))
-            got = later
+            near_got[q + 1], got[q + 1], sent = lax.optimization_barrier(
+                (near_got[q + 1], got[q + 1], sent)
+            )
         hidden.append(made)
         returned.append(swap(sent, "chan"))
     hidden, returned[0] = lax.optimization_barrier((hidden, returned[0]))

time: 169 us -> 165 us (0.976)
  waiting for transfers between devices: 78.3 us -> 69.3 us
  starting transfers between devices: 28.1 us -> 35.4 us
    ppermute x12, waiting for transfers between devices: 58 us -> 35 us  [ahead(): lax.ppermute(array, 'seq', [(j, (j + offset) % chips) for j in range(chip...]
    ppermute x14, waiting for transfers between devices: 20.3 us -> 34.3 us  [swap(): return lax.ppermute(array, axis, [(0, 1), (1, 0)])]
    ppermute x12, starting transfers between devices: 16.2 us -> 21.9 us  [ahead(): lax.ppermute(array, 'seq', [(j, (j + offset) % chips) for j in range(chip...]
    ppermute x14, starting transfers between devices: 10.9 us -> 13.5 us  [swap(): return lax.ppermute(array, axis, [(0, 1), (1, 0)])]
    dynamic_slice x2 -> x3, local copies, waits for them, and re-layouts: 3.15 us -> 4.49 us  [the longest x1 3.09 us: by_tokens(): half = lax.dynamic_slice_in_dim(out_piece, core * 2 * depth, 2 * depth, 0)]
    pallas_call x4 -> x3, Pallas kernels: 5.97 us -> 5.28 us  [the longest x1 3.04 us: run_pair(): pl.pallas_call(pair_kernel, in_specs=[pl.BlockSpec(memory_space=pltpu.HBM...]
  transfers between devices with their start and end apart: 28 -> 26, of which waited for: 14 -> 14; matrix products, arithmetic and copies ran while one was open for 2% -> 3% of each run, Pallas kernels for 23% -> 24%
where the time goes in v5:
time: 165 us
  waiting for transfers between devices  69.3 us (42%)
  Pallas kernels  51.9 us (31%)
  starting transfers between devices  35.4 us (21%)
  local copies, waits for them, and re-layouts  7.98 us (5%)
    ppermute x12, waiting for transfers between devices, ahead(): lax.ppermute(array, 'seq', [(j, (j + offset) % chips) for j in range(chip...  35 us
    ppermute x14, waiting for transfers between devices, swap(): return lax.ppermute(array, axis, [(0, 1), (1, 0)])  34.3 us
    ppermute x12, starting transfers between devices, ahead(): lax.ppermute(array, 'seq', [(j, (j + offset) % chips) for j in range(chip...  21.9 us
    ppermute x14, starting transfers between devices, swap(): return lax.ppermute(array, axis, [(0, 1), (1, 0)])  13.5 us
    pallas_call x1, Pallas kernels, run_filter(): pl.pallas_call(functools.partial(levels_kernel, live, chips), out_shape=[...  13.2 us
    pallas_call x2, Pallas kernels, run_hidden(): pl.pallas_call(functools.partial(hidden_kernel, chips, min(512, channels)...  12.2 us
    pallas_call x2, Pallas kernels, run_send(): pl.pallas_call(send_kernel, grid_spec=pltpu.PrefetchScalarGridSpec(num_sc...  6.8 us
    pallas_call x2, Pallas kernels, add_far(): pl.pallas_call(add_kernel, grid_spec=pltpu.PrefetchScalarGridSpec(num_sca...  5.33 us
  transfers between devices with their start and end apart: 26, of which 14 were waited for; matrix products, arithmetic and copies ran while one was open for 3% of the time, Pallas kernels for 24%

profile of v5, /device:TPU:0, one launch (start us, length us, event | category | flops | bytes accessed | tf_op | source)
XLA Modules:
  0.0 165.0 jit_solution(17031219650454411651)
XLA Ops:
  0.0 3.0 %pair.1 = bf16[2,512,1024]{2,1,0:T(8,128)(2,1)} custom-call(bf16[2048,1024]{1,0:T(8,128)(2,1)} %refs_1_.1, bf16[2048,1024]{1,0:T(8,128)(2,1)} %refs_2_.2), custom_call_target="tpu_custom_call" | custom-call | tf_op jit(solution)/shard_map/pair/pallas_call | solution.py:136
  3.0 3.0 %collective-permute-start.3 = (bf16[2,512,1024]{2,1,0:T(8,128)(2,1)}, bf16[2,512,1024]{2,1,0:T(8,128)(2,1)}, u32[]{:S(2)}, u32[]{:S(2)}) collective-permute-start(bf16[2,512,1024]{2,1,0:T(8,128)(2,1)} %pair.1), channel_id=1, source_target_pairs={{0,2},{2,0},{1,3},{3,1},{4,6},{6,4},{5,7},{7,5},{8,10},{10,8},{9,1... | collective-permute-start | bytes 6291464 | tf_op jit(solution)/shard_map/ppermute | solution.py:492
  6.1 1.3 constant_dynamic-slice_fusion.2
  7.3 1.6 collective-permute-start
  8.9 2.6 %collective-permute-start.1 = (bf16[1024,256]{1,0:T(8,128)(2,1)}, bf16[1024,256]{1,0:T(8,128)(2,1)S(1)}, u32[]{:S(2)}, u32[]{:S(2)}) collective-permute-start(bf16[1024,256]{1,0:T(8,128)(2,1)} %get-tuple-element.84), channel_id=1, source_target_pairs={{0,8},{4,12},{8,0},{12,4},{1,9},{5,13},{9,1},{13,5},{2,10},{6,14},... | collective-permute-start | bytes 1572872 | tf_op jit(solution)/shard_map/ppermute | solution.py:497
  11.5 1.3 collective-permute-start.2
  12.8 3.1 %constant_dynamic-slice_fusion.1 = bf16[1024,1024]{1,0:T(8,128)(2,1)} fusion(bf16[2048,1024]{1,0:T(8,128)(2,1)} %refs_2_.3, s32[]{:T(128)S(6)} %select_n.47), kind=kLoop, calls=%fused_computation.11 | loop fusion | bytes 4194308 | tf_op jit(solution)/shard_map/dynamic_slice | solution.py:561
  15.9 8.4 %collective-permute-done.refs_0_ = bf16[1024,256]{1,0:T(8,128)(2,1)S(1)} collective-permute-done((bf16[1024,256]{1,0:T(8,128)(2,1)}, bf16[1024,256]{1,0:T(8,128)(2,1)S(1)}, u32[]{:S(2)}, u32[]{:S(2)}) %collective-permute-start) | collective-permute-done | bytes 524320 | tf_op jit(solution)/shard_map/ppermute | solution.py:497
  24.3 21.1 %collective-permute-done.1.refs_1_ = bf16[1024,256]{1,0:T(8,128)(2,1)S(1)} collective-permute-done((bf16[1024,256]{1,0:T(8,128)(2,1)}, bf16[1024,256]{1,0:T(8,128)(2,1)S(1)}, u32[]{:S(2)}, u32[]{:S(2)}) %collective-permute-start.1) | collective-permute-done | bytes 524320 | tf_op jit(solution)/shard_map/ppermute | solution.py:497
  45.4 6.6 %collective-permute-done.3.refs_3_ = bf16[2,512,1024]{2,1,0:T(8,128)(2,1)} collective-permute-done((bf16[2,512,1024]{2,1,0:T(8,128)(2,1)}, bf16[2,512,1024]{2,1,0:T(8,128)(2,1)}, u32[]{:S(2)}, u32[]{:S(2)}) %collective-permute-start.3) | collective-permute-done | bytes 2097184 | tf_op jit(solution)/shard_map/ppermute | solution.py:492
  52.0 1.8 %collective-permute-start.12 = (bf16[2,512,1024]{2,1,0:T(8,128)(2,1)}, bf16[2,512,1024]{2,1,0:T(8,128)(2,1)}, u32[]{:S(2)}, u32[]{:S(2)}) collective-permute-start(bf16[2,512,1024]{2,1,0:T(8,128)(2,1)} %collective-permute-done.3.refs_3_), channel_id=1, source_target_pairs={{0,16},{16,0},{1,17},{17,1},{2,18},{18,2},{3,19},{19,3},{4,20},{20... | collective-permute-start | bytes 6291464 | tf_op jit(solution)/shard_map/ppermute | solution.py:492
  53.8 1.5 collective-permute-start.13
  55.4 2.1 %others.1 = bf16[3,1024,128]{2,1,0:T(8,128)(2,1)} custom-call(s32[5]{0:T(128)S(1)} %stack.49.place.refs_0_, bf16[1024,256]{1,0:T(8,128)(2,1)S(1)} %collective-permute-done.refs_0_, bf16[1024,256]{1,0:T(8,128)(2,1)S(1)} %collective-permute-done.1.refs_1_, bf16[1024,256]{1,0:T(8,128)(2,1)} %collective-permute-done.2.refs_2_), custom_call_target="tpu_custom_call" | custom-call | flops 5000000000 | tf_op jit(solution)/shard_map/others/pallas_call | solution.py:525
  57.5 0.8 copy-done.4
  58.4 0.6 collective-permute-start.4
  59.0 1.9 %collective-permute-done.4.refs_3_ = bf16[1024,128]{1,0:T(8,128)(2,1)S(1)} collective-permute-done((bf16[1024,128]{1,0:T(8,128)(2,1)S(1)}, bf16[1024,128]{1,0:T(8,128)(2,1)S(1)}, u32[]{:S(2)}, u32[]{:S(2)}) %collective-permute-start.4) | collective-permute-done | bytes 262176 | tf_op jit(solution)/shard_map/ppermute | solution.py:492
  60.9 1.0 copy-done.5
  62.0 13.2 %levels.1 = (bf16[4,512,128]{2,1,0:T(8,128)(2,1)S(1)}, bf16[4,512,128]{2,1,0:T(8,128)(2,1)S(1)}, bf16[4,512,128]{2,1,0:T(8,128)(2,1)S(1)}, bf16[4,512,128]{2,1,0:T(8,128)(2,1)S(1)}) custom-call(s32[5]{0:T(128)S(1)} %stack.49.place.refs_0_, f32[1,1024]{1,0:T(1,128)S(1)} %bitcast.21, f32[2,1024]{1,0:T(2,128)S(1)} %copy-done.7, f32[17,1024]{1,0:T(8,128)S(1)} %copy-done.6, ...), custom_call_target="tpu_custom_call" | custom-call | tf_op jit(solution)/shard_map/levels/pallas_call | solution.py:248
  75.8 1.4 collective-permute-done.6.refs_2_
  77.2 0.7 collective-permute-done.7.refs_3_
  78.1 3.1 %collective-permute-start.10 = (bf16[2,512,128]{2,1,0:T(8,128)(2,1)S(1)}, bf16[2,512,128]{2,1,0:T(8,128)(2,1)S(1)}, u32[]{:S(2)}, u32[]{:S(2)}) collective-permute-start(bf16[2,512,128]{2,1,0:T(8,128)(2,1)S(1)} %get-tuple-element.104), channel_id=1, source_target_pairs={{0,8},{4,12},{8,0},{12,4},{1,9},{5,13},{9,1},{13,5},{2,10},{6,14},... | collective-permute-start | bytes 786440 | tf_op jit(solution)/shard_map/ppermute | solution.py:497
  81.1 3.4 %collective-permute-start.11 = (bf16[2,512,128]{2,1,0:T(8,128)(2,1)S(1)}, bf16[2,512,128]{2,1,0:T(8,128)(2,1)S(1)}, u32[]{:S(2)}, u32[]{:S(2)}) collective-permute-start(bf16[2,512,128]{2,1,0:T(8,128)(2,1)S(1)} %get-tuple-element.105), channel_id=1, source_target_pairs={{0,12},{4,0},{8,4},{12,8},{1,13},{5,1},{9,5},{13,9},{2,14},{6,2},{... | collective-permute-start | bytes 786440 | tf_op jit(solution)/shard_map/ppermute | solution.py:497
  84.5 15.9 %collective-permute-done.12.refs_4_ = bf16[2,512,1024]{2,1,0:T(8,128)(2,1)} collective-permute-done((bf16[2,512,1024]{2,1,0:T(8,128)(2,1)}, bf16[2,512,1024]{2,1,0:T(8,128)(2,1)}, u32[]{:S(2)}, u32[]{:S(2)}) %collective-permute-start.12) | collective-permute-done | bytes 2097184 | tf_op jit(solution)/shard_map/ppermute | solution.py:492
  100.4 1.5 collective-permute-done.13.mine
  102.2 5.1 %collective-permute-start.15 = (bf16[2,256,128]{2,1,0:T(8,128)(2,1)S(1)}, bf16[2,256,128]{2,1,0:T(8,128)(2,1)S(1)}, u32[]{:S(2)}, u32[]{:S(2)}) collective-permute-start(bf16[2,256,128]{2,1,0:T(8,128)(2,1)S(1)} %get-tuple-element.111), channel_id=1, source_target_pairs={{0,8},{4,12},{8,0},{12,4},{1,9},{5,13},{9,1},{13,5},{2,10},{6,14},... | collective-permute-start | bytes 393224 | tf_op jit(solution)/shard_map/ppermute | solution.py:497
  107.5 1.6 collective-permute-start.17
  109.1 1.0 collective-permute-start.16
  110.1 1.0 collective-permute-start.14
  111.1 4.0 %collective-permute-done.15.refs_2_ = bf16[2,256,128]{2,1,0:T(8,128)(2,1)S(1)} collective-permute-done((bf16[2,256,128]{2,1,0:T(8,128)(2,1)S(1)}, bf16[2,256,128]{2,1,0:T(8,128)(2,1)S(1)}, u32[]{:S(2)}, u32[]{:S(2)}) %collective-permute-start.15) | collective-permute-done | bytes 131104 | tf_op jit(solution)/shard_map/ppermute | solution.py:497
  115.1 4.6 %load.1 = (bf16[2048,1024]{1,0:T(8,128)(2,1)S(1)}, bf16[2048,1024]{1,0:T(8,128)(2,1)S(1)}, bf16[2,512,1024]{2,1,0:T(8,128)(2,1)S(1)}, bf16[2,512,1024]{2,1,0:T(8...) custom-call(s32[5]{0:T(128)S(1)} %stack.49.place.refs_0_, bf16[2048,1024]{1,0:T(8,128)(2,1)S(1)} %copy-done.2, ...), custom_call_target="tpu_custom_call" | custom-call | flops 99999997952 | tf_op jit(solution)/shard_map/load/pallas_call | solution.py:318
  119.7 1.5 collective-permute-done.17.refs_4_
  121.2 2.5 %collective-permute-start.22 = (bf16[4,2,256,128]{3,2,1,0:T(8,128)(2,1)S(1)}, bf16[4,2,256,128]{3,2,1,0:T(8,128)(2,1)S(1)}, u32[]{:S(2)}, u32[]{:S(2)}) collective-permute-start(bf16[4,2,256,128]{3,2,1,0:T(8,128)(2,1)S(1)} %get-tuple-element.137), channel_id=1, source_target_pairs={{0,2},{2,0},{1,3},{3,1},{4,6},{6,4},{5,7},{7,5},{8,10},{10,8},{9,1... | collective-permute-start | bytes 1572872 | tf_op jit(solution)/shard_map/ppermute | solution.py:492
  123.6 2.3 %collective-permute-start.21 = (bf16[2,256,128]{2,1,0:T(8,128)(2,1)S(1)}, bf16[2,256,128]{2,1,0:T(8,128)(2,1)S(1)}, u32[]{:S(2)}, u32[]{:S(2)}) collective-permute-start(bf16[2,256,128]{2,1,0:T(8,128)(2,1)S(1)} %get-tuple-element.136), channel_id=1, source_target_pairs={{0,12},{4,0},{8,4},{12,8},{1,13},{5,1},{9,5},{13,9},{2,14},{6,2},{... | collective-permute-start | bytes 393224 | tf_op jit(solution)/shard_map/ppermute | solution.py:497
  126.0 0.6 collective-permute-start.19
  126.5 6.1 %hidden.2.refs_0_ = bf16[256,2048]{1,0:T(8,128)(2,1)S(1)} custom-call(s32[5]{0:T(128)S(1)} %get-tuple-element.126.place, bf16[2,256,128]{2,1,0:T(8,128)(2,1)S(1)} %get-tuple-element.138.refs_0_, bf16[2,256,128]{2,1,0:T(8,128)(2,1)S(1)} %collective-permute-done.14.refs_1_, bf16[2,256,128]{2,1,0:T(8,128)(2,1)S(1)} %collective-permute-done.15.refs_2_, ...), custom_call_target="tpu_custom_call" | custom-call | flops 4294967296 | bytes 19922944 | tf_op jit(solution)/shard_map/hidden/pallas_call | solution.py:379
  132.6 3.3 %send.2 = bf16[256,1024]{1,0:T(8,128)(2,1)S(1)} custom-call(s32[5]{0:T(128)S(1)} %get-tuple-element.126.place, bf16[256,2048]{1,0:T(8,128)(2,1)S(1)} %hidden.2.refs_0_, bf16[1024,1024]{1,0:T(8,128)(2,1)} %collective-permute-done.13.mine, bf16[1024,1024]{1,0:T(8,128)(2,1)S(1)} %collective-permute-done.23.twin), custom_call_target="tpu_custom_call" | custom-call | flops 1073741824 | bytes 5767168 | tf_op jit(solution)/shard_map/send/pallas_call | solution.py:411
  135.9 1.2 collective-permute-done.20.refs_2_
  137.2 1.6 collective-permute-start.25
  138.8 6.1 %hidden.3.refs_1_ = bf16[256,2048]{1,0:T(8,128)(2,1)S(1)} custom-call(s32[5]{0:T(128)S(1)} %get-tuple-element.126.place, bf16[2,256,128]{2,1,0:T(8,128)(2,1)S(1)} %get-tuple-element.150.refs_0_, bf16[2,256,128]{2,1,0:T(8,128)(2,1)S(1)} %collective-permute-done.19.refs_1_, bf16[2,256,128]{2,1,0:T(8,128)(2,1)S(1)} %collective-permute-done.20.refs_2_, ...), custom_call_target="tpu_custom_call" | custom-call | flops 4294967296 | bytes 19922944 | tf_op jit(solution)/shard_map/hidden/pallas_call | solution.py:379
  144.9 3.5 %send.3 = bf16[256,1024]{1,0:T(8,128)(2,1)S(1)} custom-call(s32[5]{0:T(128)S(1)} %get-tuple-element.126.place, bf16[256,2048]{1,0:T(8,128)(2,1)S(1)} %hidden.3.refs_1_, bf16[1024,1024]{1,0:T(8,128)(2,1)} %collective-permute-done.13.mine, bf16[1024,1024]{1,0:T(8,128)(2,1)S(1)} %collective-permute-done.23.twin), custom_call_target="tpu_custom_call" | custom-call | flops 1073741824 | bytes 5767168 | tf_op jit(solution)/shard_map/send/pallas_call | solution.py:411
  148.5 0.4 collective-permute-start.24
  148.9 0.7 slice.31.side
  149.6 1.2 collective-permute-done.25.got
  150.8 4.5 %finish.1.kept = bf16[1024,1024]{1,0:T(8,128)(2,1)} custom-call(s32[1]{0:T(128)} %slice.31.side, bf16[256,2048]{1,0:T(8,128)(2,1)S(1)} %hidden.2.refs_0_, bf16[256,2048]{1,0:T(8,128)(2,1)S(1)} %hidden.3.refs_1_, bf16[2048,1024]{1,0:T(8,128)(2,1)S(1)} %copy-done.1, bf16[1024,1024]{1,0:T(8,128)(2,1)S(1)} %copy-done), custom_call_target="tpu_custom_call" | custom-call | flops 2147483648 | bytes 7340032 | tf_op jit(solution)/shard_map/finish/pallas_call | solution.py:440
  155.3 2.7 %add_far.2.kept = bf16[1024,1024]{1,0:T(8,128)(2,1)} custom-call(s32[1]{0:T(128)} %slice.31.side, bf16[256,1024]{1,0:T(8,128)(2,1)} %copy-done.9, bf16[1024,1024]{1,0:T(8,128)(2,1)} %tokens.1, bf16[1024,1024]{1,0:T(8,128)(2,1)} %finish.1.kept), custom_call_target="tpu_custom_call", output_to_operand_aliasing={{}: (3, {})} | custom-call | tf_op jit(solution)/shard_map/add_far/pallas_call | solution.py:472
  157.9 3.6 %collective-permute-done.24.got = bf16[256,1024]{1,0:T(8,128)(2,1)S(1)} collective-permute-done((bf16[256,1024]{1,0:T(8,128)(2,1)S(1)}, bf16[256,1024]{1,0:T(8,128)(2,1)S(1)}, u32[]{:S(2)}, u32[]{:S(2)}) %collective-permute-start.24) | collective-permute-done | bytes 524320 | tf_op jit(solution)/shard_map/ppermute | solution.py:492
  161.5 0.8 copy-done.10
  162.3 2.7 %add_far.3 = bf16[1024,1024]{1,0:T(8,128)(2,1)} custom-call(s32[1]{0:T(128)} %slice.31.side, bf16[256,1024]{1,0:T(8,128)(2,1)} %copy-done.10, bf16[1024,1024]{1,0:T(8,128)(2,1)} %tokens.1, bf16[1024,1024]{1,0:T(8,128)(2,1)} %add_far.2.kept), custom_call_target="tpu_custom_call", output_to_operand_aliasing={{}: (3, {})} | custom-call | tf_op jit(solution)/shard_map/add_far/pallas_call | solution.py:472
  (48 shorter events, 1.6 us)
Async XLA Ops:
  0.0 6.1 %copy-start = (bf16[1024,1024]{1,0:T(8,128)(2,1)S(1)}, bf16[1024,1024]{1,0:T(8,128)(2,1)}, u32[]{:S(2)}) copy-start(bf16[1024,1024]{1,0:T(8,128)(2,1)} %tokens.1) | copy-start | bytes 6291460
  3.0 49.0 %collective-permute-start.3 = (bf16[2,512,1024]{2,1,0:T(8,128)(2,1)}, bf16[2,512,1024]{2,1,0:T(8,128)(2,1)}, u32[]{:S(2)}, u32[]{:S(2)}) collective-permute-start(bf16[2,512,1024]{2,1,0:T(8,128)(2,1)} %pair.1), channel_id=1, source_target_pairs={{0,2},{2,0},{1,3},{3,1},{4,6},{6,4},{5,7},{7,5},{8,10},{10,8},{9,1... | collective-permute-start | bytes 6291464 | tf_op jit(solution)/shard_map/ppermute | solution.py:492
  7.3 17.0 %collective-permute-start = (bf16[1024,256]{1,0:T(8,128)(2,1)}, bf16[1024,256]{1,0:T(8,128)(2,1)S(1)}, u32[]{:S(2)}, u32[]{:S(2)}) collective-permute-start(bf16[1024,256]{1,0:T(8,128)(2,1)} %get-tuple-element.83), channel_id=1, source_target_pairs={{0,4},{4,8},{8,12},{12,0},{1,5},{5,9},{9,13},{13,1},{2,6},{6,10},{... | collective-permute-start | bytes 1572872 | tf_op jit(solution)/shard_map/ppermute | solution.py:497
  8.9 36.5 %collective-permute-start.1 = (bf16[1024,256]{1,0:T(8,128)(2,1)}, bf16[1024,256]{1,0:T(8,128)(2,1)S(1)}, u32[]{:S(2)}, u32[]{:S(2)}) collective-permute-start(bf16[1024,256]{1,0:T(8,128)(2,1)} %get-tuple-element.84), channel_id=1, source_target_pairs={{0,8},{4,12},{8,0},{12,4},{1,9},{5,13},{9,1},{13,5},{2,10},{6,14},... | collective-permute-start | bytes 1572872 | tf_op jit(solution)/shard_map/ppermute | solution.py:497
  11.5 33.9 %collective-permute-start.2 = (bf16[1024,256]{1,0:T(8,128)(2,1)}, bf16[1024,256]{1,0:T(8,128)(2,1)}, u32[]{:S(2)}, u32[]{:S(2)}) collective-permute-start(bf16[1024,256]{1,0:T(8,128)(2,1)} %get-tuple-element.85), channel_id=1, source_target_pairs={{0,12},{4,0},{8,4},{12,8},{1,13},{5,1},{9,5},{13,9},{2,14},{6,2},{... | collective-permute-start | bytes 1572872 | tf_op jit(solution)/shard_map/ppermute | solution.py:497
  52.0 26.1 %collective-permute-start.8 = (bf16[2,512,1024]{2,1,0:T(8,128)(2,1)}, bf16[2,512,1024]{2,1,0:T(8,128)(2,1)}, u32[]{:S(2)}, u32[]{:S(2)}) collective-permute-start(bf16[2,512,1024]{2,1,0:T(8,128)(2,1)} %collective-permute-done.3.refs_3_), channel_id=1, source_target_pairs={{0,1},{1,0},{2,3},{3,2},{4,5},{5,4},{6,7},{7,6},{8,9},{9,8},{10,11... | collective-permute-start | bytes 6291464 | tf_op jit(solution)/shard_map/ppermute | solution.py:492
  52.0 48.4 %collective-permute-start.12 = (bf16[2,512,1024]{2,1,0:T(8,128)(2,1)}, bf16[2,512,1024]{2,1,0:T(8,128)(2,1)}, u32[]{:S(2)}, u32[]{:S(2)}) collective-permute-start(bf16[2,512,1024]{2,1,0:T(8,128)(2,1)} %collective-permute-done.3.refs_3_), channel_id=1, source_target_pairs={{0,16},{16,0},{1,17},{17,1},{2,18},{18,2},{3,19},{19,3},{4,20},{20... | collective-permute-start | bytes 6291464 | tf_op jit(solution)/shard_map/ppermute | solution.py:492
  53.8 48.1 %collective-permute-start.13 = (bf16[1024,1024]{1,0:T(8,128)(2,1)}, bf16[1024,1024]{1,0:T(8,128)(2,1)}, u32[]{:S(2)}, u32[]{:S(2)}) collective-permute-start(bf16[1024,1024]{1,0:T(8,128)(2,1)} %constant_dynamic-slice_fusion.1), channel_id=1, source_target_pairs={{0,2},{2,0},{1,3},{3,1},{4,6},{6,4},{5,7},{7,5},{8,10},{10,8},{9,1... | collective-permute-start | bytes 6291464 | tf_op jit(solution)/shard_map/ppermute | solution.py:492
  55.3 5.6 %copy-start.6 = (f32[17,1024]{1,0:T(8,128)S(1)}, f32[17,1024]{1,0:T(8,128)}, u32[]{:S(2)}) copy-start(f32[17,1024]{1,0:T(8,128)} %mix_ref.1) | copy-start | bytes 208900
  55.3 5.6 %copy-start.7 = (f32[2,1024]{1,0:T(2,128)S(1)}, f32[2,1024]{1,0:T(2,128)}, u32[]{:S(2)}) copy-start(f32[2,1024]{1,0:T(2,128)} %high_ref.1) | copy-start | bytes 24580
  55.3 5.6 %copy-start.8 = (f32[1024]{0:T(1024)S(1)}, f32[1024]{0:T(1024)}, u32[]{:S(2)}) copy-start(f32[1024]{0:T(1024)} %param.8) | copy-start | bytes 12292
  57.5 0.8 copy-start.4
  58.3 2.7 %collective-permute-start.5 = (bf16[3,1024,128]{2,1,0:T(8,128)(2,1)}, bf16[3,1024,128]{2,1,0:T(8,128)(2,1)S(1)}, u32[]{:S(2)}, u32[]{:S(2)}) collective-permute-start(bf16[3,1024,128]{2,1,0:T(8,128)(2,1)} %others.1), channel_id=1, source_target_pairs={{0,1},{1,0},{2,3},{3,2},{4,5},{5,4},{6,7},{7,6},{8,9},{9,8},{10,11... | collective-permute-start | bytes 2359304 | tf_op jit(solution)/shard_map/ppermute | solution.py:492
  58.4 2.5 %collective-permute-start.4 = (bf16[1024,128]{1,0:T(8,128)(2,1)S(1)}, bf16[1024,128]{1,0:T(8,128)(2,1)S(1)}, u32[]{:S(2)}, u32[]{:S(2)}) collective-permute-start(bf16[1024,128]{1,0:T(8,128)(2,1)S(1)} %get-tuple-element.159), channel_id=1, source_target_pairs={{0,1},{1,0},{2,3},{3,2},{4,5},{5,4},{6,7},{7,6},{8,9},{9,8},{10,11... | collective-permute-start | bytes 786440 | tf_op jit(solution)/shard_map/ppermute | solution.py:492
  60.9 1.0 copy-start.5
  62.0 53.1 %copy-start.3 = (bf16[2048,1024]{1,0:T(8,128)(2,1)S(1)}, bf16[2048,1024]{1,0:T(8,128)(2,1)}, u32[]{:S(2)}) copy-start(bf16[2048,1024]{1,0:T(8,128)(2,1)} %refs_2_.2) | copy-start | bytes 12582916
  75.2 2.0 %collective-permute-start.6 = (bf16[4,512,128]{2,1,0:T(8,128)(2,1)S(1)}, bf16[4,512,128]{2,1,0:T(8,128)(2,1)S(1)}, u32[]{:S(2)}, u32[]{:S(2)}) collective-permute-start(bf16[4,512,128]{2,1,0:T(8,128)(2,1)S(1)} %get-tuple-element.93), channel_id=1, source_target_pairs={{0,1},{1,0},{2,3},{3,2},{4,5},{5,4},{6,7},{7,6},{8,9},{9,8},{10,11... | collective-permute-start | bytes 1572872 | tf_op jit(solution)/shard_map/ppermute | solution.py:492
  75.4 2.5 %collective-permute-start.7 = (bf16[4,512,128]{2,1,0:T(8,128)(2,1)S(1)}, bf16[4,512,128]{2,1,0:T(8,128)(2,1)S(1)}, u32[]{:S(2)}, u32[]{:S(2)}) collective-permute-start(bf16[4,512,128]{2,1,0:T(8,128)(2,1)S(1)} %get-tuple-element.94), channel_id=1, source_target_pairs={{0,1},{1,0},{2,3},{3,2},{4,5},{5,4},{6,7},{7,6},{8,9},{9,8},{10,11... | collective-permute-start | bytes 1572872 | tf_op jit(solution)/shard_map/ppermute | solution.py:492
  78.1 23.8 %collective-permute-start.10 = (bf16[2,512,128]{2,1,0:T(8,128)(2,1)S(1)}, bf16[2,512,128]{2,1,0:T(8,128)(2,1)S(1)}, u32[]{:S(2)}, u32[]{:S(2)}) collective-permute-start(bf16[2,512,128]{2,1,0:T(8,128)(2,1)S(1)} %get-tuple-element.104), channel_id=1, source_target_pairs={{0,8},{4,12},{8,0},{12,4},{1,9},{5,13},{9,1},{13,5},{2,10},{6,14},... | collective-permute-start | bytes 786440 | tf_op jit(solution)/shard_map/ppermute | solution.py:497
  81.1 20.7 %collective-permute-start.11 = (bf16[2,512,128]{2,1,0:T(8,128)(2,1)S(1)}, bf16[2,512,128]{2,1,0:T(8,128)(2,1)S(1)}, u32[]{:S(2)}, u32[]{:S(2)}) collective-permute-start(bf16[2,512,128]{2,1,0:T(8,128)(2,1)S(1)} %get-tuple-element.105), channel_id=1, source_target_pairs={{0,12},{4,0},{8,4},{12,8},{1,13},{5,1},{9,5},{13,9},{2,14},{6,2},{... | collective-permute-start | bytes 786440 | tf_op jit(solution)/shard_map/ppermute | solution.py:497
  84.5 17.7 %collective-permute-start.9 = (bf16[2,512,128]{2,1,0:T(8,128)(2,1)S(1)}, bf16[2,512,128]{2,1,0:T(8,128)(2,1)S(1)}, u32[]{:S(2)}, u32[]{:S(2)}) collective-permute-start(bf16[2,512,128]{2,1,0:T(8,128)(2,1)S(1)} %get-tuple-element.103), channel_id=1, source_target_pairs={{0,4},{4,8},{8,12},{12,0},{1,5},{5,9},{9,13},{13,1},{2,6},{6,10},{... | collective-permute-start | bytes 786440 | tf_op jit(solution)/shard_map/ppermute | solution.py:497
  102.2 12.9 %collective-permute-start.15 = (bf16[2,256,128]{2,1,0:T(8,128)(2,1)S(1)}, bf16[2,256,128]{2,1,0:T(8,128)(2,1)S(1)}, u32[]{:S(2)}, u32[]{:S(2)}) collective-permute-start(bf16[2,256,128]{2,1,0:T(8,128)(2,1)S(1)} %get-tuple-element.111), channel_id=1, source_target_pairs={{0,8},{4,12},{8,0},{12,4},{1,9},{5,13},{9,1},{13,5},{2,10},{6,14},... | collective-permute-start | bytes 393224 | tf_op jit(solution)/shard_map/ppermute | solution.py:497
  107.3 7.8 %copy-start.2 = (bf16[2048,1024]{1,0:T(8,128)(2,1)S(1)}, bf16[2048,1024]{1,0:T(8,128)(2,1)}, u32[]{:S(2)}) copy-start(bf16[2048,1024]{1,0:T(8,128)(2,1)} %refs_1_.1) | copy-start | bytes 12582916
  107.5 13.6 %collective-permute-start.17 = (bf16[4,2,256,128]{3,2,1,0:T(8,128)(2,1)S(1)}, bf16[4,2,256,128]{3,2,1,0:T(8,128)(2,1)S(1)}, u32[]{:S(2)}, u32[]{:S(2)}) collective-permute-start(bf16[4,2,256,128]{3,2,1,0:T(8,128)(2,1)S(1)} %get-tuple-element.122), channel_id=1, source_target_pairs={{0,2},{2,0},{1,3},{3,1},{4,6},{6,4},{5,7},{7,5},{8,10},{10,8},{9,1... | collective-permute-start | bytes 1572872 | tf_op jit(solution)/shard_map/ppermute | solution.py:492
  109.1 10.6 %collective-permute-start.16 = (bf16[2,256,128]{2,1,0:T(8,128)(2,1)S(1)}, bf16[2,256,128]{2,1,0:T(8,128)(2,1)S(1)}, u32[]{:S(2)}, u32[]{:S(2)}) collective-permute-start(bf16[2,256,128]{2,1,0:T(8,128)(2,1)S(1)} %get-tuple-element.116), channel_id=1, source_target_pairs={{0,12},{4,0},{8,4},{12,8},{1,13},{5,1},{9,5},{13,9},{2,14},{6,2},{... | collective-permute-start | bytes 393224 | tf_op jit(solution)/shard_map/ppermute | solution.py:497
  110.1 9.6 %collective-permute-start.14 = (bf16[2,256,128]{2,1,0:T(8,128)(2,1)S(1)}, bf16[2,256,128]{2,1,0:T(8,128)(2,1)S(1)}, u32[]{:S(2)}, u32[]{:S(2)}) collective-permute-start(bf16[2,256,128]{2,1,0:T(8,128)(2,1)S(1)} %get-tuple-element.108), channel_id=1, source_target_pairs={{0,4},{4,8},{8,12},{12,0},{1,5},{5,9},{9,13},{13,1},{2,6},{6,10},{... | collective-permute-start | bytes 393224 | tf_op jit(solution)/shard_map/ppermute | solution.py:497
  115.1 6.1 %collective-permute-start.18 = (bf16[2,512,1024]{2,1,0:T(8,128)(2,1)}, bf16[2,512,1024]{2,1,0:T(8,128)(2,1)S(1)}, u32[]{:S(2)}, u32[]{:S(2)}) collective-permute-start(bf16[2,512,1024]{2,1,0:T(8,128)(2,1)} %collective-permute-done.12.refs_4_), channel_id=1, source_target_pairs={{0,1},{1,0},{2,3},{3,2},{4,5},{5,4},{6,7},{7,6},{8,9},{9,8},{10,11... | collective-permute-start | bytes 6291464 | tf_op jit(solution)/shard_map/ppermute | solution.py:492
  121.2 11.5 %collective-permute-start.23 = (bf16[1024,1024]{1,0:T(8,128)(2,1)}, bf16[1024,1024]{1,0:T(8,128)(2,1)S(1)}, u32[]{:S(2)}, u32[]{:S(2)}) collective-permute-start(bf16[1024,1024]{1,0:T(8,128)(2,1)} %collective-permute-done.13.mine), channel_id=1, source_target_pairs={{0,1},{1,0},{2,3},{3,2},{4,5},{5,4},{6,7},{7,6},{8,9},{9,8},{10,11... | collective-permute-start | bytes 6291464 | tf_op jit(solution)/shard_map/ppermute | solution.py:492
  121.2 14.7 %collective-permute-start.22 = (bf16[4,2,256,128]{3,2,1,0:T(8,128)(2,1)S(1)}, bf16[4,2,256,128]{3,2,1,0:T(8,128)(2,1)S(1)}, u32[]{:S(2)}, u32[]{:S(2)}) collective-permute-start(bf16[4,2,256,128]{3,2,1,0:T(8,128)(2,1)S(1)} %get-tuple-element.137), channel_id=1, source_target_pairs={{0,2},{2,0},{1,3},{3,1},{4,6},{6,4},{5,7},{7,5},{8,10},{10,8},{9,1... | collective-permute-start | bytes 1572872 | tf_op jit(solution)/shard_map/ppermute | solution.py:492
  123.6 12.3 %collective-permute-start.21 = (bf16[2,256,128]{2,1,0:T(8,128)(2,1)S(1)}, bf16[2,256,128]{2,1,0:T(8,128)(2,1)S(1)}, u32[]{:S(2)}, u32[]{:S(2)}) collective-permute-start(bf16[2,256,128]{2,1,0:T(8,128)(2,1)S(1)} %get-tuple-element.136), channel_id=1, source_target_pairs={{0,12},{4,0},{8,4},{12,8},{1,13},{5,1},{9,5},{13,9},{2,14},{6,2},{... | collective-permute-start | bytes 393224 | tf_op jit(solution)/shard_map/ppermute | solution.py:497
  126.0 11.2 %collective-permute-start.20 = (bf16[2,256,128]{2,1,0:T(8,128)(2,1)S(1)}, bf16[2,256,128]{2,1,0:T(8,128)(2,1)S(1)}, u32[]{:S(2)}, u32[]{:S(2)}) collective-permute-start(bf16[2,256,128]{2,1,0:T(8,128)(2,1)S(1)} %get-tuple-element.133), channel_id=1, source_target_pairs={{0,8},{4,12},{8,0},{12,4},{1,9},{5,13},{9,1},{13,5},{2,10},{6,14},... | collective-permute-start | bytes 393224 | tf_op jit(solution)/shard_map/ppermute | solution.py:497
  126.0 11.2 %collective-permute-start.19 = (bf16[2,256,128]{2,1,0:T(8,128)(2,1)S(1)}, bf16[2,256,128]{2,1,0:T(8,128)(2,1)S(1)}, u32[]{:S(2)}, u32[]{:S(2)}) collective-permute-start(bf16[2,256,128]{2,1,0:T(8,128)(2,1)S(1)} %get-tuple-element.130), channel_id=1, source_target_pairs={{0,4},{4,8},{8,12},{12,0},{1,5},{5,9},{9,13},{13,1},{2,6},{6,10},{... | collective-permute-start | bytes 393224 | tf_op jit(solution)/shard_map/ppermute | solution.py:497
  137.2 13.6 %collective-permute-start.25 = (bf16[256,1024]{1,0:T(8,128)(2,1)S(1)}, bf16[256,1024]{1,0:T(8,128)(2,1)S(1)}, u32[]{:S(2)}, u32[]{:S(2)}) collective-permute-start(bf16[256,1024]{1,0:T(8,128)(2,1)S(1)} %send.2), channel_id=1, source_target_pairs={{0,2},{2,0},{1,3},{3,1},{4,6},{6,4},{5,7},{7,5},{8,10},{10,8},{9,1... | collective-permute-start | bytes 1572872 | tf_op jit(solution)/shard_map/ppermute | solution.py:492
  144.9 5.8 %copy-start.1 = (bf16[2048,1024]{1,0:T(8,128)(2,1)S(1)}, bf16[2048,1024]{1,0:T(8,128)(2,1)}, u32[]{:S(2)}) copy-start(bf16[2048,1024]{1,0:T(8,128)(2,1)} %refs_2_.3) | copy-start | bytes 12582916
  148.5 13.1 %collective-permute-start.24 = (bf16[256,1024]{1,0:T(8,128)(2,1)S(1)}, bf16[256,1024]{1,0:T(8,128)(2,1)S(1)}, u32[]{:S(2)}, u32[]{:S(2)}) collective-permute-start(bf16[256,1024]{1,0:T(8,128)(2,1)S(1)} %send.3), channel_id=1, source_target_pairs={{0,2},{2,0},{1,3},{3,1},{4,6},{6,4},{5,7},{7,5},{8,10},{10,8},{9,1... | collective-permute-start | bytes 1572872 | tf_op jit(solution)/shard_map/ppermute | solution.py:492
  150.8 4.5 %copy-start.9 = (bf16[256,1024]{1,0:T(8,128)(2,1)}, bf16[256,1024]{1,0:T(8,128)(2,1)S(1)}, u32[]{:S(2)}) copy-start(bf16[256,1024]{1,0:T(8,128)(2,1)S(1)} %collective-permute-done.25.got) | copy-start | bytes 1572868
  161.5 0.8 copy-start.10

commit v6 on v5

--- a/solution.py
+++ b/solution.py
@@ -456,34 +456,54 @@
     )(side, *parts, weight, tokens)
 
 
-def add_kernel(side, got, tokens, kept, out_ref):
-    out_ref[...] = (got[...].astype(jnp.float32) + tokens[...].astype(jnp.float32)).astype(
-        jnp.bfloat16
-    )
+def add_kernel(q, side, got, tokens, kept, out_ref, before, after, loads, stores):
+    rows = got.shape[0]
+    part = rows // PARTS
+    start = (SPLIT * (1 - side[0]) + q) * rows
+
+    def here(p):
+        return pl.ds(pl.multiple_of(start + p * part, part), part)
+
+    def piece(p):
+        return pl.ds(p * part, part)
+
+    def load(p):
+        return pltpu.make_async_copy(tokens.at[here(p)], before.at[piece(p)], loads.at[p])
+
+    def store(p):
+        return pltpu.make_async_copy(after.at[piece(p)], out_ref.at[here(p)], stores.at[p])
+
+    for p in range(PARTS):
+        load(p).start()
+    for p in range(PARTS):
+        load(p).wait()
+        added = got[piece(p), :].astype(jnp.float32) + before[piece(p), :].astype(jnp.float32)
+        after[piece(p), :] = added.astype(jnp.bfloat16)
+        store(p).start()
+    for p in range(PARTS):
+        store(p).wait()
 
 
 def add_far(side, q, got, tokens, result):
-    rows, channels = got.shape
-
-    def spot(j, side):
-        return (SPLIT * (1 - side[0]) + q, j)
-
-    block = min(512, channels)
-    return pl.pallas_call(
-        add_kernel,
-        grid_spec=pltpu.PrefetchScalarGridSpec(
-            num_scalar_prefetch=1,
-            grid=(channels // block,),
-            in_specs=[
-                pl.BlockSpec((rows, block), lambda j, side: (0, j)),
-                pl.BlockSpec((rows, block), spot),
-                pl.BlockSpec(memory_space=pl.ANY),
-            ],
-            out_specs=pl.BlockSpec((rows, block), spot),
-        ),
+    anywhere = pl.BlockSpec(memory_space=pl.ANY)
+    return pl.pallas_call(
+        functools.partial(add_kernel, q),
+        in_specs=[
+            pl.BlockSpec(memory_space=pltpu.SMEM),
+            pl.BlockSpec(memory_space=pltpu.VMEM),
+            anywhere,
+            anywhere,
+        ],
+        out_specs=anywhere,
         out_shape=jax.ShapeDtypeStruct(tokens.shape, jnp.bfloat16),
         input_output_aliases={3: 0},
-        compiler_params=pltpu.CompilerParams(vmem_limit_bytes=LARGE),
+        scratch_shapes=[
+            pltpu.VMEM(got.shape, got.dtype),
+            pltpu.VMEM(got.shape, got.dtype),
+            pltpu.SemaphoreType.DMA((PARTS,)),
+            pltpu.SemaphoreType.DMA((PARTS,)),
+        ],
+        compiler_params=pltpu.CompilerParams(vmem_limit_bytes=LITTLE),
         name="add_far",
     )(side, got, tokens, result)
 

time: 165 us -> 164 us (level)
  no operation moved by 1% of the time
where the time goes in v6:
time: 164 us
  waiting for transfers between devices  70.1 us (43%)
  Pallas kernels  50.8 us (31%)
  starting transfers between devices  35.4 us (22%)
  local copies, waits for them, and re-layouts  7.04 us (4%)
    ppermute x14, waiting for transfers between devices, swap(): return lax.ppermute(array, axis, [(0, 1), (1, 0)])  35.1 us
    ppermute x12, waiting for transfers between devices, ahead(): lax.ppermute(array, 'seq', [(j, (j + offset) % chips) for j in range(chip...  35 us
    ppermute x12, starting transfers between devices, ahead(): lax.ppermute(array, 'seq', [(j, (j + offset) % chips) for j in range(chip...  21.9 us
    ppermute x14, starting transfers between devices, swap(): return lax.ppermute(array, axis, [(0, 1), (1, 0)])  13.5 us
    pallas_call x1, Pallas kernels, run_filter(): pl.pallas_call(functools.partial(levels_kernel, live, chips), out_shape=[...  13.2 us
    pallas_call x2, Pallas kernels, run_hidden(): pl.pallas_call(functools.partial(hidden_kernel, chips, min(512, channels)...  12.2 us
    pallas_call x2, Pallas kernels, run_send(): pl.pallas_call(send_kernel, grid_spec=pltpu.PrefetchScalarGridSpec(num_sc...  6.77 us
    pallas_call x1, Pallas kernels, run_load(): pl.pallas_call(functools.partial(load_kernel, count), in_specs=[smem] + [...  4.6 us
  transfers between devices with their start and end apart: 26, of which 14 were waited for; matrix products, arithmetic and copies ran while one was open for 3% of the time, Pallas kernels for 24%

profile of v6, /device:TPU:0, one launch (start us, length us, event | category | flops | bytes accessed | tf_op | source)
XLA Modules:
  0.0 163.7 jit_solution(14702197050293048841)
XLA Ops:
  0.0 3.0 %pair.1 = bf16[2,512,1024]{2,1,0:T(8,128)(2,1)} custom-call(bf16[2048,1024]{1,0:T(8,128)(2,1)} %refs_1_.1, bf16[2048,1024]{1,0:T(8,128)(2,1)} %refs_2_.2), custom_call_target="tpu_custom_call" | custom-call | tf_op jit(solution)/shard_map/pair/pallas_call | solution.py:136
  3.0 3.0 %collective-permute-start.3 = (bf16[2,512,1024]{2,1,0:T(8,128)(2,1)}, bf16[2,512,1024]{2,1,0:T(8,128)(2,1)}, u32[]{:S(2)}, u32[]{:S(2)}) collective-permute-start(bf16[2,512,1024]{2,1,0:T(8,128)(2,1)} %pair.1), channel_id=1, source_target_pairs={{0,2},{2,0},{1,3},{3,1},{4,6},{6,4},{5,7},{7,5},{8,10},{10,8},{9,1... | collective-permute-start | bytes 6291464 | tf_op jit(solution)/shard_map/ppermute | solution.py:512
  6.1 1.2 constant_dynamic-slice_fusion.2
  7.3 1.6 collective-permute-start
  8.9 2.6 %collective-permute-start.1 = (bf16[1024,256]{1,0:T(8,128)(2,1)}, bf16[1024,256]{1,0:T(8,128)(2,1)S(1)}, u32[]{:S(2)}, u32[]{:S(2)}) collective-permute-start(bf16[1024,256]{1,0:T(8,128)(2,1)} %get-tuple-element.84), channel_id=1, source_target_pairs={{0,8},{4,12},{8,0},{12,4},{1,9},{5,13},{9,1},{13,5},{2,10},{6,14},... | collective-permute-start | bytes 1572872 | tf_op jit(solution)/shard_map/ppermute | solution.py:517
  11.4 1.3 collective-permute-start.2
  12.8 3.1 %constant_dynamic-slice_fusion.1 = bf16[1024,1024]{1,0:T(8,128)(2,1)} fusion(bf16[2048,1024]{1,0:T(8,128)(2,1)} %refs_2_.3, s32[]{:T(128)S(6)} %select_n.47), kind=kLoop, calls=%fused_computation.11 | loop fusion | bytes 4194308 | tf_op jit(solution)/shard_map/dynamic_slice | solution.py:581
  15.9 8.4 %collective-permute-done.refs_0_ = bf16[1024,256]{1,0:T(8,128)(2,1)S(1)} collective-permute-done((bf16[1024,256]{1,0:T(8,128)(2,1)}, bf16[1024,256]{1,0:T(8,128)(2,1)S(1)}, u32[]{:S(2)}, u32[]{:S(2)}) %collective-permute-start) | collective-permute-done | bytes 524320 | tf_op jit(solution)/shard_map/ppermute | solution.py:517
  24.3 21.1 %collective-permute-done.1.refs_1_ = bf16[1024,256]{1,0:T(8,128)(2,1)S(1)} collective-permute-done((bf16[1024,256]{1,0:T(8,128)(2,1)}, bf16[1024,256]{1,0:T(8,128)(2,1)S(1)}, u32[]{:S(2)}, u32[]{:S(2)}) %collective-permute-start.1) | collective-permute-done | bytes 524320 | tf_op jit(solution)/shard_map/ppermute | solution.py:517
  45.3 6.7 %collective-permute-done.3.refs_3_ = bf16[2,512,1024]{2,1,0:T(8,128)(2,1)} collective-permute-done((bf16[2,512,1024]{2,1,0:T(8,128)(2,1)}, bf16[2,512,1024]{2,1,0:T(8,128)(2,1)}, u32[]{:S(2)}, u32[]{:S(2)}) %collective-permute-start.3) | collective-permute-done | bytes 2097184 | tf_op jit(solution)/shard_map/ppermute | solution.py:512
  52.0 1.8 %collective-permute-start.12 = (bf16[2,512,1024]{2,1,0:T(8,128)(2,1)}, bf16[2,512,1024]{2,1,0:T(8,128)(2,1)}, u32[]{:S(2)}, u32[]{:S(2)}) collective-permute-start(bf16[2,512,1024]{2,1,0:T(8,128)(2,1)} %collective-permute-done.3.refs_3_), channel_id=1, source_target_pairs={{0,16},{16,0},{1,17},{17,1},{2,18},{18,2},{3,19},{19,3},{4,20},{20... | collective-permute-start | bytes 6291464 | tf_op jit(solution)/shard_map/ppermute | solution.py:512
  53.8 1.5 collective-permute-start.13
  55.4 2.1 %others.1 = bf16[3,1024,128]{2,1,0:T(8,128)(2,1)} custom-call(s32[5]{0:T(128)S(1)} %stack.49.place.refs_0_, bf16[1024,256]{1,0:T(8,128)(2,1)S(1)} %collective-permute-done.refs_0_, bf16[1024,256]{1,0:T(8,128)(2,1)S(1)} %collective-permute-done.1.refs_1_, bf16[1024,256]{1,0:T(8,128)(2,1)} %collective-permute-done.2.refs_2_), custom_call_target="tpu_custom_call" | custom-call | flops 5000000000 | tf_op jit(solution)/shard_map/others/pallas_call | solution.py:545
  57.5 0.8 copy-done.4
  58.4 0.6 collective-permute-start.4
  59.0 1.9 %collective-permute-done.4.refs_3_ = bf16[1024,128]{1,0:T(8,128)(2,1)S(1)} collective-permute-done((bf16[1024,128]{1,0:T(8,128)(2,1)S(1)}, bf16[1024,128]{1,0:T(8,128)(2,1)S(1)}, u32[]{:S(2)}, u32[]{:S(2)}) %collective-permute-start.4) | collective-permute-done | bytes 262176 | tf_op jit(solution)/shard_map/ppermute | solution.py:512
  60.9 1.0 copy-done.5
  62.0 13.2 %levels.1 = (bf16[4,512,128]{2,1,0:T(8,128)(2,1)S(1)}, bf16[4,512,128]{2,1,0:T(8,128)(2,1)S(1)}, bf16[4,512,128]{2,1,0:T(8,128)(2,1)S(1)}, bf16[4,512,128]{2,1,0:T(8,128)(2,1)S(1)}) custom-call(s32[5]{0:T(128)S(1)} %stack.49.place.refs_0_, f32[1,1024]{1,0:T(1,128)S(1)} %bitcast.21, f32[2,1024]{1,0:T(2,128)S(1)} %copy-done.7, f32[17,1024]{1,0:T(8,128)S(1)} %copy-done.6, ...), custom_call_target="tpu_custom_call" | custom-call | tf_op jit(solution)/shard_map/levels/pallas_call | solution.py:248
  75.4 0.4 collective-permute-start.7
  75.8 1.4 collective-permute-done.6.refs_2_
  77.2 0.7 collective-permute-done.7.refs_3_
  78.1 3.0 %collective-permute-start.10 = (bf16[2,512,128]{2,1,0:T(8,128)(2,1)S(1)}, bf16[2,512,128]{2,1,0:T(8,128)(2,1)S(1)}, u32[]{:S(2)}, u32[]{:S(2)}) collective-permute-start(bf16[2,512,128]{2,1,0:T(8,128)(2,1)S(1)} %get-tuple-element.104), channel_id=1, source_target_pairs={{0,8},{4,12},{8,0},{12,4},{1,9},{5,13},{9,1},{13,5},{2,10},{6,14},... | collective-permute-start | bytes 786440 | tf_op jit(solution)/shard_map/ppermute | solution.py:517
  81.1 3.4 %collective-permute-start.11 = (bf16[2,512,128]{2,1,0:T(8,128)(2,1)S(1)}, bf16[2,512,128]{2,1,0:T(8,128)(2,1)S(1)}, u32[]{:S(2)}, u32[]{:S(2)}) collective-permute-start(bf16[2,512,128]{2,1,0:T(8,128)(2,1)S(1)} %get-tuple-element.105), channel_id=1, source_target_pairs={{0,12},{4,0},{8,4},{12,8},{1,13},{5,1},{9,5},{13,9},{2,14},{6,2},{... | collective-permute-start | bytes 786440 | tf_op jit(solution)/shard_map/ppermute | solution.py:517
  84.5 15.9 %collective-permute-done.12.refs_4_ = bf16[2,512,1024]{2,1,0:T(8,128)(2,1)} collective-permute-done((bf16[2,512,1024]{2,1,0:T(8,128)(2,1)}, bf16[2,512,1024]{2,1,0:T(8,128)(2,1)}, u32[]{:S(2)}, u32[]{:S(2)}) %collective-permute-start.12) | collective-permute-done | bytes 2097184 | tf_op jit(solution)/shard_map/ppermute | solution.py:512
  100.4 1.5 collective-permute-done.13.mine
  102.2 5.1 %collective-permute-start.15 = (bf16[2,256,128]{2,1,0:T(8,128)(2,1)S(1)}, bf16[2,256,128]{2,1,0:T(8,128)(2,1)S(1)}, u32[]{:S(2)}, u32[]{:S(2)}) collective-permute-start(bf16[2,256,128]{2,1,0:T(8,128)(2,1)S(1)} %get-tuple-element.111), channel_id=1, source_target_pairs={{0,8},{4,12},{8,0},{12,4},{1,9},{5,13},{9,1},{13,5},{2,10},{6,14},... | collective-permute-start | bytes 393224 | tf_op jit(solution)/shard_map/ppermute | solution.py:517
  107.5 1.6 collective-permute-start.17
  109.0 1.0 collective-permute-start.16
  110.0 1.0 collective-permute-start.14
  111.0 4.0 %collective-permute-done.15.refs_2_ = bf16[2,256,128]{2,1,0:T(8,128)(2,1)S(1)} collective-permute-done((bf16[2,256,128]{2,1,0:T(8,128)(2,1)S(1)}, bf16[2,256,128]{2,1,0:T(8,128)(2,1)S(1)}, u32[]{:S(2)}, u32[]{:S(2)}) %collective-permute-start.15) | collective-permute-done | bytes 131104 | tf_op jit(solution)/shard_map/ppermute | solution.py:517
  115.0 4.6 %load.1 = (bf16[2048,1024]{1,0:T(8,128)(2,1)S(1)}, bf16[2048,1024]{1,0:T(8,128)(2,1)S(1)}, bf16[2,512,1024]{2,1,0:T(8,128)(2,1)S(1)}, bf16[2,512,1024]{2,1,0:T(8...) custom-call(s32[5]{0:T(128)S(1)} %stack.49.place.refs_0_, bf16[2048,1024]{1,0:T(8,128)(2,1)S(1)} %copy-done.2, ...), custom_call_target="tpu_custom_call" | custom-call | flops 99999997952 | tf_op jit(solution)/shard_map/load/pallas_call | solution.py:318
  119.7 1.5 collective-permute-done.17.refs_4_
  121.1 2.5 %collective-permute-start.22 = (bf16[4,2,256,128]{3,2,1,0:T(8,128)(2,1)S(1)}, bf16[4,2,256,128]{3,2,1,0:T(8,128)(2,1)S(1)}, u32[]{:S(2)}, u32[]{:S(2)}) collective-permute-start(bf16[4,2,256,128]{3,2,1,0:T(8,128)(2,1)S(1)} %get-tuple-element.137), channel_id=1, source_target_pairs={{0,2},{2,0},{1,3},{3,1},{4,6},{6,4},{5,7},{7,5},{8,10},{10,8},{9,1... | collective-permute-start | bytes 1572872 | tf_op jit(solution)/shard_map/ppermute | solution.py:512
  123.6 2.3 %collective-permute-start.21 = (bf16[2,256,128]{2,1,0:T(8,128)(2,1)S(1)}, bf16[2,256,128]{2,1,0:T(8,128)(2,1)S(1)}, u32[]{:S(2)}, u32[]{:S(2)}) collective-permute-start(bf16[2,256,128]{2,1,0:T(8,128)(2,1)S(1)} %get-tuple-element.136), channel_id=1, source_target_pairs={{0,12},{4,0},{8,4},{12,8},{1,13},{5,1},{9,5},{13,9},{2,14},{6,2},{... | collective-permute-start | bytes 393224 | tf_op jit(solution)/shard_map/ppermute | solution.py:517
  125.9 0.6 collective-permute-start.19
  126.5 6.1 %hidden.2.refs_0_ = bf16[256,2048]{1,0:T(8,128)(2,1)S(1)} custom-call(s32[5]{0:T(128)S(1)} %get-tuple-element.126.place, bf16[2,256,128]{2,1,0:T(8,128)(2,1)S(1)} %get-tuple-element.138.refs_0_, bf16[2,256,128]{2,1,0:T(8,128)(2,1)S(1)} %collective-permute-done.14.refs_1_, bf16[2,256,128]{2,1,0:T(8,128)(2,1)S(1)} %collective-permute-done.15.refs_2_, ...), custom_call_target="tpu_custom_call" | custom-call | flops 4294967296 | bytes 19922944 | tf_op jit(solution)/shard_map/hidden/pallas_call | solution.py:379
  132.6 3.3 %send.2 = bf16[256,1024]{1,0:T(8,128)(2,1)S(1)} custom-call(s32[5]{0:T(128)S(1)} %get-tuple-element.126.place, bf16[256,2048]{1,0:T(8,128)(2,1)S(1)} %hidden.2.refs_0_, bf16[1024,1024]{1,0:T(8,128)(2,1)} %collective-permute-done.13.mine, bf16[1024,1024]{1,0:T(8,128)(2,1)S(1)} %collective-permute-done.23.twin), custom_call_target="tpu_custom_call" | custom-call | flops 1073741824 | bytes 5767168 | tf_op jit(solution)/shard_map/send/pallas_call | solution.py:411
  135.9 1.2 collective-permute-done.20.refs_2_
  137.1 1.6 collective-permute-start.25
  138.8 6.1 %hidden.3.refs_1_ = bf16[256,2048]{1,0:T(8,128)(2,1)S(1)} custom-call(s32[5]{0:T(128)S(1)} %get-tuple-element.126.place, bf16[2,256,128]{2,1,0:T(8,128)(2,1)S(1)} %get-tuple-element.150.refs_0_, bf16[2,256,128]{2,1,0:T(8,128)(2,1)S(1)} %collective-permute-done.19.refs_1_, bf16[2,256,128]{2,1,0:T(8,128)(2,1)S(1)} %collective-permute-done.20.refs_2_, ...), custom_call_target="tpu_custom_call" | custom-call | flops 4294967296 | bytes 19922944 | tf_op jit(solution)/shard_map/hidden/pallas_call | solution.py:379
  144.9 3.5 %send.3 = bf16[256,1024]{1,0:T(8,128)(2,1)S(1)} custom-call(s32[5]{0:T(128)S(1)} %get-tuple-element.126.place, bf16[256,2048]{1,0:T(8,128)(2,1)S(1)} %hidden.3.refs_1_, bf16[1024,1024]{1,0:T(8,128)(2,1)} %collective-permute-done.13.mine, bf16[1024,1024]{1,0:T(8,128)(2,1)S(1)} %collective-permute-done.23.twin), custom_call_target="tpu_custom_call" | custom-call | flops 1073741824 | bytes 5767168 | tf_op jit(solution)/shard_map/send/pallas_call | solution.py:411
  148.4 0.5 collective-permute-start.24
  148.9 0.6 slice.31.side
  149.5 1.3 collective-permute-done.25.got
  150.7 4.4 %finish.1.kept = bf16[1024,1024]{1,0:T(8,128)(2,1)} custom-call(s32[1]{0:T(128)} %slice.31.side, bf16[256,2048]{1,0:T(8,128)(2,1)S(1)} %hidden.2.refs_0_, bf16[256,2048]{1,0:T(8,128)(2,1)S(1)} %hidden.3.refs_1_, bf16[2048,1024]{1,0:T(8,128)(2,1)S(1)} %copy-done.1, bf16[1024,1024]{1,0:T(8,128)(2,1)S(1)} %copy-done), custom_call_target="tpu_custom_call" | custom-call | flops 2147483648 | bytes 7340032 | tf_op jit(solution)/shard_map/finish/pallas_call | solution.py:440
  155.1 2.2 %add_far.2.kept = bf16[1024,1024]{1,0:T(8,128)(2,1)} custom-call(s32[1]{0:T(128)} %slice.31.side, bf16[256,1024]{1,0:T(8,128)(2,1)S(1)} %collective-permute-done.25.got, bf16[1024,1024]{1,0:T(8,128)(2,1)S(1)} %copy-done, bf16[1024,1024]{1,0:T(8,128)(2,1)} %finish.1.kept), custom_call_target="tpu_custom_call", output_to_operand_aliasing={{}: (3, {})} | custom-call | tf_op jit(solution)/shard_map/add_far/pallas_call | solution.py:489
  157.3 4.2 %collective-permute-done.24.got = bf16[256,1024]{1,0:T(8,128)(2,1)S(1)} collective-permute-done((bf16[256,1024]{1,0:T(8,128)(2,1)S(1)}, bf16[256,1024]{1,0:T(8,128)(2,1)S(1)}, u32[]{:S(2)}, u32[]{:S(2)}) %collective-permute-start.24) | collective-permute-done | bytes 524320 | tf_op jit(solution)/shard_map/ppermute | solution.py:512
  161.5 2.2 %add_far.3 = bf16[1024,1024]{1,0:T(8,128)(2,1)} custom-call(s32[1]{0:T(128)} %slice.31.side, bf16[256,1024]{1,0:T(8,128)(2,1)S(1)} %collective-permute-done.24.got, bf16[1024,1024]{1,0:T(8,128)(2,1)S(1)} %copy-done, bf16[1024,1024]{1,0:T(8,128)(2,1)} %add_far.2.kept), custom_call_target="tpu_custom_call", output_to_operand_aliasing={{}: (3, {})} | custom-call | tf_op jit(solution)/shard_map/add_far/pallas_call | solution.py:489
  (44 shorter events, 1.1 us)
Async XLA Ops:
  0.0 6.1 %copy-start = (bf16[1024,1024]{1,0:T(8,128)(2,1)S(1)}, bf16[1024,1024]{1,0:T(8,128)(2,1)}, u32[]{:S(2)}) copy-start(bf16[1024,1024]{1,0:T(8,128)(2,1)} %tokens.1) | copy-start | bytes 6291460
  3.0 49.0 %collective-permute-start.3 = (bf16[2,512,1024]{2,1,0:T(8,128)(2,1)}, bf16[2,512,1024]{2,1,0:T(8,128)(2,1)}, u32[]{:S(2)}, u32[]{:S(2)}) collective-permute-start(bf16[2,512,1024]{2,1,0:T(8,128)(2,1)} %pair.1), channel_id=1, source_target_pairs={{0,2},{2,0},{1,3},{3,1},{4,6},{6,4},{5,7},{7,5},{8,10},{10,8},{9,1... | collective-permute-start | bytes 6291464 | tf_op jit(solution)/shard_map/ppermute | solution.py:512
  7.3 17.0 %collective-permute-start = (bf16[1024,256]{1,0:T(8,128)(2,1)}, bf16[1024,256]{1,0:T(8,128)(2,1)S(1)}, u32[]{:S(2)}, u32[]{:S(2)}) collective-permute-start(bf16[1024,256]{1,0:T(8,128)(2,1)} %get-tuple-element.83), channel_id=1, source_target_pairs={{0,4},{4,8},{8,12},{12,0},{1,5},{5,9},{9,13},{13,1},{2,6},{6,10},{... | collective-permute-start | bytes 1572872 | tf_op jit(solution)/shard_map/ppermute | solution.py:517
  8.9 36.5 %collective-permute-start.1 = (bf16[1024,256]{1,0:T(8,128)(2,1)}, bf16[1024,256]{1,0:T(8,128)(2,1)S(1)}, u32[]{:S(2)}, u32[]{:S(2)}) collective-permute-start(bf16[1024,256]{1,0:T(8,128)(2,1)} %get-tuple-element.84), channel_id=1, source_target_pairs={{0,8},{4,12},{8,0},{12,4},{1,9},{5,13},{9,1},{13,5},{2,10},{6,14},... | collective-permute-start | bytes 1572872 | tf_op jit(solution)/shard_map/ppermute | solution.py:517
  11.4 33.9 %collective-permute-start.2 = (bf16[1024,256]{1,0:T(8,128)(2,1)}, bf16[1024,256]{1,0:T(8,128)(2,1)}, u32[]{:S(2)}, u32[]{:S(2)}) collective-permute-start(bf16[1024,256]{1,0:T(8,128)(2,1)} %get-tuple-element.85), channel_id=1, source_target_pairs={{0,12},{4,0},{8,4},{12,8},{1,13},{5,1},{9,5},{13,9},{2,14},{6,2},{... | collective-permute-start | bytes 1572872 | tf_op jit(solution)/shard_map/ppermute | solution.py:517
  52.0 26.1 %collective-permute-start.8 = (bf16[2,512,1024]{2,1,0:T(8,128)(2,1)}, bf16[2,512,1024]{2,1,0:T(8,128)(2,1)}, u32[]{:S(2)}, u32[]{:S(2)}) collective-permute-start(bf16[2,512,1024]{2,1,0:T(8,128)(2,1)} %collective-permute-done.3.refs_3_), channel_id=1, source_target_pairs={{0,1},{1,0},{2,3},{3,2},{4,5},{5,4},{6,7},{7,6},{8,9},{9,8},{10,11... | collective-permute-start | bytes 6291464 | tf_op jit(solution)/shard_map/ppermute | solution.py:512
  52.0 48.4 %collective-permute-start.12 = (bf16[2,512,1024]{2,1,0:T(8,128)(2,1)}, bf16[2,512,1024]{2,1,0:T(8,128)(2,1)}, u32[]{:S(2)}, u32[]{:S(2)}) collective-permute-start(bf16[2,512,1024]{2,1,0:T(8,128)(2,1)} %collective-permute-done.3.refs_3_), channel_id=1, source_target_pairs={{0,16},{16,0},{1,17},{17,1},{2,18},{18,2},{3,19},{19,3},{4,20},{20... | collective-permute-start | bytes 6291464 | tf_op jit(solution)/shard_map/ppermute | solution.py:512
  53.8 48.1 %collective-permute-start.13 = (bf16[1024,1024]{1,0:T(8,128)(2,1)}, bf16[1024,1024]{1,0:T(8,128)(2,1)}, u32[]{:S(2)}, u32[]{:S(2)}) collective-permute-start(bf16[1024,1024]{1,0:T(8,128)(2,1)} %constant_dynamic-slice_fusion.1), channel_id=1, source_target_pairs={{0,2},{2,0},{1,3},{3,1},{4,6},{6,4},{5,7},{7,5},{8,10},{10,8},{9,1... | collective-permute-start | bytes 6291464 | tf_op jit(solution)/shard_map/ppermute | solution.py:512
  55.3 5.6 %copy-start.6 = (f32[17,1024]{1,0:T(8,128)S(1)}, f32[17,1024]{1,0:T(8,128)}, u32[]{:S(2)}) copy-start(f32[17,1024]{1,0:T(8,128)} %mix_ref.1) | copy-start | bytes 208900
  55.3 5.6 %copy-start.7 = (f32[2,1024]{1,0:T(2,128)S(1)}, f32[2,1024]{1,0:T(2,128)}, u32[]{:S(2)}) copy-start(f32[2,1024]{1,0:T(2,128)} %high_ref.1) | copy-start | bytes 24580
  55.3 5.6 %copy-start.8 = (f32[1024]{0:T(1024)S(1)}, f32[1024]{0:T(1024)}, u32[]{:S(2)}) copy-start(f32[1024]{0:T(1024)} %param.8) | copy-start | bytes 12292
  57.5 0.8 copy-start.4
  58.2 2.7 %collective-permute-start.5 = (bf16[3,1024,128]{2,1,0:T(8,128)(2,1)}, bf16[3,1024,128]{2,1,0:T(8,128)(2,1)S(1)}, u32[]{:S(2)}, u32[]{:S(2)}) collective-permute-start(bf16[3,1024,128]{2,1,0:T(8,128)(2,1)} %others.1), channel_id=1, source_target_pairs={{0,1},{1,0},{2,3},{3,2},{4,5},{5,4},{6,7},{7,6},{8,9},{9,8},{10,11... | collective-permute-start | bytes 2359304 | tf_op jit(solution)/shard_map/ppermute | solution.py:512
  58.4 2.5 %collective-permute-start.4 = (bf16[1024,128]{1,0:T(8,128)(2,1)S(1)}, bf16[1024,128]{1,0:T(8,128)(2,1)S(1)}, u32[]{:S(2)}, u32[]{:S(2)}) collective-permute-start(bf16[1024,128]{1,0:T(8,128)(2,1)S(1)} %get-tuple-element.159), channel_id=1, source_target_pairs={{0,1},{1,0},{2,3},{3,2},{4,5},{5,4},{6,7},{7,6},{8,9},{9,8},{10,11... | collective-permute-start | bytes 786440 | tf_op jit(solution)/shard_map/ppermute | solution.py:512
  60.9 1.0 copy-start.5
  62.0 53.1 %copy-start.3 = (bf16[2048,1024]{1,0:T(8,128)(2,1)S(1)}, bf16[2048,1024]{1,0:T(8,128)(2,1)}, u32[]{:S(2)}) copy-start(bf16[2048,1024]{1,0:T(8,128)(2,1)} %refs_2_.2) | copy-start | bytes 12582916
  75.2 2.0 %collective-permute-start.6 = (bf16[4,512,128]{2,1,0:T(8,128)(2,1)S(1)}, bf16[4,512,128]{2,1,0:T(8,128)(2,1)S(1)}, u32[]{:S(2)}, u32[]{:S(2)}) collective-permute-start(bf16[4,512,128]{2,1,0:T(8,128)(2,1)S(1)} %get-tuple-element.93), channel_id=1, source_target_pairs={{0,1},{1,0},{2,3},{3,2},{4,5},{5,4},{6,7},{7,6},{8,9},{9,8},{10,11... | collective-permute-start | bytes 1572872 | tf_op jit(solution)/shard_map/ppermute | solution.py:512
  75.4 2.5 %collective-permute-start.7 = (bf16[4,512,128]{2,1,0:T(8,128)(2,1)S(1)}, bf16[4,512,128]{2,1,0:T(8,128)(2,1)S(1)}, u32[]{:S(2)}, u32[]{:S(2)}) collective-permute-start(bf16[4,512,128]{2,1,0:T(8,128)(2,1)S(1)} %get-tuple-element.94), channel_id=1, source_target_pairs={{0,1},{1,0},{2,3},{3,2},{4,5},{5,4},{6,7},{7,6},{8,9},{9,8},{10,11... | collective-permute-start | bytes 1572872 | tf_op jit(solution)/shard_map/ppermute | solution.py:512
  78.1 23.8 %collective-permute-start.10 = (bf16[2,512,128]{2,1,0:T(8,128)(2,1)S(1)}, bf16[2,512,128]{2,1,0:T(8,128)(2,1)S(1)}, u32[]{:S(2)}, u32[]{:S(2)}) collective-permute-start(bf16[2,512,128]{2,1,0:T(8,128)(2,1)S(1)} %get-tuple-element.104), channel_id=1, source_target_pairs={{0,8},{4,12},{8,0},{12,4},{1,9},{5,13},{9,1},{13,5},{2,10},{6,14},... | collective-permute-start | bytes 786440 | tf_op jit(solution)/shard_map/ppermute | solution.py:517
  81.1 20.8 %collective-permute-start.11 = (bf16[2,512,128]{2,1,0:T(8,128)(2,1)S(1)}, bf16[2,512,128]{2,1,0:T(8,128)(2,1)S(1)}, u32[]{:S(2)}, u32[]{:S(2)}) collective-permute-start(bf16[2,512,128]{2,1,0:T(8,128)(2,1)S(1)} %get-tuple-element.105), channel_id=1, source_target_pairs={{0,12},{4,0},{8,4},{12,8},{1,13},{5,1},{9,5},{13,9},{2,14},{6,2},{... | collective-permute-start | bytes 786440 | tf_op jit(solution)/shard_map/ppermute | solution.py:517
  84.5 17.7 %collective-permute-start.9 = (bf16[2,512,128]{2,1,0:T(8,128)(2,1)S(1)}, bf16[2,512,128]{2,1,0:T(8,128)(2,1)S(1)}, u32[]{:S(2)}, u32[]{:S(2)}) collective-permute-start(bf16[2,512,128]{2,1,0:T(8,128)(2,1)S(1)} %get-tuple-element.103), channel_id=1, source_target_pairs={{0,4},{4,8},{8,12},{12,0},{1,5},{5,9},{9,13},{13,1},{2,6},{6,10},{... | collective-permute-start | bytes 786440 | tf_op jit(solution)/shard_map/ppermute | solution.py:517
  102.2 12.9 %collective-permute-start.15 = (bf16[2,256,128]{2,1,0:T(8,128)(2,1)S(1)}, bf16[2,256,128]{2,1,0:T(8,128)(2,1)S(1)}, u32[]{:S(2)}, u32[]{:S(2)}) collective-permute-start(bf16[2,256,128]{2,1,0:T(8,128)(2,1)S(1)} %get-tuple-element.111), channel_id=1, source_target_pairs={{0,8},{4,12},{8,0},{12,4},{1,9},{5,13},{9,1},{13,5},{2,10},{6,14},... | collective-permute-start | bytes 393224 | tf_op jit(solution)/shard_map/ppermute | solution.py:517
  107.2 7.8 %copy-start.2 = (bf16[2048,1024]{1,0:T(8,128)(2,1)S(1)}, bf16[2048,1024]{1,0:T(8,128)(2,1)}, u32[]{:S(2)}) copy-start(bf16[2048,1024]{1,0:T(8,128)(2,1)} %refs_1_.1) | copy-start | bytes 12582916
  107.5 13.6 %collective-permute-start.17 = (bf16[4,2,256,128]{3,2,1,0:T(8,128)(2,1)S(1)}, bf16[4,2,256,128]{3,2,1,0:T(8,128)(2,1)S(1)}, u32[]{:S(2)}, u32[]{:S(2)}) collective-permute-start(bf16[4,2,256,128]{3,2,1,0:T(8,128)(2,1)S(1)} %get-tuple-element.122), channel_id=1, source_target_pairs={{0,2},{2,0},{1,3},{3,1},{4,6},{6,4},{5,7},{7,5},{8,10},{10,8},{9,1... | collective-permute-start | bytes 1572872 | tf_op jit(solution)/shard_map/ppermute | solution.py:512
  109.0 10.6 %collective-permute-start.16 = (bf16[2,256,128]{2,1,0:T(8,128)(2,1)S(1)}, bf16[2,256,128]{2,1,0:T(8,128)(2,1)S(1)}, u32[]{:S(2)}, u32[]{:S(2)}) collective-permute-start(bf16[2,256,128]{2,1,0:T(8,128)(2,1)S(1)} %get-tuple-element.116), channel_id=1, source_target_pairs={{0,12},{4,0},{8,4},{12,8},{1,13},{5,1},{9,5},{13,9},{2,14},{6,2},{... | collective-permute-start | bytes 393224 | tf_op jit(solution)/shard_map/ppermute | solution.py:517
  110.0 9.6 %collective-permute-start.14 = (bf16[2,256,128]{2,1,0:T(8,128)(2,1)S(1)}, bf16[2,256,128]{2,1,0:T(8,128)(2,1)S(1)}, u32[]{:S(2)}, u32[]{:S(2)}) collective-permute-start(bf16[2,256,128]{2,1,0:T(8,128)(2,1)S(1)} %get-tuple-element.108), channel_id=1, source_target_pairs={{0,4},{4,8},{8,12},{12,0},{1,5},{5,9},{9,13},{13,1},{2,6},{6,10},{... | collective-permute-start | bytes 393224 | tf_op jit(solution)/shard_map/ppermute | solution.py:517
  115.0 6.1 %collective-permute-start.18 = (bf16[2,512,1024]{2,1,0:T(8,128)(2,1)}, bf16[2,512,1024]{2,1,0:T(8,128)(2,1)S(1)}, u32[]{:S(2)}, u32[]{:S(2)}) collective-permute-start(bf16[2,512,1024]{2,1,0:T(8,128)(2,1)} %collective-permute-done.12.refs_4_), channel_id=1, source_target_pairs={{0,1},{1,0},{2,3},{3,2},{4,5},{5,4},{6,7},{7,6},{8,9},{9,8},{10,11... | collective-permute-start | bytes 6291464 | tf_op jit(solution)/shard_map/ppermute | solution.py:512
  121.1 11.5 %collective-permute-start.23 = (bf16[1024,1024]{1,0:T(8,128)(2,1)}, bf16[1024,1024]{1,0:T(8,128)(2,1)S(1)}, u32[]{:S(2)}, u32[]{:S(2)}) collective-permute-start(bf16[1024,1024]{1,0:T(8,128)(2,1)} %collective-permute-done.13.mine), channel_id=1, source_target_pairs={{0,1},{1,0},{2,3},{3,2},{4,5},{5,4},{6,7},{7,6},{8,9},{9,8},{10,11... | collective-permute-start | bytes 6291464 | tf_op jit(solution)/shard_map/ppermute | solution.py:512
  121.1 14.8 %collective-permute-start.22 = (bf16[4,2,256,128]{3,2,1,0:T(8,128)(2,1)S(1)}, bf16[4,2,256,128]{3,2,1,0:T(8,128)(2,1)S(1)}, u32[]{:S(2)}, u32[]{:S(2)}) collective-permute-start(bf16[4,2,256,128]{3,2,1,0:T(8,128)(2,1)S(1)} %get-tuple-element.137), channel_id=1, source_target_pairs={{0,2},{2,0},{1,3},{3,1},{4,6},{6,4},{5,7},{7,5},{8,10},{10,8},{9,1... | collective-permute-start | bytes 1572872 | tf_op jit(solution)/shard_map/ppermute | solution.py:512
  123.6 12.3 %collective-permute-start.21 = (bf16[2,256,128]{2,1,0:T(8,128)(2,1)S(1)}, bf16[2,256,128]{2,1,0:T(8,128)(2,1)S(1)}, u32[]{:S(2)}, u32[]{:S(2)}) collective-permute-start(bf16[2,256,128]{2,1,0:T(8,128)(2,1)S(1)} %get-tuple-element.136), channel_id=1, source_target_pairs={{0,12},{4,0},{8,4},{12,8},{1,13},{5,1},{9,5},{13,9},{2,14},{6,2},{... | collective-permute-start | bytes 393224 | tf_op jit(solution)/shard_map/ppermute | solution.py:517
  125.9 11.2 %collective-permute-start.20 = (bf16[2,256,128]{2,1,0:T(8,128)(2,1)S(1)}, bf16[2,256,128]{2,1,0:T(8,128)(2,1)S(1)}, u32[]{:S(2)}, u32[]{:S(2)}) collective-permute-start(bf16[2,256,128]{2,1,0:T(8,128)(2,1)S(1)} %get-tuple-element.133), channel_id=1, source_target_pairs={{0,8},{4,12},{8,0},{12,4},{1,9},{5,13},{9,1},{13,5},{2,10},{6,14},... | collective-permute-start | bytes 393224 | tf_op jit(solution)/shard_map/ppermute | solution.py:517
  125.9 11.2 %collective-permute-start.19 = (bf16[2,256,128]{2,1,0:T(8,128)(2,1)S(1)}, bf16[2,256,128]{2,1,0:T(8,128)(2,1)S(1)}, u32[]{:S(2)}, u32[]{:S(2)}) collective-permute-start(bf16[2,256,128]{2,1,0:T(8,128)(2,1)S(1)} %get-tuple-element.130), channel_id=1, source_target_pairs={{0,4},{4,8},{8,12},{12,0},{1,5},{5,9},{9,13},{13,1},{2,6},{6,10},{... | collective-permute-start | bytes 393224 | tf_op jit(solution)/shard_map/ppermute | solution.py:517
  137.1 13.6 %collective-permute-start.25 = (bf16[256,1024]{1,0:T(8,128)(2,1)S(1)}, bf16[256,1024]{1,0:T(8,128)(2,1)S(1)}, u32[]{:S(2)}, u32[]{:S(2)}) collective-permute-start(bf16[256,1024]{1,0:T(8,128)(2,1)S(1)} %send.2), channel_id=1, source_target_pairs={{0,2},{2,0},{1,3},{3,1},{4,6},{6,4},{5,7},{7,5},{8,10},{10,8},{9,1... | collective-permute-start | bytes 1572872 | tf_op jit(solution)/shard_map/ppermute | solution.py:512
  144.9 5.8 %copy-start.1 = (bf16[2048,1024]{1,0:T(8,128)(2,1)S(1)}, bf16[2048,1024]{1,0:T(8,128)(2,1)}, u32[]{:S(2)}) copy-start(bf16[2048,1024]{1,0:T(8,128)(2,1)} %refs_2_.3) | copy-start | bytes 12582916
  148.4 13.1 %collective-permute-start.24 = (bf16[256,1024]{1,0:T(8,128)(2,1)S(1)}, bf16[256,1024]{1,0:T(8,128)(2,1)S(1)}, u32[]{:S(2)}, u32[]{:S(2)}) collective-permute-start(bf16[256,1024]{1,0:T(8,128)(2,1)S(1)} %send.3), channel_id=1, source_target_pairs={{0,2},{2,0},{1,3},{3,1},{4,6},{6,4},{5,7},{7,5},{8,10},{10,8},{9,1... | collective-permute-start | bytes 1572872 | tf_op jit(solution)/shard_map/ppermute | solution.py:512

commit v7 on v6

--- a/solution.py
+++ b/solution.py
@@ -580,7 +580,7 @@
     depth = w_value.shape[0] // 4
     half = lax.dynamic_slice_in_dim(out_piece, core * 2 * depth, 2 * depth, 0)
     pair_first = swap(pair, "chan")
-    direct, pair_first, half = lax.optimization_barrier((direct, pair_first, half))
+    direct[2], pair_first, half = lax.optimization_barrier((direct[2], pair_first, half))
     pair_second = swap(pair_first, "groups")
     half_first = swap(half, "chan")
     pair_third = swap(pair_first, "sub")

time: 164 us -> 163 us (level)
  starting transfers between devices: 35.4 us -> 32.3 us
    ppermute x14, starting transfers between devices: 13.5 us -> 10.7 us  [swap(): return lax.ppermute(array, axis, [(0, 1), (1, 0)])]
  transfers between devices with their start and end apart: 26 -> 26, of which waited for: 14 -> 12; matrix products, arithmetic and copies ran while one was open for 3% -> 3% of each run, Pallas kernels for 24% -> 24%
where the time goes in v7:
time: 163 us; the launch traced here: 162 us
  waiting for transfers between devices  71.7 us (44%)
  Pallas kernels  50.8 us (31%)
  starting transfers between devices  32.3 us (20%)
  local copies, waits for them, and re-layouts  7.12 us (4%)
    ppermute x14, waiting for transfers between devices, swap(): return lax.ppermute(array, axis, [(0, 1), (1, 0)])  36.3 us
    ppermute x12, waiting for transfers between devices, ahead(): lax.ppermute(array, 'seq', [(j, (j + offset) % chips) for j in range(chip...  35.5 us
    ppermute x12, starting transfers between devices, ahead(): lax.ppermute(array, 'seq', [(j, (j + offset) % chips) for j in range(chip...  21.6 us
    pallas_call x1, Pallas kernels, run_filter(): pl.pallas_call(functools.partial(levels_kernel, live, chips), out_shape=[...  13.2 us
    pallas_call x2, Pallas kernels, run_hidden(): pl.pallas_call(functools.partial(hidden_kernel, chips, min(512, channels)...  12.2 us
    ppermute x14, starting transfers between devices, swap(): return lax.ppermute(array, axis, [(0, 1), (1, 0)])  10.7 us
    pallas_call x2, Pallas kernels, run_send(): pl.pallas_call(send_kernel, grid_spec=pltpu.PrefetchScalarGridSpec(num_sc...  6.77 us
    pallas_call x1, Pallas kernels, run_load(): pl.pallas_call(functools.partial(load_kernel, count), in_specs=[smem] + [...  4.6 us
  transfers between devices with their start and end apart: 26, of which 12 were waited for; matrix products, arithmetic and copies ran while one was open for 3% of the time, Pallas kernels for 24%

profile of v7, /device:TPU:0, one launch (start us, length us, event | category | flops | bytes accessed | tf_op | source)
XLA Modules:
  0.0 162.3 jit_solution(6908505730991526258)
XLA Ops:
  0.0 3.0 %pair.1 = bf16[2,512,1024]{2,1,0:T(8,128)(2,1)} custom-call(bf16[2048,1024]{1,0:T(8,128)(2,1)} %refs_1_.1, bf16[2048,1024]{1,0:T(8,128)(2,1)} %refs_2_.2), custom_call_target="tpu_custom_call" | custom-call | tf_op jit(solution)/shard_map/pair/pallas_call | solution.py:136
  3.0 3.0 %collective-permute-start.2 = (bf16[2,512,1024]{2,1,0:T(8,128)(2,1)}, bf16[2,512,1024]{2,1,0:T(8,128)(2,1)}, u32[]{:S(2)}, u32[]{:S(2)}) collective-permute-start(bf16[2,512,1024]{2,1,0:T(8,128)(2,1)} %pair.1), channel_id=1, source_target_pairs={{0,2},{2,0},{1,3},{3,1},{4,6},{6,4},{5,7},{7,5},{8,10},{10,8},{9,1... | collective-permute-start | bytes 6291464 | tf_op jit(solution)/shard_map/ppermute | solution.py:512
  6.1 1.2 constant_dynamic-slice_fusion.2
  7.3 2.6 %collective-permute-start.1 = (bf16[1024,256]{1,0:T(8,128)(2,1)}, bf16[1024,256]{1,0:T(8,128)(2,1)S(1)}, u32[]{:S(2)}, u32[]{:S(2)}) collective-permute-start(bf16[1024,256]{1,0:T(8,128)(2,1)} %get-tuple-element.82), channel_id=1, source_target_pairs={{0,8},{4,12},{8,0},{12,4},{1,9},{5,13},{9,1},{13,5},{2,10},{6,14},... | collective-permute-start | bytes 1572872 | tf_op jit(solution)/shard_map/ppermute | solution.py:517
  9.9 1.6 collective-permute-start
  11.4 2.2 %collective-permute-start.3 = (bf16[1024,256]{1,0:T(8,128)(2,1)}, bf16[1024,256]{1,0:T(8,128)(2,1)}, u32[]{:S(2)}, u32[]{:S(2)}) collective-permute-start(bf16[1024,256]{1,0:T(8,128)(2,1)} %get-tuple-element.86), channel_id=1, source_target_pairs={{0,12},{4,0},{8,4},{12,8},{1,13},{5,1},{9,5},{13,9},{2,14},{6,2},{... | collective-permute-start | bytes 1572872 | tf_op jit(solution)/shard_map/ppermute | solution.py:517
  13.7 3.2 %constant_dynamic-slice_fusion.1 = bf16[1024,1024]{1,0:T(8,128)(2,1)} fusion(bf16[2048,1024]{1,0:T(8,128)(2,1)} %refs_2_.3, s32[]{:T(128)S(6)} %select_n.47), kind=kLoop, calls=%fused_computation.11 | loop fusion | bytes 4194308 | tf_op jit(solution)/shard_map/dynamic_slice | solution.py:581
  16.8 28.6 %collective-permute-done.1.refs_1_ = bf16[1024,256]{1,0:T(8,128)(2,1)S(1)} collective-permute-done((bf16[1024,256]{1,0:T(8,128)(2,1)}, bf16[1024,256]{1,0:T(8,128)(2,1)S(1)}, u32[]{:S(2)}, u32[]{:S(2)}) %collective-permute-start.1) | collective-permute-done | bytes 524320 | tf_op jit(solution)/shard_map/ppermute | solution.py:517
  45.4 6.6 %collective-permute-done.2.refs_3_ = bf16[2,512,1024]{2,1,0:T(8,128)(2,1)} collective-permute-done((bf16[2,512,1024]{2,1,0:T(8,128)(2,1)}, bf16[2,512,1024]{2,1,0:T(8,128)(2,1)}, u32[]{:S(2)}, u32[]{:S(2)}) %collective-permute-start.2) | collective-permute-done | bytes 2097184 | tf_op jit(solution)/shard_map/ppermute | solution.py:512
  52.0 1.8 %collective-permute-start.12 = (bf16[2,512,1024]{2,1,0:T(8,128)(2,1)}, bf16[2,512,1024]{2,1,0:T(8,128)(2,1)}, u32[]{:S(2)}, u32[]{:S(2)}) collective-permute-start(bf16[2,512,1024]{2,1,0:T(8,128)(2,1)} %collective-permute-done.2.refs_3_), channel_id=1, source_target_pairs={{0,16},{16,0},{1,17},{17,1},{2,18},{18,2},{3,19},{19,3},{4,20},{20... | collective-permute-start | bytes 6291464 | tf_op jit(solution)/shard_map/ppermute | solution.py:512
  53.8 1.5 collective-permute-start.13
  55.4 2.1 %others.1 = bf16[3,1024,128]{2,1,0:T(8,128)(2,1)} custom-call(s32[5]{0:T(128)S(1)} %stack.49.place.refs_0_, bf16[1024,256]{1,0:T(8,128)(2,1)S(1)} %collective-permute-done.refs_0_, bf16[1024,256]{1,0:T(8,128)(2,1)S(1)} %collective-permute-done.1.refs_1_, bf16[1024,256]{1,0:T(8,128)(2,1)} %collective-permute-done.3.refs_2_), custom_call_target="tpu_custom_call" | custom-call | flops 5000000000 | tf_op jit(solution)/shard_map/others/pallas_call | solution.py:545
  57.5 0.8 copy-done.4
  58.4 0.6 collective-permute-start.4
  59.0 1.9 %collective-permute-done.4.refs_3_ = bf16[1024,128]{1,0:T(8,128)(2,1)S(1)} collective-permute-done((bf16[1024,128]{1,0:T(8,128)(2,1)S(1)}, bf16[1024,128]{1,0:T(8,128)(2,1)S(1)}, u32[]{:S(2)}, u32[]{:S(2)}) %collective-permute-start.4) | collective-permute-done | bytes 262176 | tf_op jit(solution)/shard_map/ppermute | solution.py:512
  61.0 1.0 copy-done.5
  62.0 13.2 %levels.1 = (bf16[4,512,128]{2,1,0:T(8,128)(2,1)S(1)}, bf16[4,512,128]{2,1,0:T(8,128)(2,1)S(1)}, bf16[4,512,128]{2,1,0:T(8,128)(2,1)S(1)}, bf16[4,512,128]{2,1,0:T(8,128)(2,1)S(1)}) custom-call(s32[5]{0:T(128)S(1)} %stack.49.place.refs_0_, f32[1,1024]{1,0:T(1,128)S(1)} %bitcast.21, f32[2,1024]{1,0:T(2,128)S(1)} %copy-done.7, f32[17,1024]{1,0:T(8,128)S(1)} %copy-done.6, ...), custom_call_target="tpu_custom_call" | custom-call | tf_op jit(solution)/shard_map/levels/pallas_call | solution.py:248
  75.2 0.2 collective-permute-start.6
  75.4 0.4 collective-permute-start.7
  75.8 1.4 collective-permute-done.6.refs_2_
  77.2 0.7 collective-permute-done.7.refs_3_
  78.1 2.7 %collective-permute-start.10 = (bf16[2,512,128]{2,1,0:T(8,128)(2,1)S(1)}, bf16[2,512,128]{2,1,0:T(8,128)(2,1)S(1)}, u32[]{:S(2)}, u32[]{:S(2)}) collective-permute-start(bf16[2,512,128]{2,1,0:T(8,128)(2,1)S(1)} %get-tuple-element.100), channel_id=1, source_target_pairs={{0,8},{4,12},{8,0},{12,4},{1,9},{5,13},{9,1},{13,5},{2,10},{6,14},... | collective-permute-start | bytes 786440 | tf_op jit(solution)/shard_map/ppermute | solution.py:517
  80.8 1.3 collective-permute-start.11
  82.1 0.7 collective-permute-start.9
  82.8 17.5 %collective-permute-done.12.refs_4_ = bf16[2,512,1024]{2,1,0:T(8,128)(2,1)} collective-permute-done((bf16[2,512,1024]{2,1,0:T(8,128)(2,1)}, bf16[2,512,1024]{2,1,0:T(8,128)(2,1)}, u32[]{:S(2)}, u32[]{:S(2)}) %collective-permute-start.12) | collective-permute-done | bytes 2097184 | tf_op jit(solution)/shard_map/ppermute | solution.py:512
  100.4 1.5 collective-permute-done.13.mine
  101.9 5.1 %collective-permute-start.15 = (bf16[2,256,128]{2,1,0:T(8,128)(2,1)S(1)}, bf16[2,256,128]{2,1,0:T(8,128)(2,1)S(1)}, u32[]{:S(2)}, u32[]{:S(2)}) collective-permute-start(bf16[2,256,128]{2,1,0:T(8,128)(2,1)S(1)} %get-tuple-element.107), channel_id=1, source_target_pairs={{0,8},{4,12},{8,0},{12,4},{1,9},{5,13},{9,1},{13,5},{2,10},{6,14},... | collective-permute-start | bytes 393224 | tf_op jit(solution)/shard_map/ppermute | solution.py:517
  107.2 0.6 collective-permute-start.17
  107.8 0.4 collective-permute-start.16
  108.2 1.6 collective-permute-start.14
  109.8 6.7 %collective-permute-done.15.refs_2_ = bf16[2,256,128]{2,1,0:T(8,128)(2,1)S(1)} collective-permute-done((bf16[2,256,128]{2,1,0:T(8,128)(2,1)S(1)}, bf16[2,256,128]{2,1,0:T(8,128)(2,1)S(1)}, u32[]{:S(2)}, u32[]{:S(2)}) %collective-permute-start.15) | collective-permute-done | bytes 131104 | tf_op jit(solution)/shard_map/ppermute | solution.py:517
  116.6 4.6 %load.1 = (bf16[2048,1024]{1,0:T(8,128)(2,1)S(1)}, bf16[2048,1024]{1,0:T(8,128)(2,1)S(1)}, bf16[2,512,1024]{2,1,0:T(8,128)(2,1)S(1)}, bf16[2,512,1024]{2,1,0:T(8...) custom-call(s32[5]{0:T(128)S(1)} %stack.49.place.refs_0_, bf16[2048,1024]{1,0:T(8,128)(2,1)S(1)} %copy-done.2, ...), custom_call_target="tpu_custom_call" | custom-call | flops 99999997952 | tf_op jit(solution)/shard_map/load/pallas_call | solution.py:318
  121.2 0.6 collective-permute-start.23
  121.8 2.8 %collective-permute-start.21 = (bf16[2,256,128]{2,1,0:T(8,128)(2,1)S(1)}, bf16[2,256,128]{2,1,0:T(8,128)(2,1)S(1)}, u32[]{:S(2)}, u32[]{:S(2)}) collective-permute-start(bf16[2,256,128]{2,1,0:T(8,128)(2,1)S(1)} %get-tuple-element.132), channel_id=1, source_target_pairs={{0,12},{4,0},{8,4},{12,8},{1,13},{5,1},{9,5},{13,9},{2,14},{6,2},{... | collective-permute-start | bytes 393224 | tf_op jit(solution)/shard_map/ppermute | solution.py:517
  124.6 0.6 collective-permute-start.19
  125.1 6.1 %hidden.2.refs_0_ = bf16[256,2048]{1,0:T(8,128)(2,1)S(1)} custom-call(s32[5]{0:T(128)S(1)} %get-tuple-element.122.place, bf16[2,256,128]{2,1,0:T(8,128)(2,1)S(1)} %get-tuple-element.134.refs_0_, bf16[2,256,128]{2,1,0:T(8,128)(2,1)S(1)} %collective-permute-done.14.refs_1_, bf16[2,256,128]{2,1,0:T(8,128)(2,1)S(1)} %collective-permute-done.15.refs_2_, ...), custom_call_target="tpu_custom_call" | custom-call | flops 4294967296 | bytes 19922944 | tf_op jit(solution)/shard_map/hidden/pallas_call | solution.py:379
  131.3 3.3 %send.2 = bf16[256,1024]{1,0:T(8,128)(2,1)S(1)} custom-call(s32[5]{0:T(128)S(1)} %get-tuple-element.122.place, bf16[256,2048]{1,0:T(8,128)(2,1)S(1)} %hidden.2.refs_0_, bf16[1024,1024]{1,0:T(8,128)(2,1)} %collective-permute-done.13.mine, bf16[1024,1024]{1,0:T(8,128)(2,1)S(1)} %collective-permute-done.23.twin), custom_call_target="tpu_custom_call" | custom-call | flops 1073741824 | bytes 5767168 | tf_op jit(solution)/shard_map/send/pallas_call | solution.py:411
  134.5 1.2 collective-permute-done.22.refs_4_
  135.8 0.6 collective-permute-start.25
  136.4 6.1 %hidden.3.refs_1_ = bf16[256,2048]{1,0:T(8,128)(2,1)S(1)} custom-call(s32[5]{0:T(128)S(1)} %get-tuple-element.122.place, bf16[2,256,128]{2,1,0:T(8,128)(2,1)S(1)} %get-tuple-element.146.refs_0_, bf16[2,256,128]{2,1,0:T(8,128)(2,1)S(1)} %collective-permute-done.19.refs_1_, bf16[2,256,128]{2,1,0:T(8,128)(2,1)S(1)} %collective-permute-done.20.refs_2_, ...), custom_call_target="tpu_custom_call" | custom-call | flops 4294967296 | bytes 19922944 | tf_op jit(solution)/shard_map/hidden/pallas_call | solution.py:379
  142.5 3.5 %send.3 = bf16[256,1024]{1,0:T(8,128)(2,1)S(1)} custom-call(s32[5]{0:T(128)S(1)} %get-tuple-element.122.place, bf16[256,2048]{1,0:T(8,128)(2,1)S(1)} %hidden.3.refs_1_, bf16[1024,1024]{1,0:T(8,128)(2,1)} %collective-permute-done.13.mine, bf16[1024,1024]{1,0:T(8,128)(2,1)S(1)} %collective-permute-done.23.twin), custom_call_target="tpu_custom_call" | custom-call | flops 1073741824 | bytes 5767168 | tf_op jit(solution)/shard_map/send/pallas_call | solution.py:411
  146.0 1.5 collective-permute-start.24
  147.6 0.6 slice.31.side
  148.1 1.7 %collective-permute-done.25.got = bf16[256,1024]{1,0:T(8,128)(2,1)S(1)} collective-permute-done((bf16[256,1024]{1,0:T(8,128)(2,1)S(1)}, bf16[256,1024]{1,0:T(8,128)(2,1)S(1)}, u32[]{:S(2)}, u32[]{:S(2)}) %collective-permute-start.25) | collective-permute-done | bytes 524320 | tf_op jit(solution)/shard_map/ppermute | solution.py:512
  149.8 4.4 %finish.1.kept = bf16[1024,1024]{1,0:T(8,128)(2,1)} custom-call(s32[1]{0:T(128)} %slice.31.side, bf16[256,2048]{1,0:T(8,128)(2,1)S(1)} %hidden.2.refs_0_, bf16[256,2048]{1,0:T(8,128)(2,1)S(1)} %hidden.3.refs_1_, bf16[2048,1024]{1,0:T(8,128)(2,1)S(1)} %copy-done.1, bf16[1024,1024]{1,0:T(8,128)(2,1)S(1)} %copy-done), custom_call_target="tpu_custom_call" | custom-call | flops 2147483648 | bytes 7340032 | tf_op jit(solution)/shard_map/finish/pallas_call | solution.py:440
  154.2 2.2 %add_far.2.kept = bf16[1024,1024]{1,0:T(8,128)(2,1)} custom-call(s32[1]{0:T(128)} %slice.31.side, bf16[256,1024]{1,0:T(8,128)(2,1)S(1)} %collective-permute-done.25.got, bf16[1024,1024]{1,0:T(8,128)(2,1)S(1)} %copy-done, bf16[1024,1024]{1,0:T(8,128)(2,1)} %finish.1.kept), custom_call_target="tpu_custom_call", output_to_operand_aliasing={{}: (3, {})} | custom-call | tf_op jit(solution)/shard_map/add_far/pallas_call | solution.py:489
  156.4 3.8 %collective-permute-done.24.got = bf16[256,1024]{1,0:T(8,128)(2,1)S(1)} collective-permute-done((bf16[256,1024]{1,0:T(8,128)(2,1)S(1)}, bf16[256,1024]{1,0:T(8,128)(2,1)S(1)}, u32[]{:S(2)}, u32[]{:S(2)}) %collective-permute-start.24) | collective-permute-done | bytes 524320 | tf_op jit(solution)/shard_map/ppermute | solution.py:512
  160.2 2.2 %add_far.3 = bf16[1024,1024]{1,0:T(8,128)(2,1)} custom-call(s32[1]{0:T(128)} %slice.31.side, bf16[256,1024]{1,0:T(8,128)(2,1)S(1)} %collective-permute-done.24.got, bf16[1024,1024]{1,0:T(8,128)(2,1)S(1)} %copy-done, bf16[1024,1024]{1,0:T(8,128)(2,1)} %add_far.2.kept), custom_call_target="tpu_custom_call", output_to_operand_aliasing={{}: (3, {})} | custom-call | tf_op jit(solution)/shard_map/add_far/pallas_call | solution.py:489
  (44 shorter events, 0.7 us)
Async XLA Ops:
  0.0 6.1 %copy-start = (bf16[1024,1024]{1,0:T(8,128)(2,1)S(1)}, bf16[1024,1024]{1,0:T(8,128)(2,1)}, u32[]{:S(2)}) copy-start(bf16[1024,1024]{1,0:T(8,128)(2,1)} %tokens.1) | copy-start | bytes 6291460
  3.0 49.0 %collective-permute-start.2 = (bf16[2,512,1024]{2,1,0:T(8,128)(2,1)}, bf16[2,512,1024]{2,1,0:T(8,128)(2,1)}, u32[]{:S(2)}, u32[]{:S(2)}) collective-permute-start(bf16[2,512,1024]{2,1,0:T(8,128)(2,1)} %pair.1), channel_id=1, source_target_pairs={{0,2},{2,0},{1,3},{3,1},{4,6},{6,4},{5,7},{7,5},{8,10},{10,8},{9,1... | collective-permute-start | bytes 6291464 | tf_op jit(solution)/shard_map/ppermute | solution.py:512
  7.3 38.2 %collective-permute-start.1 = (bf16[1024,256]{1,0:T(8,128)(2,1)}, bf16[1024,256]{1,0:T(8,128)(2,1)S(1)}, u32[]{:S(2)}, u32[]{:S(2)}) collective-permute-start(bf16[1024,256]{1,0:T(8,128)(2,1)} %get-tuple-element.82), channel_id=1, source_target_pairs={{0,8},{4,12},{8,0},{12,4},{1,9},{5,13},{9,1},{13,5},{2,10},{6,14},... | collective-permute-start | bytes 1572872 | tf_op jit(solution)/shard_map/ppermute | solution.py:517
  9.9 45.5 %collective-permute-start = (bf16[1024,256]{1,0:T(8,128)(2,1)}, bf16[1024,256]{1,0:T(8,128)(2,1)S(1)}, u32[]{:S(2)}, u32[]{:S(2)}) collective-permute-start(bf16[1024,256]{1,0:T(8,128)(2,1)} %get-tuple-element.81), channel_id=1, source_target_pairs={{0,4},{4,8},{8,12},{12,0},{1,5},{5,9},{9,13},{13,1},{2,6},{6,10},{... | collective-permute-start | bytes 1572872 | tf_op jit(solution)/shard_map/ppermute | solution.py:517
  11.4 43.9 %collective-permute-start.3 = (bf16[1024,256]{1,0:T(8,128)(2,1)}, bf16[1024,256]{1,0:T(8,128)(2,1)}, u32[]{:S(2)}, u32[]{:S(2)}) collective-permute-start(bf16[1024,256]{1,0:T(8,128)(2,1)} %get-tuple-element.86), channel_id=1, source_target_pairs={{0,12},{4,0},{8,4},{12,8},{1,13},{5,1},{9,5},{13,9},{2,14},{6,2},{... | collective-permute-start | bytes 1572872 | tf_op jit(solution)/shard_map/ppermute | solution.py:517
  52.0 26.1 %collective-permute-start.8 = (bf16[2,512,1024]{2,1,0:T(8,128)(2,1)}, bf16[2,512,1024]{2,1,0:T(8,128)(2,1)}, u32[]{:S(2)}, u32[]{:S(2)}) collective-permute-start(bf16[2,512,1024]{2,1,0:T(8,128)(2,1)} %collective-permute-done.2.refs_3_), channel_id=1, source_target_pairs={{0,1},{1,0},{2,3},{3,2},{4,5},{5,4},{6,7},{7,6},{8,9},{9,8},{10,11... | collective-permute-start | bytes 6291464 | tf_op jit(solution)/shard_map/ppermute | solution.py:512
  52.0 48.4 %collective-permute-start.12 = (bf16[2,512,1024]{2,1,0:T(8,128)(2,1)}, bf16[2,512,1024]{2,1,0:T(8,128)(2,1)}, u32[]{:S(2)}, u32[]{:S(2)}) collective-permute-start(bf16[2,512,1024]{2,1,0:T(8,128)(2,1)} %collective-permute-done.2.refs_3_), channel_id=1, source_target_pairs={{0,16},{16,0},{1,17},{17,1},{2,18},{18,2},{3,19},{19,3},{4,20},{20... | collective-permute-start | bytes 6291464 | tf_op jit(solution)/shard_map/ppermute | solution.py:512
  53.8 48.1 %collective-permute-start.13 = (bf16[1024,1024]{1,0:T(8,128)(2,1)}, bf16[1024,1024]{1,0:T(8,128)(2,1)}, u32[]{:S(2)}, u32[]{:S(2)}) collective-permute-start(bf16[1024,1024]{1,0:T(8,128)(2,1)} %constant_dynamic-slice_fusion.1), channel_id=1, source_target_pairs={{0,2},{2,0},{1,3},{3,1},{4,6},{6,4},{5,7},{7,5},{8,10},{10,8},{9,1... | collective-permute-start | bytes 6291464 | tf_op jit(solution)/shard_map/ppermute | solution.py:512
  55.3 5.6 %copy-start.6 = (f32[17,1024]{1,0:T(8,128)S(1)}, f32[17,1024]{1,0:T(8,128)}, u32[]{:S(2)}) copy-start(f32[17,1024]{1,0:T(8,128)} %mix_ref.1) | copy-start | bytes 208900
  55.3 5.6 %copy-start.7 = (f32[2,1024]{1,0:T(2,128)S(1)}, f32[2,1024]{1,0:T(2,128)}, u32[]{:S(2)}) copy-start(f32[2,1024]{1,0:T(2,128)} %high_ref.1) | copy-start | bytes 24580
  55.3 5.6 %copy-start.8 = (f32[1024]{0:T(1024)S(1)}, f32[1024]{0:T(1024)}, u32[]{:S(2)}) copy-start(f32[1024]{0:T(1024)} %param.8) | copy-start | bytes 12292
  57.5 0.8 copy-start.4
  58.3 2.7 %collective-permute-start.5 = (bf16[3,1024,128]{2,1,0:T(8,128)(2,1)}, bf16[3,1024,128]{2,1,0:T(8,128)(2,1)S(1)}, u32[]{:S(2)}, u32[]{:S(2)}) collective-permute-start(bf16[3,1024,128]{2,1,0:T(8,128)(2,1)} %others.1), channel_id=1, source_target_pairs={{0,1},{1,0},{2,3},{3,2},{4,5},{5,4},{6,7},{7,6},{8,9},{9,8},{10,11... | collective-permute-start | bytes 2359304 | tf_op jit(solution)/shard_map/ppermute | solution.py:512
  58.4 2.5 %collective-permute-start.4 = (bf16[1024,128]{1,0:T(8,128)(2,1)S(1)}, bf16[1024,128]{1,0:T(8,128)(2,1)S(1)}, u32[]{:S(2)}, u32[]{:S(2)}) collective-permute-start(bf16[1024,128]{1,0:T(8,128)(2,1)S(1)} %get-tuple-element.155), channel_id=1, source_target_pairs={{0,1},{1,0},{2,3},{3,2},{4,5},{5,4},{6,7},{7,6},{8,9},{9,8},{10,11... | collective-permute-start | bytes 786440 | tf_op jit(solution)/shard_map/ppermute | solution.py:512
  61.0 1.0 copy-start.5
  62.0 54.6 %copy-start.3 = (bf16[2048,1024]{1,0:T(8,128)(2,1)S(1)}, bf16[2048,1024]{1,0:T(8,128)(2,1)}, u32[]{:S(2)}) copy-start(bf16[2048,1024]{1,0:T(8,128)(2,1)} %refs_2_.2) | copy-start | bytes 12582916
  75.2 2.0 %collective-permute-start.6 = (bf16[4,512,128]{2,1,0:T(8,128)(2,1)S(1)}, bf16[4,512,128]{2,1,0:T(8,128)(2,1)S(1)}, u32[]{:S(2)}, u32[]{:S(2)}) collective-permute-start(bf16[4,512,128]{2,1,0:T(8,128)(2,1)S(1)} %get-tuple-element.89), channel_id=1, source_target_pairs={{0,1},{1,0},{2,3},{3,2},{4,5},{5,4},{6,7},{7,6},{8,9},{9,8},{10,11... | collective-permute-start | bytes 1572872 | tf_op jit(solution)/shard_map/ppermute | solution.py:512
  75.4 2.5 %collective-permute-start.7 = (bf16[4,512,128]{2,1,0:T(8,128)(2,1)S(1)}, bf16[4,512,128]{2,1,0:T(8,128)(2,1)S(1)}, u32[]{:S(2)}, u32[]{:S(2)}) collective-permute-start(bf16[4,512,128]{2,1,0:T(8,128)(2,1)S(1)} %get-tuple-element.90), channel_id=1, source_target_pairs={{0,1},{1,0},{2,3},{3,2},{4,5},{5,4},{6,7},{7,6},{8,9},{9,8},{10,11... | collective-permute-start | bytes 1572872 | tf_op jit(solution)/shard_map/ppermute | solution.py:512
  78.1 23.7 %collective-permute-start.10 = (bf16[2,512,128]{2,1,0:T(8,128)(2,1)S(1)}, bf16[2,512,128]{2,1,0:T(8,128)(2,1)S(1)}, u32[]{:S(2)}, u32[]{:S(2)}) collective-permute-start(bf16[2,512,128]{2,1,0:T(8,128)(2,1)S(1)} %get-tuple-element.100), channel_id=1, source_target_pairs={{0,8},{4,12},{8,0},{12,4},{1,9},{5,13},{9,1},{13,5},{2,10},{6,14},... | collective-permute-start | bytes 786440 | tf_op jit(solution)/shard_map/ppermute | solution.py:517
  80.8 21.0 %collective-permute-start.11 = (bf16[2,512,128]{2,1,0:T(8,128)(2,1)S(1)}, bf16[2,512,128]{2,1,0:T(8,128)(2,1)S(1)}, u32[]{:S(2)}, u32[]{:S(2)}) collective-permute-start(bf16[2,512,128]{2,1,0:T(8,128)(2,1)S(1)} %get-tuple-element.101), channel_id=1, source_target_pairs={{0,12},{4,0},{8,4},{12,8},{1,13},{5,1},{9,5},{13,9},{2,14},{6,2},{... | collective-permute-start | bytes 786440 | tf_op jit(solution)/shard_map/ppermute | solution.py:517
  82.1 19.8 %collective-permute-start.9 = (bf16[2,512,128]{2,1,0:T(8,128)(2,1)S(1)}, bf16[2,512,128]{2,1,0:T(8,128)(2,1)S(1)}, u32[]{:S(2)}, u32[]{:S(2)}) collective-permute-start(bf16[2,512,128]{2,1,0:T(8,128)(2,1)S(1)} %get-tuple-element.99), channel_id=1, source_target_pairs={{0,4},{4,8},{8,12},{12,0},{1,5},{5,9},{9,13},{13,1},{2,6},{6,10},{... | collective-permute-start | bytes 786440 | tf_op jit(solution)/shard_map/ppermute | solution.py:517
  101.9 14.7 %collective-permute-start.15 = (bf16[2,256,128]{2,1,0:T(8,128)(2,1)S(1)}, bf16[2,256,128]{2,1,0:T(8,128)(2,1)S(1)}, u32[]{:S(2)}, u32[]{:S(2)}) collective-permute-start(bf16[2,256,128]{2,1,0:T(8,128)(2,1)S(1)} %get-tuple-element.107), channel_id=1, source_target_pairs={{0,8},{4,12},{8,0},{12,4},{1,9},{5,13},{9,1},{13,5},{2,10},{6,14},... | collective-permute-start | bytes 393224 | tf_op jit(solution)/shard_map/ppermute | solution.py:517
  107.0 9.6 %copy-start.2 = (bf16[2048,1024]{1,0:T(8,128)(2,1)S(1)}, bf16[2048,1024]{1,0:T(8,128)(2,1)}, u32[]{:S(2)}) copy-start(bf16[2048,1024]{1,0:T(8,128)(2,1)} %refs_1_.1) | copy-start | bytes 12582916
  107.2 14.0 %collective-permute-start.17 = (bf16[4,2,256,128]{3,2,1,0:T(8,128)(2,1)S(1)}, bf16[4,2,256,128]{3,2,1,0:T(8,128)(2,1)S(1)}, u32[]{:S(2)}, u32[]{:S(2)}) collective-permute-start(bf16[4,2,256,128]{3,2,1,0:T(8,128)(2,1)S(1)} %get-tuple-element.118), channel_id=1, source_target_pairs={{0,2},{2,0},{1,3},{3,1},{4,6},{6,4},{5,7},{7,5},{8,10},{10,8},{9,1... | collective-permute-start | bytes 1572872 | tf_op jit(solution)/shard_map/ppermute | solution.py:512
  107.8 13.4 %collective-permute-start.16 = (bf16[2,256,128]{2,1,0:T(8,128)(2,1)S(1)}, bf16[2,256,128]{2,1,0:T(8,128)(2,1)S(1)}, u32[]{:S(2)}, u32[]{:S(2)}) collective-permute-start(bf16[2,256,128]{2,1,0:T(8,128)(2,1)S(1)} %get-tuple-element.112), channel_id=1, source_target_pairs={{0,12},{4,0},{8,4},{12,8},{1,13},{5,1},{9,5},{13,9},{2,14},{6,2},{... | collective-permute-start | bytes 393224 | tf_op jit(solution)/shard_map/ppermute | solution.py:517
  108.2 13.0 %collective-permute-start.14 = (bf16[2,256,128]{2,1,0:T(8,128)(2,1)S(1)}, bf16[2,256,128]{2,1,0:T(8,128)(2,1)S(1)}, u32[]{:S(2)}, u32[]{:S(2)}) collective-permute-start(bf16[2,256,128]{2,1,0:T(8,128)(2,1)S(1)} %get-tuple-element.104), channel_id=1, source_target_pairs={{0,4},{4,8},{8,12},{12,0},{1,5},{5,9},{9,13},{13,1},{2,6},{6,10},{... | collective-permute-start | bytes 393224 | tf_op jit(solution)/shard_map/ppermute | solution.py:517
  116.6 4.7 %collective-permute-start.18 = (bf16[2,512,1024]{2,1,0:T(8,128)(2,1)}, bf16[2,512,1024]{2,1,0:T(8,128)(2,1)S(1)}, u32[]{:S(2)}, u32[]{:S(2)}) collective-permute-start(bf16[2,512,1024]{2,1,0:T(8,128)(2,1)} %collective-permute-done.12.refs_4_), channel_id=1, source_target_pairs={{0,1},{1,0},{2,3},{3,2},{4,5},{5,4},{6,7},{7,6},{8,9},{9,8},{10,11... | collective-permute-start | bytes 6291464 | tf_op jit(solution)/shard_map/ppermute | solution.py:512
  121.2 10.0 %collective-permute-start.23 = (bf16[1024,1024]{1,0:T(8,128)(2,1)}, bf16[1024,1024]{1,0:T(8,128)(2,1)S(1)}, u32[]{:S(2)}, u32[]{:S(2)}) collective-permute-start(bf16[1024,1024]{1,0:T(8,128)(2,1)} %collective-permute-done.13.mine), channel_id=1, source_target_pairs={{0,1},{1,0},{2,3},{3,2},{4,5},{5,4},{6,7},{7,6},{8,9},{9,8},{10,11... | collective-permute-start | bytes 6291464 | tf_op jit(solution)/shard_map/ppermute | solution.py:512
  121.8 13.9 %collective-permute-start.22 = (bf16[4,2,256,128]{3,2,1,0:T(8,128)(2,1)S(1)}, bf16[4,2,256,128]{3,2,1,0:T(8,128)(2,1)S(1)}, u32[]{:S(2)}, u32[]{:S(2)}) collective-permute-start(bf16[4,2,256,128]{3,2,1,0:T(8,128)(2,1)S(1)} %get-tuple-element.133), channel_id=1, source_target_pairs={{0,2},{2,0},{1,3},{3,1},{4,6},{6,4},{5,7},{7,5},{8,10},{10,8},{9,1... | collective-permute-start | bytes 1572872 | tf_op jit(solution)/shard_map/ppermute | solution.py:512
  121.8 13.9 %collective-permute-start.21 = (bf16[2,256,128]{2,1,0:T(8,128)(2,1)S(1)}, bf16[2,256,128]{2,1,0:T(8,128)(2,1)S(1)}, u32[]{:S(2)}, u32[]{:S(2)}) collective-permute-start(bf16[2,256,128]{2,1,0:T(8,128)(2,1)S(1)} %get-tuple-element.132), channel_id=1, source_target_pairs={{0,12},{4,0},{8,4},{12,8},{1,13},{5,1},{9,5},{13,9},{2,14},{6,2},{... | collective-permute-start | bytes 393224 | tf_op jit(solution)/shard_map/ppermute | solution.py:517
  124.6 11.2 %collective-permute-start.20 = (bf16[2,256,128]{2,1,0:T(8,128)(2,1)S(1)}, bf16[2,256,128]{2,1,0:T(8,128)(2,1)S(1)}, u32[]{:S(2)}, u32[]{:S(2)}) collective-permute-start(bf16[2,256,128]{2,1,0:T(8,128)(2,1)S(1)} %get-tuple-element.129), channel_id=1, source_target_pairs={{0,8},{4,12},{8,0},{12,4},{1,9},{5,13},{9,1},{13,5},{2,10},{6,14},... | collective-permute-start | bytes 393224 | tf_op jit(solution)/shard_map/ppermute | solution.py:517
  124.6 11.2 %collective-permute-start.19 = (bf16[2,256,128]{2,1,0:T(8,128)(2,1)S(1)}, bf16[2,256,128]{2,1,0:T(8,128)(2,1)S(1)}, u32[]{:S(2)}, u32[]{:S(2)}) collective-permute-start(bf16[2,256,128]{2,1,0:T(8,128)(2,1)S(1)} %get-tuple-element.126), channel_id=1, source_target_pairs={{0,4},{4,8},{8,12},{12,0},{1,5},{5,9},{9,13},{13,1},{2,6},{6,10},{... | collective-permute-start | bytes 393224 | tf_op jit(solution)/shard_map/ppermute | solution.py:517
  135.8 14.0 %collective-permute-start.25 = (bf16[256,1024]{1,0:T(8,128)(2,1)S(1)}, bf16[256,1024]{1,0:T(8,128)(2,1)S(1)}, u32[]{:S(2)}, u32[]{:S(2)}) collective-permute-start(bf16[256,1024]{1,0:T(8,128)(2,1)S(1)} %send.2), channel_id=1, source_target_pairs={{0,2},{2,0},{1,3},{3,1},{4,6},{6,4},{5,7},{7,5},{8,10},{10,8},{9,1... | collective-permute-start | bytes 1572872 | tf_op jit(solution)/shard_map/ppermute | solution.py:512
  142.5 7.4 %copy-start.1 = (bf16[2048,1024]{1,0:T(8,128)(2,1)S(1)}, bf16[2048,1024]{1,0:T(8,128)(2,1)}, u32[]{:S(2)}) copy-start(bf16[2048,1024]{1,0:T(8,128)(2,1)} %refs_2_.3) | copy-start | bytes 12582916
  146.0 14.2 %collective-permute-start.24 = (bf16[256,1024]{1,0:T(8,128)(2,1)S(1)}, bf16[256,1024]{1,0:T(8,128)(2,1)S(1)}, u32[]{:S(2)}, u32[]{:S(2)}) collective-permute-start(bf16[256,1024]{1,0:T(8,128)(2,1)S(1)} %send.3), channel_id=1, source_target_pairs={{0,2},{2,0},{1,3},{3,1},{4,6},{6,4},{5,7},{7,5},{8,10},{10,8},{9,1... | collective-permute-start | bytes 1572872 | tf_op jit(solution)/shard_map/ppermute | solution.py:512

commit v8 on v7

--- a/solution.py
+++ b/solution.py
@@ -388,7 +388,6 @@
         ],
         out_shape=jax.ShapeDtypeStruct((rows, width), jnp.bfloat16),
         compiler_params=pltpu.CompilerParams(vmem_limit_bytes=LITTLE),
-        cost_estimate=work(rows, width, 2 * width),
         name="hidden",
     )(place, *direct, got, *weights)
 
@@ -405,21 +404,15 @@
 
 
 def run_send(place, hidden, halves):
-    rows, width = hidden.shape
-    depth, channels = halves[0].shape
-    block = min(512, channels)
+    rows = hidden.shape[0]
+    channels = halves[0].shape[1]
+    in_vmem = pl.BlockSpec(memory_space=pltpu.VMEM)
     return pl.pallas_call(
         send_kernel,
-        grid_spec=pltpu.PrefetchScalarGridSpec(
-            num_scalar_prefetch=1,
-            grid=(channels // block,),
-            in_specs=[pl.BlockSpec((rows, width), lambda j, place: (0, 0))]
-            + [pl.BlockSpec((depth, block), lambda j, place: (0, j))] * 2,
-            out_specs=pl.BlockSpec((rows, block), lambda j, place: (0, j)),
-        ),
+        in_specs=[pl.BlockSpec(memory_space=pltpu.SMEM)] + [in_vmem] * 3,
+        out_specs=in_vmem,
         out_shape=jax.ShapeDtypeStruct((rows, channels), jnp.bfloat16),
         compiler_params=pltpu.CompilerParams(vmem_limit_bytes=LITTLE),
-        cost_estimate=work(rows, width, channels),
         name="send",
     )(place, hidden, *halves)
 
@@ -620,9 +613,6 @@
         return swap(mine, "chan")
 
     got = [exchange(q, half_first) for q in range(SPLIT)]
-    near_got[0][order[0]], pair_second = lax.optimization_barrier(
-        (near_got[0][order[0]], pair_second)
-    )
     pair_fourth = swap(pair_second, "sub")
     loaded, place = run_load(
         place, [w_value, w_gate, pair_first, pair_second, pair_third], far_got[1:]

time: 163 us -> 163 us (level)
    ppermute x14, starting transfers between devices: 10.7 us -> 12.7 us  [swap(): return lax.ppermute(array, axis, [(0, 1), (1, 0)])]
where the time goes in v8:
time: 163 us; the launch traced here: 162 us
  waiting for transfers between devices  71.8 us (44%)
  Pallas kernels  49.9 us (31%)
  starting transfers between devices  33.1 us (20%)
  local copies, waits for them, and re-layouts  7.12 us (4%)
    ppermute x14, waiting for transfers between devices, swap(): return lax.ppermute(array, axis, [(0, 1), (1, 0)])  36.6 us
    ppermute x12, waiting for transfers between devices, ahead(): lax.ppermute(array, 'seq', [(j, (j + offset) % chips) for j in range(chip...  35.1 us
    ppermute x12, starting transfers between devices, ahead(): lax.ppermute(array, 'seq', [(j, (j + offset) % chips) for j in range(chip...  20.4 us
    pallas_call x1, Pallas kernels, run_filter(): pl.pallas_call(functools.partial(levels_kernel, live, chips), out_shape=[...  13.2 us
    ppermute x14, starting transfers between devices, swap(): return lax.ppermute(array, axis, [(0, 1), (1, 0)])  12.7 us
    pallas_call x2, Pallas kernels, run_hidden(): pl.pallas_call(functools.partial(hidden_kernel, chips, min(512, channels)...  12.2 us
    pallas_call x2, Pallas kernels, run_send(): pl.pallas_call(send_kernel, in_specs=[pl.BlockSpec(memory_space=pltpu.SME...  5.87 us
    pallas_call x1, Pallas kernels, run_load(): pl.pallas_call(functools.partial(load_kernel, count), in_specs=[smem] + [...  4.59 us
  transfers between devices with their start and end apart: 26, of which 12 were waited for; matrix products, arithmetic and copies ran while one was open for 3% of the time, Pallas kernels for 24%

profile of v8, /device:TPU:0, one launch (start us, length us, event | category | flops | bytes accessed | tf_op | source)
XLA Modules:
  0.0 162.3 jit_solution(7961151419847647323)
XLA Ops:
  0.0 3.0 %pair.1 = bf16[2,512,1024]{2,1,0:T(8,128)(2,1)} custom-call(bf16[2048,1024]{1,0:T(8,128)(2,1)} %refs_1_.1, bf16[2048,1024]{1,0:T(8,128)(2,1)} %refs_2_.2), custom_call_target="tpu_custom_call" | custom-call | tf_op jit(solution)/shard_map/pair/pallas_call | solution.py:136
  3.0 3.0 %collective-permute-start.2 = (bf16[2,512,1024]{2,1,0:T(8,128)(2,1)}, bf16[2,512,1024]{2,1,0:T(8,128)(2,1)}, u32[]{:S(2)}, u32[]{:S(2)}) collective-permute-start(bf16[2,512,1024]{2,1,0:T(8,128)(2,1)} %pair.1), channel_id=1, source_target_pairs={{0,2},{2,0},{1,3},{3,1},{4,6},{6,4},{5,7},{7,5},{8,10},{10,8},{9,1... | collective-permute-start | bytes 6291464 | tf_op jit(solution)/shard_map/ppermute | solution.py:505
  6.1 1.2 constant_dynamic-slice_fusion.2
  7.3 2.6 %collective-permute-start.1 = (bf16[1024,256]{1,0:T(8,128)(2,1)}, bf16[1024,256]{1,0:T(8,128)(2,1)S(1)}, u32[]{:S(2)}, u32[]{:S(2)}) collective-permute-start(bf16[1024,256]{1,0:T(8,128)(2,1)} %get-tuple-element.80), channel_id=1, source_target_pairs={{0,8},{4,12},{8,0},{12,4},{1,9},{5,13},{9,1},{13,5},{2,10},{6,14},... | collective-permute-start | bytes 1572872 | tf_op jit(solution)/shard_map/ppermute | solution.py:510
  9.9 1.6 collective-permute-start
  11.4 2.2 %collective-permute-start.3 = (bf16[1024,256]{1,0:T(8,128)(2,1)}, bf16[1024,256]{1,0:T(8,128)(2,1)}, u32[]{:S(2)}, u32[]{:S(2)}) collective-permute-start(bf16[1024,256]{1,0:T(8,128)(2,1)} %get-tuple-element.84), channel_id=1, source_target_pairs={{0,12},{4,0},{8,4},{12,8},{1,13},{5,1},{9,5},{13,9},{2,14},{6,2},{... | collective-permute-start | bytes 1572872 | tf_op jit(solution)/shard_map/ppermute | solution.py:510
  13.7 3.2 %constant_dynamic-slice_fusion.1 = bf16[1024,1024]{1,0:T(8,128)(2,1)} fusion(bf16[2048,1024]{1,0:T(8,128)(2,1)} %refs_2_.3, s32[]{:T(128)S(6)} %select_n.47), kind=kLoop, calls=%fused_computation.11 | loop fusion | bytes 4194308 | tf_op jit(solution)/shard_map/dynamic_slice | solution.py:574
  16.8 28.6 %collective-permute-done.1.refs_1_ = bf16[1024,256]{1,0:T(8,128)(2,1)S(1)} collective-permute-done((bf16[1024,256]{1,0:T(8,128)(2,1)}, bf16[1024,256]{1,0:T(8,128)(2,1)S(1)}, u32[]{:S(2)}, u32[]{:S(2)}) %collective-permute-start.1) | collective-permute-done | bytes 524320 | tf_op jit(solution)/shard_map/ppermute | solution.py:510
  45.4 6.6 %collective-permute-done.2.refs_3_ = bf16[2,512,1024]{2,1,0:T(8,128)(2,1)} collective-permute-done((bf16[2,512,1024]{2,1,0:T(8,128)(2,1)}, bf16[2,512,1024]{2,1,0:T(8,128)(2,1)}, u32[]{:S(2)}, u32[]{:S(2)}) %collective-permute-start.2) | collective-permute-done | bytes 2097184 | tf_op jit(solution)/shard_map/ppermute | solution.py:505
  52.0 1.8 %collective-permute-start.12 = (bf16[2,512,1024]{2,1,0:T(8,128)(2,1)}, bf16[2,512,1024]{2,1,0:T(8,128)(2,1)}, u32[]{:S(2)}, u32[]{:S(2)}) collective-permute-start(bf16[2,512,1024]{2,1,0:T(8,128)(2,1)} %collective-permute-done.2.refs_3_), channel_id=1, source_target_pairs={{0,16},{16,0},{1,17},{17,1},{2,18},{18,2},{3,19},{19,3},{4,20},{20... | collective-permute-start | bytes 6291464 | tf_op jit(solution)/shard_map/ppermute | solution.py:505
  53.8 1.5 collective-permute-start.13
  55.4 2.1 %others.1 = bf16[3,1024,128]{2,1,0:T(8,128)(2,1)} custom-call(s32[5]{0:T(128)S(1)} %stack.49.place.refs_0_, bf16[1024,256]{1,0:T(8,128)(2,1)S(1)} %collective-permute-done.refs_0_, bf16[1024,256]{1,0:T(8,128)(2,1)S(1)} %collective-permute-done.1.refs_1_, bf16[1024,256]{1,0:T(8,128)(2,1)} %collective-permute-done.3.refs_2_), custom_call_target="tpu_custom_call" | custom-call | flops 5000000000 | tf_op jit(solution)/shard_map/others/pallas_call | solution.py:538
  57.5 0.8 copy-done.4
  58.4 0.6 collective-permute-start.4
  59.0 1.9 %collective-permute-done.4.refs_3_ = bf16[1024,128]{1,0:T(8,128)(2,1)S(1)} collective-permute-done((bf16[1024,128]{1,0:T(8,128)(2,1)S(1)}, bf16[1024,128]{1,0:T(8,128)(2,1)S(1)}, u32[]{:S(2)}, u32[]{:S(2)}) %collective-permute-start.4) | collective-permute-done | bytes 262176 | tf_op jit(solution)/shard_map/ppermute | solution.py:505
  61.0 1.0 copy-done.5
  62.0 13.2 %levels.1 = (bf16[4,512,128]{2,1,0:T(8,128)(2,1)S(1)}, bf16[4,512,128]{2,1,0:T(8,128)(2,1)S(1)}, bf16[4,512,128]{2,1,0:T(8,128)(2,1)S(1)}, bf16[4,512,128]{2,1,0:T(8,128)(2,1)S(1)}) custom-call(s32[5]{0:T(128)S(1)} %stack.49.place.refs_0_, f32[1,1024]{1,0:T(1,128)S(1)} %bitcast.21, f32[2,1024]{1,0:T(2,128)S(1)} %copy-done.7, f32[17,1024]{1,0:T(8,128)S(1)} %copy-done.6, ...), custom_call_target="tpu_custom_call" | custom-call | tf_op jit(solution)/shard_map/levels/pallas_call | solution.py:248
  75.4 0.4 collective-permute-start.7
  75.8 1.4 collective-permute-done.6.refs_2_
  77.2 0.7 collective-permute-done.7.refs_3_
  78.1 2.7 %collective-permute-start.10 = (bf16[2,512,128]{2,1,0:T(8,128)(2,1)S(1)}, bf16[2,512,128]{2,1,0:T(8,128)(2,1)S(1)}, u32[]{:S(2)}, u32[]{:S(2)}) collective-permute-start(bf16[2,512,128]{2,1,0:T(8,128)(2,1)S(1)} %get-tuple-element.98), channel_id=1, source_target_pairs={{0,8},{4,12},{8,0},{12,4},{1,9},{5,13},{9,1},{13,5},{2,10},{6,14},... | collective-permute-start | bytes 786440 | tf_op jit(solution)/shard_map/ppermute | solution.py:510
  80.8 1.3 collective-permute-start.11
  82.1 0.7 collective-permute-start.9
  82.8 17.5 %collective-permute-done.12.refs_4_ = bf16[2,512,1024]{2,1,0:T(8,128)(2,1)} collective-permute-done((bf16[2,512,1024]{2,1,0:T(8,128)(2,1)}, bf16[2,512,1024]{2,1,0:T(8,128)(2,1)}, u32[]{:S(2)}, u32[]{:S(2)}) %collective-permute-start.12) | collective-permute-done | bytes 2097184 | tf_op jit(solution)/shard_map/ppermute | solution.py:505
  100.4 1.5 collective-permute-done.13.mine
  102.1 1.6 collective-permute-start.17
  103.7 3.6 %collective-permute-start.16 = (bf16[2,256,128]{2,1,0:T(8,128)(2,1)S(1)}, bf16[2,256,128]{2,1,0:T(8,128)(2,1)S(1)}, u32[]{:S(2)}, u32[]{:S(2)}) collective-permute-start(bf16[2,256,128]{2,1,0:T(8,128)(2,1)S(1)} %get-tuple-element.108), channel_id=1, source_target_pairs={{0,12},{4,0},{8,4},{12,8},{1,13},{5,1},{9,5},{13,9},{2,14},{6,2},{... | collective-permute-start | bytes 393224 | tf_op jit(solution)/shard_map/ppermute | solution.py:510
  107.3 0.5 collective-permute-start.15
  107.8 2.0 %collective-permute-start.14 = (bf16[2,256,128]{2,1,0:T(8,128)(2,1)S(1)}, bf16[2,256,128]{2,1,0:T(8,128)(2,1)S(1)}, u32[]{:S(2)}, u32[]{:S(2)}) collective-permute-start(bf16[2,256,128]{2,1,0:T(8,128)(2,1)S(1)} %get-tuple-element.102), channel_id=1, source_target_pairs={{0,4},{4,8},{8,12},{12,0},{1,5},{5,9},{9,13},{13,1},{2,6},{6,10},{... | collective-permute-start | bytes 393224 | tf_op jit(solution)/shard_map/ppermute | solution.py:510
  109.8 4.6 %load.1 = (bf16[2048,1024]{1,0:T(8,128)(2,1)S(1)}, bf16[2048,1024]{1,0:T(8,128)(2,1)S(1)}, bf16[2,512,1024]{2,1,0:T(8,128)(2,1)S(1)}, bf16[2,512,1024]{2,1,0:T(8...) custom-call(s32[5]{0:T(128)S(1)} %stack.49.place.refs_0_, bf16[2048,1024]{1,0:T(8,128)(2,1)S(1)} %copy-done.2, ...), custom_call_target="tpu_custom_call" | custom-call | flops 99999997952 | tf_op jit(solution)/shard_map/load/pallas_call | solution.py:318
  114.4 5.9 %collective-permute-done.15.refs_2_ = bf16[2,256,128]{2,1,0:T(8,128)(2,1)S(1)} collective-permute-done((bf16[2,256,128]{2,1,0:T(8,128)(2,1)S(1)}, bf16[2,256,128]{2,1,0:T(8,128)(2,1)S(1)}, u32[]{:S(2)}, u32[]{:S(2)}) %collective-permute-start.15) | collective-permute-done | bytes 131104 | tf_op jit(solution)/shard_map/ppermute | solution.py:510
  120.5 1.6 collective-permute-start.22
  122.0 1.1 collective-permute-start.20
  123.2 2.0 %collective-permute-start.19 = (bf16[2,256,128]{2,1,0:T(8,128)(2,1)S(1)}, bf16[2,256,128]{2,1,0:T(8,128)(2,1)S(1)}, u32[]{:S(2)}, u32[]{:S(2)}) collective-permute-start(bf16[2,256,128]{2,1,0:T(8,128)(2,1)S(1)} %get-tuple-element.122), channel_id=1, source_target_pairs={{0,4},{4,8},{8,12},{12,0},{1,5},{5,9},{9,13},{13,1},{2,6},{6,10},{... | collective-permute-start | bytes 393224 | tf_op jit(solution)/shard_map/ppermute | solution.py:510
  125.2 6.1 %hidden.2.refs_0_ = bf16[256,2048]{1,0:T(8,128)(2,1)S(1)} custom-call(s32[5]{0:T(128)S(1)} %get-tuple-element.118.place, bf16[2,256,128]{2,1,0:T(8,128)(2,1)S(1)} %get-tuple-element.130.refs_0_, bf16[2,256,128]{2,1,0:T(8,128)(2,1)S(1)} %collective-permute-done.14.refs_1_, bf16[2,256,128]{2,1,0:T(8,128)(2,1)S(1)} %collective-permute-done.15.refs_2_, ...), custom_call_target="tpu_custom_call" | custom-call | tf_op jit(solution)/shard_map/hidden/pallas_call | solution.py:379
  131.3 2.9 %send.2 = bf16[256,1024]{1,0:T(8,128)(2,1)S(1)} custom-call(s32[5]{0:T(128)S(1)} %get-tuple-element.118.place, bf16[256,2048]{1,0:T(8,128)(2,1)S(1)} %hidden.2.refs_0_, bf16[1024,1024]{1,0:T(8,128)(2,1)} %collective-permute-done.13.mine, bf16[1024,1024]{1,0:T(8,128)(2,1)S(1)} %collective-permute-done.23.twin), custom_call_target="tpu_custom_call" | custom-call | tf_op jit(solution)/shard_map/send/pallas_call | solution.py:410
  134.2 0.7 collective-permute-done.22.refs_4_
  134.8 0.6 collective-permute-done.20.refs_2_
  135.4 1.5 collective-permute-start.25
  136.9 6.1 %hidden.3.refs_1_ = bf16[256,2048]{1,0:T(8,128)(2,1)S(1)} custom-call(s32[5]{0:T(128)S(1)} %get-tuple-element.118.place, bf16[2,256,128]{2,1,0:T(8,128)(2,1)S(1)} %get-tuple-element.142.refs_0_, bf16[2,256,128]{2,1,0:T(8,128)(2,1)S(1)} %collective-permute-done.19.refs_1_, bf16[2,256,128]{2,1,0:T(8,128)(2,1)S(1)} %collective-permute-done.20.refs_2_, ...), custom_call_target="tpu_custom_call" | custom-call | tf_op jit(solution)/shard_map/hidden/pallas_call | solution.py:379
  143.0 3.0 %send.3 = bf16[256,1024]{1,0:T(8,128)(2,1)S(1)} custom-call(s32[5]{0:T(128)S(1)} %get-tuple-element.118.place, bf16[256,2048]{1,0:T(8,128)(2,1)S(1)} %hidden.3.refs_1_, bf16[1024,1024]{1,0:T(8,128)(2,1)} %collective-permute-done.13.mine, bf16[1024,1024]{1,0:T(8,128)(2,1)S(1)} %collective-permute-done.23.twin), custom_call_target="tpu_custom_call" | custom-call | tf_op jit(solution)/shard_map/send/pallas_call | solution.py:410
  146.1 0.6 collective-permute-start.24
  146.6 0.6 slice.31.side
  147.2 2.3 %collective-permute-done.25.got = bf16[256,1024]{1,0:T(8,128)(2,1)S(1)} collective-permute-done((bf16[256,1024]{1,0:T(8,128)(2,1)S(1)}, bf16[256,1024]{1,0:T(8,128)(2,1)S(1)}, u32[]{:S(2)}, u32[]{:S(2)}) %collective-permute-start.25) | collective-permute-done | bytes 524320 | tf_op jit(solution)/shard_map/ppermute | solution.py:505
  149.6 4.4 %finish.1.kept = bf16[1024,1024]{1,0:T(8,128)(2,1)} custom-call(s32[1]{0:T(128)} %slice.31.side, bf16[256,2048]{1,0:T(8,128)(2,1)S(1)} %hidden.2.refs_0_, bf16[256,2048]{1,0:T(8,128)(2,1)S(1)} %hidden.3.refs_1_, bf16[2048,1024]{1,0:T(8,128)(2,1)S(1)} %copy-done.1, bf16[1024,1024]{1,0:T(8,128)(2,1)S(1)} %copy-done), custom_call_target="tpu_custom_call" | custom-call | flops 2147483648 | bytes 7340032 | tf_op jit(solution)/shard_map/finish/pallas_call | solution.py:433
  154.0 2.2 %add_far.2.kept = bf16[1024,1024]{1,0:T(8,128)(2,1)} custom-call(s32[1]{0:T(128)} %slice.31.side, bf16[256,1024]{1,0:T(8,128)(2,1)S(1)} %collective-permute-done.25.got, bf16[1024,1024]{1,0:T(8,128)(2,1)S(1)} %copy-done, bf16[1024,1024]{1,0:T(8,128)(2,1)} %finish.1.kept), custom_call_target="tpu_custom_call", output_to_operand_aliasing={{}: (3, {})} | custom-call | tf_op jit(solution)/shard_map/add_far/pallas_call | solution.py:482
  156.1 4.0 %collective-permute-done.24.got = bf16[256,1024]{1,0:T(8,128)(2,1)S(1)} collective-permute-done((bf16[256,1024]{1,0:T(8,128)(2,1)S(1)}, bf16[256,1024]{1,0:T(8,128)(2,1)S(1)}, u32[]{:S(2)}, u32[]{:S(2)}) %collective-permute-start.24) | collective-permute-done | bytes 524320 | tf_op jit(solution)/shard_map/ppermute | solution.py:505
  160.1 2.2 %add_far.3 = bf16[1024,1024]{1,0:T(8,128)(2,1)} custom-call(s32[1]{0:T(128)} %slice.31.side, bf16[256,1024]{1,0:T(8,128)(2,1)S(1)} %collective-permute-done.24.got, bf16[1024,1024]{1,0:T(8,128)(2,1)S(1)} %copy-done, bf16[1024,1024]{1,0:T(8,128)(2,1)} %add_far.2.kept), custom_call_target="tpu_custom_call", output_to_operand_aliasing={{}: (3, {})} | custom-call | tf_op jit(solution)/shard_map/add_far/pallas_call | solution.py:482
  (44 shorter events, 0.9 us)
Async XLA Ops:
  0.0 6.1 %copy-start = (bf16[1024,1024]{1,0:T(8,128)(2,1)S(1)}, bf16[1024,1024]{1,0:T(8,128)(2,1)}, u32[]{:S(2)}) copy-start(bf16[1024,1024]{1,0:T(8,128)(2,1)} %tokens.1) | copy-start | bytes 6291460
  3.0 49.0 %collective-permute-start.2 = (bf16[2,512,1024]{2,1,0:T(8,128)(2,1)}, bf16[2,512,1024]{2,1,0:T(8,128)(2,1)}, u32[]{:S(2)}, u32[]{:S(2)}) collective-permute-start(bf16[2,512,1024]{2,1,0:T(8,128)(2,1)} %pair.1), channel_id=1, source_target_pairs={{0,2},{2,0},{1,3},{3,1},{4,6},{6,4},{5,7},{7,5},{8,10},{10,8},{9,1... | collective-permute-start | bytes 6291464 | tf_op jit(solution)/shard_map/ppermute | solution.py:505
  7.3 38.2 %collective-permute-start.1 = (bf16[1024,256]{1,0:T(8,128)(2,1)}, bf16[1024,256]{1,0:T(8,128)(2,1)S(1)}, u32[]{:S(2)}, u32[]{:S(2)}) collective-permute-start(bf16[1024,256]{1,0:T(8,128)(2,1)} %get-tuple-element.80), channel_id=1, source_target_pairs={{0,8},{4,12},{8,0},{12,4},{1,9},{5,13},{9,1},{13,5},{2,10},{6,14},... | collective-permute-start | bytes 1572872 | tf_op jit(solution)/shard_map/ppermute | solution.py:510
  9.9 45.5 %collective-permute-start = (bf16[1024,256]{1,0:T(8,128)(2,1)}, bf16[1024,256]{1,0:T(8,128)(2,1)S(1)}, u32[]{:S(2)}, u32[]{:S(2)}) collective-permute-start(bf16[1024,256]{1,0:T(8,128)(2,1)} %get-tuple-element.79), channel_id=1, source_target_pairs={{0,4},{4,8},{8,12},{12,0},{1,5},{5,9},{9,13},{13,1},{2,6},{6,10},{... | collective-permute-start | bytes 1572872 | tf_op jit(solution)/shard_map/ppermute | solution.py:510
  11.4 43.9 %collective-permute-start.3 = (bf16[1024,256]{1,0:T(8,128)(2,1)}, bf16[1024,256]{1,0:T(8,128)(2,1)}, u32[]{:S(2)}, u32[]{:S(2)}) collective-permute-start(bf16[1024,256]{1,0:T(8,128)(2,1)} %get-tuple-element.84), channel_id=1, source_target_pairs={{0,12},{4,0},{8,4},{12,8},{1,13},{5,1},{9,5},{13,9},{2,14},{6,2},{... | collective-permute-start | bytes 1572872 | tf_op jit(solution)/shard_map/ppermute | solution.py:510
  52.0 26.1 %collective-permute-start.8 = (bf16[2,512,1024]{2,1,0:T(8,128)(2,1)}, bf16[2,512,1024]{2,1,0:T(8,128)(2,1)}, u32[]{:S(2)}, u32[]{:S(2)}) collective-permute-start(bf16[2,512,1024]{2,1,0:T(8,128)(2,1)} %collective-permute-done.2.refs_3_), channel_id=1, source_target_pairs={{0,1},{1,0},{2,3},{3,2},{4,5},{5,4},{6,7},{7,6},{8,9},{9,8},{10,11... | collective-permute-start | bytes 6291464 | tf_op jit(solution)/shard_map/ppermute | solution.py:505
  52.0 48.4 %collective-permute-start.12 = (bf16[2,512,1024]{2,1,0:T(8,128)(2,1)}, bf16[2,512,1024]{2,1,0:T(8,128)(2,1)}, u32[]{:S(2)}, u32[]{:S(2)}) collective-permute-start(bf16[2,512,1024]{2,1,0:T(8,128)(2,1)} %collective-permute-done.2.refs_3_), channel_id=1, source_target_pairs={{0,16},{16,0},{1,17},{17,1},{2,18},{18,2},{3,19},{19,3},{4,20},{20... | collective-permute-start | bytes 6291464 | tf_op jit(solution)/shard_map/ppermute | solution.py:505
  53.8 48.1 %collective-permute-start.13 = (bf16[1024,1024]{1,0:T(8,128)(2,1)}, bf16[1024,1024]{1,0:T(8,128)(2,1)}, u32[]{:S(2)}, u32[]{:S(2)}) collective-permute-start(bf16[1024,1024]{1,0:T(8,128)(2,1)} %constant_dynamic-slice_fusion.1), channel_id=1, source_target_pairs={{0,2},{2,0},{1,3},{3,1},{4,6},{6,4},{5,7},{7,5},{8,10},{10,8},{9,1... | collective-permute-start | bytes 6291464 | tf_op jit(solution)/shard_map/ppermute | solution.py:505
  55.3 5.6 %copy-start.6 = (f32[17,1024]{1,0:T(8,128)S(1)}, f32[17,1024]{1,0:T(8,128)}, u32[]{:S(2)}) copy-start(f32[17,1024]{1,0:T(8,128)} %mix_ref.1) | copy-start | bytes 208900
  55.3 5.6 %copy-start.7 = (f32[2,1024]{1,0:T(2,128)S(1)}, f32[2,1024]{1,0:T(2,128)}, u32[]{:S(2)}) copy-start(f32[2,1024]{1,0:T(2,128)} %high_ref.1) | copy-start | bytes 24580
  55.3 5.6 %copy-start.8 = (f32[1024]{0:T(1024)S(1)}, f32[1024]{0:T(1024)}, u32[]{:S(2)}) copy-start(f32[1024]{0:T(1024)} %param.8) | copy-start | bytes 12292
  57.5 0.8 copy-start.4
  58.3 2.7 %collective-permute-start.5 = (bf16[3,1024,128]{2,1,0:T(8,128)(2,1)}, bf16[3,1024,128]{2,1,0:T(8,128)(2,1)S(1)}, u32[]{:S(2)}, u32[]{:S(2)}) collective-permute-start(bf16[3,1024,128]{2,1,0:T(8,128)(2,1)} %others.1), channel_id=1, source_target_pairs={{0,1},{1,0},{2,3},{3,2},{4,5},{5,4},{6,7},{7,6},{8,9},{9,8},{10,11... | collective-permute-start | bytes 2359304 | tf_op jit(solution)/shard_map/ppermute | solution.py:505
  58.4 2.5 %collective-permute-start.4 = (bf16[1024,128]{1,0:T(8,128)(2,1)S(1)}, bf16[1024,128]{1,0:T(8,128)(2,1)S(1)}, u32[]{:S(2)}, u32[]{:S(2)}) collective-permute-start(bf16[1024,128]{1,0:T(8,128)(2,1)S(1)} %get-tuple-element.151), channel_id=1, source_target_pairs={{0,1},{1,0},{2,3},{3,2},{4,5},{5,4},{6,7},{7,6},{8,9},{9,8},{10,11... | collective-permute-start | bytes 786440 | tf_op jit(solution)/shard_map/ppermute | solution.py:505
  61.0 1.0 copy-start.5
  62.0 47.8 %copy-start.3 = (bf16[2048,1024]{1,0:T(8,128)(2,1)S(1)}, bf16[2048,1024]{1,0:T(8,128)(2,1)}, u32[]{:S(2)}) copy-start(bf16[2048,1024]{1,0:T(8,128)(2,1)} %refs_2_.2) | copy-start | bytes 12582916
  75.2 2.0 %collective-permute-start.6 = (bf16[4,512,128]{2,1,0:T(8,128)(2,1)S(1)}, bf16[4,512,128]{2,1,0:T(8,128)(2,1)S(1)}, u32[]{:S(2)}, u32[]{:S(2)}) collective-permute-start(bf16[4,512,128]{2,1,0:T(8,128)(2,1)S(1)} %get-tuple-element.87), channel_id=1, source_target_pairs={{0,1},{1,0},{2,3},{3,2},{4,5},{5,4},{6,7},{7,6},{8,9},{9,8},{10,11... | collective-permute-start | bytes 1572872 | tf_op jit(solution)/shard_map/ppermute | solution.py:505
  75.4 2.5 %collective-permute-start.7 = (bf16[4,512,128]{2,1,0:T(8,128)(2,1)S(1)}, bf16[4,512,128]{2,1,0:T(8,128)(2,1)S(1)}, u32[]{:S(2)}, u32[]{:S(2)}) collective-permute-start(bf16[4,512,128]{2,1,0:T(8,128)(2,1)S(1)} %get-tuple-element.88), channel_id=1, source_target_pairs={{0,1},{1,0},{2,3},{3,2},{4,5},{5,4},{6,7},{7,6},{8,9},{9,8},{10,11... | collective-permute-start | bytes 1572872 | tf_op jit(solution)/shard_map/ppermute | solution.py:505
  78.1 23.7 %collective-permute-start.10 = (bf16[2,512,128]{2,1,0:T(8,128)(2,1)S(1)}, bf16[2,512,128]{2,1,0:T(8,128)(2,1)S(1)}, u32[]{:S(2)}, u32[]{:S(2)}) collective-permute-start(bf16[2,512,128]{2,1,0:T(8,128)(2,1)S(1)} %get-tuple-element.98), channel_id=1, source_target_pairs={{0,8},{4,12},{8,0},{12,4},{1,9},{5,13},{9,1},{13,5},{2,10},{6,14},... | collective-permute-start | bytes 786440 | tf_op jit(solution)/shard_map/ppermute | solution.py:510
  80.8 21.0 %collective-permute-start.11 = (bf16[2,512,128]{2,1,0:T(8,128)(2,1)S(1)}, bf16[2,512,128]{2,1,0:T(8,128)(2,1)S(1)}, u32[]{:S(2)}, u32[]{:S(2)}) collective-permute-start(bf16[2,512,128]{2,1,0:T(8,128)(2,1)S(1)} %get-tuple-element.99), channel_id=1, source_target_pairs={{0,12},{4,0},{8,4},{12,8},{1,13},{5,1},{9,5},{13,9},{2,14},{6,2},{... | collective-permute-start | bytes 786440 | tf_op jit(solution)/shard_map/ppermute | solution.py:510
  82.1 19.8 %collective-permute-start.9 = (bf16[2,512,128]{2,1,0:T(8,128)(2,1)S(1)}, bf16[2,512,128]{2,1,0:T(8,128)(2,1)S(1)}, u32[]{:S(2)}, u32[]{:S(2)}) collective-permute-start(bf16[2,512,128]{2,1,0:T(8,128)(2,1)S(1)} %get-tuple-element.97), channel_id=1, source_target_pairs={{0,4},{4,8},{8,12},{12,0},{1,5},{5,9},{9,13},{13,1},{2,6},{6,10},{... | collective-permute-start | bytes 786440 | tf_op jit(solution)/shard_map/ppermute | solution.py:510
  101.9 8.0 %copy-start.2 = (bf16[2048,1024]{1,0:T(8,128)(2,1)S(1)}, bf16[2048,1024]{1,0:T(8,128)(2,1)}, u32[]{:S(2)}) copy-start(bf16[2048,1024]{1,0:T(8,128)(2,1)} %refs_1_.1) | copy-start | bytes 12582916
  102.1 18.3 %collective-permute-start.17 = (bf16[4,2,256,128]{3,2,1,0:T(8,128)(2,1)S(1)}, bf16[4,2,256,128]{3,2,1,0:T(8,128)(2,1)S(1)}, u32[]{:S(2)}, u32[]{:S(2)}) collective-permute-start(bf16[4,2,256,128]{3,2,1,0:T(8,128)(2,1)S(1)} %get-tuple-element.114), channel_id=1, source_target_pairs={{0,2},{2,0},{1,3},{3,1},{4,6},{6,4},{5,7},{7,5},{8,10},{10,8},{9,1... | collective-permute-start | bytes 1572872 | tf_op jit(solution)/shard_map/ppermute | solution.py:505
  103.7 16.7 %collective-permute-start.18 = (bf16[2,512,1024]{2,1,0:T(8,128)(2,1)}, bf16[2,512,1024]{2,1,0:T(8,128)(2,1)S(1)}, u32[]{:S(2)}, u32[]{:S(2)}) collective-permute-start(bf16[2,512,1024]{2,1,0:T(8,128)(2,1)} %collective-permute-done.12.refs_4_), channel_id=1, source_target_pairs={{0,1},{1,0},{2,3},{3,2},{4,5},{5,4},{6,7},{7,6},{8,9},{9,8},{10,11... | collective-permute-start | bytes 6291464 | tf_op jit(solution)/shard_map/ppermute | solution.py:505
  103.7 10.8 %collective-permute-start.16 = (bf16[2,256,128]{2,1,0:T(8,128)(2,1)S(1)}, bf16[2,256,128]{2,1,0:T(8,128)(2,1)S(1)}, u32[]{:S(2)}, u32[]{:S(2)}) collective-permute-start(bf16[2,256,128]{2,1,0:T(8,128)(2,1)S(1)} %get-tuple-element.108), channel_id=1, source_target_pairs={{0,12},{4,0},{8,4},{12,8},{1,13},{5,1},{9,5},{13,9},{2,14},{6,2},{... | collective-permute-start | bytes 393224 | tf_op jit(solution)/shard_map/ppermute | solution.py:510
  107.3 13.1 %collective-permute-start.15 = (bf16[2,256,128]{2,1,0:T(8,128)(2,1)S(1)}, bf16[2,256,128]{2,1,0:T(8,128)(2,1)S(1)}, u32[]{:S(2)}, u32[]{:S(2)}) collective-permute-start(bf16[2,256,128]{2,1,0:T(8,128)(2,1)S(1)} %get-tuple-element.105), channel_id=1, source_target_pairs={{0,8},{4,12},{8,0},{12,4},{1,9},{5,13},{9,1},{13,5},{2,10},{6,14},... | collective-permute-start | bytes 393224 | tf_op jit(solution)/shard_map/ppermute | solution.py:510
  107.8 12.6 %collective-permute-start.14 = (bf16[2,256,128]{2,1,0:T(8,128)(2,1)S(1)}, bf16[2,256,128]{2,1,0:T(8,128)(2,1)S(1)}, u32[]{:S(2)}, u32[]{:S(2)}) collective-permute-start(bf16[2,256,128]{2,1,0:T(8,128)(2,1)S(1)} %get-tuple-element.102), channel_id=1, source_target_pairs={{0,4},{4,8},{8,12},{12,0},{1,5},{5,9},{9,13},{13,1},{2,6},{6,10},{... | collective-permute-start | bytes 393224 | tf_op jit(solution)/shard_map/ppermute | solution.py:510
  120.4 10.9 %collective-permute-start.23 = (bf16[1024,1024]{1,0:T(8,128)(2,1)}, bf16[1024,1024]{1,0:T(8,128)(2,1)S(1)}, u32[]{:S(2)}, u32[]{:S(2)}) collective-permute-start(bf16[1024,1024]{1,0:T(8,128)(2,1)} %collective-permute-done.13.mine), channel_id=1, source_target_pairs={{0,1},{1,0},{2,3},{3,2},{4,5},{5,4},{6,7},{7,6},{8,9},{9,8},{10,11... | collective-permute-start | bytes 6291464 | tf_op jit(solution)/shard_map/ppermute | solution.py:505
  120.5 14.3 %collective-permute-start.22 = (bf16[4,2,256,128]{3,2,1,0:T(8,128)(2,1)S(1)}, bf16[4,2,256,128]{3,2,1,0:T(8,128)(2,1)S(1)}, u32[]{:S(2)}, u32[]{:S(2)}) collective-permute-start(bf16[4,2,256,128]{3,2,1,0:T(8,128)(2,1)S(1)} %get-tuple-element.129), channel_id=1, source_target_pairs={{0,2},{2,0},{1,3},{3,1},{4,6},{6,4},{5,7},{7,5},{8,10},{10,8},{9,1... | collective-permute-start | bytes 1572872 | tf_op jit(solution)/shard_map/ppermute | solution.py:505
  122.0 12.8 %collective-permute-start.21 = (bf16[2,256,128]{2,1,0:T(8,128)(2,1)S(1)}, bf16[2,256,128]{2,1,0:T(8,128)(2,1)S(1)}, u32[]{:S(2)}, u32[]{:S(2)}) collective-permute-start(bf16[2,256,128]{2,1,0:T(8,128)(2,1)S(1)} %get-tuple-element.128), channel_id=1, source_target_pairs={{0,12},{4,0},{8,4},{12,8},{1,13},{5,1},{9,5},{13,9},{2,14},{6,2},{... | collective-permute-start | bytes 393224 | tf_op jit(solution)/shard_map/ppermute | solution.py:510
  122.0 13.3 %collective-permute-start.20 = (bf16[2,256,128]{2,1,0:T(8,128)(2,1)S(1)}, bf16[2,256,128]{2,1,0:T(8,128)(2,1)S(1)}, u32[]{:S(2)}, u32[]{:S(2)}) collective-permute-start(bf16[2,256,128]{2,1,0:T(8,128)(2,1)S(1)} %get-tuple-element.125), channel_id=1, source_target_pairs={{0,8},{4,12},{8,0},{12,4},{1,9},{5,13},{9,1},{13,5},{2,10},{6,14},... | collective-permute-start | bytes 393224 | tf_op jit(solution)/shard_map/ppermute | solution.py:510
  123.2 12.2 %collective-permute-start.19 = (bf16[2,256,128]{2,1,0:T(8,128)(2,1)S(1)}, bf16[2,256,128]{2,1,0:T(8,128)(2,1)S(1)}, u32[]{:S(2)}, u32[]{:S(2)}) collective-permute-start(bf16[2,256,128]{2,1,0:T(8,128)(2,1)S(1)} %get-tuple-element.122), channel_id=1, source_target_pairs={{0,4},{4,8},{8,12},{12,0},{1,5},{5,9},{9,13},{13,1},{2,6},{6,10},{... | collective-permute-start | bytes 393224 | tf_op jit(solution)/shard_map/ppermute | solution.py:510
  135.4 14.2 %collective-permute-start.25 = (bf16[256,1024]{1,0:T(8,128)(2,1)S(1)}, bf16[256,1024]{1,0:T(8,128)(2,1)S(1)}, u32[]{:S(2)}, u32[]{:S(2)}) collective-permute-start(bf16[256,1024]{1,0:T(8,128)(2,1)S(1)} %send.2), channel_id=1, source_target_pairs={{0,2},{2,0},{1,3},{3,1},{4,6},{6,4},{5,7},{7,5},{8,10},{10,8},{9,1... | collective-permute-start | bytes 1572872 | tf_op jit(solution)/shard_map/ppermute | solution.py:505
  143.0 6.6 %copy-start.1 = (bf16[2048,1024]{1,0:T(8,128)(2,1)S(1)}, bf16[2048,1024]{1,0:T(8,128)(2,1)}, u32[]{:S(2)}) copy-start(bf16[2048,1024]{1,0:T(8,128)(2,1)} %refs_2_.3) | copy-start | bytes 12582916
  146.1 14.0 %collective-permute-start.24 = (bf16[256,1024]{1,0:T(8,128)(2,1)S(1)}, bf16[256,1024]{1,0:T(8,128)(2,1)S(1)}, u32[]{:S(2)}, u32[]{:S(2)}) collective-permute-start(bf16[256,1024]{1,0:T(8,128)(2,1)S(1)} %send.3), channel_id=1, source_target_pairs={{0,2},{2,0},{1,3},{3,1},{4,6},{6,4},{5,7},{7,5},{8,10},{10,8},{9,1... | collective-permute-start | bytes 1572872 | tf_op jit(solution)/shard_map/ppermute | solution.py:505

commit v9 on v8

--- a/solution.py
+++ b/solution.py
@@ -17,7 +17,7 @@
 GRANT = 16 * 2**20
 LITTLE = 12 * 2**20
 LARGE = 54 * 2**20
-PARTS = 4
+PARTS = 8
 HOP = 5*10**9
 
 

time: 163 us -> 163 us (level)
  no operation moved by 1% of the time
where the time goes in v9:
time: 163 us
  waiting for transfers between devices  71.7 us (44%)
  Pallas kernels  50.2 us (31%)
  starting transfers between devices  33.1 us (20%)
  local copies, waits for them, and re-layouts  7.12 us (4%)
    ppermute x14, waiting for transfers between devices, swap(): return lax.ppermute(array, axis, [(0, 1), (1, 0)])  36.6 us
    ppermute x12, waiting for transfers between devices, ahead(): lax.ppermute(array, 'seq', [(j, (j + offset) % chips) for j in range(chip...  35.1 us
    ppermute x12, starting transfers between devices, ahead(): lax.ppermute(array, 'seq', [(j, (j + offset) % chips) for j in range(chip...  20.4 us
    pallas_call x1, Pallas kernels, run_filter(): pl.pallas_call(functools.partial(levels_kernel, live, chips), out_shape=[...  13.2 us
    ppermute x14, starting transfers between devices, swap(): return lax.ppermute(array, axis, [(0, 1), (1, 0)])  12.7 us
    pallas_call x2, Pallas kernels, run_hidden(): pl.pallas_call(functools.partial(hidden_kernel, chips, min(512, channels)...  12.2 us
    pallas_call x2, Pallas kernels, run_send(): pl.pallas_call(send_kernel, in_specs=[pl.BlockSpec(memory_space=pltpu.SME...  5.87 us
    pallas_call x1, Pallas kernels, run_load(): pl.pallas_call(functools.partial(load_kernel, count), in_specs=[smem] + [...  4.59 us
  transfers between devices with their start and end apart: 26, of which 12 were waited for; matrix products, arithmetic and copies ran while one was open for 3% of the time, Pallas kernels for 24%

profile of v9, /device:TPU:0, one launch (start us, length us, event | category | flops | bytes accessed | tf_op | source)
XLA Modules:
  0.0 162.5 jit_solution(14458684759320070956)
XLA Ops:
  0.0 3.2 %pair.1 = bf16[2,512,1024]{2,1,0:T(8,128)(2,1)} custom-call(bf16[2048,1024]{1,0:T(8,128)(2,1)} %refs_1_.1, bf16[2048,1024]{1,0:T(8,128)(2,1)} %refs_2_.2), custom_call_target="tpu_custom_call" | custom-call | tf_op jit(solution)/shard_map/pair/pallas_call | solution.py:136
  3.2 3.0 %collective-permute-start.2 = (bf16[2,512,1024]{2,1,0:T(8,128)(2,1)}, bf16[2,512,1024]{2,1,0:T(8,128)(2,1)}, u32[]{:S(2)}, u32[]{:S(2)}) collective-permute-start(bf16[2,512,1024]{2,1,0:T(8,128)(2,1)} %pair.1), channel_id=1, source_target_pairs={{0,2},{2,0},{1,3},{3,1},{4,6},{6,4},{5,7},{7,5},{8,10},{10,8},{9,1... | collective-permute-start | bytes 6291464 | tf_op jit(solution)/shard_map/ppermute | solution.py:505
  6.2 1.2 constant_dynamic-slice_fusion.2
  7.4 2.6 %collective-permute-start.1 = (bf16[1024,256]{1,0:T(8,128)(2,1)}, bf16[1024,256]{1,0:T(8,128)(2,1)S(1)}, u32[]{:S(2)}, u32[]{:S(2)}) collective-permute-start(bf16[1024,256]{1,0:T(8,128)(2,1)} %get-tuple-element.80), channel_id=1, source_target_pairs={{0,8},{4,12},{8,0},{12,4},{1,9},{5,13},{9,1},{13,5},{2,10},{6,14},... | collective-permute-start | bytes 1572872 | tf_op jit(solution)/shard_map/ppermute | solution.py:510
  10.0 1.6 collective-permute-start
  11.6 2.2 %collective-permute-start.3 = (bf16[1024,256]{1,0:T(8,128)(2,1)}, bf16[1024,256]{1,0:T(8,128)(2,1)}, u32[]{:S(2)}, u32[]{:S(2)}) collective-permute-start(bf16[1024,256]{1,0:T(8,128)(2,1)} %get-tuple-element.84), channel_id=1, source_target_pairs={{0,12},{4,0},{8,4},{12,8},{1,13},{5,1},{9,5},{13,9},{2,14},{6,2},{... | collective-permute-start | bytes 1572872 | tf_op jit(solution)/shard_map/ppermute | solution.py:510
  13.8 3.2 %constant_dynamic-slice_fusion.1 = bf16[1024,1024]{1,0:T(8,128)(2,1)} fusion(bf16[2048,1024]{1,0:T(8,128)(2,1)} %refs_2_.3, s32[]{:T(128)S(6)} %select_n.47), kind=kLoop, calls=%fused_computation.11 | loop fusion | bytes 4194308 | tf_op jit(solution)/shard_map/dynamic_slice | solution.py:574
  17.0 28.6 %collective-permute-done.1.refs_1_ = bf16[1024,256]{1,0:T(8,128)(2,1)S(1)} collective-permute-done((bf16[1024,256]{1,0:T(8,128)(2,1)}, bf16[1024,256]{1,0:T(8,128)(2,1)S(1)}, u32[]{:S(2)}, u32[]{:S(2)}) %collective-permute-start.1) | collective-permute-done | bytes 524320 | tf_op jit(solution)/shard_map/ppermute | solution.py:510
  45.6 6.6 %collective-permute-done.2.refs_3_ = bf16[2,512,1024]{2,1,0:T(8,128)(2,1)} collective-permute-done((bf16[2,512,1024]{2,1,0:T(8,128)(2,1)}, bf16[2,512,1024]{2,1,0:T(8,128)(2,1)}, u32[]{:S(2)}, u32[]{:S(2)}) %collective-permute-start.2) | collective-permute-done | bytes 2097184 | tf_op jit(solution)/shard_map/ppermute | solution.py:505
  52.2 1.8 %collective-permute-start.12 = (bf16[2,512,1024]{2,1,0:T(8,128)(2,1)}, bf16[2,512,1024]{2,1,0:T(8,128)(2,1)}, u32[]{:S(2)}, u32[]{:S(2)}) collective-permute-start(bf16[2,512,1024]{2,1,0:T(8,128)(2,1)} %collective-permute-done.2.refs_3_), channel_id=1, source_target_pairs={{0,16},{16,0},{1,17},{17,1},{2,18},{18,2},{3,19},{19,3},{4,20},{20... | collective-permute-start | bytes 6291464 | tf_op jit(solution)/shard_map/ppermute | solution.py:505
  53.9 1.5 collective-permute-start.13
  55.5 2.1 %others.1 = bf16[3,1024,128]{2,1,0:T(8,128)(2,1)} custom-call(s32[5]{0:T(128)S(1)} %stack.49.place.refs_0_, bf16[1024,256]{1,0:T(8,128)(2,1)S(1)} %collective-permute-done.refs_0_, bf16[1024,256]{1,0:T(8,128)(2,1)S(1)} %collective-permute-done.1.refs_1_, bf16[1024,256]{1,0:T(8,128)(2,1)} %collective-permute-done.3.refs_2_), custom_call_target="tpu_custom_call" | custom-call | flops 5000000000 | tf_op jit(solution)/shard_map/others/pallas_call | solution.py:538
  57.6 0.8 copy-done.4
  58.6 0.6 collective-permute-start.4
  59.2 1.9 %collective-permute-done.4.refs_3_ = bf16[1024,128]{1,0:T(8,128)(2,1)S(1)} collective-permute-done((bf16[1024,128]{1,0:T(8,128)(2,1)S(1)}, bf16[1024,128]{1,0:T(8,128)(2,1)S(1)}, u32[]{:S(2)}, u32[]{:S(2)}) %collective-permute-start.4) | collective-permute-done | bytes 262176 | tf_op jit(solution)/shard_map/ppermute | solution.py:505
  61.1 1.0 copy-done.5
  62.2 13.2 %levels.1 = (bf16[4,512,128]{2,1,0:T(8,128)(2,1)S(1)}, bf16[4,512,128]{2,1,0:T(8,128)(2,1)S(1)}, bf16[4,512,128]{2,1,0:T(8,128)(2,1)S(1)}, bf16[4,512,128]{2,1,0:T(8,128)(2,1)S(1)}) custom-call(s32[5]{0:T(128)S(1)} %stack.49.place.refs_0_, f32[1,1024]{1,0:T(1,128)S(1)} %bitcast.21, f32[2,1024]{1,0:T(2,128)S(1)} %copy-done.7, f32[17,1024]{1,0:T(8,128)S(1)} %copy-done.6, ...), custom_call_target="tpu_custom_call" | custom-call | tf_op jit(solution)/shard_map/levels/pallas_call | solution.py:248
  75.6 0.4 collective-permute-start.7
  76.0 1.4 collective-permute-done.6.refs_2_
  77.4 0.7 collective-permute-done.7.refs_3_
  78.3 2.7 %collective-permute-start.10 = (bf16[2,512,128]{2,1,0:T(8,128)(2,1)S(1)}, bf16[2,512,128]{2,1,0:T(8,128)(2,1)S(1)}, u32[]{:S(2)}, u32[]{:S(2)}) collective-permute-start(bf16[2,512,128]{2,1,0:T(8,128)(2,1)S(1)} %get-tuple-element.98), channel_id=1, source_target_pairs={{0,8},{4,12},{8,0},{12,4},{1,9},{5,13},{9,1},{13,5},{2,10},{6,14},... | collective-permute-start | bytes 786440 | tf_op jit(solution)/shard_map/ppermute | solution.py:510
  81.0 1.3 collective-permute-start.11
  82.3 0.7 collective-permute-start.9
  83.0 17.5 %collective-permute-done.12.refs_4_ = bf16[2,512,1024]{2,1,0:T(8,128)(2,1)} collective-permute-done((bf16[2,512,1024]{2,1,0:T(8,128)(2,1)}, bf16[2,512,1024]{2,1,0:T(8,128)(2,1)}, u32[]{:S(2)}, u32[]{:S(2)}) %collective-permute-start.12) | collective-permute-done | bytes 2097184 | tf_op jit(solution)/shard_map/ppermute | solution.py:505
  100.5 1.5 collective-permute-done.13.mine
  102.3 1.6 collective-permute-start.17
  103.8 3.6 %collective-permute-start.16 = (bf16[2,256,128]{2,1,0:T(8,128)(2,1)S(1)}, bf16[2,256,128]{2,1,0:T(8,128)(2,1)S(1)}, u32[]{:S(2)}, u32[]{:S(2)}) collective-permute-start(bf16[2,256,128]{2,1,0:T(8,128)(2,1)S(1)} %get-tuple-element.108), channel_id=1, source_target_pairs={{0,12},{4,0},{8,4},{12,8},{1,13},{5,1},{9,5},{13,9},{2,14},{6,2},{... | collective-permute-start | bytes 393224 | tf_op jit(solution)/shard_map/ppermute | solution.py:510
  107.4 0.5 collective-permute-start.15
  108.0 2.0 %collective-permute-start.14 = (bf16[2,256,128]{2,1,0:T(8,128)(2,1)S(1)}, bf16[2,256,128]{2,1,0:T(8,128)(2,1)S(1)}, u32[]{:S(2)}, u32[]{:S(2)}) collective-permute-start(bf16[2,256,128]{2,1,0:T(8,128)(2,1)S(1)} %get-tuple-element.102), channel_id=1, source_target_pairs={{0,4},{4,8},{8,12},{12,0},{1,5},{5,9},{9,13},{13,1},{2,6},{6,10},{... | collective-permute-start | bytes 393224 | tf_op jit(solution)/shard_map/ppermute | solution.py:510
  110.0 4.6 %load.1 = (bf16[2048,1024]{1,0:T(8,128)(2,1)S(1)}, bf16[2048,1024]{1,0:T(8,128)(2,1)S(1)}, bf16[2,512,1024]{2,1,0:T(8,128)(2,1)S(1)}, bf16[2,512,1024]{2,1,0:T(8...) custom-call(s32[5]{0:T(128)S(1)} %stack.49.place.refs_0_, bf16[2048,1024]{1,0:T(8,128)(2,1)S(1)} %copy-done.2, ...), custom_call_target="tpu_custom_call" | custom-call | flops 99999997952 | tf_op jit(solution)/shard_map/load/pallas_call | solution.py:318
  114.6 5.9 %collective-permute-done.15.refs_2_ = bf16[2,256,128]{2,1,0:T(8,128)(2,1)S(1)} collective-permute-done((bf16[2,256,128]{2,1,0:T(8,128)(2,1)S(1)}, bf16[2,256,128]{2,1,0:T(8,128)(2,1)S(1)}, u32[]{:S(2)}, u32[]{:S(2)}) %collective-permute-start.15) | collective-permute-done | bytes 131104 | tf_op jit(solution)/shard_map/ppermute | solution.py:510
  120.6 1.6 collective-permute-start.22
  122.2 1.1 collective-permute-start.20
  123.3 2.0 %collective-permute-start.19 = (bf16[2,256,128]{2,1,0:T(8,128)(2,1)S(1)}, bf16[2,256,128]{2,1,0:T(8,128)(2,1)S(1)}, u32[]{:S(2)}, u32[]{:S(2)}) collective-permute-start(bf16[2,256,128]{2,1,0:T(8,128)(2,1)S(1)} %get-tuple-element.122), channel_id=1, source_target_pairs={{0,4},{4,8},{8,12},{12,0},{1,5},{5,9},{9,13},{13,1},{2,6},{6,10},{... | collective-permute-start | bytes 393224 | tf_op jit(solution)/shard_map/ppermute | solution.py:510
  125.3 6.1 %hidden.2.refs_0_ = bf16[256,2048]{1,0:T(8,128)(2,1)S(1)} custom-call(s32[5]{0:T(128)S(1)} %get-tuple-element.118.place, bf16[2,256,128]{2,1,0:T(8,128)(2,1)S(1)} %get-tuple-element.130.refs_0_, bf16[2,256,128]{2,1,0:T(8,128)(2,1)S(1)} %collective-permute-done.14.refs_1_, bf16[2,256,128]{2,1,0:T(8,128)(2,1)S(1)} %collective-permute-done.15.refs_2_, ...), custom_call_target="tpu_custom_call" | custom-call | tf_op jit(solution)/shard_map/hidden/pallas_call | solution.py:379
  131.5 2.9 %send.2 = bf16[256,1024]{1,0:T(8,128)(2,1)S(1)} custom-call(s32[5]{0:T(128)S(1)} %get-tuple-element.118.place, bf16[256,2048]{1,0:T(8,128)(2,1)S(1)} %hidden.2.refs_0_, bf16[1024,1024]{1,0:T(8,128)(2,1)} %collective-permute-done.13.mine, bf16[1024,1024]{1,0:T(8,128)(2,1)S(1)} %collective-permute-done.23.twin), custom_call_target="tpu_custom_call" | custom-call | tf_op jit(solution)/shard_map/send/pallas_call | solution.py:410
  134.3 0.7 collective-permute-done.22.refs_4_
  135.0 0.6 collective-permute-done.20.refs_2_
  135.6 1.5 collective-permute-start.25
  137.1 6.1 %hidden.3.refs_1_ = bf16[256,2048]{1,0:T(8,128)(2,1)S(1)} custom-call(s32[5]{0:T(128)S(1)} %get-tuple-element.118.place, bf16[2,256,128]{2,1,0:T(8,128)(2,1)S(1)} %get-tuple-element.142.refs_0_, bf16[2,256,128]{2,1,0:T(8,128)(2,1)S(1)} %collective-permute-done.19.refs_1_, bf16[2,256,128]{2,1,0:T(8,128)(2,1)S(1)} %collective-permute-done.20.refs_2_, ...), custom_call_target="tpu_custom_call" | custom-call | tf_op jit(solution)/shard_map/hidden/pallas_call | solution.py:379
  143.2 3.0 %send.3 = bf16[256,1024]{1,0:T(8,128)(2,1)S(1)} custom-call(s32[5]{0:T(128)S(1)} %get-tuple-element.118.place, bf16[256,2048]{1,0:T(8,128)(2,1)S(1)} %hidden.3.refs_1_, bf16[1024,1024]{1,0:T(8,128)(2,1)} %collective-permute-done.13.mine, bf16[1024,1024]{1,0:T(8,128)(2,1)S(1)} %collective-permute-done.23.twin), custom_call_target="tpu_custom_call" | custom-call | tf_op jit(solution)/shard_map/send/pallas_call | solution.py:410
  146.2 0.6 collective-permute-start.24
  146.8 0.6 slice.31.side
  147.4 2.4 %collective-permute-done.25.got = bf16[256,1024]{1,0:T(8,128)(2,1)S(1)} collective-permute-done((bf16[256,1024]{1,0:T(8,128)(2,1)S(1)}, bf16[256,1024]{1,0:T(8,128)(2,1)S(1)}, u32[]{:S(2)}, u32[]{:S(2)}) %collective-permute-start.25) | collective-permute-done | bytes 524320 | tf_op jit(solution)/shard_map/ppermute | solution.py:505
  149.8 4.4 %finish.1.kept = bf16[1024,1024]{1,0:T(8,128)(2,1)} custom-call(s32[1]{0:T(128)} %slice.31.side, bf16[256,2048]{1,0:T(8,128)(2,1)S(1)} %hidden.2.refs_0_, bf16[256,2048]{1,0:T(8,128)(2,1)S(1)} %hidden.3.refs_1_, bf16[2048,1024]{1,0:T(8,128)(2,1)S(1)} %copy-done.1, bf16[1024,1024]{1,0:T(8,128)(2,1)S(1)} %copy-done), custom_call_target="tpu_custom_call" | custom-call | flops 2147483648 | bytes 7340032 | tf_op jit(solution)/shard_map/finish/pallas_call | solution.py:433
  154.1 2.2 %add_far.2.kept = bf16[1024,1024]{1,0:T(8,128)(2,1)} custom-call(s32[1]{0:T(128)} %slice.31.side, bf16[256,1024]{1,0:T(8,128)(2,1)S(1)} %collective-permute-done.25.got, bf16[1024,1024]{1,0:T(8,128)(2,1)S(1)} %copy-done, bf16[1024,1024]{1,0:T(8,128)(2,1)} %finish.1.kept), custom_call_target="tpu_custom_call", output_to_operand_aliasing={{}: (3, {})} | custom-call | tf_op jit(solution)/shard_map/add_far/pallas_call | solution.py:482
  156.4 3.9 %collective-permute-done.24.got = bf16[256,1024]{1,0:T(8,128)(2,1)S(1)} collective-permute-done((bf16[256,1024]{1,0:T(8,128)(2,1)S(1)}, bf16[256,1024]{1,0:T(8,128)(2,1)S(1)}, u32[]{:S(2)}, u32[]{:S(2)}) %collective-permute-start.24) | collective-permute-done | bytes 524320 | tf_op jit(solution)/shard_map/ppermute | solution.py:505
  160.3 2.2 %add_far.3 = bf16[1024,1024]{1,0:T(8,128)(2,1)} custom-call(s32[1]{0:T(128)} %slice.31.side, bf16[256,1024]{1,0:T(8,128)(2,1)S(1)} %collective-permute-done.24.got, bf16[1024,1024]{1,0:T(8,128)(2,1)S(1)} %copy-done, bf16[1024,1024]{1,0:T(8,128)(2,1)} %add_far.2.kept), custom_call_target="tpu_custom_call", output_to_operand_aliasing={{}: (3, {})} | custom-call | tf_op jit(solution)/shard_map/add_far/pallas_call | solution.py:482
  (44 shorter events, 0.9 us)
Async XLA Ops:
  0.0 6.2 %copy-start = (bf16[1024,1024]{1,0:T(8,128)(2,1)S(1)}, bf16[1024,1024]{1,0:T(8,128)(2,1)}, u32[]{:S(2)}) copy-start(bf16[1024,1024]{1,0:T(8,128)(2,1)} %tokens.1) | copy-start | bytes 6291460
  3.2 49.0 %collective-permute-start.2 = (bf16[2,512,1024]{2,1,0:T(8,128)(2,1)}, bf16[2,512,1024]{2,1,0:T(8,128)(2,1)}, u32[]{:S(2)}, u32[]{:S(2)}) collective-permute-start(bf16[2,512,1024]{2,1,0:T(8,128)(2,1)} %pair.1), channel_id=1, source_target_pairs={{0,2},{2,0},{1,3},{3,1},{4,6},{6,4},{5,7},{7,5},{8,10},{10,8},{9,1... | collective-permute-start | bytes 6291464 | tf_op jit(solution)/shard_map/ppermute | solution.py:505
  7.4 38.2 %collective-permute-start.1 = (bf16[1024,256]{1,0:T(8,128)(2,1)}, bf16[1024,256]{1,0:T(8,128)(2,1)S(1)}, u32[]{:S(2)}, u32[]{:S(2)}) collective-permute-start(bf16[1024,256]{1,0:T(8,128)(2,1)} %get-tuple-element.80), channel_id=1, source_target_pairs={{0,8},{4,12},{8,0},{12,4},{1,9},{5,13},{9,1},{13,5},{2,10},{6,14},... | collective-permute-start | bytes 1572872 | tf_op jit(solution)/shard_map/ppermute | solution.py:510
  10.0 45.5 %collective-permute-start = (bf16[1024,256]{1,0:T(8,128)(2,1)}, bf16[1024,256]{1,0:T(8,128)(2,1)S(1)}, u32[]{:S(2)}, u32[]{:S(2)}) collective-permute-start(bf16[1024,256]{1,0:T(8,128)(2,1)} %get-tuple-element.79), channel_id=1, source_target_pairs={{0,4},{4,8},{8,12},{12,0},{1,5},{5,9},{9,13},{13,1},{2,6},{6,10},{... | collective-permute-start | bytes 1572872 | tf_op jit(solution)/shard_map/ppermute | solution.py:510
  11.6 43.9 %collective-permute-start.3 = (bf16[1024,256]{1,0:T(8,128)(2,1)}, bf16[1024,256]{1,0:T(8,128)(2,1)}, u32[]{:S(2)}, u32[]{:S(2)}) collective-permute-start(bf16[1024,256]{1,0:T(8,128)(2,1)} %get-tuple-element.84), channel_id=1, source_target_pairs={{0,12},{4,0},{8,4},{12,8},{1,13},{5,1},{9,5},{13,9},{2,14},{6,2},{... | collective-permute-start | bytes 1572872 | tf_op jit(solution)/shard_map/ppermute | solution.py:510
  52.2 26.1 %collective-permute-start.8 = (bf16[2,512,1024]{2,1,0:T(8,128)(2,1)}, bf16[2,512,1024]{2,1,0:T(8,128)(2,1)}, u32[]{:S(2)}, u32[]{:S(2)}) collective-permute-start(bf16[2,512,1024]{2,1,0:T(8,128)(2,1)} %collective-permute-done.2.refs_3_), channel_id=1, source_target_pairs={{0,1},{1,0},{2,3},{3,2},{4,5},{5,4},{6,7},{7,6},{8,9},{9,8},{10,11... | collective-permute-start | bytes 6291464 | tf_op jit(solution)/shard_map/ppermute | solution.py:505
  52.2 48.4 %collective-permute-start.12 = (bf16[2,512,1024]{2,1,0:T(8,128)(2,1)}, bf16[2,512,1024]{2,1,0:T(8,128)(2,1)}, u32[]{:S(2)}, u32[]{:S(2)}) collective-permute-start(bf16[2,512,1024]{2,1,0:T(8,128)(2,1)} %collective-permute-done.2.refs_3_), channel_id=1, source_target_pairs={{0,16},{16,0},{1,17},{17,1},{2,18},{18,2},{3,19},{19,3},{4,20},{20... | collective-permute-start | bytes 6291464 | tf_op jit(solution)/shard_map/ppermute | solution.py:505
  53.9 48.1 %collective-permute-start.13 = (bf16[1024,1024]{1,0:T(8,128)(2,1)}, bf16[1024,1024]{1,0:T(8,128)(2,1)}, u32[]{:S(2)}, u32[]{:S(2)}) collective-permute-start(bf16[1024,1024]{1,0:T(8,128)(2,1)} %constant_dynamic-slice_fusion.1), channel_id=1, source_target_pairs={{0,2},{2,0},{1,3},{3,1},{4,6},{6,4},{5,7},{7,5},{8,10},{10,8},{9,1... | collective-permute-start | bytes 6291464 | tf_op jit(solution)/shard_map/ppermute | solution.py:505
  55.5 5.6 %copy-start.6 = (f32[17,1024]{1,0:T(8,128)S(1)}, f32[17,1024]{1,0:T(8,128)}, u32[]{:S(2)}) copy-start(f32[17,1024]{1,0:T(8,128)} %mix_ref.1) | copy-start | bytes 208900
  55.5 5.6 %copy-start.7 = (f32[2,1024]{1,0:T(2,128)S(1)}, f32[2,1024]{1,0:T(2,128)}, u32[]{:S(2)}) copy-start(f32[2,1024]{1,0:T(2,128)} %high_ref.1) | copy-start | bytes 24580
  55.5 5.6 %copy-start.8 = (f32[1024]{0:T(1024)S(1)}, f32[1024]{0:T(1024)}, u32[]{:S(2)}) copy-start(f32[1024]{0:T(1024)} %param.8) | copy-start | bytes 12292
  57.6 0.8 copy-start.4
  58.4 2.7 %collective-permute-start.5 = (bf16[3,1024,128]{2,1,0:T(8,128)(2,1)}, bf16[3,1024,128]{2,1,0:T(8,128)(2,1)S(1)}, u32[]{:S(2)}, u32[]{:S(2)}) collective-permute-start(bf16[3,1024,128]{2,1,0:T(8,128)(2,1)} %others.1), channel_id=1, source_target_pairs={{0,1},{1,0},{2,3},{3,2},{4,5},{5,4},{6,7},{7,6},{8,9},{9,8},{10,11... | collective-permute-start | bytes 2359304 | tf_op jit(solution)/shard_map/ppermute | solution.py:505
  58.6 2.5 %collective-permute-start.4 = (bf16[1024,128]{1,0:T(8,128)(2,1)S(1)}, bf16[1024,128]{1,0:T(8,128)(2,1)S(1)}, u32[]{:S(2)}, u32[]{:S(2)}) collective-permute-start(bf16[1024,128]{1,0:T(8,128)(2,1)S(1)} %get-tuple-element.151), channel_id=1, source_target_pairs={{0,1},{1,0},{2,3},{3,2},{4,5},{5,4},{6,7},{7,6},{8,9},{9,8},{10,11... | collective-permute-start | bytes 786440 | tf_op jit(solution)/shard_map/ppermute | solution.py:505
  61.1 1.0 copy-start.5
  62.2 47.8 %copy-start.3 = (bf16[2048,1024]{1,0:T(8,128)(2,1)S(1)}, bf16[2048,1024]{1,0:T(8,128)(2,1)}, u32[]{:S(2)}) copy-start(bf16[2048,1024]{1,0:T(8,128)(2,1)} %refs_2_.2) | copy-start | bytes 12582916
  75.4 2.0 %collective-permute-start.6 = (bf16[4,512,128]{2,1,0:T(8,128)(2,1)S(1)}, bf16[4,512,128]{2,1,0:T(8,128)(2,1)S(1)}, u32[]{:S(2)}, u32[]{:S(2)}) collective-permute-start(bf16[4,512,128]{2,1,0:T(8,128)(2,1)S(1)} %get-tuple-element.87), channel_id=1, source_target_pairs={{0,1},{1,0},{2,3},{3,2},{4,5},{5,4},{6,7},{7,6},{8,9},{9,8},{10,11... | collective-permute-start | bytes 1572872 | tf_op jit(solution)/shard_map/ppermute | solution.py:505
  75.6 2.5 %collective-permute-start.7 = (bf16[4,512,128]{2,1,0:T(8,128)(2,1)S(1)}, bf16[4,512,128]{2,1,0:T(8,128)(2,1)S(1)}, u32[]{:S(2)}, u32[]{:S(2)}) collective-permute-start(bf16[4,512,128]{2,1,0:T(8,128)(2,1)S(1)} %get-tuple-element.88), channel_id=1, source_target_pairs={{0,1},{1,0},{2,3},{3,2},{4,5},{5,4},{6,7},{7,6},{8,9},{9,8},{10,11... | collective-permute-start | bytes 1572872 | tf_op jit(solution)/shard_map/ppermute | solution.py:505
  78.3 23.7 %collective-permute-start.10 = (bf16[2,512,128]{2,1,0:T(8,128)(2,1)S(1)}, bf16[2,512,128]{2,1,0:T(8,128)(2,1)S(1)}, u32[]{:S(2)}, u32[]{:S(2)}) collective-permute-start(bf16[2,512,128]{2,1,0:T(8,128)(2,1)S(1)} %get-tuple-element.98), channel_id=1, source_target_pairs={{0,8},{4,12},{8,0},{12,4},{1,9},{5,13},{9,1},{13,5},{2,10},{6,14},... | collective-permute-start | bytes 786440 | tf_op jit(solution)/shard_map/ppermute | solution.py:510
  81.0 21.0 %collective-permute-start.11 = (bf16[2,512,128]{2,1,0:T(8,128)(2,1)S(1)}, bf16[2,512,128]{2,1,0:T(8,128)(2,1)S(1)}, u32[]{:S(2)}, u32[]{:S(2)}) collective-permute-start(bf16[2,512,128]{2,1,0:T(8,128)(2,1)S(1)} %get-tuple-element.99), channel_id=1, source_target_pairs={{0,12},{4,0},{8,4},{12,8},{1,13},{5,1},{9,5},{13,9},{2,14},{6,2},{... | collective-permute-start | bytes 786440 | tf_op jit(solution)/shard_map/ppermute | solution.py:510
  82.3 19.8 %collective-permute-start.9 = (bf16[2,512,128]{2,1,0:T(8,128)(2,1)S(1)}, bf16[2,512,128]{2,1,0:T(8,128)(2,1)S(1)}, u32[]{:S(2)}, u32[]{:S(2)}) collective-permute-start(bf16[2,512,128]{2,1,0:T(8,128)(2,1)S(1)} %get-tuple-element.97), channel_id=1, source_target_pairs={{0,4},{4,8},{8,12},{12,0},{1,5},{5,9},{9,13},{13,1},{2,6},{6,10},{... | collective-permute-start | bytes 786440 | tf_op jit(solution)/shard_map/ppermute | solution.py:510
  102.0 8.0 %copy-start.2 = (bf16[2048,1024]{1,0:T(8,128)(2,1)S(1)}, bf16[2048,1024]{1,0:T(8,128)(2,1)}, u32[]{:S(2)}) copy-start(bf16[2048,1024]{1,0:T(8,128)(2,1)} %refs_1_.1) | copy-start | bytes 12582916
  102.3 18.3 %collective-permute-start.17 = (bf16[4,2,256,128]{3,2,1,0:T(8,128)(2,1)S(1)}, bf16[4,2,256,128]{3,2,1,0:T(8,128)(2,1)S(1)}, u32[]{:S(2)}, u32[]{:S(2)}) collective-permute-start(bf16[4,2,256,128]{3,2,1,0:T(8,128)(2,1)S(1)} %get-tuple-element.114), channel_id=1, source_target_pairs={{0,2},{2,0},{1,3},{3,1},{4,6},{6,4},{5,7},{7,5},{8,10},{10,8},{9,1... | collective-permute-start | bytes 1572872 | tf_op jit(solution)/shard_map/ppermute | solution.py:505
  103.8 16.7 %collective-permute-start.18 = (bf16[2,512,1024]{2,1,0:T(8,128)(2,1)}, bf16[2,512,1024]{2,1,0:T(8,128)(2,1)S(1)}, u32[]{:S(2)}, u32[]{:S(2)}) collective-permute-start(bf16[2,512,1024]{2,1,0:T(8,128)(2,1)} %collective-permute-done.12.refs_4_), channel_id=1, source_target_pairs={{0,1},{1,0},{2,3},{3,2},{4,5},{5,4},{6,7},{7,6},{8,9},{9,8},{10,11... | collective-permute-start | bytes 6291464 | tf_op jit(solution)/shard_map/ppermute | solution.py:505
  103.8 10.8 %collective-permute-start.16 = (bf16[2,256,128]{2,1,0:T(8,128)(2,1)S(1)}, bf16[2,256,128]{2,1,0:T(8,128)(2,1)S(1)}, u32[]{:S(2)}, u32[]{:S(2)}) collective-permute-start(bf16[2,256,128]{2,1,0:T(8,128)(2,1)S(1)} %get-tuple-element.108), channel_id=1, source_target_pairs={{0,12},{4,0},{8,4},{12,8},{1,13},{5,1},{9,5},{13,9},{2,14},{6,2},{... | collective-permute-start | bytes 393224 | tf_op jit(solution)/shard_map/ppermute | solution.py:510
  107.4 13.1 %collective-permute-start.15 = (bf16[2,256,128]{2,1,0:T(8,128)(2,1)S(1)}, bf16[2,256,128]{2,1,0:T(8,128)(2,1)S(1)}, u32[]{:S(2)}, u32[]{:S(2)}) collective-permute-start(bf16[2,256,128]{2,1,0:T(8,128)(2,1)S(1)} %get-tuple-element.105), channel_id=1, source_target_pairs={{0,8},{4,12},{8,0},{12,4},{1,9},{5,13},{9,1},{13,5},{2,10},{6,14},... | collective-permute-start | bytes 393224 | tf_op jit(solution)/shard_map/ppermute | solution.py:510
  108.0 12.6 %collective-permute-start.14 = (bf16[2,256,128]{2,1,0:T(8,128)(2,1)S(1)}, bf16[2,256,128]{2,1,0:T(8,128)(2,1)S(1)}, u32[]{:S(2)}, u32[]{:S(2)}) collective-permute-start(bf16[2,256,128]{2,1,0:T(8,128)(2,1)S(1)} %get-tuple-element.102), channel_id=1, source_target_pairs={{0,4},{4,8},{8,12},{12,0},{1,5},{5,9},{9,13},{13,1},{2,6},{6,10},{... | collective-permute-start | bytes 393224 | tf_op jit(solution)/shard_map/ppermute | solution.py:510
  120.6 10.9 %collective-permute-start.23 = (bf16[1024,1024]{1,0:T(8,128)(2,1)}, bf16[1024,1024]{1,0:T(8,128)(2,1)S(1)}, u32[]{:S(2)}, u32[]{:S(2)}) collective-permute-start(bf16[1024,1024]{1,0:T(8,128)(2,1)} %collective-permute-done.13.mine), channel_id=1, source_target_pairs={{0,1},{1,0},{2,3},{3,2},{4,5},{5,4},{6,7},{7,6},{8,9},{9,8},{10,11... | collective-permute-start | bytes 6291464 | tf_op jit(solution)/shard_map/ppermute | solution.py:505
  120.6 14.3 %collective-permute-start.22 = (bf16[4,2,256,128]{3,2,1,0:T(8,128)(2,1)S(1)}, bf16[4,2,256,128]{3,2,1,0:T(8,128)(2,1)S(1)}, u32[]{:S(2)}, u32[]{:S(2)}) collective-permute-start(bf16[4,2,256,128]{3,2,1,0:T(8,128)(2,1)S(1)} %get-tuple-element.129), channel_id=1, source_target_pairs={{0,2},{2,0},{1,3},{3,1},{4,6},{6,4},{5,7},{7,5},{8,10},{10,8},{9,1... | collective-permute-start | bytes 1572872 | tf_op jit(solution)/shard_map/ppermute | solution.py:505
  122.2 12.8 %collective-permute-start.21 = (bf16[2,256,128]{2,1,0:T(8,128)(2,1)S(1)}, bf16[2,256,128]{2,1,0:T(8,128)(2,1)S(1)}, u32[]{:S(2)}, u32[]{:S(2)}) collective-permute-start(bf16[2,256,128]{2,1,0:T(8,128)(2,1)S(1)} %get-tuple-element.128), channel_id=1, source_target_pairs={{0,12},{4,0},{8,4},{12,8},{1,13},{5,1},{9,5},{13,9},{2,14},{6,2},{... | collective-permute-start | bytes 393224 | tf_op jit(solution)/shard_map/ppermute | solution.py:510
  122.2 13.3 %collective-permute-start.20 = (bf16[2,256,128]{2,1,0:T(8,128)(2,1)S(1)}, bf16[2,256,128]{2,1,0:T(8,128)(2,1)S(1)}, u32[]{:S(2)}, u32[]{:S(2)}) collective-permute-start(bf16[2,256,128]{2,1,0:T(8,128)(2,1)S(1)} %get-tuple-element.125), channel_id=1, source_target_pairs={{0,8},{4,12},{8,0},{12,4},{1,9},{5,13},{9,1},{13,5},{2,10},{6,14},... | collective-permute-start | bytes 393224 | tf_op jit(solution)/shard_map/ppermute | solution.py:510
  123.3 12.2 %collective-permute-start.19 = (bf16[2,256,128]{2,1,0:T(8,128)(2,1)S(1)}, bf16[2,256,128]{2,1,0:T(8,128)(2,1)S(1)}, u32[]{:S(2)}, u32[]{:S(2)}) collective-permute-start(bf16[2,256,128]{2,1,0:T(8,128)(2,1)S(1)} %get-tuple-element.122), channel_id=1, source_target_pairs={{0,4},{4,8},{8,12},{12,0},{1,5},{5,9},{9,13},{13,1},{2,6},{6,10},{... | collective-permute-start | bytes 393224 | tf_op jit(solution)/shard_map/ppermute | solution.py:510
  135.6 14.2 %collective-permute-start.25 = (bf16[256,1024]{1,0:T(8,128)(2,1)S(1)}, bf16[256,1024]{1,0:T(8,128)(2,1)S(1)}, u32[]{:S(2)}, u32[]{:S(2)}) collective-permute-start(bf16[256,1024]{1,0:T(8,128)(2,1)S(1)} %send.2), channel_id=1, source_target_pairs={{0,2},{2,0},{1,3},{3,1},{4,6},{6,4},{5,7},{7,5},{8,10},{10,8},{9,1... | collective-permute-start | bytes 1572872 | tf_op jit(solution)/shard_map/ppermute | solution.py:505
  143.2 6.6 %copy-start.1 = (bf16[2048,1024]{1,0:T(8,128)(2,1)S(1)}, bf16[2048,1024]{1,0:T(8,128)(2,1)}, u32[]{:S(2)}) copy-start(bf16[2048,1024]{1,0:T(8,128)(2,1)} %refs_2_.3) | copy-start | bytes 12582916
  146.2 14.0 %collective-permute-start.24 = (bf16[256,1024]{1,0:T(8,128)(2,1)S(1)}, bf16[256,1024]{1,0:T(8,128)(2,1)S(1)}, u32[]{:S(2)}, u32[]{:S(2)}) collective-permute-start(bf16[256,1024]{1,0:T(8,128)(2,1)S(1)} %send.3), channel_id=1, source_target_pairs={{0,2},{2,0},{1,3},{3,1},{4,6},{6,4},{5,7},{7,5},{8,10},{10,8},{9,1... | collective-permute-start | bytes 1572872 | tf_op jit(solution)/shard_map/ppermute | solution.py:505
